TPU v7x, 512 devices: a whole 4x4x16 slice. The times are simulated.
512 devices in a mesh: dp: 128 (over x_hi, z, y), fsdp: 4 (over x_lo, core).
Axes of the slice: x: 4 (x_hi: 2, x_lo: 2; x = x_hi * 2 + x_lo), y: 4, z: 16, core: 2. Of those that a mesh axis runs over, the one named last changes fastest.
Arguments:
- layer_input: bfloat16 [65536, 2048], P(('dp', 'fsdp')), may hold values from -1.1953125 to 1.1953125
- queries: bfloat16 [65536, 2048], P(('dp', 'fsdp')), may hold values from -16 to 16
- key_vectors: bfloat16 [65536, 2048], P(('dp', 'fsdp')), may hold values from -16 to 16
- value_vectors: bfloat16 [65536, 2048], P(('dp', 'fsdp')), may hold values from -6 to 6
- output_grad: bfloat16 [65536, 2048], P(('dp', 'fsdp')), may hold values from -96 to 96
- partner_offsets: int32 [128, 2], P('dp'), may hold values from -2 to 2, as said below
Outputs:
- weight_grad: bfloat16 [128, 2048, 2048], P('dp', 'fsdp')
- value_grad: bfloat16 [65536, 2048], P(('dp', 'fsdp'))
Inputs may be any that keep to these rules, and one draw needn't show every extreme that they name: `partner_offsets`: each replica's 2 offsets are distinct and nonzero.
All inputs are finite; a program needn't handle non-finite values.
Results may differ from a plain program's by a relative error of at most 0.0086.
Values may be sent and summed in bfloat16 or wider, within the bound.
No kernel may reach another device: no remote copies, remote signals or barrier semaphores. Data moves between devices by JAX's collectives and lax.ppermute only.
A program may use at most 64 MiB of HBM per device.

v0:
```python
import jax
import jax.numpy as jnp
from jax import lax
from jax.sharding import PartitionSpec as P

HD = 128
HOPS = 2
PARTNERS = 2


def shifted(value, axis, steps):
    count = lax.axis_size(axis)
    pairs = [(source, (source + steps) % count) for source in range(count)]
    return lax.ppermute(value, axis, pairs)


def added_bf(running, extra):
    return (running.astype(jnp.float32) + extra.astype(jnp.float32)).astype(jnp.bfloat16)


def local(layer_input, queries, key_vectors, value_vectors, output_grad, partner_offsets):
    row_count = queries.shape[0]
    feature_count = queries.shape[1]
    head_count = feature_count // HD
    scaling = HD ** (-0.5)
    query_heads = queries.reshape(row_count, head_count, HD)
    grads_heads = output_grad.reshape(row_count, head_count, HD)
    stacked = jnp.stack([key_vectors, value_vectors])
    offsets_list = []
    for stride in range(1, HOPS + 1):
        offsets_list = offsets_list + [stride, -stride]
    fetched = {}
    for partner_hop in offsets_list:
        fetched[partner_hop] = shifted(stacked, "dp", -partner_hop)
    my_offsets = partner_offsets[0]
    selected = []
    for slot_index in range(PARTNERS):
        chosen_block = jnp.zeros_like(stacked)
        for partner_hop in offsets_list:
            chosen_block = jnp.where(
                my_offsets[slot_index] == partner_hop, fetched[partner_hop], chosen_block
            )
        selected.append(chosen_block)
    all_keys = jnp.concatenate([key_vectors] + [block[0] for block in selected], 0)
    all_values = jnp.concatenate([value_vectors] + [block[1] for block in selected], 0)
    key_count = all_keys.shape[0]
    keys_heads = all_keys.reshape(key_count, head_count, HD)
    value_heads = all_values.reshape(key_count, head_count, HD)
    causal = jnp.arange(row_count)[None, :] <= jnp.arange(row_count)[:, None]
    allowed = jnp.concatenate([causal, jnp.ones((row_count, key_count - row_count), dtype=bool)], 1)
    scores = (
        jnp.einsum("qhd,khd->hqk", query_heads, keys_heads, preferred_element_type=jnp.float32)
        * scaling
    )
    scores = jnp.where(allowed, scores, -jnp.inf)
    probs = jax.nn.softmax(scores, axis=-1)
    probs_bf = probs.astype(jnp.bfloat16)
    attended = jnp.einsum("hqk,khd->qhd", probs_bf, value_heads, preferred_element_type=jnp.float32)
    row_delta = jnp.sum(grads_heads.astype(jnp.float32) * attended, -1).T
    prob_grad = jnp.einsum(
        "qhd,khd->hqk", grads_heads, value_heads, preferred_element_type=jnp.float32
    )
    score_grad = (probs * (prob_grad - row_delta[..., None]) * scaling).astype(jnp.bfloat16)
    key_part = jnp.einsum(
        "hqk,qhd->khd", score_grad, query_heads, preferred_element_type=jnp.float32
    ).reshape(key_count, feature_count)
    value_part = jnp.einsum(
        "hqk,qhd->khd", probs_bf, grads_heads, preferred_element_type=jnp.float32
    ).reshape(key_count, feature_count)
    key_total = key_part[:row_count]
    value_total = value_part[:row_count]
    partner_parts = []
    for slot_index in range(PARTNERS):
        low = (slot_index + 1) * row_count
        partner_parts.append(
            jnp.stack([key_part[low : low + row_count], value_part[low : low + row_count]]).astype(
                jnp.bfloat16
            )
        )
    parts = {}
    for partner_hop in offsets_list:
        routed = jnp.zeros((2, row_count, feature_count), jnp.bfloat16)
        for slot_index in range(PARTNERS):
            routed = jnp.where(
                my_offsets[slot_index] == partner_hop, partner_parts[slot_index], routed
            )
        parts[partner_hop] = routed
    arrived = {}
    for partner_hop in offsets_list:
        arrived[partner_hop] = shifted(parts[partner_hop], "dp", partner_hop)
    upper = arrived[HOPS]
    lower = arrived[-HOPS]
    stride = 1
    upper = added_bf(upper, arrived[stride])
    lower = added_bf(lower, arrived[-stride])
    key_total = key_total + upper[0].astype(jnp.float32) + lower[0].astype(jnp.float32)
    value_total = value_total + upper[1].astype(jnp.float32) + lower[1].astype(jnp.float32)
    value_grad = value_total.astype(jnp.bfloat16)
    key_grad = key_total.astype(jnp.bfloat16)
    slice_width = layer_input.shape[1] // lax.axis_size("fsdp")
    mine = lax.axis_index("fsdp")
    inputs_part = lax.all_gather(layer_input, "fsdp", axis=0, tiled=True)
    grads_part = lax.all_gather(key_grad, "fsdp", axis=0, tiled=True)
    columns = lax.dynamic_slice_in_dim(inputs_part, mine * slice_width, slice_width, 1)
    weight_sum = lax.dot_general(
        columns, grads_part, (((0,), (0,)), ((), ())), preferred_element_type=jnp.float32
    )
    return (weight_sum.astype(jnp.bfloat16)[None], value_grad)


def solution(mesh):
    return jax.shard_map(
        local,
        mesh=mesh,
        in_specs=(
            P(("dp", "fsdp"), None),
            P(("dp", "fsdp"), None),
            P(("dp", "fsdp"), None),
            P(("dp", "fsdp"), None),
            P(("dp", "fsdp"), None),
            P("dp", None),
        ),
        out_specs=(P("dp", "fsdp", None), P(("dp", "fsdp"), None)),
        check_vma=False,
    )
```

profile of v0, /device:TPU:1, one launch (start us, length us, event | category | flops | bytes accessed | tf_op | source)
XLA Modules:
  0.0 267.1 jit_solution(5037570329192057170)
XLA Ops:
  7.2 0.0 copy-start.5
  7.2 0.0 copy-start
  7.2 0.0 all-gather.3.cloned.1.call-start
  7.2 1.4 copy.49
  8.6 1.3 copy.51
  9.9 0.1 pad_maximum_fusion.1
  10.0 5.7 %collective-permute-start = (bf16[2,128,2048]{1,2,0:T(8,128)(2,1)S(1)}, bf16[2,128,2048]{1,2,0:T(8,128)(2,1)}, u32[]{:S(2)}, u32[]{:S(2)}) collective-permute-start(bf16[2,128,2048]{1,2,0:T(8,128)(2,1)S(1)} %pad_maximum_fusion.1), channel_id=1, source_target_pairs={{0,8},{4,12},{8,16},{12,20},{16,24},{20,28},{24,32},{28,36},{32,40... | collective-permute-start | bytes 3145736 | tf_op jit(solution)/shard_map/ppermute | solution.py:14
  15.7 13.3 %collective-permute-start.1 = (bf16[2,128,2048]{1,2,0:T(8,128)(2,1)S(1)}, bf16[2,128,2048]{1,2,0:T(8,128)(2,1)}, u32[]{:S(2)}, u32[]{:S(2)}) collective-permute-start(bf16[2,128,2048]{1,2,0:T(8,128)(2,1)S(1)} %pad_maximum_fusion.1), channel_id=1, source_target_pairs={{0,504},{4,508},{8,0},{12,4},{16,8},{20,12},{24,16},{28,20},{32,24... | collective-permute-start | bytes 3145736 | tf_op jit(solution)/shard_map/ppermute | solution.py:14
  29.0 2.3 collective-permute-start.2
  31.3 8.7 %collective-permute-start.3 = (bf16[2,128,2048]{1,2,0:T(8,128)(2,1)S(1)}, bf16[2,128,2048]{1,2,0:T(8,128)(2,1)}, u32[]{:S(2)}, u32[]{:S(2)}) collective-permute-start(bf16[2,128,2048]{1,2,0:T(8,128)(2,1)S(1)} %pad_maximum_fusion.1), channel_id=1, source_target_pairs={{0,508},{4,0},{8,4},{12,8},{16,12},{20,16},{24,20},{28,24},{32,28}... | collective-permute-start | bytes 3145736 | tf_op jit(solution)/shard_map/ppermute | solution.py:14
  40.0 0.0 all-gather.3.cloned.1.call-update
  40.1 0.0 all-gather.5.cloned.1.call-start
  40.1 0.0 copy-done.5
  40.1 0.6 fusion.34
  45.9 0.3 copy.52
  46.2 0.0 copy-done
  46.2 0.3 copy.77
  46.5 1.0 copy.57
  47.5 2.1 copy.60
  49.6 8.2 %collective-permute-done = bf16[2,128,2048]{1,2,0:T(8,128)(2,1)} collective-permute-done((bf16[2,128,2048]{1,2,0:T(8,128)(2,1)S(1)}, bf16[2,128,2048]{1,2,0:T(8,128)(2,1)}, u32[]{:S(2)}, u32[]{:S(2)}) %collective-permute-start) | collective-permute-done | bytes 1048608 | tf_op jit(solution)/shard_map/ppermute | solution.py:14
  57.8 27.6 %collective-permute-done.1 = bf16[2,128,2048]{1,2,0:T(8,128)(2,1)} collective-permute-done((bf16[2,128,2048]{1,2,0:T(8,128)(2,1)S(1)}, bf16[2,128,2048]{1,2,0:T(8,128)(2,1)}, u32[]{:S(2)}, u32[]{:S(2)}) %collective-permute-start.1) | collective-permute-done | bytes 1048608 | tf_op jit(solution)/shard_map/ppermute | solution.py:14
  85.3 0.0 collective-permute-done.2
  85.3 15.1 %collective-permute-done.3 = bf16[2,128,2048]{1,2,0:T(8,128)(2,1)} collective-permute-done((bf16[2,128,2048]{1,2,0:T(8,128)(2,1)S(1)}, bf16[2,128,2048]{1,2,0:T(8,128)(2,1)}, u32[]{:S(2)}, u32[]{:S(2)}) %collective-permute-start.3) | collective-permute-done | bytes 1048608 | tf_op jit(solution)/shard_map/ppermute | solution.py:14
  100.5 2.4 select_select_fusion.5
  102.9 0.9 fusion.32
  103.9 0.3 copy.53
  104.2 1.3 copy.54
  105.5 1.0 copy.58
  106.5 1.0 copy.59
  107.5 0.6 fusion.5
  108.1 0.0 copy-start.2
  108.1 0.9 fusion.35
  109.0 0.1 copy-done.2
  109.1 0.0 copy-start.1
  109.1 0.0 copy-start.3
  109.1 0.0 copy-start.4
  109.1 2.4 fusion.36
  111.6 0.2 copy-done.6
  111.8 0.0 copy-done.1
  111.8 0.0 copy-done.3
  111.8 0.0 copy-done.4
  111.8 0.8 fusion.16
  112.6 5.8 %fusion.37 = (bf16[384,16,128]{0,2,1:T(8,128)(2,1)}, f32[384,16,128]{0,2,1:T(8,128)}) fusion(bf16[128,16,128]{0,2,1:T(8,128)(2,1)S(1)} %bitcast.99, bf16[128,16,128]{0,2,1:T(8,128)(2,1)S(1)} %bitcast.106, f32[16,128]{1,0:T(8,128)S(1)} %bitcast.107, f32[16,128,384]{1,2,0:T(8,128)} %copy-done.6, f32[16,128]{1,0:T(8,128)S(1)} %get-tuple-element.25, ...), kind=kOutput, calls=%fused_computation.63 | convolution fusion | flops 412090368 | bytes 10502144 | tf_op jit(solution)/shard_map/hqk,qhd->khd/dot_general | solution.py:64
  118.4 1.3 fusion.30
  119.6 0.3 fusion.31
  119.9 0.3 select_select_fusion.3
  120.3 8.5 %collective-permute-start.4 = (bf16[2,128,2048]{1,2,0:T(8,128)(2,1)S(1)}, bf16[2,128,2048]{1,2,0:T(8,128)(2,1)S(1)}, u32[]{:S(2)}, u32[]{:S(2)}) collective-permute-start(bf16[2,128,2048]{1,2,0:T(8,128)(2,1)S(1)} %get-tuple-element.12), channel_id=1, source_target_pairs={{0,8},{4,12},{8,16},{12,20},{16,24},{20,28},{24,32},{28,36},{32,40... | collective-permute-start | bytes 3145736 | tf_op jit(solution)/shard_map/ppermute | solution.py:14
  128.8 3.6 %collective-permute-start.5 = (bf16[2,128,2048]{1,2,0:T(8,128)(2,1)S(1)}, bf16[2,128,2048]{1,2,0:T(8,128)(2,1)S(1)}, u32[]{:S(2)}, u32[]{:S(2)}) collective-permute-start(bf16[2,128,2048]{1,2,0:T(8,128)(2,1)S(1)} %get-tuple-element.13), channel_id=1, source_target_pairs={{0,4},{4,8},{8,12},{12,16},{16,20},{20,24},{24,28},{28,32},{32,36}... | collective-permute-start | bytes 3145736 | tf_op jit(solution)/shard_map/ppermute | solution.py:14
  132.4 0.2 select_select_fusion
  132.6 12.3 %collective-permute-start.6 = (bf16[2,128,2048]{1,2,0:T(8,128)(2,1)S(1)}, bf16[2,128,2048]{1,2,0:T(8,128)(2,1)S(1)}, u32[]{:S(2)}, u32[]{:S(2)}) collective-permute-start(bf16[2,128,2048]{1,2,0:T(8,128)(2,1)S(1)} %get-tuple-element.14), channel_id=1, source_target_pairs={{0,504},{4,508},{8,0},{12,4},{16,8},{20,12},{24,16},{28,20},{32,24... | collective-permute-start | bytes 3145736 | tf_op jit(solution)/shard_map/ppermute | solution.py:14
  144.9 3.7 %collective-permute-start.7 = (bf16[2,128,2048]{1,2,0:T(8,128)(2,1)S(1)}, bf16[2,128,2048]{1,2,0:T(8,128)(2,1)S(1)}, u32[]{:S(2)}, u32[]{:S(2)}) collective-permute-start(bf16[2,128,2048]{1,2,0:T(8,128)(2,1)S(1)} %select_select_fusion), channel_id=1, source_target_pairs={{0,508},{4,0},{8,4},{12,8},{16,12},{20,16},{24,20},{28,24},{32,28}... | collective-permute-start | bytes 3145736 | tf_op jit(solution)/shard_map/ppermute | solution.py:14
  148.6 1.3 slice.100
  149.9 1.3 slice.107
  151.2 18.5 %collective-permute-done.4 = bf16[2,128,2048]{1,2,0:T(8,128)(2,1)S(1)} collective-permute-done((bf16[2,128,2048]{1,2,0:T(8,128)(2,1)S(1)}, bf16[2,128,2048]{1,2,0:T(8,128)(2,1)S(1)}, u32[]{:S(2)}, u32[]{:S(2)}) %collective-permute-start.4) | collective-permute-done | bytes 1048608 | tf_op jit(solution)/shard_map/ppermute | solution.py:14
  169.7 22.5 %collective-permute-done.5 = bf16[2,128,2048]{1,2,0:T(8,128)(2,1)S(1)} collective-permute-done((bf16[2,128,2048]{1,2,0:T(8,128)(2,1)S(1)}, bf16[2,128,2048]{1,2,0:T(8,128)(2,1)S(1)}, u32[]{:S(2)}, u32[]{:S(2)}) %collective-permute-start.5) | collective-permute-done | bytes 1048608 | tf_op jit(solution)/shard_map/ppermute | solution.py:14
  192.1 0.3 add_convert_fusion.1
  192.4 11.3 %collective-permute-done.6 = bf16[2,128,2048]{1,2,0:T(8,128)(2,1)S(1)} collective-permute-done((bf16[2,128,2048]{1,2,0:T(8,128)(2,1)S(1)}, bf16[2,128,2048]{1,2,0:T(8,128)(2,1)S(1)}, u32[]{:S(2)}, u32[]{:S(2)}) %collective-permute-start.6) | collective-permute-done | bytes 1048608 | tf_op jit(solution)/shard_map/ppermute | solution.py:14
  203.7 5.2 %collective-permute-done.7 = bf16[2,128,2048]{1,2,0:T(8,128)(2,1)S(1)} collective-permute-done((bf16[2,128,2048]{1,2,0:T(8,128)(2,1)S(1)}, bf16[2,128,2048]{1,2,0:T(8,128)(2,1)S(1)}, u32[]{:S(2)}, u32[]{:S(2)}) %collective-permute-start.7) | collective-permute-done | bytes 1048608 | tf_op jit(solution)/shard_map/ppermute | solution.py:14
  208.9 0.3 add_convert_fusion
  209.2 1.1 fusion.17
  210.3 0.0 all-gather.5.cloned.1.call-update
  210.3 1.0 copy.69
  211.4 44.5 %all-gather.5.cloned.1.call-done = bf16[512,2048]{0,1:T(8,128)(2,1)} async-done(((bf16[128,2048]{0,1:T(8,128)(2,1)}), bf16[512,2048]{0,1:T(8,128)(2,1)}) %all-gather.5.cloned.1.call-update) | async-done | bytes 2097168 | tf_op jit(solution)/shard_map/all_gather | solution.py:103
  255.8 4.4 %fusion.3 = bf16[1,512,2048]{2,1,0:T(8,128)(2,1)} fusion(bf16[512,2048]{0,1:T(8,128)(2,1)} %all-gather.5.cloned.1.call-done, bf16[512,2048]{1,0:T(8,128)(2,1)} %all-gather.3.cloned.1.call-done, s32[]{:T(128)S(6)} %select_n.89), kind=kOutput, calls=%fused_computation.7 | convolution fusion | flops 1074790400 | bytes 4718596 | tf_op jit(solution)/shard_map/dot_general | solution.py:105
  (4 shorter events, 0.0 us)
Async XLA Ops:
  7.2 32.9 %copy-start.5 = (s32[1,2]{1,0:T(1,128)S(1)}, s32[1,2]{1,0:T(1,128)}, u32[]{:S(2)}) copy-start(s32[1,2]{1,0:T(1,128)} %param.11) | copy-start | bytes 28
  7.2 39.0 %copy-start = (bf16[128,2048]{1,0:T(8,128)(2,1)S(1)}, bf16[128,2048]{1,0:T(8,128)(2,1)}, u32[]{:S(2)}) copy-start(bf16[128,2048]{1,0:T(8,128)(2,1)} %param.7) | copy-start | bytes 1572868
  7.2 204.2 %all-gather.3.cloned.1.call-start = ((), (), s32[]{:S(2)}) async-start(), calls=%async_computation | async-start | bytes 2621440 | tf_op jit(solution)/shard_map/all_gather | solution.py:102
  10.0 47.7 %collective-permute-start = (bf16[2,128,2048]{1,2,0:T(8,128)(2,1)S(1)}, bf16[2,128,2048]{1,2,0:T(8,128)(2,1)}, u32[]{:S(2)}, u32[]{:S(2)}) collective-permute-start(bf16[2,128,2048]{1,2,0:T(8,128)(2,1)S(1)} %pad_maximum_fusion.1), channel_id=1, source_target_pairs={{0,8},{4,12},{8,16},{12,20},{16,24},{20,28},{24,32},{28,36},{32,40... | collective-permute-start | bytes 3145736 | tf_op jit(solution)/shard_map/ppermute | solution.py:14
  15.7 69.7 %collective-permute-start.1 = (bf16[2,128,2048]{1,2,0:T(8,128)(2,1)S(1)}, bf16[2,128,2048]{1,2,0:T(8,128)(2,1)}, u32[]{:S(2)}, u32[]{:S(2)}) collective-permute-start(bf16[2,128,2048]{1,2,0:T(8,128)(2,1)S(1)} %pad_maximum_fusion.1), channel_id=1, source_target_pairs={{0,504},{4,508},{8,0},{12,4},{16,8},{20,12},{24,16},{28,20},{32,24... | collective-permute-start | bytes 3145736 | tf_op jit(solution)/shard_map/ppermute | solution.py:14
  29.0 56.3 %collective-permute-start.2 = (bf16[2,128,2048]{1,2,0:T(8,128)(2,1)S(1)}, bf16[2,128,2048]{1,2,0:T(8,128)(2,1)}, u32[]{:S(2)}, u32[]{:S(2)}) collective-permute-start(bf16[2,128,2048]{1,2,0:T(8,128)(2,1)S(1)} %pad_maximum_fusion.1), channel_id=1, source_target_pairs={{0,4},{4,8},{8,12},{12,16},{16,20},{20,24},{24,28},{28,32},{32,36}... | collective-permute-start | bytes 3145736 | tf_op jit(solution)/shard_map/ppermute | solution.py:14
  31.3 69.2 %collective-permute-start.3 = (bf16[2,128,2048]{1,2,0:T(8,128)(2,1)S(1)}, bf16[2,128,2048]{1,2,0:T(8,128)(2,1)}, u32[]{:S(2)}, u32[]{:S(2)}) collective-permute-start(bf16[2,128,2048]{1,2,0:T(8,128)(2,1)S(1)} %pad_maximum_fusion.1), channel_id=1, source_target_pairs={{0,508},{4,0},{8,4},{12,8},{16,12},{20,16},{24,20},{28,24},{32,28}... | collective-permute-start | bytes 3145736 | tf_op jit(solution)/shard_map/ppermute | solution.py:14
  40.1 215.8 %all-gather.5.cloned.1.call-start = ((), (), s32[]{:S(2)}) async-start(), calls=%async_computation.1 | async-start | bytes 2621440 | tf_op jit(solution)/shard_map/all_gather | solution.py:103
  108.1 1.0 copy-start.2
  109.0 2.7 %copy-start.6 = (f32[16,128,384]{1,2,0:T(8,128)}, f32[16,128,384]{1,2,0:T(8,128)S(1)}, u32[]{:S(2)}) copy-start(f32[16,128,384]{1,2,0:T(8,128)S(1)} %get-tuple-element.26) | copy-start | bytes 9437188
  109.1 2.7 copy-start.1
  109.1 2.7 copy-start.3
  109.1 2.7 copy-start.4
  120.3 49.4 %collective-permute-start.4 = (bf16[2,128,2048]{1,2,0:T(8,128)(2,1)S(1)}, bf16[2,128,2048]{1,2,0:T(8,128)(2,1)S(1)}, u32[]{:S(2)}, u32[]{:S(2)}) collective-permute-start(bf16[2,128,2048]{1,2,0:T(8,128)(2,1)S(1)} %get-tuple-element.12), channel_id=1, source_target_pairs={{0,8},{4,12},{8,16},{12,20},{16,24},{20,28},{24,32},{28,36},{32,40... | collective-permute-start | bytes 3145736 | tf_op jit(solution)/shard_map/ppermute | solution.py:14
  128.8 63.4 %collective-permute-start.5 = (bf16[2,128,2048]{1,2,0:T(8,128)(2,1)S(1)}, bf16[2,128,2048]{1,2,0:T(8,128)(2,1)S(1)}, u32[]{:S(2)}, u32[]{:S(2)}) collective-permute-start(bf16[2,128,2048]{1,2,0:T(8,128)(2,1)S(1)} %get-tuple-element.13), channel_id=1, source_target_pairs={{0,4},{4,8},{8,12},{12,16},{16,20},{20,24},{24,28},{28,32},{32,36}... | collective-permute-start | bytes 3145736 | tf_op jit(solution)/shard_map/ppermute | solution.py:14
  132.6 71.2 %collective-permute-start.6 = (bf16[2,128,2048]{1,2,0:T(8,128)(2,1)S(1)}, bf16[2,128,2048]{1,2,0:T(8,128)(2,1)S(1)}, u32[]{:S(2)}, u32[]{:S(2)}) collective-permute-start(bf16[2,128,2048]{1,2,0:T(8,128)(2,1)S(1)} %get-tuple-element.14), channel_id=1, source_target_pairs={{0,504},{4,508},{8,0},{12,4},{16,8},{20,12},{24,16},{28,20},{32,24... | collective-permute-start | bytes 3145736 | tf_op jit(solution)/shard_map/ppermute | solution.py:14
  144.9 64.0 %collective-permute-start.7 = (bf16[2,128,2048]{1,2,0:T(8,128)(2,1)S(1)}, bf16[2,128,2048]{1,2,0:T(8,128)(2,1)S(1)}, u32[]{:S(2)}, u32[]{:S(2)}) collective-permute-start(bf16[2,128,2048]{1,2,0:T(8,128)(2,1)S(1)} %select_select_fusion), channel_id=1, source_target_pairs={{0,508},{4,0},{8,4},{12,8},{16,12},{20,16},{24,20},{28,24},{32,28}... | collective-permute-start | bytes 3145736 | tf_op jit(solution)/shard_map/ppermute | solution.py:14
Sparse Core Ops, SparseCore 0:
  40.2 28.7 all-gather.2
  210.5 45.3 all-gather.4
where the time goes:
time: 268 us; the launch traced here: 267 us
  waiting for transfers between devices  153 us (57%)
  starting transfers between devices  58.2 us (22%)
  between operations  19.5 us (7%)
  local copies, waits for them, and re-layouts  17 us (6%)
  matrix products  14 us (5%)
  other arithmetic  5.69 us (2%)
    ppermute x8, waiting for transfers between devices, shifted(): return lax.ppermute(value, axis, pairs)  108 us
    ppermute x8, starting transfers between devices, shifted(): return lax.ppermute(value, axis, pairs)  58.1 us
    all_gather x1, waiting for transfers between devices, local(): grads_part = lax.all_gather(key_grad, 'fsdp', axis=0, tiled=True)  44.5 us
    unnamed x18, local copies, waits for them, and re-layouts  6.08 us
    dot_general x1, matrix products, local(): jnp.einsum('hqk,qhd->khd', score_grad, query_heads, preferred_element_typ...  5.78 us
  transfers between devices with their start and end apart: 10, of which 8 were waited for; matrix products, arithmetic and copies ran while one was open for 11% of the time, Pallas kernels for 0%

commit v1 on v0

v1 whole, which is shorter than its diff:
```python
import functools

import jax
import jax.numpy as jnp
from jax import lax
from jax.experimental import pallas as pl
from jax.experimental.pallas import tpu as pltpu
from jax.sharding import PartitionSpec as P

HD = 128
DOCS = (0, 1, -1, 2, -2)
HOPS = 2
GROUP = 4
STEP = 4
TILE = 8
FAR = 1e30


def shifted(value, axis, steps):
    count = lax.axis_size(axis)
    pairs = [(source, (source + steps) % count) for source in range(count)]
    return lax.ppermute(value, axis, pairs)


def swapped(value, axis, mask):
    pairs = [(source, source ^ mask) for source in range(lax.axis_size(axis))]
    return lax.ppermute(value, axis, pairs)


def dot_nt(a, b):
    return lax.dot_general(a, b, (((1,), (1,)), ((), ())), preferred_element_type=jnp.float32)


def dot_nn(a, b):
    return lax.dot_general(a, b, (((1,), (0,)), ((), ())), preferred_element_type=jnp.float32)


def scores_of(keys, query_rows):
    scores = dot_nt(keys, query_rows) * (HD ** (-0.5))
    rows = keys.shape[0]
    own = scores[:, :rows]
    key_at = lax.broadcasted_iota(jnp.int32, own.shape, 0)
    query_at = lax.broadcasted_iota(jnp.int32, own.shape, 1)
    own = jnp.where(key_at <= query_at, own, -FAR)
    return jnp.concatenate([own, scores[:, rows:]], 1)


def head_rows(refs, head):
    return jnp.concatenate([ref[:, head * HD : (head + 1) * HD] for ref in refs], 0)


def stats_kernel(offsets_ref, keys_ref, values_ref, *refs):
    count = len(DOCS)
    query_refs, grad_refs, out_ref = refs[:count], refs[count : 2 * count], refs[2 * count]
    rows = keys_ref.shape[0]
    step = pl.program_id(0)
    base = pl.multiple_of(step * (count * TILE), TILE)
    for head in range(STEP):
        cols = slice(head * HD, (head + 1) * HD)
        scores = scores_of(keys_ref[:, cols], head_rows(query_refs, head))
        prob_grad = dot_nt(values_ref[:, cols], head_rows(grad_refs, head))
        top = jnp.max(scores, 0, keepdims=True)
        weights = jnp.exp(scores - top)
        total = jnp.sum(weights, 0, keepdims=True)
        mean = jnp.sum(weights * prob_grad, 0, keepdims=True) / total
        lse = top + jnp.log(total)
        for doc in range(count):
            cut = slice(doc * rows, (doc + 1) * rows)
            out_ref[pl.ds(base + doc * TILE + head, 1), :] = lse[:, cut]
            out_ref[pl.ds(base + doc * TILE + STEP + head, 1), :] = mean[:, cut]

    @pl.when(step == 0)
    def _():
        tail = out_ref.shape[0] - TILE
        for slot in range(2):
            value = offsets_ref[0, slot].astype(jnp.float32)
            low = tail + slot * STEP
            out_ref[low : low + STEP, :] = jnp.full((STEP, rows), value, jnp.float32)


def merged(stat_refs, me, step, stride):
    def tile(place, row):
        start = pl.multiple_of(place * stride + row, TILE)
        return stat_refs[pl.ds(start, TILE), :]

    count = len(DOCS)
    lse_rows, delta_rows = [], []
    for doc in DOCS:
        owner = me + GROUP + doc
        offsets = tile(owner, stride - TILE)
        first, second = offsets[:STEP], offsets[STEP:]
        parts = []
        for hop in DOCS:
            low = step * (count * TILE) + DOCS.index(-hop) * TILE
            stat = tile(owner + hop, low)
            lse, mean = stat[:STEP], stat[STEP:]
            if hop:
                lse = jnp.where((first == hop) | (second == hop), lse, -FAR)
            parts.append((lse, mean))
        top = functools.reduce(jnp.maximum, [lse for lse, _ in parts])
        weights = [jnp.exp(lse - top) for lse, _ in parts]
        total = sum(weights)
        delta = sum(weight * mean for weight, (_, mean) in zip(weights, parts)) / total
        lse = top + jnp.log(total)
        if doc:
            lse = jnp.where((first == -doc) | (second == -doc), lse, FAR)
        lse_rows.append(lse)
        delta_rows.append(delta)
    return jnp.concatenate(lse_rows, 1), jnp.concatenate(delta_rows, 1)


def grads_kernel(first_step, place_ref, stat_ref, keys_ref, values_ref, *refs):
    count = len(DOCS)
    query_refs, grad_refs = refs[:count], refs[count : 2 * count]
    key_out, value_out = refs[2 * count :]
    step = pl.program_id(0) + first_step
    stride = stat_ref.shape[0] // (3 * GROUP)
    lse, delta = merged(stat_ref, place_ref[0], step, stride)
    for head in range(STEP):
        cols = slice(head * HD, (head + 1) * HD)
        query_rows = head_rows(query_refs, head)
        grad_rows = head_rows(grad_refs, head)
        scores = scores_of(keys_ref[:, cols], query_rows)
        prob_grad = dot_nt(values_ref[:, cols], grad_rows)
        probs = jnp.exp(scores - lse[head : head + 1])
        score_grad = probs * (prob_grad - delta[head : head + 1]) * (HD ** (-0.5))
        key_total = dot_nn(score_grad.astype(jnp.bfloat16), query_rows)
        value_total = dot_nn(probs.astype(jnp.bfloat16), grad_rows)
        key_out[:, cols] = key_total.astype(jnp.bfloat16)
        value_out[:, cols] = value_total.astype(jnp.bfloat16)


def weight_kernel(inputs_ref, *refs):
    grads = jnp.concatenate([ref[...] for ref in refs[:-1]], 0)
    refs[-1][...] = dot_nn(inputs_ref[...], grads).astype(jnp.bfloat16)


def local(layer_input, queries, key_vectors, value_vectors, output_grad, partner_offsets):
    rows, features = queries.shape
    steps = features // (HD * STEP)
    wide = STEP * HD
    mine = lax.axis_index("fsdp")
    places = lax.axis_size("fsdp")
    inputs_all = lax.all_gather(layer_input, "fsdp", axis=0, tiled=True)

    by_doc = {0: (queries, output_grad)}
    up_q, down_q = shifted(queries, "dp", -1), shifted(queries, "dp", 1)
    up_g, down_g = shifted(output_grad, "dp", -1), shifted(output_grad, "dp", 1)
    by_doc[1], by_doc[-1] = (up_q, up_g), (down_q, down_g)
    by_doc[2] = shifted(up_q, "dp", -1), shifted(up_g, "dp", -1)
    by_doc[-2] = shifted(down_q, "dp", 1), shifted(down_g, "dp", 1)
    query_docs = [by_doc[doc][0] for doc in DOCS]
    grad_docs = [by_doc[doc][1] for doc in DOCS]

    width = layer_input.shape[1] // places
    grad_docs[-1], inputs_all = lax.optimization_barrier((grad_docs[-1], inputs_all))
    columns = lax.dynamic_slice_in_dim(inputs_all, mine * width, width, 1)
    columns = columns.reshape(places, rows, width)
    columns = jnp.concatenate(
        [lax.dynamic_index_in_dim(columns, mine ^ k, 0, False) for k in range(places)], 0
    )
    columns = columns.T

    block = pl.BlockSpec((rows, wide), lambda step: (0, step))
    docs = len(DOCS)
    stat_rows = steps * docs * TILE + TILE
    pair = rows * rows * docs * HD * 2
    stats = pl.pallas_call(
        stats_kernel,
        grid=(steps,),
        in_specs=[pl.BlockSpec(memory_space=pltpu.SMEM)] + [block] * (2 + 2 * docs),
        out_specs=pl.BlockSpec((stat_rows, rows), lambda step: (0, 0)),
        out_shape=jax.ShapeDtypeStruct((stat_rows, rows), jnp.float32),
        compiler_params=pltpu.CompilerParams(vmem_limit_bytes=40 << 20),
        cost_estimate=pl.CostEstimate(
            flops=2 * pair * features // HD,
            bytes_accessed=12 * rows * features * 2,
            transcendentals=rows * rows * docs * features // HD,
        ),
        name="stats",
    )(partner_offsets, key_vectors, value_vectors, *query_docs, *grad_docs)

    replicas = lax.axis_size("dp")
    groups = [list(range(low, low + GROUP)) for low in range(0, replicas, GROUP)]
    here = lax.all_gather(stats, "dp", axis=0, tiled=True, axis_index_groups=groups)
    below = shifted(here, "dp", GROUP)
    above = shifted(here, "dp", -GROUP)
    stat_all = jnp.concatenate([below, here, above], 0)
    place = (lax.axis_index("dp") % GROUP).astype(jnp.int32).reshape(1)

    halves = 2
    each = steps // halves
    key_parts, value_parts = [], []
    for half in range(halves):
        low = half * each
        shifted_block = pl.BlockSpec((rows, wide), lambda step, low=low: (0, step + low))
        key_grad, value_grad = pl.pallas_call(
            functools.partial(grads_kernel, low),
            grid=(each,),
            in_specs=[
                pl.BlockSpec(memory_space=pltpu.SMEM),
                pl.BlockSpec(stat_all.shape, lambda step: (0, 0)),
            ]
            + [shifted_block] * (2 + 2 * docs),
            out_specs=[block] * 2,
            out_shape=[jax.ShapeDtypeStruct((rows, each * wide), jnp.bfloat16)] * 2,
            compiler_params=pltpu.CompilerParams(vmem_limit_bytes=40 << 20),
            cost_estimate=pl.CostEstimate(
                flops=4 * pair * features // HD // halves,
                bytes_accessed=14 * rows * features * 2 // halves,
                transcendentals=rows * rows * docs * features // HD // halves,
            ),
            name="grads",
        )(place, stat_all, key_vectors, value_vectors, *query_docs, *grad_docs)
        key_parts.append(key_grad)
        value_parts.append(value_grad)

    weight = None
    full = jax.ShapeDtypeStruct((width, features), jnp.bfloat16)
    for half in range(halves):
        own = key_parts[half]
        across = swapped(own, "fsdp", 2)
        pieces = [own, swapped(own, "fsdp", 1), across, swapped(across, "fsdp", 1)]
        low = half * each
        extra, alias = [], {}
        if weight is not None:
            extra, alias = [weight], {1 + len(pieces): 0}

        def body(inputs_ref, *refs, count=len(pieces)):
            weight_kernel(inputs_ref, *refs[:count], refs[-1])

        weight = pl.pallas_call(
            body,
            grid=(each,),
            in_specs=[pl.BlockSpec(columns.shape, lambda step: (0, 0))]
            + [block] * len(pieces)
            + [pl.BlockSpec(memory_space=pl.ANY)] * len(extra),
            out_specs=pl.BlockSpec((width, wide), lambda step, low=low: (0, step + low)),
            out_shape=full,
            input_output_aliases=alias,
            compiler_params=pltpu.CompilerParams(vmem_limit_bytes=40 << 20),
            cost_estimate=pl.CostEstimate(
                flops=2 * width * columns.shape[1] * each * wide,
                bytes_accessed=2 * each * wide * (columns.shape[1] + width),
                transcendentals=0,
            ),
            name="weight",
        )(columns, *pieces, *extra)
    return weight[None], jnp.concatenate(value_parts, 1)


def solution(mesh):
    return jax.shard_map(
        local,
        mesh=mesh,
        in_specs=(
            P(("dp", "fsdp"), None),
            P(("dp", "fsdp"), None),
            P(("dp", "fsdp"), None),
            P(("dp", "fsdp"), None),
            P(("dp", "fsdp"), None),
            P("dp", None),
        ),
        out_specs=(P("dp", "fsdp", None), P(("dp", "fsdp"), None)),
        check_vma=False,
    )
```

time: 268 us -> 175 us (0.65)
  waiting for transfers between devices: 153 us -> 35.9 us
  Pallas kernels: 0 us -> 17.8 us
  blocking collectives: 0 us -> 16.2 us
  matrix products: 14 us -> 0 us
  starting transfers between devices: 58.2 us -> 72.1 us
  between operations: 19.5 us -> 14.4 us
  other arithmetic: 5.69 us -> 0.89 us
    ppermute x8 -> x10, waiting for transfers between devices: 108 us -> 35.2 us  [shifted(): return lax.ppermute(value, axis, pairs)]
    all_gather x2 -> x1, waiting for transfers between devices: 44.5 us -> 0.02 us  [local(): inputs_all = lax.all_gather(layer_input, 'fsdp', axis=0, tiled=True)]
    ppermute x0 -> x6, starting transfers between devices: none -> 18.6 us  [swapped(): return lax.ppermute(value, axis, pairs)]
    pallas_call x0 -> x5, Pallas kernels: none -> 17.8 us  [the longest x2 8.16 us: local(): pl.pallas_call(functools.partial(grads_kernel, low), grid=(each,), in_spe...]
    all_gather x0 -> x1, blocking collectives: none -> 16.2 us  [local(): lax.all_gather(stats, 'dp', axis=0, tiled=True, axis_index_groups=groups)]
    dot_general x5 -> x0, matrix products: 14 us -> none  [the longest x1 5.78 us: local(): jnp.einsum('hqk,qhd->khd', score_grad, query_heads, preferred_element_typ...]
    unnamed x18 -> x44, local copies, waits for them, and re-layouts: 6.08 us -> 13.9 us
    slice x6 -> x0, local copies, waits for them, and re-layouts: 5.66 us -> none  [the longest x1 1.3 us: local(): key_total = key_part[:row_count]]
  transfers between devices with their start and end apart: 10 -> 17, of which waited for: 8 -> 6; matrix products, arithmetic and copies ran while one was open for 11% -> 2% of each run, Pallas kernels for 0% -> 4%
where the time goes in v1:
time: 175 us; the launch traced here: 174 us
  starting transfers between devices  72.1 us (41%)
  waiting for transfers between devices  35.9 us (21%)
  Pallas kernels  17.8 us (10%)
  local copies, waits for them, and re-layouts  16.5 us (9%)
  blocking collectives  16.2 us (9%)
  between operations  14.4 us (8%)
    ppermute x10, starting transfers between devices, shifted(): return lax.ppermute(value, axis, pairs)  53.5 us
    ppermute x10, waiting for transfers between devices, shifted(): return lax.ppermute(value, axis, pairs)  35.2 us
    ppermute x6, starting transfers between devices, swapped(): return lax.ppermute(value, axis, pairs)  18.6 us
    all_gather x1, blocking collectives, local(): lax.all_gather(stats, 'dp', axis=0, tiled=True, axis_index_groups=groups)  16.2 us
    unnamed x44, local copies, waits for them, and re-layouts  13.9 us
    pallas_call x2, Pallas kernels, local(): pl.pallas_call(functools.partial(grads_kernel, low), grid=(each,), in_spe...  8.16 us
    pallas_call x2, Pallas kernels, local(): pl.pallas_call(body, grid=(each,), in_specs=[pl.BlockSpec(columns.shape,...  5.23 us
    pallas_call x1, Pallas kernels, local(): pl.pallas_call(stats_kernel, grid=(steps,), in_specs=[pl.BlockSpec(memory...  4.36 us
  transfers between devices with their start and end apart: 17, of which 6 were waited for; matrix products, arithmetic and copies ran while one was open for 2% of the time, Pallas kernels for 4%

profile of v1, /device:TPU:1, one launch (start us, length us, event | category | flops | bytes accessed | tf_op | source)
XLA Modules:
  0.0 173.8 jit_solution(8501753088898442363)
XLA Ops:
  7.2 0.0 all-gather.2.cloned.1.call-start
  7.2 0.7 all-gather.2.cloned.1.call-update
  7.9 4.0 %collective-permute-start = (bf16[128,2048]{1,0:T(8,128)(2,1)}, bf16[128,2048]{1,0:T(8,128)(2,1)S(1)}, u32[]{:S(2)}, u32[]{:S(2)}) collective-permute-start(bf16[128,2048]{1,0:T(8,128)(2,1)} %refs_5_.5), channel_id=1, source_target_pairs={{0,4},{4,8},{8,12},{12,16},{16,20},{20,24},{24,28},{28,32},{32,36}... | collective-permute-start | bytes 1572872 | tf_op jit(solution)/shard_map/ppermute | solution.py:22
  11.9 3.2 %collective-permute-start.3 = (bf16[128,2048]{1,0:T(8,128)(2,1)}, bf16[128,2048]{1,0:T(8,128)(2,1)S(1)}, u32[]{:S(2)}, u32[]{:S(2)}) collective-permute-start(bf16[128,2048]{1,0:T(8,128)(2,1)} %refs_0_.5), channel_id=1, source_target_pairs={{0,4},{4,8},{8,12},{12,16},{16,20},{20,24},{24,28},{28,32},{32,36}... | collective-permute-start | bytes 1572872 | tf_op jit(solution)/shard_map/ppermute | solution.py:22
  15.2 13.5 %collective-permute-start.2 = (bf16[128,2048]{1,0:T(8,128)(2,1)}, bf16[128,2048]{1,0:T(8,128)(2,1)S(1)}, u32[]{:S(2)}, u32[]{:S(2)}) collective-permute-start(bf16[128,2048]{1,0:T(8,128)(2,1)} %refs_0_.5), channel_id=1, source_target_pairs={{0,508},{4,0},{8,4},{12,8},{16,12},{20,16},{24,20},{28,24},{32,28}... | collective-permute-start | bytes 1572872 | tf_op jit(solution)/shard_map/ppermute | solution.py:22
  28.6 3.4 %collective-permute-start.6 = (bf16[128,2048]{1,0:T(8,128)(2,1)}, bf16[128,2048]{1,0:T(8,128)(2,1)S(1)}, u32[]{:S(2)}, u32[]{:S(2)}) collective-permute-start(bf16[128,2048]{1,0:T(8,128)(2,1)} %refs_5_.5), channel_id=1, source_target_pairs={{0,508},{4,0},{8,4},{12,8},{16,12},{20,16},{24,20},{28,24},{32,28}... | collective-permute-start | bytes 1572872 | tf_op jit(solution)/shard_map/ppermute | solution.py:22
  32.0 4.6 %collective-permute-done.refs_7_ = bf16[128,2048]{1,0:T(8,128)(2,1)S(1)} collective-permute-done((bf16[128,2048]{1,0:T(8,128)(2,1)}, bf16[128,2048]{1,0:T(8,128)(2,1)S(1)}, u32[]{:S(2)}, u32[]{:S(2)}) %collective-permute-start) | collective-permute-done | bytes 524320 | tf_op jit(solution)/shard_map/ppermute | solution.py:22
  36.6 1.9 %collective-permute-start.1 = (bf16[128,2048]{1,0:T(8,128)(2,1)S(1)}, bf16[128,2048]{1,0:T(8,128)(2,1)S(1)}, u32[]{:S(2)}, u32[]{:S(2)}) collective-permute-start(bf16[128,2048]{1,0:T(8,128)(2,1)S(1)} %collective-permute-done.refs_7_), channel_id=1, source_target_pairs={{0,4},{4,8},{8,12},{12,16},{16,20},{20,24},{24,28},{28,32},{32,36}... | collective-permute-start | bytes 1572872 | tf_op jit(solution)/shard_map/ppermute | solution.py:22
  38.5 9.4 %collective-permute-done.3.refs_2_ = bf16[128,2048]{1,0:T(8,128)(2,1)S(1)} collective-permute-done((bf16[128,2048]{1,0:T(8,128)(2,1)}, bf16[128,2048]{1,0:T(8,128)(2,1)S(1)}, u32[]{:S(2)}, u32[]{:S(2)}) %collective-permute-start.3) | collective-permute-done | bytes 524320 | tf_op jit(solution)/shard_map/ppermute | solution.py:22
  47.9 1.9 %collective-permute-start.5 = (bf16[128,2048]{1,0:T(8,128)(2,1)S(1)}, bf16[128,2048]{1,0:T(8,128)(2,1)S(1)}, u32[]{:S(2)}, u32[]{:S(2)}) collective-permute-start(bf16[128,2048]{1,0:T(8,128)(2,1)S(1)} %collective-permute-done.3.refs_2_), channel_id=1, source_target_pairs={{0,4},{4,8},{8,12},{12,16},{16,20},{20,24},{24,28},{28,32},{32,36}... | collective-permute-start | bytes 1572872 | tf_op jit(solution)/shard_map/ppermute | solution.py:22
  49.8 9.1 %collective-permute-start.4 = (bf16[128,2048]{1,0:T(8,128)(2,1)S(1)}, bf16[128,2048]{1,0:T(8,128)(2,1)}, u32[]{:S(2)}, u32[]{:S(2)}) collective-permute-start(bf16[128,2048]{1,0:T(8,128)(2,1)S(1)} %collective-permute-done.2.refs_1_), channel_id=1, source_target_pairs={{0,508},{4,0},{8,4},{12,8},{16,12},{20,16},{24,20},{28,24},{32,28}... | collective-permute-start | bytes 1572872 | tf_op jit(solution)/shard_map/ppermute | solution.py:22
  58.9 1.9 %collective-permute-start.7 = (bf16[128,2048]{1,0:T(8,128)(2,1)S(1)}, bf16[128,2048]{1,0:T(8,128)(2,1)}, u32[]{:S(2)}, u32[]{:S(2)}) collective-permute-start(bf16[128,2048]{1,0:T(8,128)(2,1)S(1)} %collective-permute-done.6.refs_6_), channel_id=1, source_target_pairs={{0,508},{4,0},{8,4},{12,8},{16,12},{20,16},{24,20},{28,24},{32,28}... | collective-permute-start | bytes 1572872 | tf_op jit(solution)/shard_map/ppermute | solution.py:22
  60.9 0.0 all-gather.2.cloned.1.call-done
  60.9 9.5 %collective-permute-done.5.refs_4_ = bf16[128,2048]{1,0:T(8,128)(2,1)S(1)} collective-permute-done((bf16[128,2048]{1,0:T(8,128)(2,1)S(1)}, bf16[128,2048]{1,0:T(8,128)(2,1)S(1)}, u32[]{:S(2)}, u32[]{:S(2)}) %collective-permute-start.5) | collective-permute-done | bytes 524320 | tf_op jit(solution)/shard_map/ppermute | solution.py:22
  70.4 0.0 collective-permute-done.4.refs_3_
  70.4 8.7 %collective-permute-done.7.refs_8_ = bf16[128,2048]{1,0:T(8,128)(2,1)} collective-permute-done((bf16[128,2048]{1,0:T(8,128)(2,1)S(1)}, bf16[128,2048]{1,0:T(8,128)(2,1)}, u32[]{:S(2)}, u32[]{:S(2)}) %collective-permute-start.7) | collective-permute-done | bytes 524320 | tf_op jit(solution)/shard_map/ppermute | solution.py:22
  79.0 1.0 copy-done
  80.1 1.0 copy-done.2
  81.1 1.0 copy-done.4
  82.2 1.0 copy-done.6
  83.2 0.7 copy-done.20
  83.9 4.4 %stats.1 = f32[168,128]{1,0:T(8,128)S(1)} custom-call(s32[1,2]{1,0:T(1,128)S(1)} %copy-done.20, bf16[128,2048]{1,0:T(8,128)(2,1)S(1)} %copy-done, bf16[128,2048]{1,0:T(8,128)(2,1)S(1)} %copy-done.2, bf16[128,2048]{1,0:T(8,128)(2,1)S(1)} %copy-done.4, bf16[128,2048]{1,0:T(8,128)(2,1)S(1)} %collective-permute-done.2.refs_1_, ...), custom_call_target="tpu_custom_call" | custom-call | flops 671088640 | bytes 6291456 | tf_op jit(solution)/shard_map/stats/pallas_call | solution.py:168
  88.2 0.0 copy-start.8
  88.2 0.8 copy-done.8
  89.0 0.8 copy-done.10
  89.8 0.8 copy-done.12
  90.6 0.8 copy-done.14
  91.4 16.2 %all_gather.7 = f32[672,128]{1,0:T(8,128)S(1)} all-gather(f32[168,128]{1,0:T(8,128)S(1)} %stats.1), channel_id=1, replica_groups={{0,4,8,12},{16,20,24,28},{32,36,40,44},{48,52,56,60},{64,68,72,76},{80,..., dimensions={0}, use_global_device_ids=true | all-gather | bytes 430080 | tf_op jit(solution)/shard_map/all_gather | solution.py:185
  107.6 1.9 %collective-permute-start.8 = (f32[672,128]{1,0:T(8,128)S(1)}, f32[672,128]{1,0:T(8,128)}, u32[]{:S(2)}, u32[]{:S(2)}) collective-permute-start(f32[672,128]{1,0:T(8,128)S(1)} %all_gather.7), channel_id=1, source_target_pairs={{0,16},{4,20},{8,24},{12,28},{16,32},{20,36},{24,40},{28,44},{32,4... | collective-permute-start | bytes 1032200 | tf_op jit(solution)/shard_map/ppermute | solution.py:22
  109.5 12.7 %collective-permute-start.9 = (f32[672,128]{1,0:T(8,128)S(1)}, f32[672,128]{1,0:T(8,128)}, u32[]{:S(2)}, u32[]{:S(2)}) collective-permute-start(f32[672,128]{1,0:T(8,128)S(1)} %all_gather.7), channel_id=1, source_target_pairs={{0,496},{4,500},{8,504},{12,508},{16,0},{20,4},{24,8},{28,12},{32,... | collective-permute-start | bytes 1032200 | tf_op jit(solution)/shard_map/ppermute | solution.py:22
  122.2 2.8 %collective-permute-done.8 = f32[672,128]{1,0:T(8,128)} collective-permute-done((f32[672,128]{1,0:T(8,128)S(1)}, f32[672,128]{1,0:T(8,128)}, u32[]{:S(2)}, u32[]{:S(2)}) %collective-permute-start.8) | collective-permute-done | bytes 344096 | tf_op jit(solution)/shard_map/ppermute | solution.py:22
  125.0 1.0 constant_dynamic-update-slice_fusion.2
  126.0 0.3 collective-permute-done.9
  126.4 1.0 constant_dynamic-update-slice_fusion.stat_ref
  127.4 0.0 copy-start.9
  127.4 1.0 copy-done.9
  128.5 1.0 copy-done.11
  129.5 1.0 copy-done.13
  130.5 1.0 copy-done.15
  131.6 3.8 %grads.3 = (bf16[128,1024]{1,0:T(8,128)(2,1)S(1)}, bf16[128,1024]{1,0:T(8,128)(2,1)S(1)}) custom-call(s32[1]{0:T(128)} %bitcast.6.place_ref, f32[2016,128]{1,0:T(8,128)S(1)} %constant_dynamic-update-slice_fusion.stat_ref, bf16[128,2048]{1,0:T(8,128)(2,1)S(1)} %copy-done.1, bf16[128,2048]{1,0:T(8,128)(2,1)S(1)} %copy-done.3, bf16[128,2048]{1,0:T(8,128)(2,1)S(1)} %copy-done.5, ...), custom_call_target="tpu_custom_call" | custom-call | flops 671088640 | bytes 3670016 | tf_op jit(solution)/shard_map/grads/pallas_call | solution.py:197
  135.4 0.0 copy-start.16
  135.4 1.9 %collective-permute-start.14 = (bf16[128,1024]{1,0:T(8,128)(2,1)S(1)}, bf16[128,1024]{1,0:T(8,128)(2,1)}, u32[]{:S(2)}, u32[]{:S(2)}) collective-permute-start(bf16[128,1024]{1,0:T(8,128)(2,1)S(1)} %get-tuple-element.11.refs_0_), channel_id=1, source_target_pairs={{0,2},{1,3},{2,0},{3,1},{4,6},{5,7},{6,4},{7,5},{8,10},{9,11},{10,... | collective-permute-start | bytes 786440 | tf_op jit(solution)/shard_map/ppermute | solution.py:27
  137.3 4.4 %grads.2 = (bf16[128,1024]{1,0:T(8,128)(2,1)}, bf16[128,1024]{1,0:T(8,128)(2,1)S(1)}) custom-call(s32[1]{0:T(128)} %bitcast.6.place_ref, f32[2016,128]{1,0:T(8,128)S(1)} %constant_dynamic-update-slice_fusion.stat_ref, bf16[128,2048]{1,0:T(8,128)(2,1)S(1)} %copy-done.1, bf16[128,2048]{1,0:T(8,128)(2,1)S(1)} %copy-done.3, bf16[128,2048]{1,0:T(8,128)(2,1)S(1)} %copy-done.5, ...), custom_call_target="tpu_custom_call" | custom-call | flops 671088640 | bytes 3670016 | tf_op jit(solution)/shard_map/grads/pallas_call | solution.py:197
  141.7 0.7 copy-done.18
  142.4 3.5 %collective-permute-start.11 = (bf16[128,1024]{1,0:T(8,128)(2,1)}, bf16[128,1024]{1,0:T(8,128)(2,1)S(1)}, u32[]{:S(2)}, u32[]{:S(2)}) collective-permute-start(bf16[128,1024]{1,0:T(8,128)(2,1)} %get-tuple-element.10.refs_0_), channel_id=1, source_target_pairs={{0,2},{1,3},{2,0},{3,1},{4,6},{5,7},{6,4},{7,5},{8,10},{9,11},{10,... | collective-permute-start | bytes 786440 | tf_op jit(solution)/shard_map/ppermute | solution.py:27
  145.9 1.1 constant_dynamic-slice_fusion.4
  147.0 0.1 copy.9
  147.2 0.1 copy.12
  147.3 0.1 copy.11
  147.4 0.1 copy.10
  147.5 6.9 %collective-permute-start.13 = (bf16[128,1024]{1,0:T(8,128)(2,1)S(1)}, bf16[128,1024]{1,0:T(8,128)(2,1)S(1)}, u32[]{:S(2)}, u32[]{:S(2)}) collective-permute-start(bf16[128,1024]{1,0:T(8,128)(2,1)S(1)} %get-tuple-element.11.refs_0_), channel_id=1, source_target_pairs={{0,1},{1,0},{2,3},{3,2},{4,5},{5,4},{6,7},{7,6},{8,9},{9,8},{10,11... | collective-permute-start | bytes 786440 | tf_op jit(solution)/shard_map/ppermute | solution.py:27
  154.5 0.0 collective-permute-done.14.refs_2_
  154.5 1.9 %collective-permute-start.15 = (bf16[128,1024]{1,0:T(8,128)(2,1)}, bf16[128,1024]{1,0:T(8,128)(2,1)S(1)}, u32[]{:S(2)}, u32[]{:S(2)}) collective-permute-start(bf16[128,1024]{1,0:T(8,128)(2,1)} %collective-permute-done.14.refs_2_), channel_id=1, source_target_pairs={{0,1},{1,0},{2,3},{3,2},{4,5},{5,4},{6,7},{7,6},{8,9},{9,8},{10,11... | collective-permute-start | bytes 786440 | tf_op jit(solution)/shard_map/ppermute | solution.py:27
  156.4 0.1 maximum_bitcast_fusion.inputs_ref
  156.5 2.4 %collective-permute-start.10 = (bf16[128,1024]{1,0:T(8,128)(2,1)}, bf16[128,1024]{1,0:T(8,128)(2,1)S(1)}, u32[]{:S(2)}, u32[]{:S(2)}) collective-permute-start(bf16[128,1024]{1,0:T(8,128)(2,1)} %get-tuple-element.10.refs_0_), channel_id=1, source_target_pairs={{0,1},{1,0},{2,3},{3,2},{4,5},{5,4},{6,7},{7,6},{8,9},{9,8},{10,11... | collective-permute-start | bytes 786440 | tf_op jit(solution)/shard_map/ppermute | solution.py:27
  158.9 0.0 collective-permute-done.11.refs_2_
  158.9 1.9 %collective-permute-start.12 = (bf16[128,1024]{1,0:T(8,128)(2,1)S(1)}, bf16[128,1024]{1,0:T(8,128)(2,1)S(1)}, u32[]{:S(2)}, u32[]{:S(2)}) collective-permute-start(bf16[128,1024]{1,0:T(8,128)(2,1)S(1)} %collective-permute-done.11.refs_2_), channel_id=1, source_target_pairs={{0,1},{1,0},{2,3},{3,2},{4,5},{5,4},{6,7},{7,6},{8,9},{9,8},{10,11... | collective-permute-start | bytes 786440 | tf_op jit(solution)/shard_map/ppermute | solution.py:27
  160.9 0.8 pad_maximum_fusion
  161.7 0.0 collective-permute-done.13.refs_1_
  161.7 0.0 collective-permute-done.15.refs_3_
  161.7 2.6 %weight.2.refs_4_ = bf16[512,2048]{1,0:T(8,128)(2,1)} custom-call(bf16[512,512]{1,0:T(8,128)(2,1)S(1)} %maximum_bitcast_fusion.inputs_ref, bf16[128,1024]{1,0:T(8,128)(2,1)S(1)} %get-tuple-element.11.refs_0_, bf16[128,1024]{1,0:T(8,128)(2,1)S(1)} %collective-permute-done.13.refs_1_, bf16[128,1024]{1,0:T(8,128)(2,1)} %collective-permute-done.14.refs_2_, ...), custom_call_target="tpu_custom_call" | custom-call | flops 536870912 | bytes 2097152 | tf_op jit(solution)/shard_map/weight/pallas_call | solution.py:232
  164.3 0.0 collective-permute-done.10.refs_1_
  164.3 0.0 collective-permute-done.12.refs_3_
  164.3 2.6 %weight.3 = bf16[512,2048]{1,0:T(8,128)(2,1)} custom-call(bf16[512,512]{1,0:T(8,128)(2,1)S(1)} %maximum_bitcast_fusion.inputs_ref, bf16[128,1024]{1,0:T(8,128)(2,1)} %get-tuple-element.10.refs_0_, bf16[128,1024]{1,0:T(8,128)(2,1)S(1)} %collective-permute-done.10.refs_1_, ...), custom_call_target="tpu_custom_call", output_to_operand_aliasing={{}: (5, {})} | custom-call | flops 536870912 | bytes 2097152 | tf_op jit(solution)/shard_map/weight/pallas_call | solution.py:232
  (30 shorter events, 0.1 us)
Async XLA Ops:
  7.2 53.7 %all-gather.2.cloned.1.call-start = ((), (), s32[]{:S(2)}) async-start(), calls=%async_computation | async-start | bytes 2621440 | tf_op jit(solution)/shard_map/all_gather | solution.py:144
  7.9 28.7 %collective-permute-start = (bf16[128,2048]{1,0:T(8,128)(2,1)}, bf16[128,2048]{1,0:T(8,128)(2,1)S(1)}, u32[]{:S(2)}, u32[]{:S(2)}) collective-permute-start(bf16[128,2048]{1,0:T(8,128)(2,1)} %refs_5_.5), channel_id=1, source_target_pairs={{0,4},{4,8},{8,12},{12,16},{16,20},{20,24},{24,28},{28,32},{32,36}... | collective-permute-start | bytes 1572872 | tf_op jit(solution)/shard_map/ppermute | solution.py:22
  11.9 35.9 %collective-permute-start.3 = (bf16[128,2048]{1,0:T(8,128)(2,1)}, bf16[128,2048]{1,0:T(8,128)(2,1)S(1)}, u32[]{:S(2)}, u32[]{:S(2)}) collective-permute-start(bf16[128,2048]{1,0:T(8,128)(2,1)} %refs_0_.5), channel_id=1, source_target_pairs={{0,4},{4,8},{8,12},{12,16},{16,20},{20,24},{24,28},{28,32},{32,36}... | collective-permute-start | bytes 1572872 | tf_op jit(solution)/shard_map/ppermute | solution.py:22
  15.2 34.7 %collective-permute-start.2 = (bf16[128,2048]{1,0:T(8,128)(2,1)}, bf16[128,2048]{1,0:T(8,128)(2,1)S(1)}, u32[]{:S(2)}, u32[]{:S(2)}) collective-permute-start(bf16[128,2048]{1,0:T(8,128)(2,1)} %refs_0_.5), channel_id=1, source_target_pairs={{0,508},{4,0},{8,4},{12,8},{16,12},{20,16},{24,20},{28,24},{32,28}... | collective-permute-start | bytes 1572872 | tf_op jit(solution)/shard_map/ppermute | solution.py:22
  28.6 30.3 %collective-permute-start.6 = (bf16[128,2048]{1,0:T(8,128)(2,1)}, bf16[128,2048]{1,0:T(8,128)(2,1)S(1)}, u32[]{:S(2)}, u32[]{:S(2)}) collective-permute-start(bf16[128,2048]{1,0:T(8,128)(2,1)} %refs_5_.5), channel_id=1, source_target_pairs={{0,508},{4,0},{8,4},{12,8},{16,12},{20,16},{24,20},{28,24},{32,28}... | collective-permute-start | bytes 1572872 | tf_op jit(solution)/shard_map/ppermute | solution.py:22
  36.6 24.2 %collective-permute-start.1 = (bf16[128,2048]{1,0:T(8,128)(2,1)S(1)}, bf16[128,2048]{1,0:T(8,128)(2,1)S(1)}, u32[]{:S(2)}, u32[]{:S(2)}) collective-permute-start(bf16[128,2048]{1,0:T(8,128)(2,1)S(1)} %collective-permute-done.refs_7_), channel_id=1, source_target_pairs={{0,4},{4,8},{8,12},{12,16},{16,20},{20,24},{24,28},{28,32},{32,36}... | collective-permute-start | bytes 1572872 | tf_op jit(solution)/shard_map/ppermute | solution.py:22
  47.9 22.5 %collective-permute-start.5 = (bf16[128,2048]{1,0:T(8,128)(2,1)S(1)}, bf16[128,2048]{1,0:T(8,128)(2,1)S(1)}, u32[]{:S(2)}, u32[]{:S(2)}) collective-permute-start(bf16[128,2048]{1,0:T(8,128)(2,1)S(1)} %collective-permute-done.3.refs_2_), channel_id=1, source_target_pairs={{0,4},{4,8},{8,12},{12,16},{16,20},{20,24},{24,28},{28,32},{32,36}... | collective-permute-start | bytes 1572872 | tf_op jit(solution)/shard_map/ppermute | solution.py:22
  49.8 20.5 %collective-permute-start.4 = (bf16[128,2048]{1,0:T(8,128)(2,1)S(1)}, bf16[128,2048]{1,0:T(8,128)(2,1)}, u32[]{:S(2)}, u32[]{:S(2)}) collective-permute-start(bf16[128,2048]{1,0:T(8,128)(2,1)S(1)} %collective-permute-done.2.refs_1_), channel_id=1, source_target_pairs={{0,508},{4,0},{8,4},{12,8},{16,12},{20,16},{24,20},{28,24},{32,28}... | collective-permute-start | bytes 1572872 | tf_op jit(solution)/shard_map/ppermute | solution.py:22
  58.9 20.1 %collective-permute-start.7 = (bf16[128,2048]{1,0:T(8,128)(2,1)S(1)}, bf16[128,2048]{1,0:T(8,128)(2,1)}, u32[]{:S(2)}, u32[]{:S(2)}) collective-permute-start(bf16[128,2048]{1,0:T(8,128)(2,1)S(1)} %collective-permute-done.6.refs_6_), channel_id=1, source_target_pairs={{0,508},{4,0},{8,4},{12,8},{16,12},{20,16},{24,20},{28,24},{32,28}... | collective-permute-start | bytes 1572872 | tf_op jit(solution)/shard_map/ppermute | solution.py:22
  79.0 1.0 copy-start
  80.1 1.0 copy-start.2
  81.1 1.0 copy-start.4
  82.2 1.0 copy-start.6
  83.2 0.7 copy-start.20
  88.2 0.8 copy-start.8
  89.0 0.8 copy-start.10
  89.8 0.8 copy-start.12
  90.6 0.8 copy-start.14
  91.4 36.0 %copy-start.1 = (bf16[128,2048]{1,0:T(8,128)(2,1)S(1)}, bf16[128,2048]{1,0:T(8,128)(2,1)}, u32[]{:S(2)}) copy-start(bf16[128,2048]{1,0:T(8,128)(2,1)} %keys_ref.5) | copy-start | bytes 1572868
  91.4 36.0 %copy-start.3 = (bf16[128,2048]{1,0:T(8,128)(2,1)S(1)}, bf16[128,2048]{1,0:T(8,128)(2,1)}, u32[]{:S(2)}) copy-start(bf16[128,2048]{1,0:T(8,128)(2,1)} %values_ref.5) | copy-start | bytes 1572868
  91.4 36.0 %copy-start.5 = (bf16[128,2048]{1,0:T(8,128)(2,1)S(1)}, bf16[128,2048]{1,0:T(8,128)(2,1)}, u32[]{:S(2)}) copy-start(bf16[128,2048]{1,0:T(8,128)(2,1)} %refs_0_.5) | copy-start | bytes 1572868
  91.4 36.0 %copy-start.7 = (bf16[128,2048]{1,0:T(8,128)(2,1)S(1)}, bf16[128,2048]{1,0:T(8,128)(2,1)}, u32[]{:S(2)}) copy-start(bf16[128,2048]{1,0:T(8,128)(2,1)} %refs_5_.5) | copy-start | bytes 1572868
  107.6 17.4 %collective-permute-start.8 = (f32[672,128]{1,0:T(8,128)S(1)}, f32[672,128]{1,0:T(8,128)}, u32[]{:S(2)}, u32[]{:S(2)}) collective-permute-start(f32[672,128]{1,0:T(8,128)S(1)} %all_gather.7), channel_id=1, source_target_pairs={{0,16},{4,20},{8,24},{12,28},{16,32},{20,36},{24,40},{28,44},{32,4... | collective-permute-start | bytes 1032200 | tf_op jit(solution)/shard_map/ppermute | solution.py:22
  109.5 16.9 %collective-permute-start.9 = (f32[672,128]{1,0:T(8,128)S(1)}, f32[672,128]{1,0:T(8,128)}, u32[]{:S(2)}, u32[]{:S(2)}) collective-permute-start(f32[672,128]{1,0:T(8,128)S(1)} %all_gather.7), channel_id=1, source_target_pairs={{0,496},{4,500},{8,504},{12,508},{16,0},{20,4},{24,8},{28,12},{32,... | collective-permute-start | bytes 1032200 | tf_op jit(solution)/shard_map/ppermute | solution.py:22
  127.4 1.0 copy-start.9
  128.5 1.0 copy-start.11
  129.5 1.0 copy-start.13
  130.5 1.0 copy-start.15
  135.4 6.3 %copy-start.16 = (bf16[128,1024]{1,0:T(8,128)(2,1)}, bf16[128,1024]{1,0:T(8,128)(2,1)S(1)}, u32[]{:S(2)}) copy-start(bf16[128,1024]{1,0:T(8,128)(2,1)S(1)} %get-tuple-element.12) | copy-start | bytes 786436
  135.4 19.1 %collective-permute-start.14 = (bf16[128,1024]{1,0:T(8,128)(2,1)S(1)}, bf16[128,1024]{1,0:T(8,128)(2,1)}, u32[]{:S(2)}, u32[]{:S(2)}) collective-permute-start(bf16[128,1024]{1,0:T(8,128)(2,1)S(1)} %get-tuple-element.11.refs_0_), channel_id=1, source_target_pairs={{0,2},{1,3},{2,0},{3,1},{4,6},{5,7},{6,4},{7,5},{8,10},{9,11},{10,... | collective-permute-start | bytes 786440 | tf_op jit(solution)/shard_map/ppermute | solution.py:27
  141.7 0.7 copy-start.18
  142.4 18.4 %copy-start.17 = (bf16[128,1024]{1,0:T(8,128)(2,1)S(1)}, bf16[128,1024]{1,0:T(8,128)(2,1)}, u32[]{:S(2)}) copy-start(bf16[128,1024]{1,0:T(8,128)(2,1)} %copy-done.16) | copy-start | bytes 786436
  142.4 18.5 %copy-start.19 = (bf16[128,1024]{1,0:T(8,128)(2,1)S(1)}, bf16[128,1024]{1,0:T(8,128)(2,1)}, u32[]{:S(2)}) copy-start(bf16[128,1024]{1,0:T(8,128)(2,1)} %copy-done.18) | copy-start | bytes 786436
  142.4 16.5 %collective-permute-start.11 = (bf16[128,1024]{1,0:T(8,128)(2,1)}, bf16[128,1024]{1,0:T(8,128)(2,1)S(1)}, u32[]{:S(2)}, u32[]{:S(2)}) collective-permute-start(bf16[128,1024]{1,0:T(8,128)(2,1)} %get-tuple-element.10.refs_0_), channel_id=1, source_target_pairs={{0,2},{1,3},{2,0},{3,1},{4,6},{5,7},{6,4},{7,5},{8,10},{9,11},{10,... | collective-permute-start | bytes 786440 | tf_op jit(solution)/shard_map/ppermute | solution.py:27
  147.5 14.2 %collective-permute-start.13 = (bf16[128,1024]{1,0:T(8,128)(2,1)S(1)}, bf16[128,1024]{1,0:T(8,128)(2,1)S(1)}, u32[]{:S(2)}, u32[]{:S(2)}) collective-permute-start(bf16[128,1024]{1,0:T(8,128)(2,1)S(1)} %get-tuple-element.11.refs_0_), channel_id=1, source_target_pairs={{0,1},{1,0},{2,3},{3,2},{4,5},{5,4},{6,7},{7,6},{8,9},{9,8},{10,11... | collective-permute-start | bytes 786440 | tf_op jit(solution)/shard_map/ppermute | solution.py:27
  154.5 7.2 %collective-permute-start.15 = (bf16[128,1024]{1,0:T(8,128)(2,1)}, bf16[128,1024]{1,0:T(8,128)(2,1)S(1)}, u32[]{:S(2)}, u32[]{:S(2)}) collective-permute-start(bf16[128,1024]{1,0:T(8,128)(2,1)} %collective-permute-done.14.refs_2_), channel_id=1, source_target_pairs={{0,1},{1,0},{2,3},{3,2},{4,5},{5,4},{6,7},{7,6},{8,9},{9,8},{10,11... | collective-permute-start | bytes 786440 | tf_op jit(solution)/shard_map/ppermute | solution.py:27
  156.5 7.8 %collective-permute-start.10 = (bf16[128,1024]{1,0:T(8,128)(2,1)}, bf16[128,1024]{1,0:T(8,128)(2,1)S(1)}, u32[]{:S(2)}, u32[]{:S(2)}) collective-permute-start(bf16[128,1024]{1,0:T(8,128)(2,1)} %get-tuple-element.10.refs_0_), channel_id=1, source_target_pairs={{0,1},{1,0},{2,3},{3,2},{4,5},{5,4},{6,7},{7,6},{8,9},{9,8},{10,11... | collective-permute-start | bytes 786440 | tf_op jit(solution)/shard_map/ppermute | solution.py:27
  158.9 5.4 %collective-permute-start.12 = (bf16[128,1024]{1,0:T(8,128)(2,1)S(1)}, bf16[128,1024]{1,0:T(8,128)(2,1)S(1)}, u32[]{:S(2)}, u32[]{:S(2)}) collective-permute-start(bf16[128,1024]{1,0:T(8,128)(2,1)S(1)} %collective-permute-done.11.refs_2_), channel_id=1, source_target_pairs={{0,1},{1,0},{2,3},{3,2},{4,5},{5,4},{6,7},{7,6},{8,9},{9,8},{10,11... | collective-permute-start | bytes 786440 | tf_op jit(solution)/shard_map/ppermute | solution.py:27
Sparse Core Ops, SparseCore 0:
  10.1 42.6 all-gather.1

commit v2 on v1

v2 whole, which is shorter than its diff:
```python
import functools

import jax
import jax.numpy as jnp
from jax import lax
from jax.experimental import pallas as pl
from jax.experimental.pallas import tpu as pltpu
from jax.sharding import PartitionSpec as P

HD = 128
DOCS = (0, 1, -1, 2, -2)
GROUP = 4
STEP = 4
TILE = 8
NEAR = 3
HALVES = 2
VMEM = 64 << 20
FAR = 1e30


def shifted(value, axis, steps):
    count = lax.axis_size(axis)
    pairs = [(source, (source + steps) % count) for source in range(count)]
    return lax.ppermute(value, axis, pairs)


def swapped(value, axis, mask):
    pairs = [(source, source ^ mask) for source in range(lax.axis_size(axis))]
    return lax.ppermute(value, axis, pairs)


def dot_nt(a, b):
    return lax.dot_general(a, b, (((1,), (1,)), ((), ())), preferred_element_type=jnp.float32)


def dot_nn(a, b):
    return lax.dot_general(a, b, (((1,), (0,)), ((), ())), preferred_element_type=jnp.float32)


def scores_of(keys, query_rows, own_first):
    scores = dot_nt(keys, query_rows) * (HD ** (-0.5))
    if not own_first:
        return scores
    rows = keys.shape[0]
    own = scores[:, :rows]
    key_at = lax.broadcasted_iota(jnp.int32, own.shape, 0)
    query_at = lax.broadcasted_iota(jnp.int32, own.shape, 1)
    own = jnp.where(key_at <= query_at, own, -FAR)
    return jnp.concatenate([own, scores[:, rows:]], 1)


def head_rows(refs, head):
    return jnp.concatenate([ref[:, head * HD : (head + 1) * HD] for ref in refs], 0)


def stats_kernel(low, steps, offsets_ref, keys_ref, values_ref, *refs):
    count = (len(refs) - 1) // 2
    query_refs, grad_refs, out_ref = refs[:count], refs[count : 2 * count], refs[-1]
    before_ref = refs[2 * count] if low else None
    rows = keys_ref.shape[0]
    step = pl.program_id(0)
    base = pl.multiple_of(step * TILE, TILE)
    for head in range(STEP):
        cols = slice(head * HD, (head + 1) * HD)
        scores = scores_of(keys_ref[:, cols], head_rows(query_refs, head), low == 0)
        prob_grad = dot_nt(values_ref[:, cols], head_rows(grad_refs, head))
        top = jnp.max(scores, 0, keepdims=True)
        weights = jnp.exp(scores - top)
        total = jnp.sum(weights, 0, keepdims=True)
        mean = jnp.sum(weights * prob_grad, 0, keepdims=True) / total
        lse = top + jnp.log(total)
        for doc in range(count):
            cut = slice(doc * rows, (doc + 1) * rows)
            start = base + (low + doc) * steps * TILE
            out_ref[pl.ds(start + head, 1), :] = lse[:, cut]
            out_ref[pl.ds(start + STEP + head, 1), :] = mean[:, cut]

    @pl.when(step == 0)
    def _():
        if low:
            out_ref[: before_ref.shape[0], :] = before_ref[...]
            tail = out_ref.shape[0] - TILE
            for slot in range(2):
                value = offsets_ref[0, slot].astype(jnp.float32)
                at = tail + slot * STEP
                out_ref[at : at + STEP, :] = jnp.full((STEP, rows), value, jnp.float32)


def merged(stat_ref, me, step, steps):
    stride = stat_ref.shape[0] // (3 * GROUP)

    def tile(place, row):
        return stat_ref[pl.ds(pl.multiple_of(place * stride + row, TILE), TILE), :]

    lse_rows, delta_rows = [], []
    for doc in DOCS:
        owner = me + GROUP + doc
        offsets = tile(owner, stride - TILE)
        first, second = offsets[:STEP], offsets[STEP:]
        parts = []
        for hop in DOCS:
            stat = tile(owner + hop, (DOCS.index(-hop) * steps + step) * TILE)
            lse, mean = stat[:STEP], stat[STEP:]
            if hop:
                lse = jnp.where((first == hop) | (second == hop), lse, -FAR)
            parts.append((lse, mean))
        top = functools.reduce(jnp.maximum, [lse for lse, _ in parts])
        weights = [jnp.exp(lse - top) for lse, _ in parts]
        total = sum(weights)
        delta = sum(weight * mean for weight, (_, mean) in zip(weights, parts)) / total
        lse = top + jnp.log(total)
        if doc:
            lse = jnp.where((first == -doc) | (second == -doc), lse, FAR)
        lse_rows.append(lse)
        delta_rows.append(delta)
    return jnp.concatenate(lse_rows, 1), jnp.concatenate(delta_rows, 1)


def grads_kernel(first_step, steps, place_ref, *refs):
    count = len(DOCS)
    stat_refs, (keys_ref, values_ref), refs = refs[:3], refs[3:5], refs[5:]
    query_refs, grad_refs = refs[:count], refs[count : 2 * count]
    key_half, key_out, value_out, stat_ref = refs[-4:]
    each = stat_refs[0].shape[0]

    @pl.when(pl.program_id(0) == 0)
    def _():
        for at, ref in enumerate(stat_refs):
            stat_ref[at * each : (at + 1) * each, :] = ref[...]

    step = pl.program_id(0) + first_step
    lse, delta = merged(stat_ref, place_ref[0], step, steps)
    for head in range(STEP):
        cols = slice(head * HD, (head + 1) * HD)
        query_rows = head_rows(query_refs, head)
        grad_rows = head_rows(grad_refs, head)
        scores = scores_of(keys_ref[:, cols], query_rows, True)
        prob_grad = dot_nt(values_ref[:, cols], grad_rows)
        probs = jnp.exp(scores - lse[head : head + 1])
        score_grad = probs * (prob_grad - delta[head : head + 1]) * (HD ** (-0.5))
        key_total = dot_nn(score_grad.astype(jnp.bfloat16), query_rows).astype(jnp.bfloat16)
        value_total = dot_nn(probs.astype(jnp.bfloat16), grad_rows)
        key_half[:, cols] = key_total
        key_out[:, cols] = key_total
        value_out[:, cols] = value_total.astype(jnp.bfloat16)


def weight_kernel(inputs_ref, *refs):
    grads = jnp.concatenate([ref[...] for ref in refs[:4]], 0)
    refs[-1][...] = dot_nn(inputs_ref[...], grads).astype(jnp.bfloat16)


def local(layer_input, queries, key_vectors, value_vectors, output_grad, partner_offsets):
    rows, features = queries.shape
    steps = features // (HD * STEP)
    wide = STEP * HD
    docs = len(DOCS)
    mine = lax.axis_index("fsdp")
    places = lax.axis_size("fsdp")
    params = pltpu.CompilerParams(vmem_limit_bytes=VMEM)

    by_doc = {0: (queries, output_grad)}
    up_q, down_q = shifted(queries, "dp", -1), shifted(queries, "dp", 1)
    up_g, down_g = shifted(output_grad, "dp", -1), shifted(output_grad, "dp", 1)
    by_doc[1], by_doc[-1] = (up_q, up_g), (down_q, down_g)
    by_doc[2] = shifted(up_q, "dp", -1), shifted(up_g, "dp", -1)
    by_doc[-2] = shifted(down_q, "dp", 1), shifted(down_g, "dp", 1)
    query_docs = [by_doc[doc][0] for doc in DOCS]
    grad_docs = [by_doc[doc][1] for doc in DOCS]

    width = layer_input.shape[1] // places
    columns = []
    for k in range(places):
        piece = lax.dynamic_slice_in_dim(layer_input, (mine ^ k) * width, width, 1)
        columns.append(swapped(piece, "fsdp", k) if k else piece)
    columns = jnp.concatenate(columns, 0).T
    grad_docs[-1], columns = lax.optimization_barrier((grad_docs[-1], columns))

    block = pl.BlockSpec((rows, wide), lambda step: (0, step))
    pair = rows * rows * HD * 2 * (features // HD)
    exps = rows * rows * (features // HD)
    stats = None
    for low, high in ((0, NEAR), (NEAR, docs)):
        out_rows = high * steps * TILE + (TILE if high == docs else 0)
        before = [] if stats is None else [stats]
        stats = pl.pallas_call(
            functools.partial(stats_kernel, low, steps),
            grid=(steps,),
            in_specs=[pl.BlockSpec(memory_space=pltpu.SMEM)]
            + [block] * (2 + 2 * (high - low))
            + [pl.BlockSpec(array.shape, lambda step: (0, 0)) for array in before],
            out_specs=pl.BlockSpec((out_rows, rows), lambda step: (0, 0)),
            out_shape=jax.ShapeDtypeStruct((out_rows, rows), jnp.float32),
            compiler_params=params,
            cost_estimate=pl.CostEstimate(
                flops=2 * pair * (high - low),
                bytes_accessed=2 * (high - low + 1) * rows * features * 2,
                transcendentals=exps * (high - low),
            ),
            name="stats",
        )(
            partner_offsets,
            key_vectors,
            value_vectors,
            *query_docs[low:high],
            *grad_docs[low:high],
            *before,
        )

    replicas = lax.axis_size("dp")
    groups = [list(range(low, low + GROUP)) for low in range(0, replicas, GROUP)]
    here = lax.all_gather(stats, "dp", axis=0, tiled=True, axis_index_groups=groups)
    stat_parts = [shifted(here, "dp", GROUP), here, shifted(here, "dp", -GROUP)]
    place = (lax.axis_index("dp") % GROUP).astype(jnp.int32).reshape(1)

    each = steps // HALVES
    any_space = pl.BlockSpec(memory_space=pl.ANY)
    full = jax.ShapeDtypeStruct((rows, features), jnp.bfloat16)
    half_shape = jax.ShapeDtypeStruct((rows, each * wide), jnp.bfloat16)
    key_parts, key_grad, value_grad = [], None, None
    for half in range(HALVES):
        low = half * each
        at_half = pl.BlockSpec((rows, wide), lambda step, low=low: (0, step + low))
        inputs = [place, *stat_parts, key_vectors, value_vectors, *query_docs, *grad_docs]
        held = [] if half == 0 else [key_grad, value_grad]
        key_part, key_grad, value_grad = pl.pallas_call(
            functools.partial(grads_kernel, low, steps),
            grid=(each,),
            in_specs=[pl.BlockSpec(memory_space=pltpu.SMEM)]
            + [pl.BlockSpec(here.shape, lambda step: (0, 0))] * 3
            + [at_half] * (2 + 2 * docs)
            + [any_space] * len(held),
            out_specs=[block, at_half, at_half],
            out_shape=[half_shape, full, full],
            scratch_shapes=[pltpu.VMEM((3 * here.shape[0], rows), jnp.float32)],
            input_output_aliases={len(inputs) + at: 1 + at for at in range(len(held))},
            compiler_params=params,
            cost_estimate=pl.CostEstimate(
                flops=4 * pair * docs // HALVES,
                bytes_accessed=15 * rows * features * 2 // HALVES,
                transcendentals=exps * docs // HALVES,
            ),
            name="grads",
        )(*inputs, *held)
        key_parts.append(key_part)

    beside = swapped(key_grad, "fsdp", 1)
    weight = None
    for half in range(HALVES):
        low = half * each
        at_half = pl.BlockSpec((rows, wide), lambda step, low=low: (0, step + low))
        across = swapped(key_parts[half], "fsdp", 2)
        inputs = [columns, key_grad, beside, across, swapped(across, "fsdp", 1)]
        held = [] if weight is None else [weight]
        weight = pl.pallas_call(
            weight_kernel,
            grid=(each,),
            in_specs=[pl.BlockSpec(columns.shape, lambda step: (0, 0)), at_half, at_half, block, block]
            + [any_space] * len(held),
            out_specs=pl.BlockSpec((width, wide), lambda step, low=low: (0, step + low)),
            out_shape=jax.ShapeDtypeStruct((width, features), jnp.bfloat16),
            input_output_aliases={len(inputs): 0} if held else {},
            compiler_params=params,
            cost_estimate=pl.CostEstimate(
                flops=2 * width * columns.shape[1] * each * wide,
                bytes_accessed=2 * each * wide * (columns.shape[1] + width),
                transcendentals=0,
            ),
            name="weight",
        )(*inputs, *held)
    return weight[None], value_grad


def solution(mesh):
    return jax.shard_map(
        local,
        mesh=mesh,
        in_specs=(
            P(("dp", "fsdp"), None),
            P(("dp", "fsdp"), None),
            P(("dp", "fsdp"), None),
            P(("dp", "fsdp"), None),
            P(("dp", "fsdp"), None),
            P("dp", None),
        ),
        out_specs=(P("dp", "fsdp", None), P(("dp", "fsdp"), None)),
        check_vma=False,
    )
```

time: 175 us -> 157 us (0.90)
  local copies, waits for them, and re-layouts: 16.5 us -> 2.35 us
  between operations: 14.4 us -> 0.93 us
  Pallas kernels: 17.8 us -> 26.2 us
  starting transfers between devices: 72.1 us -> 79.9 us
  waiting for transfers between devices: 35.9 us -> 29.5 us
    ppermute x10, waiting for transfers between devices: 35.2 us -> 19.2 us  [shifted(): return lax.ppermute(value, axis, pairs)]
    unnamed x44 -> x10, local copies, waits for them, and re-layouts: 13.9 us -> 1.21 us
    ppermute x6 -> x8, waiting for transfers between devices: 0.02 us -> 10.3 us  [swapped(): return lax.ppermute(value, axis, pairs)]
    ppermute x6 -> x8, starting transfers between devices: 18.6 us -> 27.4 us  [swapped(): return lax.ppermute(value, axis, pairs)]
    pallas_call x5 -> x6, Pallas kernels: 17.8 us -> 26.2 us  [the longest x2 10.9 us: local(): pl.pallas_call(functools.partial(grads_kernel, low, steps), grid=(each,),...]
  transfers between devices with their start and end apart: 17 -> 18, of which waited for: 6 -> 7; matrix products, arithmetic and copies ran while one was open for 2% -> 2% of each run, Pallas kernels for 4% -> 8%
where the time goes in v2:
time: 157 us; the launch traced here: 156 us
  starting transfers between devices  79.9 us (51%)
  waiting for transfers between devices  29.5 us (19%)
  Pallas kernels  26.2 us (17%)
  blocking collectives  16 us (10%)
  local copies, waits for them, and re-layouts  2.35 us (1%)
    ppermute x10, starting transfers between devices, shifted(): return lax.ppermute(value, axis, pairs)  52.6 us
    ppermute x8, starting transfers between devices, swapped(): return lax.ppermute(value, axis, pairs)  27.4 us
    ppermute x10, waiting for transfers between devices, shifted(): return lax.ppermute(value, axis, pairs)  19.2 us
    all_gather x1, blocking collectives, local(): lax.all_gather(stats, 'dp', axis=0, tiled=True, axis_index_groups=groups)  16 us
    pallas_call x2, Pallas kernels, local(): pl.pallas_call(functools.partial(grads_kernel, low, steps), grid=(each,),...  10.9 us
    ppermute x8, waiting for transfers between devices, swapped(): return lax.ppermute(value, axis, pairs)  10.3 us
    pallas_call x2, Pallas kernels, local(): pl.pallas_call(functools.partial(stats_kernel, low, steps), grid=(steps,)...  9.09 us
    pallas_call x2, Pallas kernels, local(): pl.pallas_call(weight_kernel, grid=(each,), in_specs=[pl.BlockSpec(column...  6.24 us
  transfers between devices with their start and end apart: 18, of which 7 were waited for; matrix products, arithmetic and copies ran while one was open for 2% of the time, Pallas kernels for 8%

profile of v2, /device:TPU:1, one launch (start us, length us, event | category | flops | bytes accessed | tf_op | source)
XLA Modules:
  0.0 155.8 jit_solution(13118749005630452295)
XLA Ops:
  0.6 4.0 %collective-permute-start = (bf16[128,2048]{1,0:T(8,128)(2,1)}, bf16[128,2048]{1,0:T(8,128)(2,1)}, u32[]{:S(2)}, u32[]{:S(2)}) collective-permute-start(bf16[128,2048]{1,0:T(8,128)(2,1)} %refs_10_.3), channel_id=1, source_target_pairs={{0,4},{4,8},{8,12},{12,16},{16,20},{20,24},{24,28},{28,32},{32,36}... | collective-permute-start | bytes 1572872 | tf_op jit(solution)/shard_map/ppermute | solution.py:24
  4.7 3.2 %collective-permute-start.7 = (bf16[128,2048]{1,0:T(8,128)(2,1)}, bf16[128,2048]{1,0:T(8,128)(2,1)}, u32[]{:S(2)}, u32[]{:S(2)}) collective-permute-start(bf16[128,2048]{1,0:T(8,128)(2,1)} %refs_5_.3), channel_id=1, source_target_pairs={{0,4},{4,8},{8,12},{12,16},{16,20},{20,24},{24,28},{28,32},{32,36}... | collective-permute-start | bytes 1572872 | tf_op jit(solution)/shard_map/ppermute | solution.py:24
  7.9 13.5 %collective-permute-start.5 = (bf16[128,2048]{1,0:T(8,128)(2,1)}, bf16[128,2048]{1,0:T(8,128)(2,1)}, u32[]{:S(2)}, u32[]{:S(2)}) collective-permute-start(bf16[128,2048]{1,0:T(8,128)(2,1)} %refs_5_.3), channel_id=1, source_target_pairs={{0,508},{4,0},{8,4},{12,8},{16,12},{20,16},{24,20},{28,24},{32,28}... | collective-permute-start | bytes 1572872 | tf_op jit(solution)/shard_map/ppermute | solution.py:24
  21.4 3.4 %collective-permute-start.9 = (bf16[128,2048]{1,0:T(8,128)(2,1)}, bf16[128,2048]{1,0:T(8,128)(2,1)}, u32[]{:S(2)}, u32[]{:S(2)}) collective-permute-start(bf16[128,2048]{1,0:T(8,128)(2,1)} %refs_10_.3), channel_id=1, source_target_pairs={{0,508},{4,0},{8,4},{12,8},{16,12},{20,16},{24,20},{28,24},{32,28}... | collective-permute-start | bytes 1572872 | tf_op jit(solution)/shard_map/ppermute | solution.py:24
  24.8 1.1 constant_dynamic-slice_fusion.3
  25.9 0.1 copy.18
  26.0 3.6 %collective-permute-start.4 = (bf16[128,512]{0,1:T(8,128)(2,1)S(1)}, bf16[128,512]{0,1:T(8,128)(2,1)S(1)}, u32[]{:S(2)}, u32[]{:S(2)}) collective-permute-start(bf16[128,512]{0,1:T(8,128)(2,1)S(1)} %copy.18), channel_id=1, source_target_pairs={{0,3},{1,2},{2,1},{3,0},{4,7},{5,6},{6,5},{7,4},{8,11},{9,10},{10,... | collective-permute-start | bytes 393224 | tf_op jit(solution)/shard_map/ppermute | solution.py:29
  29.7 0.0 collective-permute-done.refs_5_.refs_12_
  29.7 1.9 %collective-permute-start.1 = (bf16[128,2048]{1,0:T(8,128)(2,1)}, bf16[128,2048]{1,0:T(8,128)(2,1)}, u32[]{:S(2)}, u32[]{:S(2)}) collective-permute-start(bf16[128,2048]{1,0:T(8,128)(2,1)} %collective-permute-done.refs_5_.refs_12_), channel_id=1, source_target_pairs={{0,4},{4,8},{8,12},{12,16},{16,20},{20,24},{24,28},{28,32},{32,36}... | collective-permute-start | bytes 1572872 | tf_op jit(solution)/shard_map/ppermute | solution.py:24
  31.6 9.1 %collective-permute-done.7.refs_2_.refs_7_ = bf16[128,2048]{1,0:T(8,128)(2,1)} collective-permute-done((bf16[128,2048]{1,0:T(8,128)(2,1)}, bf16[128,2048]{1,0:T(8,128)(2,1)}, u32[]{:S(2)}, u32[]{:S(2)}) %collective-permute-start.7) | collective-permute-done | bytes 524320 | tf_op jit(solution)/shard_map/ppermute | solution.py:24
  40.7 1.9 %collective-permute-start.8 = (bf16[128,2048]{1,0:T(8,128)(2,1)}, bf16[128,2048]{1,0:T(8,128)(2,1)}, u32[]{:S(2)}, u32[]{:S(2)}) collective-permute-start(bf16[128,2048]{1,0:T(8,128)(2,1)} %collective-permute-done.7.refs_2_.refs_7_), channel_id=1, source_target_pairs={{0,4},{4,8},{8,12},{12,16},{16,20},{20,24},{24,28},{28,32},{32,36}... | collective-permute-start | bytes 1572872 | tf_op jit(solution)/shard_map/ppermute | solution.py:24
  42.6 0.0 collective-permute-done.5.refs_1_.refs_6_
  42.7 9.1 %collective-permute-start.6 = (bf16[128,2048]{1,0:T(8,128)(2,1)}, bf16[128,2048]{1,0:T(8,128)(2,1)}, u32[]{:S(2)}, u32[]{:S(2)}) collective-permute-start(bf16[128,2048]{1,0:T(8,128)(2,1)} %collective-permute-done.5.refs_1_.refs_6_), channel_id=1, source_target_pairs={{0,508},{4,0},{8,4},{12,8},{16,12},{20,16},{24,20},{28,24},{32,28}... | collective-permute-start | bytes 1572872 | tf_op jit(solution)/shard_map/ppermute | solution.py:24
  51.8 0.0 collective-permute-done.9.refs_4_.refs_11_
  51.8 1.9 %collective-permute-start.10 = (bf16[128,2048]{1,0:T(8,128)(2,1)}, bf16[128,2048]{1,0:T(8,128)(2,1)}, u32[]{:S(2)}, u32[]{:S(2)}) collective-permute-start(bf16[128,2048]{1,0:T(8,128)(2,1)} %collective-permute-done.9.refs_4_.refs_11_), channel_id=1, source_target_pairs={{0,508},{4,0},{8,4},{12,8},{16,12},{20,16},{24,20},{28,24},{32,28}... | collective-permute-start | bytes 1572872 | tf_op jit(solution)/shard_map/ppermute | solution.py:24
  53.7 0.1 copy.16
  53.8 0.0 collective-permute-done.4
  53.8 4.6 %collective-permute-start.2 = (bf16[128,512]{0,1:T(8,128)(2,1)S(1)}, bf16[128,512]{0,1:T(8,128)(2,1)S(1)}, u32[]{:S(2)}, u32[]{:S(2)}) collective-permute-start(bf16[128,512]{0,1:T(8,128)(2,1)S(1)} %copy.16), channel_id=1, source_target_pairs={{0,1},{1,0},{2,3},{3,2},{4,5},{5,4},{6,7},{7,6},{8,9},{9,8},{10,11... | collective-permute-start | bytes 393224 | tf_op jit(solution)/shard_map/ppermute | solution.py:29
  58.4 0.1 copy.17
  58.5 0.8 collective-permute-done.2
  59.4 1.9 %collective-permute-start.3 = (bf16[128,512]{0,1:T(8,128)(2,1)S(1)}, bf16[128,512]{0,1:T(8,128)(2,1)S(1)}, u32[]{:S(2)}, u32[]{:S(2)}) collective-permute-start(bf16[128,512]{0,1:T(8,128)(2,1)S(1)} %copy.17), channel_id=1, source_target_pairs={{0,2},{1,3},{2,0},{3,1},{4,6},{5,7},{6,4},{7,5},{8,10},{9,11},{10,... | collective-permute-start | bytes 393224 | tf_op jit(solution)/shard_map/ppermute | solution.py:29
  61.3 0.1 copy.15
  61.4 4.7 %collective-permute-done.3 = bf16[128,512]{0,1:T(8,128)(2,1)S(1)} collective-permute-done((bf16[128,512]{0,1:T(8,128)(2,1)S(1)}, bf16[128,512]{0,1:T(8,128)(2,1)S(1)}, u32[]{:S(2)}, u32[]{:S(2)}) %collective-permute-start.3) | collective-permute-done | bytes 131104 | tf_op jit(solution)/shard_map/ppermute | solution.py:29
  66.1 0.9 maximum_bitcast_fusion.inputs_ref
  67.0 4.8 %stats.2.refs_4_ = f32[96,128]{1,0:T(8,128)} custom-call(s32[1,2]{1,0:T(1,128)} %offsets_ref.3, bf16[128,2048]{1,0:T(8,128)(2,1)} %refs_3_.5, bf16[128,2048]{1,0:T(8,128)(2,1)} %refs_4_.3, bf16[128,2048]{1,0:T(8,128)(2,1)} %refs_5_.3, bf16[128,2048]{1,0:T(8,128)(2,1)} %collective-permute-done.5.refs_1_.refs_6_, ...), custom_call_target="tpu_custom_call" | custom-call | flops 402653184 | bytes 4194304 | tf_op jit(solution)/shard_map/stats/pallas_call | solution.py:186
  71.7 0.0 collective-permute-done.1.refs_3_.refs_14_
  71.7 0.0 collective-permute-done.8.refs_1_.refs_9_
  71.7 0.0 collective-permute-done.6.refs_0_.refs_8_
  71.8 0.4 collective-permute-done.10.refs_2_.refs_13_
  72.1 4.3 %stats.3 = f32[168,128]{1,0:T(8,128)} custom-call(s32[1,2]{1,0:T(1,128)} %offsets_ref.3, bf16[128,2048]{1,0:T(8,128)(2,1)} %refs_3_.5, bf16[128,2048]{1,0:T(8,128)(2,1)} %refs_4_.3, bf16[128,2048]{1,0:T(8,128)(2,1)} %collective-permute-done.6.refs_0_.refs_8_, bf16[128,2048]{1,0:T(8,128)(2,1)} %collective-permute-done.8.refs_1_.refs_9_, ...), custom_call_target="tpu_custom_call" | custom-call | flops 268435456 | bytes 3145728 | tf_op jit(solution)/shard_map/stats/pallas_call | solution.py:186
  76.5 16.0 %all_gather.3.refs_1_ = f32[672,128]{1,0:T(8,128)S(1)} all-gather(f32[168,128]{1,0:T(8,128)} %stats.3), channel_id=1, replica_groups={{0,4,8,12},{16,20,24,28},{32,36,40,44},{48,52,56,60},{64,68,72,76},{80,..., dimensions={0}, use_global_device_ids=true | all-gather | bytes 430080 | tf_op jit(solution)/shard_map/all_gather | solution.py:212
  92.5 0.0 copy-start
  92.5 11.7 %collective-permute-start.12 = (f32[672,128]{1,0:T(8,128)S(1)}, f32[672,128]{1,0:T(8,128)S(1)}, u32[]{:S(2)}, u32[]{:S(2)}) collective-permute-start(f32[672,128]{1,0:T(8,128)S(1)} %all_gather.3.refs_1_), channel_id=1, source_target_pairs={{0,496},{4,500},{8,504},{12,508},{16,0},{20,4},{24,8},{28,12},{32,... | collective-permute-start | bytes 1032200 | tf_op jit(solution)/shard_map/ppermute | solution.py:24
  104.2 0.0 copy-done
  104.2 1.9 %collective-permute-start.11 = (f32[672,128]{1,0:T(8,128)S(1)}, f32[672,128]{1,0:T(8,128)S(1)}, u32[]{:S(2)}, u32[]{:S(2)}) collective-permute-start(f32[672,128]{1,0:T(8,128)S(1)} %all_gather.3.refs_1_), channel_id=1, source_target_pairs={{0,16},{4,20},{8,24},{12,28},{16,32},{20,36},{24,40},{28,44},{32,4... | collective-permute-start | bytes 1032200 | tf_op jit(solution)/shard_map/ppermute | solution.py:24
  106.1 2.2 %collective-permute-done.12.refs_2_ = f32[672,128]{1,0:T(8,128)S(1)} collective-permute-done((f32[672,128]{1,0:T(8,128)S(1)}, f32[672,128]{1,0:T(8,128)S(1)}, u32[]{:S(2)}, u32[]{:S(2)}) %collective-permute-start.12) | collective-permute-done | bytes 344096 | tf_op jit(solution)/shard_map/ppermute | solution.py:24
  108.3 0.0 copy-start.1
  108.4 7.4 %collective-permute-done.11.refs_0_ = f32[672,128]{1,0:T(8,128)S(1)} collective-permute-done((f32[672,128]{1,0:T(8,128)S(1)}, f32[672,128]{1,0:T(8,128)S(1)}, u32[]{:S(2)}, u32[]{:S(2)}) %collective-permute-start.11) | collective-permute-done | bytes 344096 | tf_op jit(solution)/shard_map/ppermute | solution.py:24
  115.8 0.0 copy-done.1
  115.8 0.0 copy-start.2
  115.8 0.7 copy-done.2
  116.5 5.5 %grads.2 = (bf16[128,1024]{1,0:T(8,128)(2,1)}, bf16[128,2048]{1,0:T(8,128)(2,1)}, bf16[128,2048]{1,0:T(8,128)(2,1)}) custom-call(s32[1]{0:T(128)} %bitcast.1.place_ref, f32[672,128]{1,0:T(8,128)} %copy-done.2, f32[672,128]{1,0:T(8,128)} %copy-done, f32[672,128]{1,0:T(8,128)} %copy-done.1, bf16[128,2048]{1,0:T(8,128)(2,1)} %refs_3_.5, ...), custom_call_target="tpu_custom_call" | custom-call | flops 671088640 | bytes 3932160 | tf_op jit(solution)/shard_map/grads/pallas_call | solution.py:226
  122.1 1.9 %collective-permute-start.16 = (bf16[128,1024]{1,0:T(8,128)(2,1)}, bf16[128,1024]{1,0:T(8,128)(2,1)}, u32[]{:S(2)}, u32[]{:S(2)}) collective-permute-start(bf16[128,1024]{1,0:T(8,128)(2,1)} %get-tuple-element.16), channel_id=1, source_target_pairs={{0,2},{1,3},{2,0},{3,1},{4,6},{5,7},{6,4},{7,5},{8,10},{9,11},{10,... | collective-permute-start | bytes 786440 | tf_op jit(solution)/shard_map/ppermute | solution.py:29
  124.0 5.3 %grads.3 = (bf16[128,1024]{1,0:T(8,128)(2,1)}, bf16[128,2048]{1,0:T(8,128)(2,1)}, bf16[128,2048]{1,0:T(8,128)(2,1)}) custom-call(s32[1]{0:T(128)} %bitcast.1.place_ref, f32[672,128]{1,0:T(8,128)} %copy-done.2, f32[672,128]{1,0:T(8,128)} %copy-done, f32[672,128]{1,0:T(8,128)} %copy-done.1, ...), custom_call_target="tpu_custom_call", output_to_operand_aliasing={{1}: (16, {}), {2}: (17, {})} | custom-call | flops 671088640 | bytes 3932160 | tf_op jit(solution)/shard_map/grads/pallas_call | solution.py:226
  129.3 7.0 %collective-permute-start.13 = (bf16[128,2048]{1,0:T(8,128)(2,1)}, bf16[128,2048]{1,0:T(8,128)(2,1)}, u32[]{:S(2)}, u32[]{:S(2)}) collective-permute-start(bf16[128,2048]{1,0:T(8,128)(2,1)} %get-tuple-element.14.refs_0_), channel_id=1, source_target_pairs={{0,1},{1,0},{2,3},{3,2},{4,5},{5,4},{6,7},{7,6},{8,9},{9,8},{10,11... | collective-permute-start | bytes 1572872 | tf_op jit(solution)/shard_map/ppermute | solution.py:29
  136.4 3.6 %collective-permute-start.14 = (bf16[128,1024]{1,0:T(8,128)(2,1)}, bf16[128,1024]{1,0:T(8,128)(2,1)}, u32[]{:S(2)}, u32[]{:S(2)}) collective-permute-start(bf16[128,1024]{1,0:T(8,128)(2,1)} %get-tuple-element.15), channel_id=1, source_target_pairs={{0,2},{1,3},{2,0},{3,1},{4,6},{5,7},{6,4},{7,5},{8,10},{9,11},{10,... | collective-permute-start | bytes 786440 | tf_op jit(solution)/shard_map/ppermute | solution.py:29
  140.0 0.0 collective-permute-done.16.refs_2_
  140.0 2.2 %collective-permute-start.17 = (bf16[128,1024]{1,0:T(8,128)(2,1)}, bf16[128,1024]{1,0:T(8,128)(2,1)}, u32[]{:S(2)}, u32[]{:S(2)}) collective-permute-start(bf16[128,1024]{1,0:T(8,128)(2,1)} %collective-permute-done.16.refs_2_), channel_id=1, source_target_pairs={{0,1},{1,0},{2,3},{3,2},{4,5},{5,4},{6,7},{7,6},{8,9},{9,8},{10,11... | collective-permute-start | bytes 786440 | tf_op jit(solution)/shard_map/ppermute | solution.py:29
  142.3 4.7 %collective-permute-done.14.refs_2_ = bf16[128,1024]{1,0:T(8,128)(2,1)} collective-permute-done((bf16[128,1024]{1,0:T(8,128)(2,1)}, bf16[128,1024]{1,0:T(8,128)(2,1)}, u32[]{:S(2)}, u32[]{:S(2)}) %collective-permute-start.14) | collective-permute-done | bytes 262176 | tf_op jit(solution)/shard_map/ppermute | solution.py:29
  147.0 2.5 %collective-permute-start.15 = (bf16[128,1024]{1,0:T(8,128)(2,1)}, bf16[128,1024]{1,0:T(8,128)(2,1)}, u32[]{:S(2)}, u32[]{:S(2)}) collective-permute-start(bf16[128,1024]{1,0:T(8,128)(2,1)} %collective-permute-done.14.refs_2_), channel_id=1, source_target_pairs={{0,1},{1,0},{2,3},{3,2},{4,5},{5,4},{6,7},{7,6},{8,9},{9,8},{10,11... | collective-permute-start | bytes 786440 | tf_op jit(solution)/shard_map/ppermute | solution.py:29
  149.5 0.0 collective-permute-done.17.refs_3_
  149.5 0.0 collective-permute-done.13.refs_1_
  149.5 3.1 %weight.2.refs_4_ = bf16[512,2048]{1,0:T(8,128)(2,1)} custom-call(bf16[512,512]{1,0:T(8,128)(2,1)} %maximum_bitcast_fusion.inputs_ref, bf16[128,2048]{1,0:T(8,128)(2,1)} %get-tuple-element.14.refs_0_, bf16[128,2048]{1,0:T(8,128)(2,1)} %collective-permute-done.13.refs_1_, bf16[128,1024]{1,0:T(8,128)(2,1)} %collective-permute-done.16.refs_2_, ...), custom_call_target="tpu_custom_call" | custom-call | flops 536870912 | bytes 2097152 | tf_op jit(solution)/shard_map/weight/pallas_call | solution.py:255
  152.6 0.0 collective-permute-done.15.refs_3_
  152.6 3.1 %weight.3 = bf16[512,2048]{1,0:T(8,128)(2,1)} custom-call(bf16[512,512]{1,0:T(8,128)(2,1)} %maximum_bitcast_fusion.inputs_ref, bf16[128,2048]{1,0:T(8,128)(2,1)} %get-tuple-element.14.refs_0_, bf16[128,2048]{1,0:T(8,128)(2,1)} %collective-permute-done.13.refs_1_, bf16[128,1024]{1,0:T(8,128)(2,1)} %collective-permute-done.14.refs_2_, ...), custom_call_target="tpu_custom_call", output_to_operand_aliasing={{}: (5, {})} | custom-call | flops 536870912 | bytes 2097152 | tf_op jit(solution)/shard_map/weight/pallas_call | solution.py:255
Async XLA Ops:
  0.6 29.0 %collective-permute-start = (bf16[128,2048]{1,0:T(8,128)(2,1)}, bf16[128,2048]{1,0:T(8,128)(2,1)}, u32[]{:S(2)}, u32[]{:S(2)}) collective-permute-start(bf16[128,2048]{1,0:T(8,128)(2,1)} %refs_10_.3), channel_id=1, source_target_pairs={{0,4},{4,8},{8,12},{12,16},{16,20},{20,24},{24,28},{28,32},{32,36}... | collective-permute-start | bytes 1572872 | tf_op jit(solution)/shard_map/ppermute | solution.py:24
  4.7 36.1 %collective-permute-start.7 = (bf16[128,2048]{1,0:T(8,128)(2,1)}, bf16[128,2048]{1,0:T(8,128)(2,1)}, u32[]{:S(2)}, u32[]{:S(2)}) collective-permute-start(bf16[128,2048]{1,0:T(8,128)(2,1)} %refs_5_.3), channel_id=1, source_target_pairs={{0,4},{4,8},{8,12},{12,16},{16,20},{20,24},{24,28},{28,32},{32,36}... | collective-permute-start | bytes 1572872 | tf_op jit(solution)/shard_map/ppermute | solution.py:24
  7.9 34.8 %collective-permute-start.5 = (bf16[128,2048]{1,0:T(8,128)(2,1)}, bf16[128,2048]{1,0:T(8,128)(2,1)}, u32[]{:S(2)}, u32[]{:S(2)}) collective-permute-start(bf16[128,2048]{1,0:T(8,128)(2,1)} %refs_5_.3), channel_id=1, source_target_pairs={{0,508},{4,0},{8,4},{12,8},{16,12},{20,16},{24,20},{28,24},{32,28}... | collective-permute-start | bytes 1572872 | tf_op jit(solution)/shard_map/ppermute | solution.py:24
  21.4 30.4 %collective-permute-start.9 = (bf16[128,2048]{1,0:T(8,128)(2,1)}, bf16[128,2048]{1,0:T(8,128)(2,1)}, u32[]{:S(2)}, u32[]{:S(2)}) collective-permute-start(bf16[128,2048]{1,0:T(8,128)(2,1)} %refs_10_.3), channel_id=1, source_target_pairs={{0,508},{4,0},{8,4},{12,8},{16,12},{20,16},{24,20},{28,24},{32,28}... | collective-permute-start | bytes 1572872 | tf_op jit(solution)/shard_map/ppermute | solution.py:24
  26.0 27.8 %collective-permute-start.4 = (bf16[128,512]{0,1:T(8,128)(2,1)S(1)}, bf16[128,512]{0,1:T(8,128)(2,1)S(1)}, u32[]{:S(2)}, u32[]{:S(2)}) collective-permute-start(bf16[128,512]{0,1:T(8,128)(2,1)S(1)} %copy.18), channel_id=1, source_target_pairs={{0,3},{1,2},{2,1},{3,0},{4,7},{5,6},{6,5},{7,4},{8,11},{9,10},{10,... | collective-permute-start | bytes 393224 | tf_op jit(solution)/shard_map/ppermute | solution.py:29
  29.7 42.1 %collective-permute-start.1 = (bf16[128,2048]{1,0:T(8,128)(2,1)}, bf16[128,2048]{1,0:T(8,128)(2,1)}, u32[]{:S(2)}, u32[]{:S(2)}) collective-permute-start(bf16[128,2048]{1,0:T(8,128)(2,1)} %collective-permute-done.refs_5_.refs_12_), channel_id=1, source_target_pairs={{0,4},{4,8},{8,12},{12,16},{16,20},{20,24},{24,28},{28,32},{32,36}... | collective-permute-start | bytes 1572872 | tf_op jit(solution)/shard_map/ppermute | solution.py:24
  40.7 31.0 %collective-permute-start.8 = (bf16[128,2048]{1,0:T(8,128)(2,1)}, bf16[128,2048]{1,0:T(8,128)(2,1)}, u32[]{:S(2)}, u32[]{:S(2)}) collective-permute-start(bf16[128,2048]{1,0:T(8,128)(2,1)} %collective-permute-done.7.refs_2_.refs_7_), channel_id=1, source_target_pairs={{0,4},{4,8},{8,12},{12,16},{16,20},{20,24},{24,28},{28,32},{32,36}... | collective-permute-start | bytes 1572872 | tf_op jit(solution)/shard_map/ppermute | solution.py:24
  42.7 29.1 %collective-permute-start.6 = (bf16[128,2048]{1,0:T(8,128)(2,1)}, bf16[128,2048]{1,0:T(8,128)(2,1)}, u32[]{:S(2)}, u32[]{:S(2)}) collective-permute-start(bf16[128,2048]{1,0:T(8,128)(2,1)} %collective-permute-done.5.refs_1_.refs_6_), channel_id=1, source_target_pairs={{0,508},{4,0},{8,4},{12,8},{16,12},{20,16},{24,20},{28,24},{32,28}... | collective-permute-start | bytes 1572872 | tf_op jit(solution)/shard_map/ppermute | solution.py:24
  51.8 20.4 %collective-permute-start.10 = (bf16[128,2048]{1,0:T(8,128)(2,1)}, bf16[128,2048]{1,0:T(8,128)(2,1)}, u32[]{:S(2)}, u32[]{:S(2)}) collective-permute-start(bf16[128,2048]{1,0:T(8,128)(2,1)} %collective-permute-done.9.refs_4_.refs_11_), channel_id=1, source_target_pairs={{0,508},{4,0},{8,4},{12,8},{16,12},{20,16},{24,20},{28,24},{32,28}... | collective-permute-start | bytes 1572872 | tf_op jit(solution)/shard_map/ppermute | solution.py:24
  53.8 5.6 %collective-permute-start.2 = (bf16[128,512]{0,1:T(8,128)(2,1)S(1)}, bf16[128,512]{0,1:T(8,128)(2,1)S(1)}, u32[]{:S(2)}, u32[]{:S(2)}) collective-permute-start(bf16[128,512]{0,1:T(8,128)(2,1)S(1)} %copy.16), channel_id=1, source_target_pairs={{0,1},{1,0},{2,3},{3,2},{4,5},{5,4},{6,7},{7,6},{8,9},{9,8},{10,11... | collective-permute-start | bytes 393224 | tf_op jit(solution)/shard_map/ppermute | solution.py:29
  59.4 6.7 %collective-permute-start.3 = (bf16[128,512]{0,1:T(8,128)(2,1)S(1)}, bf16[128,512]{0,1:T(8,128)(2,1)S(1)}, u32[]{:S(2)}, u32[]{:S(2)}) collective-permute-start(bf16[128,512]{0,1:T(8,128)(2,1)S(1)} %copy.17), channel_id=1, source_target_pairs={{0,2},{1,3},{2,0},{3,1},{4,6},{5,7},{6,4},{7,5},{8,10},{9,11},{10,... | collective-permute-start | bytes 393224 | tf_op jit(solution)/shard_map/ppermute | solution.py:29
  92.5 11.7 %copy-start = (f32[672,128]{1,0:T(8,128)}, f32[672,128]{1,0:T(8,128)S(1)}, u32[]{:S(2)}) copy-start(f32[672,128]{1,0:T(8,128)S(1)} %all_gather.3.refs_1_) | copy-start | bytes 1032196
  92.5 15.9 %collective-permute-start.12 = (f32[672,128]{1,0:T(8,128)S(1)}, f32[672,128]{1,0:T(8,128)S(1)}, u32[]{:S(2)}, u32[]{:S(2)}) collective-permute-start(f32[672,128]{1,0:T(8,128)S(1)} %all_gather.3.refs_1_), channel_id=1, source_target_pairs={{0,496},{4,500},{8,504},{12,508},{16,0},{20,4},{24,8},{28,12},{32,... | collective-permute-start | bytes 1032200 | tf_op jit(solution)/shard_map/ppermute | solution.py:24
  104.2 11.6 %collective-permute-start.11 = (f32[672,128]{1,0:T(8,128)S(1)}, f32[672,128]{1,0:T(8,128)S(1)}, u32[]{:S(2)}, u32[]{:S(2)}) collective-permute-start(f32[672,128]{1,0:T(8,128)S(1)} %all_gather.3.refs_1_), channel_id=1, source_target_pairs={{0,16},{4,20},{8,24},{12,28},{16,32},{20,36},{24,40},{28,44},{32,4... | collective-permute-start | bytes 1032200 | tf_op jit(solution)/shard_map/ppermute | solution.py:24
  108.3 7.4 %copy-start.1 = (f32[672,128]{1,0:T(8,128)}, f32[672,128]{1,0:T(8,128)S(1)}, u32[]{:S(2)}) copy-start(f32[672,128]{1,0:T(8,128)S(1)} %collective-permute-done.12.refs_2_) | copy-start | bytes 1032196
  115.8 0.7 copy-start.2
  122.1 18.0 %collective-permute-start.16 = (bf16[128,1024]{1,0:T(8,128)(2,1)}, bf16[128,1024]{1,0:T(8,128)(2,1)}, u32[]{:S(2)}, u32[]{:S(2)}) collective-permute-start(bf16[128,1024]{1,0:T(8,128)(2,1)} %get-tuple-element.16), channel_id=1, source_target_pairs={{0,2},{1,3},{2,0},{3,1},{4,6},{5,7},{6,4},{7,5},{8,10},{9,11},{10,... | collective-permute-start | bytes 786440 | tf_op jit(solution)/shard_map/ppermute | solution.py:29
  129.3 20.2 %collective-permute-start.13 = (bf16[128,2048]{1,0:T(8,128)(2,1)}, bf16[128,2048]{1,0:T(8,128)(2,1)}, u32[]{:S(2)}, u32[]{:S(2)}) collective-permute-start(bf16[128,2048]{1,0:T(8,128)(2,1)} %get-tuple-element.14.refs_0_), channel_id=1, source_target_pairs={{0,1},{1,0},{2,3},{3,2},{4,5},{5,4},{6,7},{7,6},{8,9},{9,8},{10,11... | collective-permute-start | bytes 1572872 | tf_op jit(solution)/shard_map/ppermute | solution.py:29
  136.4 10.6 %collective-permute-start.14 = (bf16[128,1024]{1,0:T(8,128)(2,1)}, bf16[128,1024]{1,0:T(8,128)(2,1)}, u32[]{:S(2)}, u32[]{:S(2)}) collective-permute-start(bf16[128,1024]{1,0:T(8,128)(2,1)} %get-tuple-element.15), channel_id=1, source_target_pairs={{0,2},{1,3},{2,0},{3,1},{4,6},{5,7},{6,4},{7,5},{8,10},{9,11},{10,... | collective-permute-start | bytes 786440 | tf_op jit(solution)/shard_map/ppermute | solution.py:29
  140.0 9.5 %collective-permute-start.17 = (bf16[128,1024]{1,0:T(8,128)(2,1)}, bf16[128,1024]{1,0:T(8,128)(2,1)}, u32[]{:S(2)}, u32[]{:S(2)}) collective-permute-start(bf16[128,1024]{1,0:T(8,128)(2,1)} %collective-permute-done.16.refs_2_), channel_id=1, source_target_pairs={{0,1},{1,0},{2,3},{3,2},{4,5},{5,4},{6,7},{7,6},{8,9},{9,8},{10,11... | collective-permute-start | bytes 786440 | tf_op jit(solution)/shard_map/ppermute | solution.py:29
  147.0 5.6 %collective-permute-start.15 = (bf16[128,1024]{1,0:T(8,128)(2,1)}, bf16[128,1024]{1,0:T(8,128)(2,1)}, u32[]{:S(2)}, u32[]{:S(2)}) collective-permute-start(bf16[128,1024]{1,0:T(8,128)(2,1)} %collective-permute-done.14.refs_2_), channel_id=1, source_target_pairs={{0,1},{1,0},{2,3},{3,2},{4,5},{5,4},{6,7},{7,6},{8,9},{9,8},{10,11... | collective-permute-start | bytes 786440 | tf_op jit(solution)/shard_map/ppermute | solution.py:29

commit v3 on v2

--- a/solution.py
+++ b/solution.py
@@ -18,9 +18,14 @@
 FAR = 1e30
 
 
-def shifted(value, axis, steps):
+def traded(value, axis, size, odd):
     count = lax.axis_size(axis)
-    pairs = [(source, (source + steps) % count) for source in range(count)]
+    blocks = count // size
+    pairs = []
+    for source in range(count):
+        block = source // size
+        step = 1 if (block % 2 == 1) == odd else -1
+        pairs.append((source, (block + step) % blocks * size + source % size))
     return lax.ppermute(value, axis, pairs)
 
 
@@ -75,31 +80,37 @@
             out_ref[pl.ds(start + head, 1), :] = lse[:, cut]
             out_ref[pl.ds(start + STEP + head, 1), :] = mean[:, cut]
 
-    @pl.when(step == 0)
-    def _():
-        if low:
+    if low:
+        each = out_ref.shape[0] // GROUP
+
+        @pl.when(step == steps - 1)
+        def _():
             out_ref[: before_ref.shape[0], :] = before_ref[...]
-            tail = out_ref.shape[0] - TILE
             for slot in range(2):
                 value = offsets_ref[0, slot].astype(jnp.float32)
-                at = tail + slot * STEP
+                at = each - TILE + slot * STEP
                 out_ref[at : at + STEP, :] = jnp.full((STEP, rows), value, jnp.float32)
+            for copy in range(1, GROUP):
+                out_ref[copy * each : (copy + 1) * each, :] = out_ref[:each, :]
 
 
 def merged(stat_ref, me, step, steps):
     stride = stat_ref.shape[0] // (3 * GROUP)
-
-    def tile(place, row):
+    sign = 1 - 2 * (me % 2)
+    sign_real = sign.astype(jnp.float32)
+
+    def tile(hops, row):
+        place = me + GROUP + sign * hops
         return stat_ref[pl.ds(pl.multiple_of(place * stride + row, TILE), TILE), :]
 
     lse_rows, delta_rows = [], []
     for doc in DOCS:
-        owner = me + GROUP + doc
-        offsets = tile(owner, stride - TILE)
+        offsets = tile(doc, stride - TILE) * sign_real
         first, second = offsets[:STEP], offsets[STEP:]
         parts = []
         for hop in DOCS:
-            stat = tile(owner + hop, (DOCS.index(-hop) * steps + step) * TILE)
+            name = -hop if (doc + hop) % 2 == 0 else hop
+            stat = tile(doc + hop, (DOCS.index(name) * steps + step) * TILE)
             lse, mean = stat[:STEP], stat[STEP:]
             if hop:
                 lse = jnp.where((first == hop) | (second == hop), lse, -FAR)
@@ -125,8 +136,9 @@
 
     @pl.when(pl.program_id(0) == 0)
     def _():
-        for at, ref in enumerate(stat_refs):
-            stat_ref[at * each : (at + 1) * each, :] = ref[...]
+        above = 2 - 2 * place_ref[1]
+        for at, ref in ((above, stat_refs[0]), (1, stat_refs[1]), (2 - above, stat_refs[2])):
+            stat_ref[pl.ds(pl.multiple_of(at * each, TILE), each), :] = ref[...]
 
     step = pl.program_id(0) + first_step
     lse, delta = merged(stat_ref, place_ref[0], step, steps)
@@ -159,14 +171,14 @@
     places = lax.axis_size("fsdp")
     params = pltpu.CompilerParams(vmem_limit_bytes=VMEM)
 
-    by_doc = {0: (queries, output_grad)}
-    up_q, down_q = shifted(queries, "dp", -1), shifted(queries, "dp", 1)
-    up_g, down_g = shifted(output_grad, "dp", -1), shifted(output_grad, "dp", 1)
-    by_doc[1], by_doc[-1] = (up_q, up_g), (down_q, down_g)
-    by_doc[2] = shifted(up_q, "dp", -1), shifted(up_g, "dp", -1)
-    by_doc[-2] = shifted(down_q, "dp", 1), shifted(down_g, "dp", 1)
-    query_docs = [by_doc[doc][0] for doc in DOCS]
-    grad_docs = [by_doc[doc][1] for doc in DOCS]
+    others = [traded(array, "dp", 1, True) for array in (queries, output_grad)]
+    firsts = [traded(array, "dp", 1, False) for array in (queries, output_grad)]
+    near = list(zip(firsts, others))
+    seconds = [traded(first, "dp", 1, True) for first in firsts]
+    far = list(zip([traded(other, "dp", 1, False) for other in others], seconds))
+    query_docs, grad_docs = (
+        [array, *near[at], *far[at]] for at, array in enumerate((queries, output_grad))
+    )
 
     width = layer_input.shape[1] // places
     columns = []
@@ -181,7 +193,7 @@
     exps = rows * rows * (features // HD)
     stats = None
     for low, high in ((0, NEAR), (NEAR, docs)):
-        out_rows = high * steps * TILE + (TILE if high == docs else 0)
+        out_rows = high * steps * TILE if high < docs else GROUP * (docs * steps + 1) * TILE
         before = [] if stats is None else [stats]
         stats = pl.pallas_call(
             functools.partial(stats_kernel, low, steps),
@@ -209,9 +221,11 @@
 
     replicas = lax.axis_size("dp")
     groups = [list(range(low, low + GROUP)) for low in range(0, replicas, GROUP)]
-    here = lax.all_gather(stats, "dp", axis=0, tiled=True, axis_index_groups=groups)
-    stat_parts = [shifted(here, "dp", GROUP), here, shifted(here, "dp", -GROUP)]
-    place = (lax.axis_index("dp") % GROUP).astype(jnp.int32).reshape(1)
+    here = lax.all_to_all(stats, "dp", 0, 0, axis_index_groups=groups, tiled=True)
+    after_odd = traded(here, "dp", GROUP, True)
+    stat_parts = [traded(here, "dp", GROUP, False), here, after_odd]
+    replica = lax.axis_index("dp")
+    place = jnp.stack([replica % GROUP, replica // GROUP % 2]).astype(jnp.int32)
 
     each = steps // HALVES
     any_space = pl.BlockSpec(memory_space=pl.ANY)

time: 157 us -> 156 us (level)
  waiting for transfers between devices: 29.5 us -> 17.7 us
  blocking collectives: 16 us -> 24.8 us
    all_to_all x0 -> x1, blocking collectives: none -> 24.8 us  [local(): lax.all_to_all(stats, 'dp', 0, 0, axis_index_groups=groups, tiled=True)]
    all_gather x1 -> x0, blocking collectives: 16 us -> none  [local(): lax.all_gather(stats, 'dp', axis=0, tiled=True, axis_index_groups=groups)]
    ppermute x10, waiting for transfers between devices: 19.2 us -> 7.5 us  [traded(): return lax.ppermute(value, axis, pairs)]
    ppermute x10, starting transfers between devices: 52.6 us -> 54.8 us  [traded(): return lax.ppermute(value, axis, pairs)]
  transfers between devices with their start and end apart: 18 -> 18, of which waited for: 7 -> 7; matrix products, arithmetic and copies ran while one was open for 2% -> 2% of each run, Pallas kernels for 8% -> 9%
where the time goes in v3:
time: 156 us; the launch traced here: 155 us
  starting transfers between devices  81 us (52%)
  Pallas kernels  26.4 us (17%)
  blocking collectives  24.8 us (16%)
  waiting for transfers between devices  17.7 us (11%)
  local copies, waits for them, and re-layouts  2.36 us (2%)
    ppermute x10, starting transfers between devices, traded(): return lax.ppermute(value, axis, pairs)  54.8 us
    ppermute x8, starting transfers between devices, swapped(): return lax.ppermute(value, axis, pairs)  26.1 us
    all_to_all x1, blocking collectives, local(): lax.all_to_all(stats, 'dp', 0, 0, axis_index_groups=groups, tiled=True)  24.8 us
    pallas_call x2, Pallas kernels, local(): pl.pallas_call(functools.partial(grads_kernel, low, steps), grid=(each,),...  11 us
    ppermute x8, waiting for transfers between devices, swapped(): return lax.ppermute(value, axis, pairs)  10.2 us
    pallas_call x2, Pallas kernels, local(): pl.pallas_call(functools.partial(stats_kernel, low, steps), grid=(steps,)...  9.22 us
    ppermute x10, waiting for transfers between devices, traded(): return lax.ppermute(value, axis, pairs)  7.5 us
    pallas_call x2, Pallas kernels, local(): pl.pallas_call(weight_kernel, grid=(each,), in_specs=[pl.BlockSpec(column...  6.24 us
  transfers between devices with their start and end apart: 18, of which 7 were waited for; matrix products, arithmetic and copies ran while one was open for 2% of the time, Pallas kernels for 9%

profile of v3, /device:TPU:1, one launch (start us, length us, event | category | flops | bytes accessed | tf_op | source)
XLA Modules:
  0.0 154.6 jit_solution(1980284870002209854)
XLA Ops:
  0.6 4.0 %collective-permute-start = (bf16[128,2048]{1,0:T(8,128)(2,1)}, bf16[128,2048]{1,0:T(8,128)(2,1)}, u32[]{:S(2)}, u32[]{:S(2)}) collective-permute-start(bf16[128,2048]{1,0:T(8,128)(2,1)} %refs_10_.3), channel_id=1, source_target_pairs={{0,4},{4,0},{8,12},{12,8},{16,20},{20,16},{24,28},{28,24},{32,36},... | collective-permute-start | bytes 1572872 | tf_op jit(solution)/shard_map/ppermute | solution.py:29
  4.7 1.9 %collective-permute-start.7 = (bf16[128,2048]{1,0:T(8,128)(2,1)}, bf16[128,2048]{1,0:T(8,128)(2,1)}, u32[]{:S(2)}, u32[]{:S(2)}) collective-permute-start(bf16[128,2048]{1,0:T(8,128)(2,1)} %refs_5_.3), channel_id=1, source_target_pairs={{0,4},{4,0},{8,12},{12,8},{16,20},{20,16},{24,28},{28,24},{32,36},... | collective-permute-start | bytes 1572872 | tf_op jit(solution)/shard_map/ppermute | solution.py:29
  6.6 16.2 %collective-permute-start.5 = (bf16[128,2048]{1,0:T(8,128)(2,1)}, bf16[128,2048]{1,0:T(8,128)(2,1)}, u32[]{:S(2)}, u32[]{:S(2)}) collective-permute-start(bf16[128,2048]{1,0:T(8,128)(2,1)} %refs_5_.3), channel_id=1, source_target_pairs={{0,508},{4,8},{8,4},{12,16},{16,12},{20,24},{24,20},{28,32},{32,28... | collective-permute-start | bytes 1572872 | tf_op jit(solution)/shard_map/ppermute | solution.py:29
  22.8 1.9 %collective-permute-start.9 = (bf16[128,2048]{1,0:T(8,128)(2,1)}, bf16[128,2048]{1,0:T(8,128)(2,1)}, u32[]{:S(2)}, u32[]{:S(2)}) collective-permute-start(bf16[128,2048]{1,0:T(8,128)(2,1)} %refs_10_.3), channel_id=1, source_target_pairs={{0,508},{4,8},{8,4},{12,16},{16,12},{20,24},{24,20},{28,32},{32,28... | collective-permute-start | bytes 1572872 | tf_op jit(solution)/shard_map/ppermute | solution.py:29
  24.8 1.1 constant_dynamic-slice_fusion.3
  25.9 0.1 copy.18
  26.0 3.6 %collective-permute-start.4 = (bf16[128,512]{0,1:T(8,128)(2,1)S(1)}, bf16[128,512]{0,1:T(8,128)(2,1)S(1)}, u32[]{:S(2)}, u32[]{:S(2)}) collective-permute-start(bf16[128,512]{0,1:T(8,128)(2,1)S(1)} %copy.18), channel_id=1, source_target_pairs={{0,3},{1,2},{2,1},{3,0},{4,7},{5,6},{6,5},{7,4},{8,11},{9,10},{10,... | collective-permute-start | bytes 393224 | tf_op jit(solution)/shard_map/ppermute | solution.py:34
  29.7 0.0 collective-permute-done.refs_4_.refs_11_
  29.7 10.0 %collective-permute-start.1 = (bf16[128,2048]{1,0:T(8,128)(2,1)}, bf16[128,2048]{1,0:T(8,128)(2,1)}, u32[]{:S(2)}, u32[]{:S(2)}) collective-permute-start(bf16[128,2048]{1,0:T(8,128)(2,1)} %collective-permute-done.refs_4_.refs_11_), channel_id=1, source_target_pairs={{0,508},{4,8},{8,4},{12,16},{16,12},{20,24},{24,20},{28,32},{32,28... | collective-permute-start | bytes 1572872 | tf_op jit(solution)/shard_map/ppermute | solution.py:29
  39.6 0.0 collective-permute-done.7.refs_1_.refs_6_
  39.7 4.1 %collective-permute-start.8 = (bf16[128,2048]{1,0:T(8,128)(2,1)}, bf16[128,2048]{1,0:T(8,128)(2,1)}, u32[]{:S(2)}, u32[]{:S(2)}) collective-permute-start(bf16[128,2048]{1,0:T(8,128)(2,1)} %collective-permute-done.7.refs_1_.refs_6_), channel_id=1, source_target_pairs={{0,508},{4,8},{8,4},{12,16},{16,12},{20,24},{24,20},{28,32},{32,28... | collective-permute-start | bytes 1572872 | tf_op jit(solution)/shard_map/ppermute | solution.py:29
  43.7 0.0 collective-permute-done.5.refs_2_.refs_7_
  43.7 1.9 %collective-permute-start.6 = (bf16[128,2048]{1,0:T(8,128)(2,1)}, bf16[128,2048]{1,0:T(8,128)(2,1)}, u32[]{:S(2)}, u32[]{:S(2)}) collective-permute-start(bf16[128,2048]{1,0:T(8,128)(2,1)} %collective-permute-done.5.refs_2_.refs_7_), channel_id=1, source_target_pairs={{0,4},{4,0},{8,12},{12,8},{16,20},{20,16},{24,28},{28,24},{32,36},... | collective-permute-start | bytes 1572872 | tf_op jit(solution)/shard_map/ppermute | solution.py:29
  45.7 0.0 collective-permute-done.9.refs_5_.refs_12_
  45.7 3.4 %collective-permute-start.10 = (bf16[128,2048]{1,0:T(8,128)(2,1)}, bf16[128,2048]{1,0:T(8,128)(2,1)}, u32[]{:S(2)}, u32[]{:S(2)}) collective-permute-start(bf16[128,2048]{1,0:T(8,128)(2,1)} %collective-permute-done.9.refs_5_.refs_12_), channel_id=1, source_target_pairs={{0,4},{4,0},{8,12},{12,8},{16,20},{20,16},{24,28},{28,24},{32,36},... | collective-permute-start | bytes 1572872 | tf_op jit(solution)/shard_map/ppermute | solution.py:29
  49.1 0.1 copy.16
  49.2 0.0 collective-permute-done.4
  49.2 4.3 %collective-permute-start.2 = (bf16[128,512]{0,1:T(8,128)(2,1)S(1)}, bf16[128,512]{0,1:T(8,128)(2,1)S(1)}, u32[]{:S(2)}, u32[]{:S(2)}) collective-permute-start(bf16[128,512]{0,1:T(8,128)(2,1)S(1)} %copy.16), channel_id=1, source_target_pairs={{0,1},{1,0},{2,3},{3,2},{4,5},{5,4},{6,7},{7,6},{8,9},{9,8},{10,11... | collective-permute-start | bytes 393224 | tf_op jit(solution)/shard_map/ppermute | solution.py:34
  53.5 0.1 copy.17
  53.6 0.8 collective-permute-done.2
  54.5 2.2 %collective-permute-start.3 = (bf16[128,512]{0,1:T(8,128)(2,1)S(1)}, bf16[128,512]{0,1:T(8,128)(2,1)S(1)}, u32[]{:S(2)}, u32[]{:S(2)}) collective-permute-start(bf16[128,512]{0,1:T(8,128)(2,1)S(1)} %copy.17), channel_id=1, source_target_pairs={{0,2},{1,3},{2,0},{3,1},{4,6},{5,7},{6,4},{7,5},{8,10},{9,11},{10,... | collective-permute-start | bytes 393224 | tf_op jit(solution)/shard_map/ppermute | solution.py:34
  56.7 0.1 copy.15
  56.8 4.4 %collective-permute-done.3 = bf16[128,512]{0,1:T(8,128)(2,1)S(1)} collective-permute-done((bf16[128,512]{0,1:T(8,128)(2,1)S(1)}, bf16[128,512]{0,1:T(8,128)(2,1)S(1)}, u32[]{:S(2)}, u32[]{:S(2)}) %collective-permute-start.3) | collective-permute-done | bytes 131104 | tf_op jit(solution)/shard_map/ppermute | solution.py:34
  61.2 0.9 maximum_bitcast_fusion.inputs_ref
  62.0 4.8 %stats.2.refs_4_ = f32[96,128]{1,0:T(8,128)} custom-call(s32[1,2]{1,0:T(1,128)} %offsets_ref.3, bf16[128,2048]{1,0:T(8,128)(2,1)} %refs_3_.5, bf16[128,2048]{1,0:T(8,128)(2,1)} %refs_4_.3, bf16[128,2048]{1,0:T(8,128)(2,1)} %refs_5_.3, bf16[128,2048]{1,0:T(8,128)(2,1)} %collective-permute-done.7.refs_1_.refs_6_, ...), custom_call_target="tpu_custom_call" | custom-call | flops 402653184 | bytes 4194304 | tf_op jit(solution)/shard_map/stats/pallas_call | solution.py:198
  66.8 0.0 collective-permute-done.1.refs_3_.refs_14_
  66.8 1.0 collective-permute-done.8.refs_1_.refs_9_
  67.9 0.0 collective-permute-done.6.refs_0_.refs_8_
  67.9 0.9 collective-permute-done.10.refs_2_.refs_13_
  68.8 4.4 %stats.3 = f32[672,128]{1,0:T(8,128)} custom-call(s32[1,2]{1,0:T(1,128)} %offsets_ref.3, bf16[128,2048]{1,0:T(8,128)(2,1)} %refs_3_.5, bf16[128,2048]{1,0:T(8,128)(2,1)} %refs_4_.3, bf16[128,2048]{1,0:T(8,128)(2,1)} %collective-permute-done.6.refs_0_.refs_8_, bf16[128,2048]{1,0:T(8,128)(2,1)} %collective-permute-done.8.refs_1_.refs_9_, ...), custom_call_target="tpu_custom_call" | custom-call | flops 268435456 | bytes 3145728 | tf_op jit(solution)/shard_map/stats/pallas_call | solution.py:198
  73.2 24.8 %all_to_all.11 = f32[4,168,128]{2,1,0:T(8,128)S(1)} all-to-all(f32[4,168,128]{2,1,0:T(8,128)} %bitcast.12), channel_id=1, replica_groups={{0,4,8,12},{16,20,24,28},{32,36,40,44},{48,52,56,60},{64,68,72,76},{80,..., dimensions={0} | all-to-all | bytes 688128 | tf_op jit(solution)/shard_map/all_to_all | solution.py:224
  98.0 0.0 copy-start
  98.0 9.5 %collective-permute-start.12 = (f32[672,128]{1,0:T(8,128)S(1)}, f32[672,128]{1,0:T(8,128)S(1)}, u32[]{:S(2)}, u32[]{:S(2)}) collective-permute-start(f32[672,128]{1,0:T(8,128)S(1)} %bitcast.8), channel_id=1, source_target_pairs={{0,496},{4,500},{8,504},{12,508},{16,32},{20,36},{24,40},{28,44},{... | collective-permute-start | bytes 1032200 | tf_op jit(solution)/shard_map/ppermute | solution.py:29
  107.5 0.0 copy-done
  107.6 1.9 %collective-permute-start.11 = (f32[672,128]{1,0:T(8,128)S(1)}, f32[672,128]{1,0:T(8,128)}, u32[]{:S(2)}, u32[]{:S(2)}) collective-permute-start(f32[672,128]{1,0:T(8,128)S(1)} %bitcast.9), channel_id=1, source_target_pairs={{0,16},{4,20},{8,24},{12,28},{16,0},{20,4},{24,8},{28,12},{32,48},... | collective-permute-start | bytes 1032200 | tf_op jit(solution)/shard_map/ppermute | solution.py:29
  109.5 0.6 pad_add_fusion.place_ref
  110.1 3.4 %collective-permute-done.12.refs_2_ = f32[672,128]{1,0:T(8,128)S(1)} collective-permute-done((f32[672,128]{1,0:T(8,128)S(1)}, f32[672,128]{1,0:T(8,128)S(1)}, u32[]{:S(2)}, u32[]{:S(2)}) %collective-permute-start.12) | collective-permute-done | bytes 344096 | tf_op jit(solution)/shard_map/ppermute | solution.py:29
  113.5 0.0 copy-start.1
  113.5 0.7 copy-done.1
  114.2 2.2 %collective-permute-done.11.refs_0_ = f32[672,128]{1,0:T(8,128)} collective-permute-done((f32[672,128]{1,0:T(8,128)S(1)}, f32[672,128]{1,0:T(8,128)}, u32[]{:S(2)}, u32[]{:S(2)}) %collective-permute-start.11) | collective-permute-done | bytes 344096 | tf_op jit(solution)/shard_map/ppermute | solution.py:29
  116.4 5.6 %grads.2 = (bf16[128,1024]{1,0:T(8,128)(2,1)}, bf16[128,2048]{1,0:T(8,128)(2,1)}, bf16[128,2048]{1,0:T(8,128)(2,1)}) custom-call(s32[2]{0:T(128)} %pad_add_fusion.place_ref, f32[672,128]{1,0:T(8,128)} %collective-permute-done.11.refs_0_, f32[672,128]{1,0:T(8,128)} %bitcast.10, f32[672,128]{1,0:T(8,128)} %copy-done.1, bf16[128,2048]{1,0:T(8,128)(2,1)} %refs_3_.5, ...), custom_call_target="tpu_custom_call" | custom-call | flops 671088640 | bytes 3932160 | tf_op jit(solution)/shard_map/grads/pallas_call | solution.py:240
  122.0 3.0 %collective-permute-start.16 = (bf16[128,1024]{1,0:T(8,128)(2,1)}, bf16[128,1024]{1,0:T(8,128)(2,1)}, u32[]{:S(2)}, u32[]{:S(2)}) collective-permute-start(bf16[128,1024]{1,0:T(8,128)(2,1)} %get-tuple-element.16), channel_id=1, source_target_pairs={{0,2},{1,3},{2,0},{3,1},{4,6},{5,7},{6,4},{7,5},{8,10},{9,11},{10,... | collective-permute-start | bytes 786440 | tf_op jit(solution)/shard_map/ppermute | solution.py:34
  125.0 5.4 %grads.3 = (bf16[128,1024]{1,0:T(8,128)(2,1)}, bf16[128,2048]{1,0:T(8,128)(2,1)}, bf16[128,2048]{1,0:T(8,128)(2,1)}) custom-call(s32[2]{0:T(128)} %pad_add_fusion.place_ref, f32[672,128]{1,0:T(8,128)} %collective-permute-done.11.refs_0_, f32[672,128]{1,0:T(8,128)} %bitcast.11, f32[672,128]{1,0:T(8,128)} %copy-done.1, ...), custom_call_target="tpu_custom_call", output_to_operand_aliasing={{1}: (16, {}), {2}: (17, {})} | custom-call | flops 671088640 | bytes 3932160 | tf_op jit(solution)/shard_map/grads/pallas_call | solution.py:240
  130.4 5.2 %collective-permute-start.13 = (bf16[128,2048]{1,0:T(8,128)(2,1)}, bf16[128,2048]{1,0:T(8,128)(2,1)}, u32[]{:S(2)}, u32[]{:S(2)}) collective-permute-start(bf16[128,2048]{1,0:T(8,128)(2,1)} %get-tuple-element.14.refs_0_), channel_id=1, source_target_pairs={{0,1},{1,0},{2,3},{3,2},{4,5},{5,4},{6,7},{7,6},{8,9},{9,8},{10,11... | collective-permute-start | bytes 1572872 | tf_op jit(solution)/shard_map/ppermute | solution.py:34
  135.5 3.0 %collective-permute-start.14 = (bf16[128,1024]{1,0:T(8,128)(2,1)}, bf16[128,1024]{1,0:T(8,128)(2,1)}, u32[]{:S(2)}, u32[]{:S(2)}) collective-permute-start(bf16[128,1024]{1,0:T(8,128)(2,1)} %get-tuple-element.15), channel_id=1, source_target_pairs={{0,2},{1,3},{2,0},{3,1},{4,6},{5,7},{6,4},{7,5},{8,10},{9,11},{10,... | collective-permute-start | bytes 786440 | tf_op jit(solution)/shard_map/ppermute | solution.py:34
  138.5 0.0 collective-permute-done.16.refs_2_
  138.5 2.2 %collective-permute-start.17 = (bf16[128,1024]{1,0:T(8,128)(2,1)}, bf16[128,1024]{1,0:T(8,128)(2,1)}, u32[]{:S(2)}, u32[]{:S(2)}) collective-permute-start(bf16[128,1024]{1,0:T(8,128)(2,1)} %collective-permute-done.16.refs_2_), channel_id=1, source_target_pairs={{0,1},{1,0},{2,3},{3,2},{4,5},{5,4},{6,7},{7,6},{8,9},{9,8},{10,11... | collective-permute-start | bytes 786440 | tf_op jit(solution)/shard_map/ppermute | solution.py:34
  140.7 4.9 %collective-permute-done.14.refs_2_ = bf16[128,1024]{1,0:T(8,128)(2,1)} collective-permute-done((bf16[128,1024]{1,0:T(8,128)(2,1)}, bf16[128,1024]{1,0:T(8,128)(2,1)}, u32[]{:S(2)}, u32[]{:S(2)}) %collective-permute-start.14) | collective-permute-done | bytes 262176 | tf_op jit(solution)/shard_map/ppermute | solution.py:34
  145.7 2.7 %collective-permute-start.15 = (bf16[128,1024]{1,0:T(8,128)(2,1)}, bf16[128,1024]{1,0:T(8,128)(2,1)}, u32[]{:S(2)}, u32[]{:S(2)}) collective-permute-start(bf16[128,1024]{1,0:T(8,128)(2,1)} %collective-permute-done.14.refs_2_), channel_id=1, source_target_pairs={{0,1},{1,0},{2,3},{3,2},{4,5},{5,4},{6,7},{7,6},{8,9},{9,8},{10,11... | collective-permute-start | bytes 786440 | tf_op jit(solution)/shard_map/ppermute | solution.py:34
  148.4 0.0 collective-permute-done.17.refs_3_
  148.4 0.0 collective-permute-done.13.refs_1_
  148.4 3.1 %weight.2.refs_4_ = bf16[512,2048]{1,0:T(8,128)(2,1)} custom-call(bf16[512,512]{1,0:T(8,128)(2,1)} %maximum_bitcast_fusion.inputs_ref, bf16[128,2048]{1,0:T(8,128)(2,1)} %get-tuple-element.14.refs_0_, bf16[128,2048]{1,0:T(8,128)(2,1)} %collective-permute-done.13.refs_1_, bf16[128,1024]{1,0:T(8,128)(2,1)} %collective-permute-done.16.refs_2_, ...), custom_call_target="tpu_custom_call" | custom-call | flops 536870912 | bytes 2097152 | tf_op jit(solution)/shard_map/weight/pallas_call | solution.py:269
  151.5 0.0 collective-permute-done.15.refs_3_
  151.5 3.1 %weight.3 = bf16[512,2048]{1,0:T(8,128)(2,1)} custom-call(bf16[512,512]{1,0:T(8,128)(2,1)} %maximum_bitcast_fusion.inputs_ref, bf16[128,2048]{1,0:T(8,128)(2,1)} %get-tuple-element.14.refs_0_, bf16[128,2048]{1,0:T(8,128)(2,1)} %collective-permute-done.13.refs_1_, bf16[128,1024]{1,0:T(8,128)(2,1)} %collective-permute-done.14.refs_2_, ...), custom_call_target="tpu_custom_call", output_to_operand_aliasing={{}: (5, {})} | custom-call | flops 536870912 | bytes 2097152 | tf_op jit(solution)/shard_map/weight/pallas_call | solution.py:269
Async XLA Ops:
  0.6 29.0 %collective-permute-start = (bf16[128,2048]{1,0:T(8,128)(2,1)}, bf16[128,2048]{1,0:T(8,128)(2,1)}, u32[]{:S(2)}, u32[]{:S(2)}) collective-permute-start(bf16[128,2048]{1,0:T(8,128)(2,1)} %refs_10_.3), channel_id=1, source_target_pairs={{0,4},{4,0},{8,12},{12,8},{16,20},{20,16},{24,28},{28,24},{32,36},... | collective-permute-start | bytes 1572872 | tf_op jit(solution)/shard_map/ppermute | solution.py:29
  4.7 35.0 %collective-permute-start.7 = (bf16[128,2048]{1,0:T(8,128)(2,1)}, bf16[128,2048]{1,0:T(8,128)(2,1)}, u32[]{:S(2)}, u32[]{:S(2)}) collective-permute-start(bf16[128,2048]{1,0:T(8,128)(2,1)} %refs_5_.3), channel_id=1, source_target_pairs={{0,4},{4,0},{8,12},{12,8},{16,20},{20,16},{24,28},{28,24},{32,36},... | collective-permute-start | bytes 1572872 | tf_op jit(solution)/shard_map/ppermute | solution.py:29
  6.6 37.1 %collective-permute-start.5 = (bf16[128,2048]{1,0:T(8,128)(2,1)}, bf16[128,2048]{1,0:T(8,128)(2,1)}, u32[]{:S(2)}, u32[]{:S(2)}) collective-permute-start(bf16[128,2048]{1,0:T(8,128)(2,1)} %refs_5_.3), channel_id=1, source_target_pairs={{0,508},{4,8},{8,4},{12,16},{16,12},{20,24},{24,20},{28,32},{32,28... | collective-permute-start | bytes 1572872 | tf_op jit(solution)/shard_map/ppermute | solution.py:29
  22.8 22.9 %collective-permute-start.9 = (bf16[128,2048]{1,0:T(8,128)(2,1)}, bf16[128,2048]{1,0:T(8,128)(2,1)}, u32[]{:S(2)}, u32[]{:S(2)}) collective-permute-start(bf16[128,2048]{1,0:T(8,128)(2,1)} %refs_10_.3), channel_id=1, source_target_pairs={{0,508},{4,8},{8,4},{12,16},{16,12},{20,24},{24,20},{28,32},{32,28... | collective-permute-start | bytes 1572872 | tf_op jit(solution)/shard_map/ppermute | solution.py:29
  26.0 23.1 %collective-permute-start.4 = (bf16[128,512]{0,1:T(8,128)(2,1)S(1)}, bf16[128,512]{0,1:T(8,128)(2,1)S(1)}, u32[]{:S(2)}, u32[]{:S(2)}) collective-permute-start(bf16[128,512]{0,1:T(8,128)(2,1)S(1)} %copy.18), channel_id=1, source_target_pairs={{0,3},{1,2},{2,1},{3,0},{4,7},{5,6},{6,5},{7,4},{8,11},{9,10},{10,... | collective-permute-start | bytes 393224 | tf_op jit(solution)/shard_map/ppermute | solution.py:34
  29.7 37.1 %collective-permute-start.1 = (bf16[128,2048]{1,0:T(8,128)(2,1)}, bf16[128,2048]{1,0:T(8,128)(2,1)}, u32[]{:S(2)}, u32[]{:S(2)}) collective-permute-start(bf16[128,2048]{1,0:T(8,128)(2,1)} %collective-permute-done.refs_4_.refs_11_), channel_id=1, source_target_pairs={{0,508},{4,8},{8,4},{12,16},{16,12},{20,24},{24,20},{28,32},{32,28... | collective-permute-start | bytes 1572872 | tf_op jit(solution)/shard_map/ppermute | solution.py:29
  39.7 28.2 %collective-permute-start.8 = (bf16[128,2048]{1,0:T(8,128)(2,1)}, bf16[128,2048]{1,0:T(8,128)(2,1)}, u32[]{:S(2)}, u32[]{:S(2)}) collective-permute-start(bf16[128,2048]{1,0:T(8,128)(2,1)} %collective-permute-done.7.refs_1_.refs_6_), channel_id=1, source_target_pairs={{0,508},{4,8},{8,4},{12,16},{16,12},{20,24},{24,20},{28,32},{32,28... | collective-permute-start | bytes 1572872 | tf_op jit(solution)/shard_map/ppermute | solution.py:29
  43.7 24.1 %collective-permute-start.6 = (bf16[128,2048]{1,0:T(8,128)(2,1)}, bf16[128,2048]{1,0:T(8,128)(2,1)}, u32[]{:S(2)}, u32[]{:S(2)}) collective-permute-start(bf16[128,2048]{1,0:T(8,128)(2,1)} %collective-permute-done.5.refs_2_.refs_7_), channel_id=1, source_target_pairs={{0,4},{4,0},{8,12},{12,8},{16,20},{20,16},{24,28},{28,24},{32,36},... | collective-permute-start | bytes 1572872 | tf_op jit(solution)/shard_map/ppermute | solution.py:29
  45.7 23.1 %collective-permute-start.10 = (bf16[128,2048]{1,0:T(8,128)(2,1)}, bf16[128,2048]{1,0:T(8,128)(2,1)}, u32[]{:S(2)}, u32[]{:S(2)}) collective-permute-start(bf16[128,2048]{1,0:T(8,128)(2,1)} %collective-permute-done.9.refs_5_.refs_12_), channel_id=1, source_target_pairs={{0,4},{4,0},{8,12},{12,8},{16,20},{20,16},{24,28},{28,24},{32,36},... | collective-permute-start | bytes 1572872 | tf_op jit(solution)/shard_map/ppermute | solution.py:29
  49.2 5.3 %collective-permute-start.2 = (bf16[128,512]{0,1:T(8,128)(2,1)S(1)}, bf16[128,512]{0,1:T(8,128)(2,1)S(1)}, u32[]{:S(2)}, u32[]{:S(2)}) collective-permute-start(bf16[128,512]{0,1:T(8,128)(2,1)S(1)} %copy.16), channel_id=1, source_target_pairs={{0,1},{1,0},{2,3},{3,2},{4,5},{5,4},{6,7},{7,6},{8,9},{9,8},{10,11... | collective-permute-start | bytes 393224 | tf_op jit(solution)/shard_map/ppermute | solution.py:34
  54.5 6.7 %collective-permute-start.3 = (bf16[128,512]{0,1:T(8,128)(2,1)S(1)}, bf16[128,512]{0,1:T(8,128)(2,1)S(1)}, u32[]{:S(2)}, u32[]{:S(2)}) collective-permute-start(bf16[128,512]{0,1:T(8,128)(2,1)S(1)} %copy.17), channel_id=1, source_target_pairs={{0,2},{1,3},{2,0},{3,1},{4,6},{5,7},{6,4},{7,5},{8,10},{9,11},{10,... | collective-permute-start | bytes 393224 | tf_op jit(solution)/shard_map/ppermute | solution.py:34
  98.0 9.5 %copy-start = (f32[4,168,128]{2,1,0:T(8,128)}, f32[4,168,128]{2,1,0:T(8,128)S(1)}, u32[]{:S(2)}) copy-start(f32[4,168,128]{2,1,0:T(8,128)S(1)} %all_to_all.11) | copy-start | bytes 1032196
  98.0 15.5 %collective-permute-start.12 = (f32[672,128]{1,0:T(8,128)S(1)}, f32[672,128]{1,0:T(8,128)S(1)}, u32[]{:S(2)}, u32[]{:S(2)}) collective-permute-start(f32[672,128]{1,0:T(8,128)S(1)} %bitcast.8), channel_id=1, source_target_pairs={{0,496},{4,500},{8,504},{12,508},{16,32},{20,36},{24,40},{28,44},{... | collective-permute-start | bytes 1032200 | tf_op jit(solution)/shard_map/ppermute | solution.py:29
  107.6 8.9 %collective-permute-start.11 = (f32[672,128]{1,0:T(8,128)S(1)}, f32[672,128]{1,0:T(8,128)}, u32[]{:S(2)}, u32[]{:S(2)}) collective-permute-start(f32[672,128]{1,0:T(8,128)S(1)} %bitcast.9), channel_id=1, source_target_pairs={{0,16},{4,20},{8,24},{12,28},{16,0},{20,4},{24,8},{28,12},{32,48},... | collective-permute-start | bytes 1032200 | tf_op jit(solution)/shard_map/ppermute | solution.py:29
  113.5 0.7 copy-start.1
  122.0 16.5 %collective-permute-start.16 = (bf16[128,1024]{1,0:T(8,128)(2,1)}, bf16[128,1024]{1,0:T(8,128)(2,1)}, u32[]{:S(2)}, u32[]{:S(2)}) collective-permute-start(bf16[128,1024]{1,0:T(8,128)(2,1)} %get-tuple-element.16), channel_id=1, source_target_pairs={{0,2},{1,3},{2,0},{3,1},{4,6},{5,7},{6,4},{7,5},{8,10},{9,11},{10,... | collective-permute-start | bytes 786440 | tf_op jit(solution)/shard_map/ppermute | solution.py:34
  130.4 18.0 %collective-permute-start.13 = (bf16[128,2048]{1,0:T(8,128)(2,1)}, bf16[128,2048]{1,0:T(8,128)(2,1)}, u32[]{:S(2)}, u32[]{:S(2)}) collective-permute-start(bf16[128,2048]{1,0:T(8,128)(2,1)} %get-tuple-element.14.refs_0_), channel_id=1, source_target_pairs={{0,1},{1,0},{2,3},{3,2},{4,5},{5,4},{6,7},{7,6},{8,9},{9,8},{10,11... | collective-permute-start | bytes 1572872 | tf_op jit(solution)/shard_map/ppermute | solution.py:34
  135.5 10.1 %collective-permute-start.14 = (bf16[128,1024]{1,0:T(8,128)(2,1)}, bf16[128,1024]{1,0:T(8,128)(2,1)}, u32[]{:S(2)}, u32[]{:S(2)}) collective-permute-start(bf16[128,1024]{1,0:T(8,128)(2,1)} %get-tuple-element.15), channel_id=1, source_target_pairs={{0,2},{1,3},{2,0},{3,1},{4,6},{5,7},{6,4},{7,5},{8,10},{9,11},{10,... | collective-permute-start | bytes 786440 | tf_op jit(solution)/shard_map/ppermute | solution.py:34
  138.5 9.8 %collective-permute-start.17 = (bf16[128,1024]{1,0:T(8,128)(2,1)}, bf16[128,1024]{1,0:T(8,128)(2,1)}, u32[]{:S(2)}, u32[]{:S(2)}) collective-permute-start(bf16[128,1024]{1,0:T(8,128)(2,1)} %collective-permute-done.16.refs_2_), channel_id=1, source_target_pairs={{0,1},{1,0},{2,3},{3,2},{4,5},{5,4},{6,7},{7,6},{8,9},{9,8},{10,11... | collective-permute-start | bytes 786440 | tf_op jit(solution)/shard_map/ppermute | solution.py:34
  145.7 5.8 %collective-permute-start.15 = (bf16[128,1024]{1,0:T(8,128)(2,1)}, bf16[128,1024]{1,0:T(8,128)(2,1)}, u32[]{:S(2)}, u32[]{:S(2)}) collective-permute-start(bf16[128,1024]{1,0:T(8,128)(2,1)} %collective-permute-done.14.refs_2_), channel_id=1, source_target_pairs={{0,1},{1,0},{2,3},{3,2},{4,5},{5,4},{6,7},{7,6},{8,9},{9,8},{10,11... | collective-permute-start | bytes 786440 | tf_op jit(solution)/shard_map/ppermute | solution.py:34

commit v4 on v3

--- a/solution.py
+++ b/solution.py
@@ -179,14 +179,6 @@
     query_docs, grad_docs = (
         [array, *near[at], *far[at]] for at, array in enumerate((queries, output_grad))
     )
-
-    width = layer_input.shape[1] // places
-    columns = []
-    for k in range(places):
-        piece = lax.dynamic_slice_in_dim(layer_input, (mine ^ k) * width, width, 1)
-        columns.append(swapped(piece, "fsdp", k) if k else piece)
-    columns = jnp.concatenate(columns, 0).T
-    grad_docs[-1], columns = lax.optimization_barrier((grad_docs[-1], columns))
 
     block = pl.BlockSpec((rows, wide), lambda step: (0, step))
     pair = rows * rows * HD * 2 * (features // HD)
@@ -222,8 +214,17 @@
     replicas = lax.axis_size("dp")
     groups = [list(range(low, low + GROUP)) for low in range(0, replicas, GROUP)]
     here = lax.all_to_all(stats, "dp", 0, 0, axis_index_groups=groups, tiled=True)
+    width = layer_input.shape[1] // places
+    here, layer_input = lax.optimization_barrier((here, layer_input))
+    columns = []
+    for k in range(places):
+        piece = lax.dynamic_slice_in_dim(layer_input, (mine ^ k) * width, width, 1)
+        columns.append(swapped(piece, "fsdp", k) if k else piece)
+    columns = jnp.concatenate(columns, 0).T
+
     after_odd = traded(here, "dp", GROUP, True)
     stat_parts = [traded(here, "dp", GROUP, False), here, after_odd]
+    stat_parts[2], columns = lax.optimization_barrier((stat_parts[2], columns))
     replica = lax.axis_index("dp")
     place = jnp.stack([replica % GROUP, replica // GROUP % 2]).astype(jnp.int32)
 

time: 156 us -> 140 us (0.90)
  blocking collectives: 24.8 us -> 0 us
  waiting for transfers between devices: 17.7 us -> 26.8 us
    all_to_all x1 -> x0, blocking collectives: 24.8 us -> none  [local(): lax.all_to_all(stats, 'dp', 0, 0, axis_index_groups=groups, tiled=True)]
    ppermute x10, waiting for transfers between devices: 7.5 us -> 14.4 us  [traded(): return lax.ppermute(value, axis, pairs)]
    all_to_all x0 -> x1, waiting for transfers between devices: none -> 5.91 us  [local(): lax.all_to_all(stats, 'dp', 0, 0, axis_index_groups=groups, tiled=True)]
    ppermute x8, waiting for transfers between devices: 10.2 us -> 6.52 us  [swapped(): return lax.ppermute(value, axis, pairs)]
    all_to_all x0 -> x1, starting transfers between devices: none -> 3.46 us  [local(): lax.all_to_all(stats, 'dp', 0, 0, axis_index_groups=groups, tiled=True)]
    ppermute x8, starting transfers between devices: 26.1 us -> 23.7 us  [swapped(): return lax.ppermute(value, axis, pairs)]
  transfers between devices with their start and end apart: 18 -> 19, of which waited for: 7 -> 5; matrix products, arithmetic and copies ran while one was open for 2% -> 2% of each run, Pallas kernels for 9% -> 10%
where the time goes in v4:
time: 140 us; the launch traced here: 139 us
  starting transfers between devices  81.3 us (58%)
  waiting for transfers between devices  26.8 us (19%)
  Pallas kernels  26.4 us (19%)
  local copies, waits for them, and re-layouts  2.1 us (2%)
  other arithmetic  1.54 us (1%)
    ppermute x10, starting transfers between devices, traded(): return lax.ppermute(value, axis, pairs)  54.1 us
    ppermute x8, starting transfers between devices, swapped(): return lax.ppermute(value, axis, pairs)  23.7 us
    ppermute x10, waiting for transfers between devices, traded(): return lax.ppermute(value, axis, pairs)  14.4 us
    pallas_call x2, Pallas kernels, local(): pl.pallas_call(functools.partial(grads_kernel, low, steps), grid=(each,),...  11 us
    pallas_call x2, Pallas kernels, local(): pl.pallas_call(functools.partial(stats_kernel, low, steps), grid=(steps,)...  9.23 us
    ppermute x8, waiting for transfers between devices, swapped(): return lax.ppermute(value, axis, pairs)  6.52 us
    pallas_call x2, Pallas kernels, local(): pl.pallas_call(weight_kernel, grid=(each,), in_specs=[pl.BlockSpec(column...  6.24 us
    all_to_all x1, waiting for transfers between devices, local(): lax.all_to_all(stats, 'dp', 0, 0, axis_index_groups=groups, tiled=True)  5.91 us
  transfers between devices with their start and end apart: 19, of which 5 were waited for; matrix products, arithmetic and copies ran while one was open for 2% of the time, Pallas kernels for 10%

profile of v4, /device:TPU:1, one launch (start us, length us, event | category | flops | bytes accessed | tf_op | source)
XLA Modules:
  0.0 139.1 jit_solution(830951322964839056)
XLA Ops:
  0.6 4.0 %collective-permute-start.2 = (bf16[128,2048]{1,0:T(8,128)(2,1)}, bf16[128,2048]{1,0:T(8,128)(2,1)}, u32[]{:S(2)}, u32[]{:S(2)}) collective-permute-start(bf16[128,2048]{1,0:T(8,128)(2,1)} %refs_5_.3), channel_id=1, source_target_pairs={{0,4},{4,0},{8,12},{12,8},{16,20},{20,16},{24,28},{28,24},{32,36},... | collective-permute-start | bytes 1572872 | tf_op jit(solution)/shard_map/ppermute | solution.py:29
  4.7 15.2 %collective-permute-start = (bf16[128,2048]{1,0:T(8,128)(2,1)}, bf16[128,2048]{1,0:T(8,128)(2,1)}, u32[]{:S(2)}, u32[]{:S(2)}) collective-permute-start(bf16[128,2048]{1,0:T(8,128)(2,1)} %refs_5_.3), channel_id=1, source_target_pairs={{0,508},{4,8},{8,4},{12,16},{16,12},{20,24},{24,20},{28,32},{32,28... | collective-permute-start | bytes 1572872 | tf_op jit(solution)/shard_map/ppermute | solution.py:29
  19.9 1.9 %collective-permute-start.6 = (bf16[128,2048]{1,0:T(8,128)(2,1)}, bf16[128,2048]{1,0:T(8,128)(2,1)}, u32[]{:S(2)}, u32[]{:S(2)}) collective-permute-start(bf16[128,2048]{1,0:T(8,128)(2,1)} %refs_10_.3), channel_id=1, source_target_pairs={{0,4},{4,0},{8,12},{12,8},{16,20},{20,16},{24,28},{28,24},{32,36},... | collective-permute-start | bytes 1572872 | tf_op jit(solution)/shard_map/ppermute | solution.py:29
  21.8 2.9 %collective-permute-start.4 = (bf16[128,2048]{1,0:T(8,128)(2,1)}, bf16[128,2048]{1,0:T(8,128)(2,1)}, u32[]{:S(2)}, u32[]{:S(2)}) collective-permute-start(bf16[128,2048]{1,0:T(8,128)(2,1)} %refs_10_.3), channel_id=1, source_target_pairs={{0,508},{4,8},{8,4},{12,16},{16,12},{20,24},{24,20},{28,32},{32,28... | collective-permute-start | bytes 1572872 | tf_op jit(solution)/shard_map/ppermute | solution.py:29
  24.7 0.0 collective-permute-done.2.refs_1_.refs_6_
  24.7 8.1 %collective-permute-start.3 = (bf16[128,2048]{1,0:T(8,128)(2,1)}, bf16[128,2048]{1,0:T(8,128)(2,1)}, u32[]{:S(2)}, u32[]{:S(2)}) collective-permute-start(bf16[128,2048]{1,0:T(8,128)(2,1)} %collective-permute-done.2.refs_1_.refs_6_), channel_id=1, source_target_pairs={{0,508},{4,8},{8,4},{12,16},{16,12},{20,24},{24,20},{28,32},{32,28... | collective-permute-start | bytes 1572872 | tf_op jit(solution)/shard_map/ppermute | solution.py:29
  32.9 0.0 collective-permute-done.refs_2_.refs_7_
  32.9 1.9 %collective-permute-start.1 = (bf16[128,2048]{1,0:T(8,128)(2,1)}, bf16[128,2048]{1,0:T(8,128)(2,1)}, u32[]{:S(2)}, u32[]{:S(2)}) collective-permute-start(bf16[128,2048]{1,0:T(8,128)(2,1)} %collective-permute-done.refs_2_.refs_7_), channel_id=1, source_target_pairs={{0,4},{4,0},{8,12},{12,8},{16,20},{20,16},{24,28},{28,24},{32,36},... | collective-permute-start | bytes 1572872 | tf_op jit(solution)/shard_map/ppermute | solution.py:29
  34.8 0.0 collective-permute-done.6.refs_4_.refs_11_
  34.8 8.9 %collective-permute-start.7 = (bf16[128,2048]{1,0:T(8,128)(2,1)}, bf16[128,2048]{1,0:T(8,128)(2,1)}, u32[]{:S(2)}, u32[]{:S(2)}) collective-permute-start(bf16[128,2048]{1,0:T(8,128)(2,1)} %collective-permute-done.6.refs_4_.refs_11_), channel_id=1, source_target_pairs={{0,508},{4,8},{8,4},{12,16},{16,12},{20,24},{24,20},{28,32},{32,28... | collective-permute-start | bytes 1572872 | tf_op jit(solution)/shard_map/ppermute | solution.py:29
  43.7 0.0 collective-permute-done.4.refs_5_.refs_12_
  43.7 1.9 %collective-permute-start.5 = (bf16[128,2048]{1,0:T(8,128)(2,1)}, bf16[128,2048]{1,0:T(8,128)(2,1)}, u32[]{:S(2)}, u32[]{:S(2)}) collective-permute-start(bf16[128,2048]{1,0:T(8,128)(2,1)} %collective-permute-done.4.refs_5_.refs_12_), channel_id=1, source_target_pairs={{0,4},{4,0},{8,12},{12,8},{16,20},{20,16},{24,28},{28,24},{32,36},... | collective-permute-start | bytes 1572872 | tf_op jit(solution)/shard_map/ppermute | solution.py:29
  45.7 4.8 %stats.2.refs_4_ = f32[96,128]{1,0:T(8,128)} custom-call(s32[1,2]{1,0:T(1,128)} %offsets_ref.3, bf16[128,2048]{1,0:T(8,128)(2,1)} %refs_3_.5, bf16[128,2048]{1,0:T(8,128)(2,1)} %refs_4_.3, bf16[128,2048]{1,0:T(8,128)(2,1)} %refs_5_.3, bf16[128,2048]{1,0:T(8,128)(2,1)} %collective-permute-done.2.refs_1_.refs_6_, ...), custom_call_target="tpu_custom_call" | custom-call | flops 402653184 | bytes 4194304 | tf_op jit(solution)/shard_map/stats/pallas_call | solution.py:190
  50.5 3.1 %collective-permute-done.3.refs_1_.refs_9_ = bf16[128,2048]{1,0:T(8,128)(2,1)} collective-permute-done((bf16[128,2048]{1,0:T(8,128)(2,1)}, bf16[128,2048]{1,0:T(8,128)(2,1)}, u32[]{:S(2)}, u32[]{:S(2)}) %collective-permute-start.3) | collective-permute-done | bytes 524320 | tf_op jit(solution)/shard_map/ppermute | solution.py:29
  53.6 0.0 collective-permute-done.1.refs_0_.refs_8_
  53.6 11.2 %collective-permute-done.7.refs_3_.refs_14_ = bf16[128,2048]{1,0:T(8,128)(2,1)} collective-permute-done((bf16[128,2048]{1,0:T(8,128)(2,1)}, bf16[128,2048]{1,0:T(8,128)(2,1)}, u32[]{:S(2)}, u32[]{:S(2)}) %collective-permute-start.7) | collective-permute-done | bytes 524320 | tf_op jit(solution)/shard_map/ppermute | solution.py:29
  64.8 0.0 collective-permute-done.5.refs_2_.refs_13_
  64.8 4.4 %stats.3 = f32[672,128]{1,0:T(8,128)} custom-call(s32[1,2]{1,0:T(1,128)} %offsets_ref.3, bf16[128,2048]{1,0:T(8,128)(2,1)} %refs_3_.5, bf16[128,2048]{1,0:T(8,128)(2,1)} %refs_4_.3, bf16[128,2048]{1,0:T(8,128)(2,1)} %collective-permute-done.1.refs_0_.refs_8_, bf16[128,2048]{1,0:T(8,128)(2,1)} %collective-permute-done.3.refs_1_.refs_9_, ...), custom_call_target="tpu_custom_call" | custom-call | flops 268435456 | bytes 3145728 | tf_op jit(solution)/shard_map/stats/pallas_call | solution.py:190
  69.3 3.5 %all-to-all-start = ((f32[4,168,128]{2,1,0:T(8,128)}), f32[4,168,128]{2,1,0:T(8,128)S(1)}, u32[]{:S(2)}, u32[]{:S(2)}) async-start(f32[4,168,128]{2,1,0:T(8,128)} %bitcast.12), calls=%async_computation | async-start | bytes 688128 | tf_op jit(solution)/shard_map/all_to_all | solution.py:216
  72.7 5.9 %all-to-all-done = f32[4,168,128]{2,1,0:T(8,128)S(1)} async-done(((f32[4,168,128]{2,1,0:T(8,128)}), f32[4,168,128]{2,1,0:T(8,128)S(1)}, u32[]{:S(2)}, u32[]{:S(2)}) %all-to-all-start) | async-done | bytes 344096 | tf_op jit(solution)/shard_map/all_to_all | solution.py:216
  78.7 0.0 copy-start
  78.7 1.9 %collective-permute-start.12 = (f32[672,128]{1,0:T(8,128)S(1)}, f32[672,128]{1,0:T(8,128)}, u32[]{:S(2)}, u32[]{:S(2)}) collective-permute-start(f32[672,128]{1,0:T(8,128)S(1)} %bitcast.8), channel_id=1, source_target_pairs={{0,16},{4,20},{8,24},{12,28},{16,0},{20,4},{24,8},{28,12},{32,48},... | collective-permute-start | bytes 1032200 | tf_op jit(solution)/shard_map/ppermute | solution.py:29
  80.6 0.0 copy-done
  80.6 7.3 %collective-permute-start.8 = (f32[672,128]{1,0:T(8,128)S(1)}, f32[672,128]{1,0:T(8,128)S(1)}, u32[]{:S(2)}, u32[]{:S(2)}) collective-permute-start(f32[672,128]{1,0:T(8,128)S(1)} %bitcast.9), channel_id=1, source_target_pairs={{0,496},{4,500},{8,504},{12,508},{16,32},{20,36},{24,40},{28,44},{... | collective-permute-start | bytes 1032200 | tf_op jit(solution)/shard_map/ppermute | solution.py:29
  87.9 1.3 copy.11
  89.3 5.7 %collective-permute-start.11 = (bf16[128,512]{0,1:T(8,128)(2,1)S(1)}, bf16[128,512]{0,1:T(8,128)(2,1)S(1)}, u32[]{:S(2)}, u32[]{:S(2)}) collective-permute-start(bf16[128,512]{0,1:T(8,128)(2,1)S(1)} %get-tuple-element.23), channel_id=1, source_target_pairs={{0,3},{1,2},{2,1},{3,0},{4,7},{5,6},{6,5},{7,4},{8,11},{9,10},{10,... | collective-permute-start | bytes 393224 | tf_op jit(solution)/shard_map/ppermute | solution.py:34
  95.0 3.1 %collective-permute-start.10 = (bf16[128,512]{0,1:T(8,128)(2,1)S(1)}, bf16[128,512]{0,1:T(8,128)(2,1)S(1)}, u32[]{:S(2)}, u32[]{:S(2)}) collective-permute-start(bf16[128,512]{0,1:T(8,128)(2,1)S(1)} %get-tuple-element.24), channel_id=1, source_target_pairs={{0,2},{1,3},{2,0},{3,1},{4,6},{5,7},{6,4},{7,5},{8,10},{9,11},{10,... | collective-permute-start | bytes 393224 | tf_op jit(solution)/shard_map/ppermute | solution.py:34
  98.0 1.9 %collective-permute-start.9 = (bf16[128,512]{0,1:T(8,128)(2,1)S(1)}, bf16[128,512]{0,1:T(8,128)(2,1)S(1)}, u32[]{:S(2)}, u32[]{:S(2)}) collective-permute-start(bf16[128,512]{0,1:T(8,128)(2,1)S(1)} %get-tuple-element.25), channel_id=1, source_target_pairs={{0,1},{1,0},{2,3},{3,2},{4,5},{5,4},{6,7},{7,6},{8,9},{9,8},{10,11... | collective-permute-start | bytes 393224 | tf_op jit(solution)/shard_map/ppermute | solution.py:34
  100.0 0.7 pad_add_fusion.place_ref
  100.7 0.0 collective-permute-done.11
  100.7 1.4 %collective-permute-done.10 = bf16[128,512]{0,1:T(8,128)(2,1)S(1)} collective-permute-done((bf16[128,512]{0,1:T(8,128)(2,1)S(1)}, bf16[128,512]{0,1:T(8,128)(2,1)S(1)}, u32[]{:S(2)}, u32[]{:S(2)}) %collective-permute-start.10) | collective-permute-done | bytes 131104 | tf_op jit(solution)/shard_map/ppermute | solution.py:34
  102.1 0.0 collective-permute-done.9
  102.1 0.9 maximum_bitcast_fusion.inputs_ref
  102.9 0.0 collective-permute-done.8.refs_2_
  103.0 0.0 copy-start.1
  103.0 0.7 copy-done.1
  103.7 0.0 collective-permute-done.12.refs_0_
  103.7 5.6 %grads.2 = (bf16[128,1024]{1,0:T(8,128)(2,1)}, bf16[128,2048]{1,0:T(8,128)(2,1)}, bf16[128,2048]{1,0:T(8,128)(2,1)}) custom-call(s32[2]{0:T(128)} %pad_add_fusion.place_ref, f32[672,128]{1,0:T(8,128)} %collective-permute-done.12.refs_0_, f32[672,128]{1,0:T(8,128)} %bitcast.10, f32[672,128]{1,0:T(8,128)} %copy-done.1, bf16[128,2048]{1,0:T(8,128)(2,1)} %refs_3_.5, ...), custom_call_target="tpu_custom_call" | custom-call | flops 671088640 | bytes 3932160 | tf_op jit(solution)/shard_map/grads/pallas_call | solution.py:241
  109.3 2.8 %collective-permute-start.16 = (bf16[128,1024]{1,0:T(8,128)(2,1)}, bf16[128,1024]{1,0:T(8,128)(2,1)}, u32[]{:S(2)}, u32[]{:S(2)}) collective-permute-start(bf16[128,1024]{1,0:T(8,128)(2,1)} %get-tuple-element.20), channel_id=1, source_target_pairs={{0,2},{1,3},{2,0},{3,1},{4,6},{5,7},{6,4},{7,5},{8,10},{9,11},{10,... | collective-permute-start | bytes 786440 | tf_op jit(solution)/shard_map/ppermute | solution.py:34
  112.1 5.4 %grads.3 = (bf16[128,1024]{1,0:T(8,128)(2,1)}, bf16[128,2048]{1,0:T(8,128)(2,1)}, bf16[128,2048]{1,0:T(8,128)(2,1)}) custom-call(s32[2]{0:T(128)} %pad_add_fusion.place_ref, f32[672,128]{1,0:T(8,128)} %collective-permute-done.12.refs_0_, f32[672,128]{1,0:T(8,128)} %bitcast.11, f32[672,128]{1,0:T(8,128)} %copy-done.1, ...), custom_call_target="tpu_custom_call", output_to_operand_aliasing={{1}: (16, {}), {2}: (17, {})} | custom-call | flops 671088640 | bytes 3932160 | tf_op jit(solution)/shard_map/grads/pallas_call | solution.py:241
  117.5 2.5 %collective-permute-start.13 = (bf16[128,2048]{1,0:T(8,128)(2,1)}, bf16[128,2048]{1,0:T(8,128)(2,1)}, u32[]{:S(2)}, u32[]{:S(2)}) collective-permute-start(bf16[128,2048]{1,0:T(8,128)(2,1)} %get-tuple-element.18.refs_0_), channel_id=1, source_target_pairs={{0,1},{1,0},{2,3},{3,2},{4,5},{5,4},{6,7},{7,6},{8,9},{9,8},{10,11... | collective-permute-start | bytes 1572872 | tf_op jit(solution)/shard_map/ppermute | solution.py:34
  120.0 2.8 %collective-permute-start.14 = (bf16[128,1024]{1,0:T(8,128)(2,1)}, bf16[128,1024]{1,0:T(8,128)(2,1)}, u32[]{:S(2)}, u32[]{:S(2)}) collective-permute-start(bf16[128,1024]{1,0:T(8,128)(2,1)} %get-tuple-element.19), channel_id=1, source_target_pairs={{0,2},{1,3},{2,0},{3,1},{4,6},{5,7},{6,4},{7,5},{8,10},{9,11},{10,... | collective-permute-start | bytes 786440 | tf_op jit(solution)/shard_map/ppermute | solution.py:34
  122.9 0.0 collective-permute-done.16.refs_2_
  122.9 2.2 %collective-permute-start.17 = (bf16[128,1024]{1,0:T(8,128)(2,1)}, bf16[128,1024]{1,0:T(8,128)(2,1)}, u32[]{:S(2)}, u32[]{:S(2)}) collective-permute-start(bf16[128,1024]{1,0:T(8,128)(2,1)} %collective-permute-done.16.refs_2_), channel_id=1, source_target_pairs={{0,1},{1,0},{2,3},{3,2},{4,5},{5,4},{6,7},{7,6},{8,9},{9,8},{10,11... | collective-permute-start | bytes 786440 | tf_op jit(solution)/shard_map/ppermute | solution.py:34
  125.1 5.1 %collective-permute-done.14.refs_2_ = bf16[128,1024]{1,0:T(8,128)(2,1)} collective-permute-done((bf16[128,1024]{1,0:T(8,128)(2,1)}, bf16[128,1024]{1,0:T(8,128)(2,1)}, u32[]{:S(2)}, u32[]{:S(2)}) %collective-permute-start.14) | collective-permute-done | bytes 262176 | tf_op jit(solution)/shard_map/ppermute | solution.py:34
  130.2 2.7 %collective-permute-start.15 = (bf16[128,1024]{1,0:T(8,128)(2,1)}, bf16[128,1024]{1,0:T(8,128)(2,1)}, u32[]{:S(2)}, u32[]{:S(2)}) collective-permute-start(bf16[128,1024]{1,0:T(8,128)(2,1)} %collective-permute-done.14.refs_2_), channel_id=1, source_target_pairs={{0,1},{1,0},{2,3},{3,2},{4,5},{5,4},{6,7},{7,6},{8,9},{9,8},{10,11... | collective-permute-start | bytes 786440 | tf_op jit(solution)/shard_map/ppermute | solution.py:34
  132.9 0.0 collective-permute-done.17.refs_3_
  132.9 0.0 collective-permute-done.13.refs_1_
  132.9 3.1 %weight.2.refs_4_ = bf16[512,2048]{1,0:T(8,128)(2,1)} custom-call(bf16[512,512]{1,0:T(8,128)(2,1)} %maximum_bitcast_fusion.inputs_ref, bf16[128,2048]{1,0:T(8,128)(2,1)} %get-tuple-element.18.refs_0_, bf16[128,2048]{1,0:T(8,128)(2,1)} %collective-permute-done.13.refs_1_, bf16[128,1024]{1,0:T(8,128)(2,1)} %collective-permute-done.16.refs_2_, ...), custom_call_target="tpu_custom_call" | custom-call | flops 536870912 | bytes 2097152 | tf_op jit(solution)/shard_map/weight/pallas_call | solution.py:270
  136.0 0.0 collective-permute-done.15.refs_3_
  136.0 3.1 %weight.3 = bf16[512,2048]{1,0:T(8,128)(2,1)} custom-call(bf16[512,512]{1,0:T(8,128)(2,1)} %maximum_bitcast_fusion.inputs_ref, bf16[128,2048]{1,0:T(8,128)(2,1)} %get-tuple-element.18.refs_0_, bf16[128,2048]{1,0:T(8,128)(2,1)} %collective-permute-done.13.refs_1_, bf16[128,1024]{1,0:T(8,128)(2,1)} %collective-permute-done.14.refs_2_, ...), custom_call_target="tpu_custom_call", output_to_operand_aliasing={{}: (5, {})} | custom-call | flops 536870912 | bytes 2097152 | tf_op jit(solution)/shard_map/weight/pallas_call | solution.py:270
  (1 shorter events, 0.0 us)
Async XLA Ops:
  0.6 24.1 %collective-permute-start.2 = (bf16[128,2048]{1,0:T(8,128)(2,1)}, bf16[128,2048]{1,0:T(8,128)(2,1)}, u32[]{:S(2)}, u32[]{:S(2)}) collective-permute-start(bf16[128,2048]{1,0:T(8,128)(2,1)} %refs_5_.3), channel_id=1, source_target_pairs={{0,4},{4,0},{8,12},{12,8},{16,20},{20,16},{24,28},{28,24},{32,36},... | collective-permute-start | bytes 1572872 | tf_op jit(solution)/shard_map/ppermute | solution.py:29
  4.7 28.2 %collective-permute-start = (bf16[128,2048]{1,0:T(8,128)(2,1)}, bf16[128,2048]{1,0:T(8,128)(2,1)}, u32[]{:S(2)}, u32[]{:S(2)}) collective-permute-start(bf16[128,2048]{1,0:T(8,128)(2,1)} %refs_5_.3), channel_id=1, source_target_pairs={{0,508},{4,8},{8,4},{12,16},{16,12},{20,24},{24,20},{28,32},{32,28... | collective-permute-start | bytes 1572872 | tf_op jit(solution)/shard_map/ppermute | solution.py:29
  19.9 14.9 %collective-permute-start.6 = (bf16[128,2048]{1,0:T(8,128)(2,1)}, bf16[128,2048]{1,0:T(8,128)(2,1)}, u32[]{:S(2)}, u32[]{:S(2)}) collective-permute-start(bf16[128,2048]{1,0:T(8,128)(2,1)} %refs_10_.3), channel_id=1, source_target_pairs={{0,4},{4,0},{8,12},{12,8},{16,20},{20,16},{24,28},{28,24},{32,36},... | collective-permute-start | bytes 1572872 | tf_op jit(solution)/shard_map/ppermute | solution.py:29
  21.8 21.9 %collective-permute-start.4 = (bf16[128,2048]{1,0:T(8,128)(2,1)}, bf16[128,2048]{1,0:T(8,128)(2,1)}, u32[]{:S(2)}, u32[]{:S(2)}) collective-permute-start(bf16[128,2048]{1,0:T(8,128)(2,1)} %refs_10_.3), channel_id=1, source_target_pairs={{0,508},{4,8},{8,4},{12,16},{16,12},{20,24},{24,20},{28,32},{32,28... | collective-permute-start | bytes 1572872 | tf_op jit(solution)/shard_map/ppermute | solution.py:29
  24.7 28.8 %collective-permute-start.3 = (bf16[128,2048]{1,0:T(8,128)(2,1)}, bf16[128,2048]{1,0:T(8,128)(2,1)}, u32[]{:S(2)}, u32[]{:S(2)}) collective-permute-start(bf16[128,2048]{1,0:T(8,128)(2,1)} %collective-permute-done.2.refs_1_.refs_6_), channel_id=1, source_target_pairs={{0,508},{4,8},{8,4},{12,16},{16,12},{20,24},{24,20},{28,32},{32,28... | collective-permute-start | bytes 1572872 | tf_op jit(solution)/shard_map/ppermute | solution.py:29
  32.9 20.7 %collective-permute-start.1 = (bf16[128,2048]{1,0:T(8,128)(2,1)}, bf16[128,2048]{1,0:T(8,128)(2,1)}, u32[]{:S(2)}, u32[]{:S(2)}) collective-permute-start(bf16[128,2048]{1,0:T(8,128)(2,1)} %collective-permute-done.refs_2_.refs_7_), channel_id=1, source_target_pairs={{0,4},{4,0},{8,12},{12,8},{16,20},{20,16},{24,28},{28,24},{32,36},... | collective-permute-start | bytes 1572872 | tf_op jit(solution)/shard_map/ppermute | solution.py:29
  34.8 30.0 %collective-permute-start.7 = (bf16[128,2048]{1,0:T(8,128)(2,1)}, bf16[128,2048]{1,0:T(8,128)(2,1)}, u32[]{:S(2)}, u32[]{:S(2)}) collective-permute-start(bf16[128,2048]{1,0:T(8,128)(2,1)} %collective-permute-done.6.refs_4_.refs_11_), channel_id=1, source_target_pairs={{0,508},{4,8},{8,4},{12,16},{16,12},{20,24},{24,20},{28,32},{32,28... | collective-permute-start | bytes 1572872 | tf_op jit(solution)/shard_map/ppermute | solution.py:29
  43.7 21.1 %collective-permute-start.5 = (bf16[128,2048]{1,0:T(8,128)(2,1)}, bf16[128,2048]{1,0:T(8,128)(2,1)}, u32[]{:S(2)}, u32[]{:S(2)}) collective-permute-start(bf16[128,2048]{1,0:T(8,128)(2,1)} %collective-permute-done.4.refs_5_.refs_12_), channel_id=1, source_target_pairs={{0,4},{4,0},{8,12},{12,8},{16,20},{20,16},{24,28},{28,24},{32,36},... | collective-permute-start | bytes 1572872 | tf_op jit(solution)/shard_map/ppermute | solution.py:29
  69.3 9.4 %all-to-all-start = ((f32[4,168,128]{2,1,0:T(8,128)}), f32[4,168,128]{2,1,0:T(8,128)S(1)}, u32[]{:S(2)}, u32[]{:S(2)}) async-start(f32[4,168,128]{2,1,0:T(8,128)} %bitcast.12), calls=%async_computation | async-start | bytes 688128 | tf_op jit(solution)/shard_map/all_to_all | solution.py:216
  78.7 1.9 %copy-start = (f32[4,168,128]{2,1,0:T(8,128)}, f32[4,168,128]{2,1,0:T(8,128)S(1)}, u32[]{:S(2)}) copy-start(f32[4,168,128]{2,1,0:T(8,128)S(1)} %all-to-all-done) | copy-start | bytes 1032196
  78.7 25.0 %collective-permute-start.12 = (f32[672,128]{1,0:T(8,128)S(1)}, f32[672,128]{1,0:T(8,128)}, u32[]{:S(2)}, u32[]{:S(2)}) collective-permute-start(f32[672,128]{1,0:T(8,128)S(1)} %bitcast.8), channel_id=1, source_target_pairs={{0,16},{4,20},{8,24},{12,28},{16,0},{20,4},{24,8},{28,12},{32,48},... | collective-permute-start | bytes 1032200 | tf_op jit(solution)/shard_map/ppermute | solution.py:29
  80.6 22.4 %collective-permute-start.8 = (f32[672,128]{1,0:T(8,128)S(1)}, f32[672,128]{1,0:T(8,128)S(1)}, u32[]{:S(2)}, u32[]{:S(2)}) collective-permute-start(f32[672,128]{1,0:T(8,128)S(1)} %bitcast.9), channel_id=1, source_target_pairs={{0,496},{4,500},{8,504},{12,508},{16,32},{20,36},{24,40},{28,44},{... | collective-permute-start | bytes 1032200 | tf_op jit(solution)/shard_map/ppermute | solution.py:29
  89.3 11.4 %collective-permute-start.11 = (bf16[128,512]{0,1:T(8,128)(2,1)S(1)}, bf16[128,512]{0,1:T(8,128)(2,1)S(1)}, u32[]{:S(2)}, u32[]{:S(2)}) collective-permute-start(bf16[128,512]{0,1:T(8,128)(2,1)S(1)} %get-tuple-element.23), channel_id=1, source_target_pairs={{0,3},{1,2},{2,1},{3,0},{4,7},{5,6},{6,5},{7,4},{8,11},{9,10},{10,... | collective-permute-start | bytes 393224 | tf_op jit(solution)/shard_map/ppermute | solution.py:34
  95.0 7.1 %collective-permute-start.10 = (bf16[128,512]{0,1:T(8,128)(2,1)S(1)}, bf16[128,512]{0,1:T(8,128)(2,1)S(1)}, u32[]{:S(2)}, u32[]{:S(2)}) collective-permute-start(bf16[128,512]{0,1:T(8,128)(2,1)S(1)} %get-tuple-element.24), channel_id=1, source_target_pairs={{0,2},{1,3},{2,0},{3,1},{4,6},{5,7},{6,4},{7,5},{8,10},{9,11},{10,... | collective-permute-start | bytes 393224 | tf_op jit(solution)/shard_map/ppermute | solution.py:34
  98.0 4.1 %collective-permute-start.9 = (bf16[128,512]{0,1:T(8,128)(2,1)S(1)}, bf16[128,512]{0,1:T(8,128)(2,1)S(1)}, u32[]{:S(2)}, u32[]{:S(2)}) collective-permute-start(bf16[128,512]{0,1:T(8,128)(2,1)S(1)} %get-tuple-element.25), channel_id=1, source_target_pairs={{0,1},{1,0},{2,3},{3,2},{4,5},{5,4},{6,7},{7,6},{8,9},{9,8},{10,11... | collective-permute-start | bytes 393224 | tf_op jit(solution)/shard_map/ppermute | solution.py:34
  103.0 0.7 copy-start.1
  109.3 13.6 %collective-permute-start.16 = (bf16[128,1024]{1,0:T(8,128)(2,1)}, bf16[128,1024]{1,0:T(8,128)(2,1)}, u32[]{:S(2)}, u32[]{:S(2)}) collective-permute-start(bf16[128,1024]{1,0:T(8,128)(2,1)} %get-tuple-element.20), channel_id=1, source_target_pairs={{0,2},{1,3},{2,0},{3,1},{4,6},{5,7},{6,4},{7,5},{8,10},{9,11},{10,... | collective-permute-start | bytes 786440 | tf_op jit(solution)/shard_map/ppermute | solution.py:34
  117.5 15.4 %collective-permute-start.13 = (bf16[128,2048]{1,0:T(8,128)(2,1)}, bf16[128,2048]{1,0:T(8,128)(2,1)}, u32[]{:S(2)}, u32[]{:S(2)}) collective-permute-start(bf16[128,2048]{1,0:T(8,128)(2,1)} %get-tuple-element.18.refs_0_), channel_id=1, source_target_pairs={{0,1},{1,0},{2,3},{3,2},{4,5},{5,4},{6,7},{7,6},{8,9},{9,8},{10,11... | collective-permute-start | bytes 1572872 | tf_op jit(solution)/shard_map/ppermute | solution.py:34
  120.0 10.1 %collective-permute-start.14 = (bf16[128,1024]{1,0:T(8,128)(2,1)}, bf16[128,1024]{1,0:T(8,128)(2,1)}, u32[]{:S(2)}, u32[]{:S(2)}) collective-permute-start(bf16[128,1024]{1,0:T(8,128)(2,1)} %get-tuple-element.19), channel_id=1, source_target_pairs={{0,2},{1,3},{2,0},{3,1},{4,6},{5,7},{6,4},{7,5},{8,10},{9,11},{10,... | collective-permute-start | bytes 786440 | tf_op jit(solution)/shard_map/ppermute | solution.py:34
  122.9 10.0 %collective-permute-start.17 = (bf16[128,1024]{1,0:T(8,128)(2,1)}, bf16[128,1024]{1,0:T(8,128)(2,1)}, u32[]{:S(2)}, u32[]{:S(2)}) collective-permute-start(bf16[128,1024]{1,0:T(8,128)(2,1)} %collective-permute-done.16.refs_2_), channel_id=1, source_target_pairs={{0,1},{1,0},{2,3},{3,2},{4,5},{5,4},{6,7},{7,6},{8,9},{9,8},{10,11... | collective-permute-start | bytes 786440 | tf_op jit(solution)/shard_map/ppermute | solution.py:34
  130.2 5.8 %collective-permute-start.15 = (bf16[128,1024]{1,0:T(8,128)(2,1)}, bf16[128,1024]{1,0:T(8,128)(2,1)}, u32[]{:S(2)}, u32[]{:S(2)}) collective-permute-start(bf16[128,1024]{1,0:T(8,128)(2,1)} %collective-permute-done.14.refs_2_), channel_id=1, source_target_pairs={{0,1},{1,0},{2,3},{3,2},{4,5},{5,4},{6,7},{7,6},{8,9},{9,8},{10,11... | collective-permute-start | bytes 786440 | tf_op jit(solution)/shard_map/ppermute | solution.py:34

commit v5 on v3

v5 whole, which is shorter than its diff:
```python
import functools

import jax
import jax.numpy as jnp
from jax import lax
from jax.experimental import pallas as pl
from jax.experimental.pallas import tpu as pltpu
from jax.sharding import PartitionSpec as P

HD = 128
DOCS = (0, 1, -1, 2, -2)
GROUP = 4
STEP = 4
TILE = 8
NEAR = 3
HALVES = 2
WIDE = 512
VMEM = pl.BlockSpec(memory_space=pltpu.VMEM)
PARAMS = pltpu.CompilerParams(vmem_limit_bytes=24 << 20)
FAR = 1e30


def traded(value, axis, size, odd):
    count = lax.axis_size(axis)
    blocks = count // size
    pairs = []
    for source in range(count):
        block = source // size
        step = 1 if (block % 2 == 1) == odd else -1
        pairs.append((source, (block + step) % blocks * size + source % size))
    return lax.ppermute(value, axis, pairs)


def swapped(value, axis, mask):
    pairs = [(source, source ^ mask) for source in range(lax.axis_size(axis))]
    return lax.ppermute(value, axis, pairs)


def dot_nt(a, b):
    return lax.dot_general(a, b, (((1,), (1,)), ((), ())), preferred_element_type=jnp.float32)


def dot_nn(a, b):
    return lax.dot_general(a, b, (((1,), (0,)), ((), ())), preferred_element_type=jnp.float32)


def scores_of(keys, query_rows, own_first):
    scores = dot_nt(keys, query_rows) * (HD ** (-0.5))
    if not own_first:
        return scores
    rows = keys.shape[0]
    own = scores[:, :rows]
    key_at = lax.broadcasted_iota(jnp.int32, own.shape, 0)
    query_at = lax.broadcasted_iota(jnp.int32, own.shape, 1)
    own = jnp.where(key_at <= query_at, own, -FAR)
    return jnp.concatenate([own, scores[:, rows:]], 1)


def in_vmem(array):
    return pltpu.with_memory_space_constraint(array, pltpu.VMEM)


def head_rows(refs, cols):
    return jnp.concatenate([ref[:, cols] for ref in refs], 0)


def stats_kernel(low, offsets_ref, keys_ref, values_ref, *refs):
    count = (len(refs) - 1) // 2
    query_refs, grad_refs, out_ref = refs[:count], refs[count : 2 * count], refs[-1]
    rows, features = keys_ref.shape
    steps = features // (STEP * HD)

    def group(step, carry):
        base = pl.multiple_of(step * TILE, TILE)
        for head in range(STEP):
            cols = pl.ds(pl.multiple_of((step * STEP + head) * HD, HD), HD)
            scores = scores_of(keys_ref[:, cols], head_rows(query_refs, cols), low == 0)
            prob_grad = dot_nt(values_ref[:, cols], head_rows(grad_refs, cols))
            top = jnp.max(scores, 0, keepdims=True)
            weights = jnp.exp(scores - top)
            total = jnp.sum(weights, 0, keepdims=True)
            mean = jnp.sum(weights * prob_grad, 0, keepdims=True) / total
            lse = top + jnp.log(total)
            for doc in range(count):
                cut = slice(doc * rows, (doc + 1) * rows)
                start = base + (low + doc) * steps * TILE
                out_ref[pl.ds(start + head, 1), :] = lse[:, cut]
                out_ref[pl.ds(start + STEP + head, 1), :] = mean[:, cut]
        return carry

    lax.fori_loop(0, steps, group, 0)
    if low:
        before_ref = refs[2 * count]
        each = out_ref.shape[0] // GROUP
        out_ref[: before_ref.shape[0], :] = before_ref[...]
        for slot in range(2):
            value = offsets_ref[0, slot].astype(jnp.float32)
            at = each - TILE + slot * STEP
            out_ref[at : at + STEP, :] = jnp.full((STEP, rows), value, jnp.float32)
        for copy in range(1, GROUP):
            out_ref[copy * each : (copy + 1) * each, :] = out_ref[:each, :]


def merged(stat_ref, me, step, steps):
    stride = stat_ref.shape[0] // (3 * GROUP)
    sign = 1 - 2 * (me % 2)
    sign_real = sign.astype(jnp.float32)

    def tile(hops, row):
        place = me + GROUP + sign * hops
        return stat_ref[pl.ds(pl.multiple_of(place * stride + row, TILE), TILE), :]

    lse_rows, delta_rows = [], []
    for doc in DOCS:
        offsets = tile(doc, stride - TILE) * sign_real
        first, second = offsets[:STEP], offsets[STEP:]
        parts = []
        for hop in DOCS:
            name = -hop if (doc + hop) % 2 == 0 else hop
            stat = tile(doc + hop, (DOCS.index(name) * steps + step) * TILE)
            lse, mean = stat[:STEP], stat[STEP:]
            if hop:
                lse = jnp.where((first == hop) | (second == hop), lse, -FAR)
            parts.append((lse, mean))
        top = functools.reduce(jnp.maximum, [lse for lse, _ in parts])
        weights = [jnp.exp(lse - top) for lse, _ in parts]
        total = sum(weights)
        delta = sum(weight * mean for weight, (_, mean) in zip(weights, parts)) / total
        lse = top + jnp.log(total)
        if doc:
            lse = jnp.where((first == -doc) | (second == -doc), lse, FAR)
        lse_rows.append(lse)
        delta_rows.append(delta)
    return jnp.concatenate(lse_rows, 1), jnp.concatenate(delta_rows, 1)


def grads_kernel(first_step, each, place_ref, *refs):
    count = len(DOCS)
    stat_refs, (keys_ref, values_ref), refs = refs[:3], refs[3:5], refs[5:]
    query_refs, grad_refs = refs[:count], refs[count : 2 * count]
    key_out, value_out, stat_ref = refs[-3:]
    steps = keys_ref.shape[1] // (STEP * HD)
    size = stat_refs[0].shape[0]

    above = 2 - 2 * place_ref[1]
    for at, ref in ((above, stat_refs[0]), (1, stat_refs[1]), (2 - above, stat_refs[2])):
        stat_ref[pl.ds(pl.multiple_of(at * size, TILE), size), :] = ref[...]

    def group(at, carry):
        step = at + first_step
        lse, delta = merged(stat_ref, place_ref[0], step, steps)
        for head in range(STEP):
            cols = pl.ds(pl.multiple_of((step * STEP + head) * HD, HD), HD)
            out_cols = pl.ds(pl.multiple_of((at * STEP + head) * HD, HD), HD)
            query_rows = head_rows(query_refs, cols)
            grad_rows = head_rows(grad_refs, cols)
            scores = scores_of(keys_ref[:, cols], query_rows, True)
            prob_grad = dot_nt(values_ref[:, cols], grad_rows)
            probs = jnp.exp(scores - lse[head : head + 1])
            score_grad = probs * (prob_grad - delta[head : head + 1]) * (HD ** (-0.5))
            key_total = dot_nn(score_grad.astype(jnp.bfloat16), query_rows)
            value_total = dot_nn(probs.astype(jnp.bfloat16), grad_rows)
            key_out[:, out_cols] = key_total.astype(jnp.bfloat16)
            value_out[:, out_cols] = value_total.astype(jnp.bfloat16)
        return carry

    lax.fori_loop(0, each, group, 0)


def weight_kernel(inputs_ref, *refs):
    low = pl.multiple_of(pl.program_id(0) * refs[-1].shape[1], HD)
    cols = pl.ds(low, refs[-1].shape[1])
    grads = jnp.concatenate([ref[:, cols] for ref in refs[:4]], 0)
    refs[-1][...] = dot_nn(inputs_ref[...], grads).astype(jnp.bfloat16)


def call_stats(low, high, partner_offsets, arrays, before):
    rows, features = arrays[0].shape
    heads = features // HD
    docs = len(DOCS)
    out_rows = high * heads // STEP * TILE if high < docs else GROUP * (docs * heads // STEP + 1) * TILE
    pairs = rows * rows * heads * (high - low)
    return pl.pallas_call(
        functools.partial(stats_kernel, low),
        in_specs=[pl.BlockSpec(memory_space=pltpu.SMEM)] + [VMEM] * (len(arrays) + len(before)),
        out_specs=VMEM,
        out_shape=pltpu.VMEM((out_rows, rows), jnp.float32),
        compiler_params=PARAMS,
        cost_estimate=pl.CostEstimate(
            flops=4 * pairs * HD, bytes_accessed=2 * len(arrays) * rows * features, transcendentals=pairs
        ),
        name="stats",
    )(partner_offsets, *map(in_vmem, arrays), *map(in_vmem, before))


def call_grads(low, each, place, stat_parts, arrays):
    rows, features = arrays[0].shape
    pairs = rows * rows * len(DOCS) * each * STEP
    half = (rows, each * STEP * HD)
    return pl.pallas_call(
        functools.partial(grads_kernel, low, each),
        in_specs=[pl.BlockSpec(memory_space=pltpu.SMEM)] + [VMEM] * (3 + len(arrays)),
        out_specs=[VMEM, VMEM],
        out_shape=[pltpu.VMEM(half, jnp.bfloat16), pltpu.VMEM(half, jnp.bfloat16)],
        scratch_shapes=[pltpu.VMEM((3 * stat_parts[0].shape[0], rows), jnp.float32)],
        compiler_params=PARAMS,
        cost_estimate=pl.CostEstimate(
            flops=8 * pairs * HD, bytes_accessed=2 * len(arrays) * half[0] * half[1], transcendentals=pairs
        ),
        name="grads",
    )(place, *map(in_vmem, stat_parts), *map(in_vmem, arrays))


def call_weight(low, columns, pieces, features, held):
    half = pieces[0].shape[1]
    blocks = half // WIDE
    width, tokens = columns.shape
    return pl.pallas_call(
        weight_kernel,
        grid=(blocks,),
        in_specs=[VMEM] * (1 + len(pieces)) + [pl.BlockSpec(memory_space=pl.ANY)] * len(held),
        out_specs=pl.BlockSpec((width, WIDE), lambda step: (0, step + low * blocks)),
        out_shape=jax.ShapeDtypeStruct((width, features), jnp.bfloat16),
        input_output_aliases={1 + len(pieces): 0} if held else {},
        compiler_params=PARAMS,
        cost_estimate=pl.CostEstimate(
            flops=2 * width * tokens * half, bytes_accessed=2 * half * (tokens + width), transcendentals=0
        ),
        name="weight",
    )(*map(in_vmem, [columns, *pieces]), *held)


def local(layer_input, queries, key_vectors, value_vectors, output_grad, partner_offsets):
    rows, features = queries.shape
    steps = features // (HD * STEP)
    docs = len(DOCS)
    mine = lax.axis_index("fsdp")
    places = lax.axis_size("fsdp")

    others = [traded(array, "dp", 1, True) for array in (queries, output_grad)]
    firsts = [traded(array, "dp", 1, False) for array in (queries, output_grad)]
    near = list(zip(firsts, others))
    seconds = [traded(first, "dp", 1, True) for first in firsts]
    far = list(zip([traded(other, "dp", 1, False) for other in others], seconds))
    query_docs, grad_docs = (
        [array, *near[at], *far[at]] for at, array in enumerate((queries, output_grad))
    )

    own = [key_vectors, value_vectors]
    stats = call_stats(0, NEAR, partner_offsets, own + query_docs[:NEAR] + grad_docs[:NEAR], [])

    stats = call_stats(NEAR, docs, partner_offsets, own + query_docs[NEAR:] + grad_docs[NEAR:], [stats])

    width = layer_input.shape[1] // places
    stats, layer_input = lax.optimization_barrier((stats, layer_input))
    columns = []
    for k in range(places):
        piece = lax.dynamic_slice_in_dim(layer_input, (mine ^ k) * width, width, 1)
        columns.append(swapped(piece, "fsdp", k) if k else piece)
    columns = jnp.concatenate(columns, 0).T

    replicas = lax.axis_size("dp")
    groups = [list(range(low, low + GROUP)) for low in range(0, replicas, GROUP)]
    here = lax.all_to_all(stats, "dp", 0, 0, axis_index_groups=groups, tiled=True)
    here, columns = lax.optimization_barrier((here, columns))
    after_odd = traded(here, "dp", GROUP, True)
    stat_parts = [traded(here, "dp", GROUP, False), here, after_odd]
    replica = lax.axis_index("dp")
    place = jnp.stack([replica % GROUP, replica // GROUP % 2]).astype(jnp.int32)

    each = steps // HALVES
    arrays = own + query_docs + grad_docs
    parts = [call_grads(half * each, each, place, stat_parts, arrays) for half in range(HALVES)]

    weight = None
    for half, (key_part, _) in enumerate(parts):
        across = swapped(key_part, "fsdp", 2)
        pieces = [key_part, swapped(key_part, "fsdp", 1), across, swapped(across, "fsdp", 1)]
        held = [] if weight is None else [weight]
        weight = call_weight(half, columns, pieces, features, held)
    return weight[None], jnp.concatenate([value_part for _, value_part in parts], 1)


def solution(mesh):
    return jax.shard_map(
        local,
        mesh=mesh,
        in_specs=(
            P(("dp", "fsdp"), None),
            P(("dp", "fsdp"), None),
            P(("dp", "fsdp"), None),
            P(("dp", "fsdp"), None),
            P(("dp", "fsdp"), None),
            P("dp", None),
        ),
        out_specs=(P("dp", "fsdp", None), P(("dp", "fsdp"), None)),
        check_vma=False,
    )
```

time: 156 us -> 140 us (0.90)
  blocking collectives: 24.8 us -> 0 us
  local copies, waits for them, and re-layouts: 2.36 us -> 13 us
  Pallas kernels: 26.4 us -> 18.3 us
  waiting for transfers between devices: 17.7 us -> 22.6 us
  starting transfers between devices: 81 us -> 82.7 us
    all_to_all x1 -> x0, blocking collectives: 24.8 us -> none  [local(): lax.all_to_all(stats, 'dp', 0, 0, axis_index_groups=groups, tiled=True)]
    ppermute x10, waiting for transfers between devices: 7.5 us -> 20.4 us  [traded(): return lax.ppermute(value, axis, pairs)]
    unnamed x8 -> x38, local copies, waits for them, and re-layouts: 1.22 us -> 11.6 us
    pallas_call x6, Pallas kernels: 26.4 us -> 18.3 us  [the longest x2 8.41 us: call_grads(): pl.pallas_call(functools.partial(grads_kernel, low, each), in_specs=[pl.B...]
    ppermute x8 -> x9, waiting for transfers between devices: 10.2 us -> 2.14 us  [swapped(): return lax.ppermute(value, axis, pairs)]
    all_to_all x0 -> x1, starting transfers between devices: none -> 3.6 us  [local(): lax.all_to_all(stats, 'dp', 0, 0, axis_index_groups=groups, tiled=True)]
    ppermute x8 -> x9, starting transfers between devices: 26.1 us -> 24.6 us  [swapped(): return lax.ppermute(value, axis, pairs)]
  transfers between devices with their start and end apart: 18 -> 20, of which waited for: 7 -> 5; matrix products, arithmetic and copies ran while one was open for 2% -> 2% of each run, Pallas kernels for 9% -> 6%
where the time goes in v5:
time: 140 us; the launch traced here: 139 us
  starting transfers between devices  82.7 us (59%)
  waiting for transfers between devices  22.6 us (16%)
  Pallas kernels  18.3 us (13%)
  local copies, waits for them, and re-layouts  13 us (9%)
    ppermute x10, starting transfers between devices, traded(): return lax.ppermute(value, axis, pairs)  54.5 us
    ppermute x9, starting transfers between devices, swapped(): return lax.ppermute(value, axis, pairs)  24.6 us
    ppermute x10, waiting for transfers between devices, traded(): return lax.ppermute(value, axis, pairs)  20.4 us
    unnamed x38, local copies, waits for them, and re-layouts  11.6 us
    pallas_call x2, Pallas kernels, call_grads(): pl.pallas_call(functools.partial(grads_kernel, low, each), in_specs=[pl.B...  8.41 us
    pallas_call x2, Pallas kernels, call_stats(): pl.pallas_call(functools.partial(stats_kernel, low), in_specs=[pl.BlockSp...  6.52 us
    all_to_all x1, starting transfers between devices, local(): lax.all_to_all(stats, 'dp', 0, 0, axis_index_groups=groups, tiled=True)  3.6 us
    pallas_call x2, Pallas kernels, call_weight(): pl.pallas_call(weight_kernel, grid=(blocks,), in_specs=[VMEM] * (1 + len(...  3.39 us
  transfers between devices with their start and end apart: 20, of which 5 were waited for; matrix products, arithmetic and copies ran while one was open for 2% of the time, Pallas kernels for 6%

profile of v5, /device:TPU:1, one launch (start us, length us, event | category | flops | bytes accessed | tf_op | source)
XLA Modules:
  0.0 138.6 jit_solution(8852374590036551822)
XLA Ops:
  0.6 4.0 %collective-permute-start.2 = (bf16[128,2048]{1,0:T(8,128)(2,1)}, bf16[128,2048]{1,0:T(8,128)(2,1)S(1)}, u32[]{:S(2)}, u32[]{:S(2)}) collective-permute-start(bf16[128,2048]{1,0:T(8,128)(2,1)} %refs_5_.3), channel_id=1, source_target_pairs={{0,4},{4,0},{8,12},{12,8},{16,20},{20,16},{24,28},{28,24},{32,36},... | collective-permute-start | bytes 1572872 | tf_op jit(solution)/shard_map/ppermute | solution.py:31
  4.7 15.2 %collective-permute-start = (bf16[128,2048]{1,0:T(8,128)(2,1)}, bf16[128,2048]{1,0:T(8,128)(2,1)S(1)}, u32[]{:S(2)}, u32[]{:S(2)}) collective-permute-start(bf16[128,2048]{1,0:T(8,128)(2,1)} %refs_5_.3), channel_id=1, source_target_pairs={{0,508},{4,8},{8,4},{12,16},{16,12},{20,24},{24,20},{28,32},{32,28... | collective-permute-start | bytes 1572872 | tf_op jit(solution)/shard_map/ppermute | solution.py:31
  19.9 1.9 %collective-permute-start.6 = (bf16[128,2048]{1,0:T(8,128)(2,1)}, bf16[128,2048]{1,0:T(8,128)(2,1)S(1)}, u32[]{:S(2)}, u32[]{:S(2)}) collective-permute-start(bf16[128,2048]{1,0:T(8,128)(2,1)} %refs_10_.3), channel_id=1, source_target_pairs={{0,4},{4,0},{8,12},{12,8},{16,20},{20,16},{24,28},{28,24},{32,36},... | collective-permute-start | bytes 1572872 | tf_op jit(solution)/shard_map/ppermute | solution.py:31
  21.8 2.9 %collective-permute-start.4 = (bf16[128,2048]{1,0:T(8,128)(2,1)}, bf16[128,2048]{1,0:T(8,128)(2,1)S(1)}, u32[]{:S(2)}, u32[]{:S(2)}) collective-permute-start(bf16[128,2048]{1,0:T(8,128)(2,1)} %refs_10_.3), channel_id=1, source_target_pairs={{0,508},{4,8},{8,4},{12,16},{16,12},{20,24},{24,20},{28,32},{32,28... | collective-permute-start | bytes 1572872 | tf_op jit(solution)/shard_map/ppermute | solution.py:31
  24.7 0.0 collective-permute-done.2.refs_1_.refs_6_
  24.7 8.1 %collective-permute-start.3 = (bf16[128,2048]{1,0:T(8,128)(2,1)S(1)}, bf16[128,2048]{1,0:T(8,128)(2,1)S(1)}, u32[]{:S(2)}, u32[]{:S(2)}) collective-permute-start(bf16[128,2048]{1,0:T(8,128)(2,1)S(1)} %collective-permute-done.2.refs_1_.refs_6_), channel_id=1, source_target_pairs={{0,508},{4,8},{8,4},{12,16},{16,12},{20,24},{24,20},{28,32},{32,28... | collective-permute-start | bytes 1572872 | tf_op jit(solution)/shard_map/ppermute | solution.py:31
  32.8 0.0 collective-permute-done.refs_2_.refs_7_
  32.9 0.0 copy-start.8
  32.9 1.9 %collective-permute-start.1 = (bf16[128,2048]{1,0:T(8,128)(2,1)S(1)}, bf16[128,2048]{1,0:T(8,128)(2,1)S(1)}, u32[]{:S(2)}, u32[]{:S(2)}) collective-permute-start(bf16[128,2048]{1,0:T(8,128)(2,1)S(1)} %collective-permute-done.refs_2_.refs_7_), channel_id=1, source_target_pairs={{0,4},{4,0},{8,12},{12,8},{16,20},{20,16},{24,28},{28,24},{32,36},... | collective-permute-start | bytes 1572872 | tf_op jit(solution)/shard_map/ppermute | solution.py:31
  34.8 0.0 collective-permute-done.6.refs_4_.refs_11_
  34.8 8.8 %collective-permute-start.7 = (bf16[128,2048]{1,0:T(8,128)(2,1)S(1)}, bf16[128,2048]{1,0:T(8,128)(2,1)}, u32[]{:S(2)}, u32[]{:S(2)}) collective-permute-start(bf16[128,2048]{1,0:T(8,128)(2,1)S(1)} %collective-permute-done.6.refs_4_.refs_11_), channel_id=1, source_target_pairs={{0,508},{4,8},{8,4},{12,16},{16,12},{20,24},{24,20},{28,32},{32,28... | collective-permute-start | bytes 1572872 | tf_op jit(solution)/shard_map/ppermute | solution.py:31
  43.6 0.0 collective-permute-done.4.refs_5_.refs_12_
  43.6 1.9 %collective-permute-start.5 = (bf16[128,2048]{1,0:T(8,128)(2,1)S(1)}, bf16[128,2048]{1,0:T(8,128)(2,1)}, u32[]{:S(2)}, u32[]{:S(2)}) collective-permute-start(bf16[128,2048]{1,0:T(8,128)(2,1)S(1)} %collective-permute-done.4.refs_5_.refs_12_), channel_id=1, source_target_pairs={{0,4},{4,0},{8,12},{12,8},{16,20},{20,16},{24,28},{28,24},{32,36},... | collective-permute-start | bytes 1572872 | tf_op jit(solution)/shard_map/ppermute | solution.py:31
  45.6 0.0 copy-start
  45.6 1.0 copy-done
  46.6 1.0 copy-done.2
  47.7 1.0 copy-done.4
  48.7 1.0 copy-done.6
  49.8 0.7 copy-done.18
  50.4 2.8 %stats.2.refs_4_ = f32[96,128]{1,0:T(8,128)S(1)} custom-call(s32[1,2]{1,0:T(1,128)S(1)} %copy-done.18, bf16[128,2048]{1,0:T(8,128)(2,1)S(1)} %copy-done, bf16[128,2048]{1,0:T(8,128)(2,1)S(1)} %copy-done.2, bf16[128,2048]{1,0:T(8,128)(2,1)S(1)} %copy-done.4, bf16[128,2048]{1,0:T(8,128)(2,1)S(1)} %collective-permute-done.2.refs_1_.refs_6_, ...), custom_call_target="tpu_custom_call" | custom-call | flops 402653184 | bytes 4194304 | tf_op jit(solution)/shard_map/stats/pallas_call | solution.py:183
  53.3 0.2 collective-permute-done.3.refs_1_.refs_9_
  53.5 0.0 collective-permute-done.1.refs_0_.refs_8_
  53.5 11.3 %collective-permute-done.7.refs_3_.refs_14_ = bf16[128,2048]{1,0:T(8,128)(2,1)} collective-permute-done((bf16[128,2048]{1,0:T(8,128)(2,1)S(1)}, bf16[128,2048]{1,0:T(8,128)(2,1)}, u32[]{:S(2)}, u32[]{:S(2)}) %collective-permute-start.7) | collective-permute-done | bytes 524320 | tf_op jit(solution)/shard_map/ppermute | solution.py:31
  64.8 0.0 collective-permute-done.5.refs_2_.refs_13_
  64.8 3.7 %stats.3 = f32[672,128]{1,0:T(8,128)} custom-call(s32[1,2]{1,0:T(1,128)S(1)} %copy-done.18, bf16[128,2048]{1,0:T(8,128)(2,1)S(1)} %copy-done, bf16[128,2048]{1,0:T(8,128)(2,1)S(1)} %copy-done.2, bf16[128,2048]{1,0:T(8,128)(2,1)S(1)} %collective-permute-done.1.refs_0_.refs_8_, bf16[128,2048]{1,0:T(8,128)(2,1)S(1)} %collective-permute-done.3.refs_1_.refs_9_, ...), custom_call_target="tpu_custom_call" | custom-call | flops 268435456 | bytes 3145728 | tf_op jit(solution)/shard_map/stats/pallas_call | solution.py:183
  68.5 0.8 copy-done.14
  69.3 0.8 copy-done.16
  70.1 3.6 %all-to-all-start = ((f32[4,168,128]{2,1,0:T(8,128)}), f32[4,168,128]{2,1,0:T(8,128)S(1)}, u32[]{:S(2)}, u32[]{:S(2)}) async-start(f32[4,168,128]{2,1,0:T(8,128)} %bitcast), calls=%async_computation | async-start | bytes 688128 | tf_op jit(solution)/shard_map/all_to_all | solution.py:264
  73.7 1.3 copy.9
  75.1 4.1 %collective-permute-start.10 = (bf16[128,512]{0,1:T(8,128)(2,1)S(1)}, bf16[128,512]{0,1:T(8,128)(2,1)S(1)}, u32[]{:S(2)}, u32[]{:S(2)}) collective-permute-start(bf16[128,512]{0,1:T(8,128)(2,1)S(1)} %get-tuple-element.19), channel_id=1, source_target_pairs={{0,3},{1,2},{2,1},{3,0},{4,7},{5,6},{6,5},{7,4},{8,11},{9,10},{10,... | collective-permute-start | bytes 393224 | tf_op jit(solution)/shard_map/ppermute | solution.py:36
  79.2 3.1 %collective-permute-start.9 = (bf16[128,512]{0,1:T(8,128)(2,1)S(1)}, bf16[128,512]{0,1:T(8,128)(2,1)S(1)}, u32[]{:S(2)}, u32[]{:S(2)}) collective-permute-start(bf16[128,512]{0,1:T(8,128)(2,1)S(1)} %get-tuple-element.20), channel_id=1, source_target_pairs={{0,2},{1,3},{2,0},{3,1},{4,6},{5,7},{6,4},{7,5},{8,10},{9,11},{10,... | collective-permute-start | bytes 393224 | tf_op jit(solution)/shard_map/ppermute | solution.py:36
  82.2 1.9 %collective-permute-start.8 = (bf16[128,512]{0,1:T(8,128)(2,1)S(1)}, bf16[128,512]{0,1:T(8,128)(2,1)S(1)}, u32[]{:S(2)}, u32[]{:S(2)}) collective-permute-start(bf16[128,512]{0,1:T(8,128)(2,1)S(1)} %get-tuple-element.21), channel_id=1, source_target_pairs={{0,1},{1,0},{2,3},{3,2},{4,5},{5,4},{6,7},{7,6},{8,9},{9,8},{10,11... | collective-permute-start | bytes 393224 | tf_op jit(solution)/shard_map/ppermute | solution.py:36
  84.2 0.0 collective-permute-done.10
  84.2 2.1 %collective-permute-done.9 = bf16[128,512]{0,1:T(8,128)(2,1)S(1)} collective-permute-done((bf16[128,512]{0,1:T(8,128)(2,1)S(1)}, bf16[128,512]{0,1:T(8,128)(2,1)S(1)}, u32[]{:S(2)}, u32[]{:S(2)}) %collective-permute-start.9) | collective-permute-done | bytes 131104 | tf_op jit(solution)/shard_map/ppermute | solution.py:36
  86.3 0.0 collective-permute-done.8
  86.3 0.1 maximum_bitcast_fusion.inputs_ref
  86.4 0.0 all-to-all-done
  86.4 7.8 %collective-permute-start.12 = (f32[672,128]{1,0:T(8,128)S(1)}, f32[672,128]{1,0:T(8,128)}, u32[]{:S(2)}, u32[]{:S(2)}) collective-permute-start(f32[672,128]{1,0:T(8,128)S(1)} %bitcast.7), channel_id=1, source_target_pairs={{0,496},{4,500},{8,504},{12,508},{16,32},{20,36},{24,40},{28,44},{... | collective-permute-start | bytes 1032200 | tf_op jit(solution)/shard_map/ppermute | solution.py:31
  94.2 1.9 %collective-permute-start.11 = (f32[672,128]{1,0:T(8,128)S(1)}, f32[672,128]{1,0:T(8,128)}, u32[]{:S(2)}, u32[]{:S(2)}) collective-permute-start(f32[672,128]{1,0:T(8,128)S(1)} %bitcast.8), channel_id=1, source_target_pairs={{0,16},{4,20},{8,24},{12,28},{16,0},{20,4},{24,8},{28,12},{32,48},... | collective-permute-start | bytes 1032200 | tf_op jit(solution)/shard_map/ppermute | solution.py:31
  96.2 0.1 pad_add_fusion.place_ref
  96.2 6.2 %collective-permute-done.12.refs_2_ = f32[672,128]{1,0:T(8,128)} collective-permute-done((f32[672,128]{1,0:T(8,128)S(1)}, f32[672,128]{1,0:T(8,128)}, u32[]{:S(2)}, u32[]{:S(2)}) %collective-permute-start.12) | collective-permute-done | bytes 344096 | tf_op jit(solution)/shard_map/ppermute | solution.py:31
  102.4 2.7 %collective-permute-done.11.refs_0_ = f32[672,128]{1,0:T(8,128)} collective-permute-done((f32[672,128]{1,0:T(8,128)S(1)}, f32[672,128]{1,0:T(8,128)}, u32[]{:S(2)}, u32[]{:S(2)}) %collective-permute-start.11) | collective-permute-done | bytes 344096 | tf_op jit(solution)/shard_map/ppermute | solution.py:31
  105.1 0.0 copy-start.9
  105.2 1.0 copy-done.9
  106.2 1.0 copy-done.11
  107.2 1.0 copy-done.13
  108.3 1.0 copy-done.15
  109.3 1.0 copy-done.17
  110.4 4.2 %grads.3 = (bf16[128,1024]{1,0:T(8,128)(2,1)S(1)}, bf16[128,1024]{1,0:T(8,128)(2,1)S(1)}) custom-call(s32[2]{0:T(128)S(1)} %pad_add_fusion.place_ref, f32[672,128]{1,0:T(8,128)} %collective-permute-done.11.refs_0_, f32[672,128]{1,0:T(8,128)S(1)} %bitcast.9, f32[672,128]{1,0:T(8,128)} %collective-permute-done.12.refs_2_, bf16[128,2048]{1,0:T(8,128)(2,1)S(1)} %copy-done.1, ...), custom_call_target="tpu_custom_call" | custom-call | flops 671088640 | bytes 3145728 | tf_op jit(solution)/shard_map/grads/pallas_call | solution.py:200
  114.6 2.3 %collective-permute-start.17 = (bf16[128,1024]{1,0:T(8,128)(2,1)S(1)}, bf16[128,1024]{1,0:T(8,128)(2,1)S(1)}, u32[]{:S(2)}, u32[]{:S(2)}) collective-permute-start(bf16[128,1024]{1,0:T(8,128)(2,1)S(1)} %get-tuple-element.15.refs_0_), channel_id=1, source_target_pairs={{0,2},{1,3},{2,0},{3,1},{4,6},{5,7},{6,4},{7,5},{8,10},{9,11},{10,... | collective-permute-start | bytes 786440 | tf_op jit(solution)/shard_map/ppermute | solution.py:36
  116.9 4.2 %grads.2 = (bf16[128,1024]{1,0:T(8,128)(2,1)S(1)}, bf16[128,1024]{1,0:T(8,128)(2,1)S(1)}) custom-call(s32[2]{0:T(128)S(1)} %pad_add_fusion.place_ref, f32[672,128]{1,0:T(8,128)} %collective-permute-done.11.refs_0_, f32[672,128]{1,0:T(8,128)S(1)} %bitcast.10, f32[672,128]{1,0:T(8,128)} %collective-permute-done.12.refs_2_, bf16[128,2048]{1,0:T(8,128)(2,1)S(1)} %copy-done.1, ...), custom_call_target="tpu_custom_call" | custom-call | flops 671088640 | bytes 3145728 | tf_op jit(solution)/shard_map/grads/pallas_call | solution.py:200
  121.1 3.0 %collective-permute-start.14 = (bf16[128,1024]{1,0:T(8,128)(2,1)S(1)}, bf16[128,1024]{1,0:T(8,128)(2,1)S(1)}, u32[]{:S(2)}, u32[]{:S(2)}) collective-permute-start(bf16[128,1024]{1,0:T(8,128)(2,1)S(1)} %get-tuple-element.14.refs_0_), channel_id=1, source_target_pairs={{0,2},{1,3},{2,0},{3,1},{4,6},{5,7},{6,4},{7,5},{8,10},{9,11},{10,... | collective-permute-start | bytes 786440 | tf_op jit(solution)/shard_map/ppermute | solution.py:36
  124.1 4.0 %collective-permute-start.16 = (bf16[128,1024]{1,0:T(8,128)(2,1)S(1)}, bf16[128,1024]{1,0:T(8,128)(2,1)S(1)}, u32[]{:S(2)}, u32[]{:S(2)}) collective-permute-start(bf16[128,1024]{1,0:T(8,128)(2,1)S(1)} %get-tuple-element.15.refs_0_), channel_id=1, source_target_pairs={{0,1},{1,0},{2,3},{3,2},{4,5},{5,4},{6,7},{7,6},{8,9},{9,8},{10,11... | collective-permute-start | bytes 786440 | tf_op jit(solution)/shard_map/ppermute | solution.py:36
  128.1 0.0 collective-permute-done.17.refs_2_
  128.1 1.9 %collective-permute-start.18 = (bf16[128,1024]{1,0:T(8,128)(2,1)S(1)}, bf16[128,1024]{1,0:T(8,128)(2,1)S(1)}, u32[]{:S(2)}, u32[]{:S(2)}) collective-permute-start(bf16[128,1024]{1,0:T(8,128)(2,1)S(1)} %collective-permute-done.17.refs_2_), channel_id=1, source_target_pairs={{0,1},{1,0},{2,3},{3,2},{4,5},{5,4},{6,7},{7,6},{8,9},{9,8},{10,11... | collective-permute-start | bytes 786440 | tf_op jit(solution)/shard_map/ppermute | solution.py:36
  130.0 2.4 %collective-permute-start.13 = (bf16[128,1024]{1,0:T(8,128)(2,1)S(1)}, bf16[128,1024]{1,0:T(8,128)(2,1)S(1)}, u32[]{:S(2)}, u32[]{:S(2)}) collective-permute-start(bf16[128,1024]{1,0:T(8,128)(2,1)S(1)} %get-tuple-element.14.refs_0_), channel_id=1, source_target_pairs={{0,1},{1,0},{2,3},{3,2},{4,5},{5,4},{6,7},{7,6},{8,9},{9,8},{10,11... | collective-permute-start | bytes 786440 | tf_op jit(solution)/shard_map/ppermute | solution.py:36
  132.5 0.0 collective-permute-done.14.refs_2_
  132.5 1.9 %collective-permute-start.15 = (bf16[128,1024]{1,0:T(8,128)(2,1)S(1)}, bf16[128,1024]{1,0:T(8,128)(2,1)S(1)}, u32[]{:S(2)}, u32[]{:S(2)}) collective-permute-start(bf16[128,1024]{1,0:T(8,128)(2,1)S(1)} %collective-permute-done.14.refs_2_), channel_id=1, source_target_pairs={{0,1},{1,0},{2,3},{3,2},{4,5},{5,4},{6,7},{7,6},{8,9},{9,8},{10,11... | collective-permute-start | bytes 786440 | tf_op jit(solution)/shard_map/ppermute | solution.py:36
  134.4 0.8 pad_maximum_fusion
  135.2 0.0 collective-permute-done.16.refs_1_
  135.2 0.0 collective-permute-done.18.refs_3_
  135.2 1.7 %weight.2.refs_4_ = bf16[512,2048]{1,0:T(8,128)(2,1)} custom-call(bf16[512,512]{1,0:T(8,128)(2,1)S(1)} %maximum_bitcast_fusion.inputs_ref, bf16[128,1024]{1,0:T(8,128)(2,1)S(1)} %get-tuple-element.15.refs_0_, bf16[128,1024]{1,0:T(8,128)(2,1)S(1)} %collective-permute-done.16.refs_1_, bf16[128,1024]{1,0:T(8,128)(2,1)S(1)} %collective-permute-done.17.refs_2_, ...), custom_call_target="tpu_custom_call" | custom-call | flops 536870912 | bytes 2097152 | tf_op jit(solution)/shard_map/weight/pallas_call | solution.py:218
  136.9 0.0 collective-permute-done.13.refs_1_
  136.9 1.7 %weight.3 = bf16[512,2048]{1,0:T(8,128)(2,1)} custom-call(bf16[512,512]{1,0:T(8,128)(2,1)S(1)} %maximum_bitcast_fusion.inputs_ref, bf16[128,1024]{1,0:T(8,128)(2,1)S(1)} %get-tuple-element.14.refs_0_, bf16[128,1024]{1,0:T(8,128)(2,1)S(1)} %collective-permute-done.13.refs_1_, ...), custom_call_target="tpu_custom_call", output_to_operand_aliasing={{}: (5, {})} | custom-call | flops 536870912 | bytes 2097152 | tf_op jit(solution)/shard_map/weight/pallas_call | solution.py:218
  (25 shorter events, 0.1 us)
Async XLA Ops:
  0.6 24.1 %collective-permute-start.2 = (bf16[128,2048]{1,0:T(8,128)(2,1)}, bf16[128,2048]{1,0:T(8,128)(2,1)S(1)}, u32[]{:S(2)}, u32[]{:S(2)}) collective-permute-start(bf16[128,2048]{1,0:T(8,128)(2,1)} %refs_5_.3), channel_id=1, source_target_pairs={{0,4},{4,0},{8,12},{12,8},{16,20},{20,16},{24,28},{28,24},{32,36},... | collective-permute-start | bytes 1572872 | tf_op jit(solution)/shard_map/ppermute | solution.py:31
  4.7 28.2 %collective-permute-start = (bf16[128,2048]{1,0:T(8,128)(2,1)}, bf16[128,2048]{1,0:T(8,128)(2,1)S(1)}, u32[]{:S(2)}, u32[]{:S(2)}) collective-permute-start(bf16[128,2048]{1,0:T(8,128)(2,1)} %refs_5_.3), channel_id=1, source_target_pairs={{0,508},{4,8},{8,4},{12,16},{16,12},{20,24},{24,20},{28,32},{32,28... | collective-permute-start | bytes 1572872 | tf_op jit(solution)/shard_map/ppermute | solution.py:31
  19.9 14.9 %collective-permute-start.6 = (bf16[128,2048]{1,0:T(8,128)(2,1)}, bf16[128,2048]{1,0:T(8,128)(2,1)S(1)}, u32[]{:S(2)}, u32[]{:S(2)}) collective-permute-start(bf16[128,2048]{1,0:T(8,128)(2,1)} %refs_10_.3), channel_id=1, source_target_pairs={{0,4},{4,0},{8,12},{12,8},{16,20},{20,16},{24,28},{28,24},{32,36},... | collective-permute-start | bytes 1572872 | tf_op jit(solution)/shard_map/ppermute | solution.py:31
  21.8 21.8 %collective-permute-start.4 = (bf16[128,2048]{1,0:T(8,128)(2,1)}, bf16[128,2048]{1,0:T(8,128)(2,1)S(1)}, u32[]{:S(2)}, u32[]{:S(2)}) collective-permute-start(bf16[128,2048]{1,0:T(8,128)(2,1)} %refs_10_.3), channel_id=1, source_target_pairs={{0,508},{4,8},{8,4},{12,16},{16,12},{20,24},{24,20},{28,32},{32,28... | collective-permute-start | bytes 1572872 | tf_op jit(solution)/shard_map/ppermute | solution.py:31
  24.7 28.7 %collective-permute-start.3 = (bf16[128,2048]{1,0:T(8,128)(2,1)S(1)}, bf16[128,2048]{1,0:T(8,128)(2,1)S(1)}, u32[]{:S(2)}, u32[]{:S(2)}) collective-permute-start(bf16[128,2048]{1,0:T(8,128)(2,1)S(1)} %collective-permute-done.2.refs_1_.refs_6_), channel_id=1, source_target_pairs={{0,508},{4,8},{8,4},{12,16},{16,12},{20,24},{24,20},{28,32},{32,28... | collective-permute-start | bytes 1572872 | tf_op jit(solution)/shard_map/ppermute | solution.py:31
  32.9 20.4 %copy-start.8 = (bf16[128,2048]{1,0:T(8,128)(2,1)}, bf16[128,2048]{1,0:T(8,128)(2,1)S(1)}, u32[]{:S(2)}) copy-start(bf16[128,2048]{1,0:T(8,128)(2,1)S(1)} %collective-permute-done.refs_2_.refs_7_) | copy-start | bytes 1572868
  32.9 20.6 %collective-permute-start.1 = (bf16[128,2048]{1,0:T(8,128)(2,1)S(1)}, bf16[128,2048]{1,0:T(8,128)(2,1)S(1)}, u32[]{:S(2)}, u32[]{:S(2)}) collective-permute-start(bf16[128,2048]{1,0:T(8,128)(2,1)S(1)} %collective-permute-done.refs_2_.refs_7_), channel_id=1, source_target_pairs={{0,4},{4,0},{8,12},{12,8},{16,20},{20,16},{24,28},{28,24},{32,36},... | collective-permute-start | bytes 1572872 | tf_op jit(solution)/shard_map/ppermute | solution.py:31
  34.8 18.4 %copy-start.10 = (bf16[128,2048]{1,0:T(8,128)(2,1)}, bf16[128,2048]{1,0:T(8,128)(2,1)S(1)}, u32[]{:S(2)}) copy-start(bf16[128,2048]{1,0:T(8,128)(2,1)S(1)} %collective-permute-done.6.refs_4_.refs_11_) | copy-start | bytes 1572868
  34.8 30.0 %collective-permute-start.7 = (bf16[128,2048]{1,0:T(8,128)(2,1)S(1)}, bf16[128,2048]{1,0:T(8,128)(2,1)}, u32[]{:S(2)}, u32[]{:S(2)}) collective-permute-start(bf16[128,2048]{1,0:T(8,128)(2,1)S(1)} %collective-permute-done.6.refs_4_.refs_11_), channel_id=1, source_target_pairs={{0,508},{4,8},{8,4},{12,16},{16,12},{20,24},{24,20},{28,32},{32,28... | collective-permute-start | bytes 1572872 | tf_op jit(solution)/shard_map/ppermute | solution.py:31
  43.6 9.6 %copy-start.12 = (bf16[128,2048]{1,0:T(8,128)(2,1)}, bf16[128,2048]{1,0:T(8,128)(2,1)S(1)}, u32[]{:S(2)}) copy-start(bf16[128,2048]{1,0:T(8,128)(2,1)S(1)} %collective-permute-done.4.refs_5_.refs_12_) | copy-start | bytes 1572868
  43.6 21.2 %collective-permute-start.5 = (bf16[128,2048]{1,0:T(8,128)(2,1)S(1)}, bf16[128,2048]{1,0:T(8,128)(2,1)}, u32[]{:S(2)}, u32[]{:S(2)}) collective-permute-start(bf16[128,2048]{1,0:T(8,128)(2,1)S(1)} %collective-permute-done.4.refs_5_.refs_12_), channel_id=1, source_target_pairs={{0,4},{4,0},{8,12},{12,8},{16,20},{20,16},{24,28},{28,24},{32,36},... | collective-permute-start | bytes 1572872 | tf_op jit(solution)/shard_map/ppermute | solution.py:31
  45.6 1.0 copy-start
  46.6 1.0 copy-start.2
  47.7 1.0 copy-start.4
  48.7 1.0 copy-start.6
  49.8 0.7 copy-start.18
  68.5 0.8 copy-start.14
  69.3 0.8 copy-start.16
  70.1 35.0 %copy-start.1 = (bf16[128,2048]{1,0:T(8,128)(2,1)S(1)}, bf16[128,2048]{1,0:T(8,128)(2,1)}, u32[]{:S(2)}) copy-start(bf16[128,2048]{1,0:T(8,128)(2,1)} %refs_3_.5) | copy-start | bytes 1572868
  70.1 35.0 %copy-start.3 = (bf16[128,2048]{1,0:T(8,128)(2,1)S(1)}, bf16[128,2048]{1,0:T(8,128)(2,1)}, u32[]{:S(2)}) copy-start(bf16[128,2048]{1,0:T(8,128)(2,1)} %refs_4_.3) | copy-start | bytes 1572868
  70.1 35.0 %copy-start.5 = (bf16[128,2048]{1,0:T(8,128)(2,1)S(1)}, bf16[128,2048]{1,0:T(8,128)(2,1)}, u32[]{:S(2)}) copy-start(bf16[128,2048]{1,0:T(8,128)(2,1)} %refs_5_.3) | copy-start | bytes 1572868
  70.1 35.0 %copy-start.7 = (bf16[128,2048]{1,0:T(8,128)(2,1)S(1)}, bf16[128,2048]{1,0:T(8,128)(2,1)}, u32[]{:S(2)}) copy-start(bf16[128,2048]{1,0:T(8,128)(2,1)} %refs_10_.3) | copy-start | bytes 1572868
  70.1 16.2 %all-to-all-start = ((f32[4,168,128]{2,1,0:T(8,128)}), f32[4,168,128]{2,1,0:T(8,128)S(1)}, u32[]{:S(2)}, u32[]{:S(2)}) async-start(f32[4,168,128]{2,1,0:T(8,128)} %bitcast), calls=%async_computation | async-start | bytes 688128 | tf_op jit(solution)/shard_map/all_to_all | solution.py:264
  75.1 9.1 %collective-permute-start.10 = (bf16[128,512]{0,1:T(8,128)(2,1)S(1)}, bf16[128,512]{0,1:T(8,128)(2,1)S(1)}, u32[]{:S(2)}, u32[]{:S(2)}) collective-permute-start(bf16[128,512]{0,1:T(8,128)(2,1)S(1)} %get-tuple-element.19), channel_id=1, source_target_pairs={{0,3},{1,2},{2,1},{3,0},{4,7},{5,6},{6,5},{7,4},{8,11},{9,10},{10,... | collective-permute-start | bytes 393224 | tf_op jit(solution)/shard_map/ppermute | solution.py:36
  79.2 7.1 %collective-permute-start.9 = (bf16[128,512]{0,1:T(8,128)(2,1)S(1)}, bf16[128,512]{0,1:T(8,128)(2,1)S(1)}, u32[]{:S(2)}, u32[]{:S(2)}) collective-permute-start(bf16[128,512]{0,1:T(8,128)(2,1)S(1)} %get-tuple-element.20), channel_id=1, source_target_pairs={{0,2},{1,3},{2,0},{3,1},{4,6},{5,7},{6,4},{7,5},{8,10},{9,11},{10,... | collective-permute-start | bytes 393224 | tf_op jit(solution)/shard_map/ppermute | solution.py:36
  82.2 4.1 %collective-permute-start.8 = (bf16[128,512]{0,1:T(8,128)(2,1)S(1)}, bf16[128,512]{0,1:T(8,128)(2,1)S(1)}, u32[]{:S(2)}, u32[]{:S(2)}) collective-permute-start(bf16[128,512]{0,1:T(8,128)(2,1)S(1)} %get-tuple-element.21), channel_id=1, source_target_pairs={{0,1},{1,0},{2,3},{3,2},{4,5},{5,4},{6,7},{7,6},{8,9},{9,8},{10,11... | collective-permute-start | bytes 393224 | tf_op jit(solution)/shard_map/ppermute | solution.py:36
  86.4 16.0 %collective-permute-start.12 = (f32[672,128]{1,0:T(8,128)S(1)}, f32[672,128]{1,0:T(8,128)}, u32[]{:S(2)}, u32[]{:S(2)}) collective-permute-start(f32[672,128]{1,0:T(8,128)S(1)} %bitcast.7), channel_id=1, source_target_pairs={{0,496},{4,500},{8,504},{12,508},{16,32},{20,36},{24,40},{28,44},{... | collective-permute-start | bytes 1032200 | tf_op jit(solution)/shard_map/ppermute | solution.py:31
  94.2 10.9 %collective-permute-start.11 = (f32[672,128]{1,0:T(8,128)S(1)}, f32[672,128]{1,0:T(8,128)}, u32[]{:S(2)}, u32[]{:S(2)}) collective-permute-start(f32[672,128]{1,0:T(8,128)S(1)} %bitcast.8), channel_id=1, source_target_pairs={{0,16},{4,20},{8,24},{12,28},{16,0},{20,4},{24,8},{28,12},{32,48},... | collective-permute-start | bytes 1032200 | tf_op jit(solution)/shard_map/ppermute | solution.py:31
  105.1 1.0 copy-start.9
  106.2 1.0 copy-start.11
  107.2 1.0 copy-start.13
  108.3 1.0 copy-start.15
  109.3 1.0 copy-start.17
  114.6 13.5 %collective-permute-start.17 = (bf16[128,1024]{1,0:T(8,128)(2,1)S(1)}, bf16[128,1024]{1,0:T(8,128)(2,1)S(1)}, u32[]{:S(2)}, u32[]{:S(2)}) collective-permute-start(bf16[128,1024]{1,0:T(8,128)(2,1)S(1)} %get-tuple-element.15.refs_0_), channel_id=1, source_target_pairs={{0,2},{1,3},{2,0},{3,1},{4,6},{5,7},{6,4},{7,5},{8,10},{9,11},{10,... | collective-permute-start | bytes 786440 | tf_op jit(solution)/shard_map/ppermute | solution.py:36
  121.1 11.4 %collective-permute-start.14 = (bf16[128,1024]{1,0:T(8,128)(2,1)S(1)}, bf16[128,1024]{1,0:T(8,128)(2,1)S(1)}, u32[]{:S(2)}, u32[]{:S(2)}) collective-permute-start(bf16[128,1024]{1,0:T(8,128)(2,1)S(1)} %get-tuple-element.14.refs_0_), channel_id=1, source_target_pairs={{0,2},{1,3},{2,0},{3,1},{4,6},{5,7},{6,4},{7,5},{8,10},{9,11},{10,... | collective-permute-start | bytes 786440 | tf_op jit(solution)/shard_map/ppermute | solution.py:36
  124.1 11.2 %collective-permute-start.16 = (bf16[128,1024]{1,0:T(8,128)(2,1)S(1)}, bf16[128,1024]{1,0:T(8,128)(2,1)S(1)}, u32[]{:S(2)}, u32[]{:S(2)}) collective-permute-start(bf16[128,1024]{1,0:T(8,128)(2,1)S(1)} %get-tuple-element.15.refs_0_), channel_id=1, source_target_pairs={{0,1},{1,0},{2,3},{3,2},{4,5},{5,4},{6,7},{7,6},{8,9},{9,8},{10,11... | collective-permute-start | bytes 786440 | tf_op jit(solution)/shard_map/ppermute | solution.py:36
  128.1 7.1 %collective-permute-start.18 = (bf16[128,1024]{1,0:T(8,128)(2,1)S(1)}, bf16[128,1024]{1,0:T(8,128)(2,1)S(1)}, u32[]{:S(2)}, u32[]{:S(2)}) collective-permute-start(bf16[128,1024]{1,0:T(8,128)(2,1)S(1)} %collective-permute-done.17.refs_2_), channel_id=1, source_target_pairs={{0,1},{1,0},{2,3},{3,2},{4,5},{5,4},{6,7},{7,6},{8,9},{9,8},{10,11... | collective-permute-start | bytes 786440 | tf_op jit(solution)/shard_map/ppermute | solution.py:36
  130.0 6.9 %collective-permute-start.13 = (bf16[128,1024]{1,0:T(8,128)(2,1)S(1)}, bf16[128,1024]{1,0:T(8,128)(2,1)S(1)}, u32[]{:S(2)}, u32[]{:S(2)}) collective-permute-start(bf16[128,1024]{1,0:T(8,128)(2,1)S(1)} %get-tuple-element.14.refs_0_), channel_id=1, source_target_pairs={{0,1},{1,0},{2,3},{3,2},{4,5},{5,4},{6,7},{7,6},{8,9},{9,8},{10,11... | collective-permute-start | bytes 786440 | tf_op jit(solution)/shard_map/ppermute | solution.py:36
  132.5 4.5 %collective-permute-start.15 = (bf16[128,1024]{1,0:T(8,128)(2,1)S(1)}, bf16[128,1024]{1,0:T(8,128)(2,1)S(1)}, u32[]{:S(2)}, u32[]{:S(2)}) collective-permute-start(bf16[128,1024]{1,0:T(8,128)(2,1)S(1)} %collective-permute-done.14.refs_2_), channel_id=1, source_target_pairs={{0,1},{1,0},{2,3},{3,2},{4,5},{5,4},{6,7},{7,6},{8,9},{9,8},{10,11... | collective-permute-start | bytes 786440 | tf_op jit(solution)/shard_map/ppermute | solution.py:36

commit v6 on v5

v6 whole, which is shorter than its diff:
```python
import functools

import jax
import jax.numpy as jnp
from jax import lax
from jax.experimental import pallas as pl
from jax.experimental.pallas import tpu as pltpu
from jax.sharding import PartitionSpec as P

HD = 128
DOCS = (0, 1, -1, 2, -2)
GROUP = 4
STEP = 4
TILE = 8
NEAR = 3
HALVES = 2
WIDE = 512
VMEM = pl.BlockSpec(memory_space=pltpu.VMEM)
ANY = pl.BlockSpec(memory_space=pl.ANY)
PARAMS = pltpu.CompilerParams(vmem_limit_bytes=64 << 20)
FAR = 1e30


def traded(value, axis, size, odd):
    count = lax.axis_size(axis)
    blocks = count // size
    pairs = []
    for source in range(count):
        block = source // size
        step = 1 if (block % 2 == 1) == odd else -1
        pairs.append((source, (block + step) % blocks * size + source % size))
    return lax.ppermute(value, axis, pairs)


def swapped(value, axis, mask):
    pairs = [(source, source ^ mask) for source in range(lax.axis_size(axis))]
    return lax.ppermute(value, axis, pairs)


def dot_nt(a, b):
    return lax.dot_general(a, b, (((1,), (1,)), ((), ())), preferred_element_type=jnp.float32)


def dot_nn(a, b):
    return lax.dot_general(a, b, (((1,), (0,)), ((), ())), preferred_element_type=jnp.float32)


def scores_of(keys, query_rows, own_first):
    scores = dot_nt(keys, query_rows) * (HD ** (-0.5))
    if not own_first:
        return scores
    rows = keys.shape[0]
    own = scores[:, :rows]
    key_at = lax.broadcasted_iota(jnp.int32, own.shape, 0)
    query_at = lax.broadcasted_iota(jnp.int32, own.shape, 1)
    own = jnp.where(key_at <= query_at, own, -FAR)
    return jnp.concatenate([own, scores[:, rows:]], 1)


def in_vmem(array):
    return pltpu.with_memory_space_constraint(array, pltpu.VMEM)


def head_rows(refs, cols):
    return jnp.concatenate([ref[:, cols] for ref in refs], 0)


def fetches(refs, buffer, sems, first, step):
    cols = pl.ds(pl.multiple_of((first + step) * STEP * HD, HD), STEP * HD)
    to = pl.ds(pl.multiple_of(step * STEP * HD, HD), STEP * HD)
    return [
        pltpu.make_async_copy(ref.at[:, cols], buffer.at[at, :, to], sems.at[step])
        for at, ref in enumerate(refs)
    ]


def stats_kernel(low, offsets_ref, *refs):
    *refs, out_ref, buffer, sems = refs
    arrays, before = (refs[:-1], refs[-1]) if low else (refs, None)
    count = (len(arrays) - 2) // 2
    rows, features = arrays[0].shape
    steps = features // (STEP * HD)
    for step in range(steps):
        for copy in fetches(arrays, buffer, sems, 0, step):
            copy.start()
    key_ref, value_ref, *doc_refs = [buffer.at[at] for at in range(len(arrays))]

    def group(step, carry):
        for copy in fetches(arrays, buffer, sems, 0, step):
            copy.wait()
        base = pl.multiple_of(step * TILE, TILE)
        for head in range(STEP):
            cols = pl.ds(pl.multiple_of((step * STEP + head) * HD, HD), HD)
            scores = scores_of(key_ref[:, cols], head_rows(doc_refs[:count], cols), low == 0)
            prob_grad = dot_nt(value_ref[:, cols], head_rows(doc_refs[count:], cols))
            top = jnp.max(scores, 0, keepdims=True)
            weights = jnp.exp(scores - top)
            total = jnp.sum(weights, 0, keepdims=True)
            mean = jnp.sum(weights * prob_grad, 0, keepdims=True) / total
            lse = top + jnp.log(total)
            for doc in range(count):
                cut = slice(doc * rows, (doc + 1) * rows)
                start = base + (low + doc) * steps * TILE
                out_ref[pl.ds(start + head, 1), :] = lse[:, cut]
                out_ref[pl.ds(start + STEP + head, 1), :] = mean[:, cut]
        return carry

    lax.fori_loop(0, steps, group, 0)
    if low:
        each = out_ref.shape[0] // GROUP
        out_ref[: before.shape[0], :] = before[...]
        for slot in range(2):
            value = offsets_ref[0, slot].astype(jnp.float32)
            at = each - TILE + slot * STEP
            out_ref[at : at + STEP, :] = jnp.full((STEP, rows), value, jnp.float32)
        for copy in range(1, GROUP):
            out_ref[copy * each : (copy + 1) * each, :] = out_ref[:each, :]


def merged(stat_ref, me, step, steps):
    stride = stat_ref.shape[0] // (3 * GROUP)
    sign = 1 - 2 * (me % 2)
    sign_real = sign.astype(jnp.float32)

    def tile(hops, row):
        place = me + GROUP + sign * hops
        return stat_ref[pl.ds(pl.multiple_of(place * stride + row, TILE), TILE), :]

    lse_rows, delta_rows = [], []
    for doc in DOCS:
        offsets = tile(doc, stride - TILE) * sign_real
        first, second = offsets[:STEP], offsets[STEP:]
        parts = []
        for hop in DOCS:
            name = -hop if (doc + hop) % 2 == 0 else hop
            stat = tile(doc + hop, (DOCS.index(name) * steps + step) * TILE)
            lse, mean = stat[:STEP], stat[STEP:]
            if hop:
                lse = jnp.where((first == hop) | (second == hop), lse, -FAR)
            parts.append((lse, mean))
        top = functools.reduce(jnp.maximum, [lse for lse, _ in parts])
        weights = [jnp.exp(lse - top) for lse, _ in parts]
        total = sum(weights)
        delta = sum(weight * mean for weight, (_, mean) in zip(weights, parts)) / total
        lse = top + jnp.log(total)
        if doc:
            lse = jnp.where((first == -doc) | (second == -doc), lse, FAR)
        lse_rows.append(lse)
        delta_rows.append(delta)
    return jnp.concatenate(lse_rows, 1), jnp.concatenate(delta_rows, 1)


def grads_kernel(first, replica_ref, *refs):
    count = len(DOCS)
    stat_refs, arrays = refs[:3], refs[3 : 5 + 2 * count]
    key_half, key_out, value_out = refs[-10:-7]
    stat_ref, buffer, key_buffer, value_buffer, stat_sem, sems, out_sem = refs[-7:]
    rows, features = arrays[0].shape
    half = key_half.shape[1]
    each = half // (STEP * HD)
    steps = features // (STEP * HD)
    size = stat_refs[0].shape[0]
    replica = replica_ref[0]

    above = 2 - 2 * (replica // GROUP % 2)
    stat_copies = [
        pltpu.make_async_copy(ref, stat_ref.at[pl.ds(pl.multiple_of(at * size, TILE), size), :], stat_sem)
        for at, ref in ((above, stat_refs[0]), (1, stat_refs[1]), (2 - above, stat_refs[2]))
    ]
    for copy in stat_copies:
        copy.start()
    for step in range(each):
        for copy in fetches(arrays, buffer, sems, first, step):
            copy.start()
    for copy in stat_copies:
        copy.wait()
    key_ref, value_ref, *doc_refs = [buffer.at[at] for at in range(len(arrays))]

    def group(step, carry):
        lse, delta = merged(stat_ref, replica % GROUP, first + step, steps)
        for copy in fetches(arrays, buffer, sems, first, step):
            copy.wait()
        for head in range(STEP):
            cols = pl.ds(pl.multiple_of((step * STEP + head) * HD, HD), HD)
            query_rows = head_rows(doc_refs[:count], cols)
            grad_rows = head_rows(doc_refs[count:], cols)
            scores = scores_of(key_ref[:, cols], query_rows, True)
            prob_grad = dot_nt(value_ref[:, cols], grad_rows)
            probs = jnp.exp(scores - lse[head : head + 1])
            score_grad = probs * (prob_grad - delta[head : head + 1]) * (HD ** (-0.5))
            key_total = dot_nn(score_grad.astype(jnp.bfloat16), query_rows)
            value_total = dot_nn(probs.astype(jnp.bfloat16), grad_rows)
            key_buffer[:, cols] = key_total.astype(jnp.bfloat16)
            value_buffer[:, cols] = value_total.astype(jnp.bfloat16)
        return carry

    lax.fori_loop(0, each, group, 0)
    cols = pl.ds(first * STEP * HD, half)
    out_copies = [
        pltpu.make_async_copy(key_buffer, key_half, out_sem.at[0]),
        pltpu.make_async_copy(key_buffer, key_out.at[:, cols], out_sem.at[1]),
        pltpu.make_async_copy(value_buffer, value_out.at[:, cols], out_sem.at[2]),
    ]
    for copy in out_copies:
        copy.start()
    for copy in out_copies:
        copy.wait()


def weight_kernel(low, mine_ref, inputs_ref, *refs):
    pieces, out_ref, grads_ref = refs[:4], refs[-2], refs[-1]
    wide = out_ref.shape[1]
    rows = pieces[0].shape[0]
    step = pl.program_id(0)
    here = pl.ds(pl.multiple_of(step * wide, HD), wide)
    whole = pl.ds(pl.multiple_of((low + step) * wide, HD), wide)
    for k, (ref, cols) in enumerate(zip(pieces, (whole, whole, here, here))):
        place = pl.multiple_of((mine_ref[0] ^ k) * rows, rows)
        grads_ref[pl.ds(place, rows), :] = ref[:, cols]
    out_ref[...] = dot_nn(inputs_ref[...], grads_ref[...]).astype(jnp.bfloat16)


def call_stats(low, high, partner_offsets, arrays, before):
    rows, features = arrays[0].shape
    heads = features // HD
    docs = len(DOCS)
    out_rows = high * heads // STEP * TILE if high < docs else GROUP * (docs * heads // STEP + 1) * TILE
    pairs = rows * rows * heads * (high - low)
    return pl.pallas_call(
        functools.partial(stats_kernel, low),
        in_specs=[pl.BlockSpec(memory_space=pltpu.SMEM)] + [ANY] * len(arrays) + [VMEM] * len(before),
        out_specs=VMEM,
        out_shape=jax.ShapeDtypeStruct((out_rows, rows), jnp.float32),
        scratch_shapes=[
            pltpu.VMEM((len(arrays), rows, features), jnp.bfloat16),
            pltpu.SemaphoreType.DMA((heads // STEP,)),
        ],
        compiler_params=PARAMS,
        cost_estimate=pl.CostEstimate(
            flops=4 * pairs * HD, bytes_accessed=2 * len(arrays) * rows * features, transcendentals=pairs
        ),
        name="stats",
    )(partner_offsets, *arrays, *before)


def call_grads(first, each, replica, stat_parts, arrays, held):
    rows, features = arrays[0].shape
    pairs = rows * rows * len(DOCS) * each * STEP
    half = (rows, each * STEP * HD)
    inputs = [replica, *stat_parts, *arrays]
    return pl.pallas_call(
        functools.partial(grads_kernel, first),
        in_specs=[pl.BlockSpec(memory_space=pltpu.SMEM)] + [ANY] * (len(inputs) - 1 + len(held)),
        out_specs=[ANY] * 3,
        out_shape=[
            jax.ShapeDtypeStruct(shape, jnp.bfloat16) for shape in (half, arrays[0].shape, arrays[0].shape)
        ],
        scratch_shapes=[
            pltpu.VMEM((3 * stat_parts[0].shape[0], rows), jnp.float32),
            pltpu.VMEM((len(arrays), *half), jnp.bfloat16),
            pltpu.VMEM(half, jnp.bfloat16),
            pltpu.VMEM(half, jnp.bfloat16),
            pltpu.SemaphoreType.DMA,
            pltpu.SemaphoreType.DMA((each,)),
            pltpu.SemaphoreType.DMA((3,)),
        ],
        input_output_aliases={len(inputs) + at: 1 + at for at in range(len(held))},
        compiler_params=PARAMS,
        cost_estimate=pl.CostEstimate(
            flops=8 * pairs * HD, bytes_accessed=2 * len(arrays) * half[0] * half[1], transcendentals=pairs
        ),
        name="grads",
    )(*inputs, *held)


def call_weight(half, mine, columns, pieces, held):
    features, part = pieces[0].shape[1], pieces[-1].shape[1]
    blocks = part // WIDE
    width, tokens = columns.shape
    return pl.pallas_call(
        functools.partial(weight_kernel, half * blocks),
        grid=(blocks,),
        in_specs=[pl.BlockSpec(memory_space=pltpu.SMEM)] + [VMEM] * (1 + len(pieces)) + [ANY] * len(held),
        out_specs=pl.BlockSpec((width, WIDE), lambda step: (0, step + half * blocks)),
        scratch_shapes=[pltpu.VMEM((tokens, WIDE), jnp.bfloat16)],
        out_shape=jax.ShapeDtypeStruct((width, features), jnp.bfloat16),
        input_output_aliases={2 + len(pieces): 0} if held else {},
        compiler_params=pltpu.CompilerParams(vmem_limit_bytes=24 << 20),
        cost_estimate=pl.CostEstimate(
            flops=2 * width * tokens * part, bytes_accessed=2 * part * (tokens + width), transcendentals=0
        ),
        name="weight",
    )(mine, *map(in_vmem, [columns, *pieces]), *held)


def local(layer_input, queries, key_vectors, value_vectors, output_grad, partner_offsets):
    rows, features = queries.shape
    steps = features // (HD * STEP)
    docs = len(DOCS)
    mine = lax.axis_index("fsdp").astype(jnp.int32).reshape(1)
    places = lax.axis_size("fsdp")

    others = [traded(array, "dp", 1, True) for array in (queries, output_grad)]
    firsts = [traded(array, "dp", 1, False) for array in (queries, output_grad)]
    near = list(zip(firsts, others))
    seconds = [traded(first, "dp", 1, True) for first in firsts]
    far = list(zip([traded(other, "dp", 1, False) for other in others], seconds))
    query_docs, grad_docs = (
        [array, *near[at], *far[at]] for at, array in enumerate((queries, output_grad))
    )

    own = [key_vectors, value_vectors]
    stats = call_stats(0, NEAR, partner_offsets, own + query_docs[:NEAR] + grad_docs[:NEAR], [])
    replica = lax.axis_index("dp").astype(jnp.int32).reshape(1)
    width = layer_input.shape[1] // places
    columns = layer_input.reshape(rows, places, width).transpose(1, 0, 2).reshape(places * rows, width)
    stats, replica, mine, columns = lax.optimization_barrier((stats, replica, mine, columns))
    stats = call_stats(NEAR, docs, partner_offsets, own + query_docs[NEAR:] + grad_docs[NEAR:], [stats])

    replicas = lax.axis_size("dp")
    groups = [list(range(low, low + GROUP)) for low in range(0, replicas, GROUP)]
    here = lax.all_to_all(stats, "dp", 0, 0, axis_index_groups=groups, tiled=True)
    stats, columns = lax.optimization_barrier((stats, columns))
    columns = lax.all_to_all(columns, "fsdp", 0, 0, tiled=True).T
    stat_parts = [traded(here, "dp", GROUP, False), here, traded(here, "dp", GROUP, True)]
    stat_parts[2], columns = lax.optimization_barrier((stat_parts[2], columns))

    each = steps // HALVES
    halves, held = [], []
    for half in range(HALVES):
        key_half, *held = call_grads(half * each, each, replica, stat_parts, own + query_docs + grad_docs, held)
        halves.append(key_half)
    key_grad, value_grad = held

    beside = swapped(key_grad, "fsdp", 1)
    held = []
    for half, key_half in enumerate(halves):
        across = swapped(key_half, "fsdp", 2)
        pieces = [key_grad, beside, across, swapped(across, "fsdp", 1)]
        held = [call_weight(half, mine, columns, pieces, held)]
    return held[0][None], value_grad


def solution(mesh):
    return jax.shard_map(
        local,
        mesh=mesh,
        in_specs=(
            P(("dp", "fsdp"), None),
            P(("dp", "fsdp"), None),
            P(("dp", "fsdp"), None),
            P(("dp", "fsdp"), None),
            P(("dp", "fsdp"), None),
            P("dp", None),
        ),
        out_specs=(P("dp", "fsdp", None), P(("dp", "fsdp"), None)),
        check_vma=False,
    )
```

time: 140 us -> 141 us (level)
  starting transfers between devices: 82.7 us -> 73.1 us
  waiting for transfers between devices: 22.6 us -> 32 us
  Pallas kernels: 18.3 us -> 25.8 us
  local copies, waits for them, and re-layouts: 13 us -> 8.03 us
    ppermute x9 -> x5, starting transfers between devices: 24.6 us -> 13.1 us  [swapped(): return lax.ppermute(value, axis, pairs)]
    all_to_all x0 -> x1, waiting for transfers between devices: none -> 9.22 us  [local(): columns = lax.all_to_all(columns, 'fsdp', 0, 0, tiled=True).T]
    unnamed x38 -> x9, local copies, waits for them, and re-layouts: 11.6 us -> 4.12 us
    all_to_all x0 -> x1, starting transfers between devices: none -> 6.45 us  [local(): columns = lax.all_to_all(columns, 'fsdp', 0, 0, tiled=True).T]
    ppermute x10, waiting for transfers between devices: 20.4 us -> 14.2 us  [traded(): return lax.ppermute(value, axis, pairs)]
    pallas_call x4, Pallas kernels: 11.8 us -> 16.4 us  [the longest x2 11.9 us: call_grads(): pl.pallas_call(functools.partial(grads_kernel, first), in_specs=[pl.Block...]
    ppermute x10, starting transfers between devices: 54.5 us -> 50 us  [traded(): return lax.ppermute(value, axis, pairs)]
    all_to_all x1, waiting for transfers between devices: 0.01 us -> 3.89 us  [local(): lax.all_to_all(stats, 'dp', 0, 0, axis_index_groups=groups, tiled=True)]
  transfers between devices with their start and end apart: 20 -> 17, of which waited for: 5 -> 8; matrix products, arithmetic and copies ran while one was open for 2% -> 4% of each run, Pallas kernels for 6% -> 10%
where the time goes in v6:
time: 141 us; the launch traced here: 140 us
  starting transfers between devices  73.1 us (52%)
  waiting for transfers between devices  32 us (23%)
  Pallas kernels  25.8 us (18%)
  local copies, waits for them, and re-layouts  8.03 us (6%)
    ppermute x10, starting transfers between devices, traded(): return lax.ppermute(value, axis, pairs)  50 us
    ppermute x10, waiting for transfers between devices, traded(): return lax.ppermute(value, axis, pairs)  14.2 us
    ppermute x5, starting transfers between devices, swapped(): return lax.ppermute(value, axis, pairs)  13.1 us
    pallas_call x2, Pallas kernels, call_grads(): pl.pallas_call(functools.partial(grads_kernel, first), in_specs=[pl.Block...  11.9 us
    pallas_call x2, Pallas kernels, call_stats(): pl.pallas_call(functools.partial(stats_kernel, low), in_specs=[pl.BlockSp...  9.42 us
    all_to_all x1, waiting for transfers between devices, local(): columns = lax.all_to_all(columns, 'fsdp', 0, 0, tiled=True).T  9.22 us
    all_to_all x1, starting transfers between devices, local(): columns = lax.all_to_all(columns, 'fsdp', 0, 0, tiled=True).T  6.45 us
    ppermute x5, waiting for transfers between devices, swapped(): return lax.ppermute(value, axis, pairs)  4.71 us
  transfers between devices with their start and end apart: 17, of which 8 were waited for; matrix products, arithmetic and copies ran while one was open for 4% of the time, Pallas kernels for 10%

profile of v6, /device:TPU:1, one launch (start us, length us, event | category | flops | bytes accessed | tf_op | source)
XLA Modules:
  0.0 139.7 jit_solution(16641998909041838530)
XLA Ops:
  0.6 16.9 %collective-permute-start.1 = (bf16[128,2048]{1,0:T(8,128)(2,1)}, bf16[128,2048]{1,0:T(8,128)(2,1)}, u32[]{:S(2)}, u32[]{:S(2)}) collective-permute-start(bf16[128,2048]{1,0:T(8,128)(2,1)} %refs_5_.5), channel_id=1, source_target_pairs={{0,508},{4,8},{8,4},{12,16},{16,12},{20,24},{24,20},{28,32},{32,28... | collective-permute-start | bytes 1572872 | tf_op jit(solution)/shard_map/ppermute | solution.py:32
  17.5 1.9 %collective-permute-start = (bf16[128,2048]{1,0:T(8,128)(2,1)}, bf16[128,2048]{1,0:T(8,128)(2,1)}, u32[]{:S(2)}, u32[]{:S(2)}) collective-permute-start(bf16[128,2048]{1,0:T(8,128)(2,1)} %refs_5_.5), channel_id=1, source_target_pairs={{0,4},{4,0},{8,12},{12,8},{16,20},{20,16},{24,28},{28,24},{32,36},... | collective-permute-start | bytes 1572872 | tf_op jit(solution)/shard_map/ppermute | solution.py:32
  19.4 2.5 %collective-permute-start.3 = (bf16[128,2048]{1,0:T(8,128)(2,1)}, bf16[128,2048]{1,0:T(8,128)(2,1)}, u32[]{:S(2)}, u32[]{:S(2)}) collective-permute-start(bf16[128,2048]{1,0:T(8,128)(2,1)} %refs_10_.3), channel_id=1, source_target_pairs={{0,508},{4,8},{8,4},{12,16},{16,12},{20,24},{24,20},{28,32},{32,28... | collective-permute-start | bytes 1572872 | tf_op jit(solution)/shard_map/ppermute | solution.py:32
  22.0 2.8 %collective-permute-start.2 = (bf16[128,2048]{1,0:T(8,128)(2,1)}, bf16[128,2048]{1,0:T(8,128)(2,1)}, u32[]{:S(2)}, u32[]{:S(2)}) collective-permute-start(bf16[128,2048]{1,0:T(8,128)(2,1)} %refs_10_.3), channel_id=1, source_target_pairs={{0,4},{4,0},{8,12},{12,8},{16,20},{20,16},{24,28},{28,24},{32,36},... | collective-permute-start | bytes 1572872 | tf_op jit(solution)/shard_map/ppermute | solution.py:32
  24.7 4.7 %collective-permute-done.1.refs_4_.refs_7_ = bf16[128,2048]{1,0:T(8,128)(2,1)} collective-permute-done((bf16[128,2048]{1,0:T(8,128)(2,1)}, bf16[128,2048]{1,0:T(8,128)(2,1)}, u32[]{:S(2)}, u32[]{:S(2)}) %collective-permute-start.1) | collective-permute-done | bytes 524320 | tf_op jit(solution)/shard_map/ppermute | solution.py:32
  29.5 1.9 %collective-permute-start.4 = (bf16[128,2048]{1,0:T(8,128)(2,1)}, bf16[128,2048]{1,0:T(8,128)(2,1)}, u32[]{:S(2)}, u32[]{:S(2)}) collective-permute-start(bf16[128,2048]{1,0:T(8,128)(2,1)} %collective-permute-done.1.refs_4_.refs_7_), channel_id=1, source_target_pairs={{0,4},{4,0},{8,12},{12,8},{16,20},{20,16},{24,28},{28,24},{32,36},... | collective-permute-start | bytes 1572872 | tf_op jit(solution)/shard_map/ppermute | solution.py:32
  31.4 0.8 collective-permute-done.refs_3_.refs_6_
  32.2 8.0 %collective-permute-start.5 = (bf16[128,2048]{1,0:T(8,128)(2,1)}, bf16[128,2048]{1,0:T(8,128)(2,1)}, u32[]{:S(2)}, u32[]{:S(2)}) collective-permute-start(bf16[128,2048]{1,0:T(8,128)(2,1)} %collective-permute-done.refs_3_.refs_6_), channel_id=1, source_target_pairs={{0,508},{4,8},{8,4},{12,16},{16,12},{20,24},{24,20},{28,32},{32,28... | collective-permute-start | bytes 1572872 | tf_op jit(solution)/shard_map/ppermute | solution.py:32
  40.2 0.1 collective-permute-done.3.refs_7_.refs_12_
  40.3 1.9 %collective-permute-start.6 = (bf16[128,2048]{1,0:T(8,128)(2,1)}, bf16[128,2048]{1,0:T(8,128)(2,1)}, u32[]{:S(2)}, u32[]{:S(2)}) collective-permute-start(bf16[128,2048]{1,0:T(8,128)(2,1)} %collective-permute-done.3.refs_7_.refs_12_), channel_id=1, source_target_pairs={{0,4},{4,0},{8,12},{12,8},{16,20},{20,16},{24,28},{28,24},{32,36},... | collective-permute-start | bytes 1572872 | tf_op jit(solution)/shard_map/ppermute | solution.py:32
  42.2 1.3 collective-permute-done.2.refs_6_.refs_11_
  43.4 8.0 %collective-permute-start.7 = (bf16[128,2048]{1,0:T(8,128)(2,1)}, bf16[128,2048]{1,0:T(8,128)(2,1)}, u32[]{:S(2)}, u32[]{:S(2)}) collective-permute-start(bf16[128,2048]{1,0:T(8,128)(2,1)} %collective-permute-done.2.refs_6_.refs_11_), channel_id=1, source_target_pairs={{0,508},{4,8},{8,4},{12,16},{16,12},{20,24},{24,20},{28,32},{32,28... | collective-permute-start | bytes 1572872 | tf_op jit(solution)/shard_map/ppermute | solution.py:32
  51.4 1.3 copy.15
  52.7 1.0 copy.16
  53.7 4.9 %stats.2.refs_6_ = f32[96,128]{1,0:T(8,128)} custom-call(s32[1,2]{1,0:T(1,128)} %offsets_ref.3, bf16[128,2048]{1,0:T(8,128)(2,1)} %refs_3_.3, bf16[128,2048]{1,0:T(8,128)(2,1)} %refs_4_.3, bf16[128,2048]{1,0:T(8,128)(2,1)} %refs_5_.5, bf16[128,2048]{1,0:T(8,128)(2,1)} %collective-permute-done.refs_3_.refs_6_, ...), custom_call_target="tpu_custom_call" | custom-call | flops 402653184 | bytes 4194304 | tf_op jit(solution)/shard_map/stats/pallas_call | solution.py:229
  58.6 0.0 collective-permute-done.4.refs_2_.refs_8_
  58.6 0.0 collective-permute-done.5.refs_3_.refs_9_
  58.6 7.3 %collective-permute-done.6.refs_4_.refs_13_ = bf16[128,2048]{1,0:T(8,128)(2,1)} collective-permute-done((bf16[128,2048]{1,0:T(8,128)(2,1)}, bf16[128,2048]{1,0:T(8,128)(2,1)}, u32[]{:S(2)}, u32[]{:S(2)}) %collective-permute-start.6) | collective-permute-done | bytes 524320 | tf_op jit(solution)/shard_map/ppermute | solution.py:32
  65.9 0.0 collective-permute-done.7.refs_5_.refs_14_
  65.9 4.5 %stats.3 = f32[672,128]{1,0:T(8,128)} custom-call(s32[1,2]{1,0:T(1,128)} %offsets_ref.3, bf16[128,2048]{1,0:T(8,128)(2,1)} %refs_3_.3, bf16[128,2048]{1,0:T(8,128)(2,1)} %refs_4_.3, bf16[128,2048]{1,0:T(8,128)(2,1)} %collective-permute-done.4.refs_2_.refs_8_, bf16[128,2048]{1,0:T(8,128)(2,1)} %collective-permute-done.5.refs_3_.refs_9_, ...), custom_call_target="tpu_custom_call" | custom-call | flops 268435456 | bytes 3145728 | tf_op jit(solution)/shard_map/stats/pallas_call | solution.py:229
  70.4 3.5 %all-to-all-start = ((f32[4,168,128]{2,1,0:T(8,128)}), f32[4,168,128]{2,1,0:T(8,128)S(1)}, u32[]{:S(2)}, u32[]{:S(2)}) async-start(f32[4,168,128]{2,1,0:T(8,128)} %bitcast.23), calls=%async_computation | async-start | bytes 688128 | tf_op jit(solution)/shard_map/all_to_all | solution.py:322
  73.9 2.0 %copy.17 = bf16[4,128,512]{1,2,0:T(8,128)(2,1)} copy(bf16[4,128,512]{2,1,0:T(8,128)(2,1)} %copy.16) | data formatting | bytes 1048576 | tf_op jit(solution)/shard_map/all_to_all | solution.py:324
  76.0 3.9 %all-to-all-done = f32[4,168,128]{2,1,0:T(8,128)S(1)} async-done(((f32[4,168,128]{2,1,0:T(8,128)}), f32[4,168,128]{2,1,0:T(8,128)S(1)}, u32[]{:S(2)}, u32[]{:S(2)}) %all-to-all-start) | async-done | bytes 344096 | tf_op jit(solution)/shard_map/all_to_all | solution.py:322
  79.9 0.0 copy-start.2
  79.9 6.5 %all-to-all-start.1 = ((bf16[4,128,512]{1,2,0:T(8,128)(2,1)}), bf16[4,128,512]{1,2,0:T(8,128)(2,1)S(1)}, u32[]{:S(2)}, u32[]{:S(2)}) async-start(bf16[4,128,512]{1,2,0:T(8,128)(2,1)} %copy.17), calls=%async_computation.1 | async-start | bytes 1048576 | tf_op jit(solution)/shard_map/all_to_all | solution.py:324
  86.3 4.3 %collective-permute-start.8 = (f32[672,128]{1,0:T(8,128)S(1)}, f32[672,128]{1,0:T(8,128)S(1)}, u32[]{:S(2)}, u32[]{:S(2)}) collective-permute-start(f32[672,128]{1,0:T(8,128)S(1)} %bitcast.18), channel_id=1, source_target_pairs={{0,496},{4,500},{8,504},{12,508},{16,32},{20,36},{24,40},{28,44},{... | collective-permute-start | bytes 1032200 | tf_op jit(solution)/shard_map/ppermute | solution.py:32
  90.6 0.0 copy-done.2
  90.6 1.9 %collective-permute-start.9 = (f32[672,128]{1,0:T(8,128)S(1)}, f32[672,128]{1,0:T(8,128)}, u32[]{:S(2)}, u32[]{:S(2)}) collective-permute-start(f32[672,128]{1,0:T(8,128)S(1)} %bitcast.19), channel_id=1, source_target_pairs={{0,16},{4,20},{8,24},{12,28},{16,0},{20,4},{24,8},{28,12},{32,48},... | collective-permute-start | bytes 1032200 | tf_op jit(solution)/shard_map/ppermute | solution.py:32
  92.5 9.2 %all-to-all-done.1 = bf16[4,128,512]{1,2,0:T(8,128)(2,1)S(1)} async-done(((bf16[4,128,512]{1,2,0:T(8,128)(2,1)}), bf16[4,128,512]{1,2,0:T(8,128)(2,1)S(1)}, u32[]{:S(2)}, u32[]{:S(2)}) %all-to-all-start.1) | async-done | bytes 524320 | tf_op jit(solution)/shard_map/all_to_all | solution.py:324
  101.8 0.9 bitcast_bitcast_fusion.inputs_ref
  102.6 0.0 collective-permute-done.8.refs_2_
  102.6 0.0 copy-start.3
  102.6 0.7 copy-done.3
  103.4 0.0 collective-permute-done.9.refs_0_
  103.4 5.9 %grads.2 = (bf16[128,1024]{1,0:T(8,128)(2,1)}, bf16[128,2048]{1,0:T(8,128)(2,1)}, bf16[128,2048]{1,0:T(8,128)(2,1)}) custom-call(s32[1]{0:T(128)} %bitcast.replica_ref, f32[672,128]{1,0:T(8,128)} %collective-permute-done.9.refs_0_, f32[672,128]{1,0:T(8,128)} %bitcast.20, f32[672,128]{1,0:T(8,128)} %copy-done.3, bf16[128,2048]{1,0:T(8,128)(2,1)} %refs_3_.3, ...), custom_call_target="tpu_custom_call" | custom-call | flops 671088640 | bytes 3145728 | tf_op jit(solution)/shard_map/grads/pallas_call | solution.py:251
  109.3 2.3 %collective-permute-start.13 = (bf16[128,1024]{1,0:T(8,128)(2,1)}, bf16[128,1024]{1,0:T(8,128)(2,1)}, u32[]{:S(2)}, u32[]{:S(2)}) collective-permute-start(bf16[128,1024]{1,0:T(8,128)(2,1)} %get-tuple-element.26), channel_id=1, source_target_pairs={{0,2},{1,3},{2,0},{3,1},{4,6},{5,7},{6,4},{7,5},{8,10},{9,11},{10,... | collective-permute-start | bytes 786440 | tf_op jit(solution)/shard_map/ppermute | solution.py:37
  111.6 6.0 %grads.3 = (bf16[128,1024]{1,0:T(8,128)(2,1)}, bf16[128,2048]{1,0:T(8,128)(2,1)}, bf16[128,2048]{1,0:T(8,128)(2,1)}) custom-call(s32[1]{0:T(128)} %bitcast.replica_ref, f32[672,128]{1,0:T(8,128)} %collective-permute-done.9.refs_0_, f32[672,128]{1,0:T(8,128)} %bitcast.21, f32[672,128]{1,0:T(8,128)} %copy-done.3, ...), custom_call_target="tpu_custom_call", output_to_operand_aliasing={{1}: (16, {}), {2}: (17, {})} | custom-call | flops 671088640 | bytes 3145728 | tf_op jit(solution)/shard_map/grads/pallas_call | solution.py:251
  117.6 2.9 %collective-permute-start.10 = (bf16[128,2048]{1,0:T(8,128)(2,1)}, bf16[128,2048]{1,0:T(8,128)(2,1)S(1)}, u32[]{:S(2)}, u32[]{:S(2)}) collective-permute-start(bf16[128,2048]{1,0:T(8,128)(2,1)} %get-tuple-element.24.refs_0_), channel_id=1, source_target_pairs={{0,1},{1,0},{2,3},{3,2},{4,5},{5,4},{6,7},{7,6},{8,9},{9,8},{10,11... | collective-permute-start | bytes 1572872 | tf_op jit(solution)/shard_map/ppermute | solution.py:37
  120.4 3.1 %collective-permute-start.11 = (bf16[128,1024]{1,0:T(8,128)(2,1)}, bf16[128,1024]{1,0:T(8,128)(2,1)S(1)}, u32[]{:S(2)}, u32[]{:S(2)}) collective-permute-start(bf16[128,1024]{1,0:T(8,128)(2,1)} %get-tuple-element.25), channel_id=1, source_target_pairs={{0,2},{1,3},{2,0},{3,1},{4,6},{5,7},{6,4},{7,5},{8,10},{9,11},{10,... | collective-permute-start | bytes 786440 | tf_op jit(solution)/shard_map/ppermute | solution.py:37
  123.6 0.0 collective-permute-done.13.refs_2_
  123.6 2.2 %collective-permute-start.14 = (bf16[128,1024]{1,0:T(8,128)(2,1)}, bf16[128,1024]{1,0:T(8,128)(2,1)S(1)}, u32[]{:S(2)}, u32[]{:S(2)}) collective-permute-start(bf16[128,1024]{1,0:T(8,128)(2,1)} %collective-permute-done.13.refs_2_), channel_id=1, source_target_pairs={{0,1},{1,0},{2,3},{3,2},{4,5},{5,4},{6,7},{7,6},{8,9},{9,8},{10,11... | collective-permute-start | bytes 786440 | tf_op jit(solution)/shard_map/ppermute | solution.py:37
  125.8 4.7 %collective-permute-done.11.refs_2_ = bf16[128,1024]{1,0:T(8,128)(2,1)S(1)} collective-permute-done((bf16[128,1024]{1,0:T(8,128)(2,1)}, bf16[128,1024]{1,0:T(8,128)(2,1)S(1)}, u32[]{:S(2)}, u32[]{:S(2)}) %collective-permute-start.11) | collective-permute-done | bytes 262176 | tf_op jit(solution)/shard_map/ppermute | solution.py:37
  130.5 2.7 %collective-permute-start.12 = (bf16[128,1024]{1,0:T(8,128)(2,1)S(1)}, bf16[128,1024]{1,0:T(8,128)(2,1)S(1)}, u32[]{:S(2)}, u32[]{:S(2)}) collective-permute-start(bf16[128,1024]{1,0:T(8,128)(2,1)S(1)} %collective-permute-done.11.refs_2_), channel_id=1, source_target_pairs={{0,1},{1,0},{2,3},{3,2},{4,5},{5,4},{6,7},{7,6},{8,9},{9,8},{10,11... | collective-permute-start | bytes 786440 | tf_op jit(solution)/shard_map/ppermute | solution.py:37
  133.2 0.0 collective-permute-done.14.refs_3_
  133.2 0.0 collective-permute-done.10.refs_1_
  133.2 0.0 copy-start
  133.2 1.0 copy-done
  134.2 0.0 copy-start.1
  134.2 1.0 copy-done.1
  135.3 2.7 %weight.2.refs_4_ = bf16[512,2048]{1,0:T(8,128)(2,1)} custom-call(s32[1]{0:T(128)} %bitcast.1.mine_ref, bf16[512,512]{1,0:T(8,128)(2,1)S(1)} %copy-done.1, bf16[128,2048]{1,0:T(8,128)(2,1)S(1)} %copy-done, bf16[128,2048]{1,0:T(8,128)(2,1)S(1)} %collective-permute-done.10.refs_1_, bf16[128,1024]{1,0:T(8,128)(2,1)} %collective-permute-done.13.refs_2_, ...), custom_call_target="tpu_custom_call" | custom-call | flops 536870912 | bytes 2097152 | tf_op jit(solution)/shard_map/weight/pallas_call | solution.py:280
  138.0 0.0 collective-permute-done.12.refs_3_
  138.0 1.8 %weight.3 = bf16[512,2048]{1,0:T(8,128)(2,1)} custom-call(s32[1]{0:T(128)} %bitcast.1.mine_ref, bf16[512,512]{1,0:T(8,128)(2,1)S(1)} %copy-done.1, bf16[128,2048]{1,0:T(8,128)(2,1)S(1)} %copy-done, bf16[128,2048]{1,0:T(8,128)(2,1)S(1)} %collective-permute-done.10.refs_1_, ...), custom_call_target="tpu_custom_call", output_to_operand_aliasing={{}: (6, {})} | custom-call | flops 536870912 | bytes 2097152 | tf_op jit(solution)/shard_map/weight/pallas_call | solution.py:280
Async XLA Ops:
  0.6 28.8 %collective-permute-start.1 = (bf16[128,2048]{1,0:T(8,128)(2,1)}, bf16[128,2048]{1,0:T(8,128)(2,1)}, u32[]{:S(2)}, u32[]{:S(2)}) collective-permute-start(bf16[128,2048]{1,0:T(8,128)(2,1)} %refs_5_.5), channel_id=1, source_target_pairs={{0,508},{4,8},{8,4},{12,16},{16,12},{20,24},{24,20},{28,32},{32,28... | collective-permute-start | bytes 1572872 | tf_op jit(solution)/shard_map/ppermute | solution.py:32
  17.5 14.7 %collective-permute-start = (bf16[128,2048]{1,0:T(8,128)(2,1)}, bf16[128,2048]{1,0:T(8,128)(2,1)}, u32[]{:S(2)}, u32[]{:S(2)}) collective-permute-start(bf16[128,2048]{1,0:T(8,128)(2,1)} %refs_5_.5), channel_id=1, source_target_pairs={{0,4},{4,0},{8,12},{12,8},{16,20},{20,16},{24,28},{28,24},{32,36},... | collective-permute-start | bytes 1572872 | tf_op jit(solution)/shard_map/ppermute | solution.py:32
  19.4 20.8 %collective-permute-start.3 = (bf16[128,2048]{1,0:T(8,128)(2,1)}, bf16[128,2048]{1,0:T(8,128)(2,1)}, u32[]{:S(2)}, u32[]{:S(2)}) collective-permute-start(bf16[128,2048]{1,0:T(8,128)(2,1)} %refs_10_.3), channel_id=1, source_target_pairs={{0,508},{4,8},{8,4},{12,16},{16,12},{20,24},{24,20},{28,32},{32,28... | collective-permute-start | bytes 1572872 | tf_op jit(solution)/shard_map/ppermute | solution.py:32
  22.0 21.4 %collective-permute-start.2 = (bf16[128,2048]{1,0:T(8,128)(2,1)}, bf16[128,2048]{1,0:T(8,128)(2,1)}, u32[]{:S(2)}, u32[]{:S(2)}) collective-permute-start(bf16[128,2048]{1,0:T(8,128)(2,1)} %refs_10_.3), channel_id=1, source_target_pairs={{0,4},{4,0},{8,12},{12,8},{16,20},{20,16},{24,28},{28,24},{32,36},... | collective-permute-start | bytes 1572872 | tf_op jit(solution)/shard_map/ppermute | solution.py:32
  29.5 29.2 %collective-permute-start.4 = (bf16[128,2048]{1,0:T(8,128)(2,1)}, bf16[128,2048]{1,0:T(8,128)(2,1)}, u32[]{:S(2)}, u32[]{:S(2)}) collective-permute-start(bf16[128,2048]{1,0:T(8,128)(2,1)} %collective-permute-done.1.refs_4_.refs_7_), channel_id=1, source_target_pairs={{0,4},{4,0},{8,12},{12,8},{16,20},{20,16},{24,28},{28,24},{32,36},... | collective-permute-start | bytes 1572872 | tf_op jit(solution)/shard_map/ppermute | solution.py:32
  32.2 26.4 %collective-permute-start.5 = (bf16[128,2048]{1,0:T(8,128)(2,1)}, bf16[128,2048]{1,0:T(8,128)(2,1)}, u32[]{:S(2)}, u32[]{:S(2)}) collective-permute-start(bf16[128,2048]{1,0:T(8,128)(2,1)} %collective-permute-done.refs_3_.refs_6_), channel_id=1, source_target_pairs={{0,508},{4,8},{8,4},{12,16},{16,12},{20,24},{24,20},{28,32},{32,28... | collective-permute-start | bytes 1572872 | tf_op jit(solution)/shard_map/ppermute | solution.py:32
  40.3 25.6 %collective-permute-start.6 = (bf16[128,2048]{1,0:T(8,128)(2,1)}, bf16[128,2048]{1,0:T(8,128)(2,1)}, u32[]{:S(2)}, u32[]{:S(2)}) collective-permute-start(bf16[128,2048]{1,0:T(8,128)(2,1)} %collective-permute-done.3.refs_7_.refs_12_), channel_id=1, source_target_pairs={{0,4},{4,0},{8,12},{12,8},{16,20},{20,16},{24,28},{28,24},{32,36},... | collective-permute-start | bytes 1572872 | tf_op jit(solution)/shard_map/ppermute | solution.py:32
  43.4 22.5 %collective-permute-start.7 = (bf16[128,2048]{1,0:T(8,128)(2,1)}, bf16[128,2048]{1,0:T(8,128)(2,1)}, u32[]{:S(2)}, u32[]{:S(2)}) collective-permute-start(bf16[128,2048]{1,0:T(8,128)(2,1)} %collective-permute-done.2.refs_6_.refs_11_), channel_id=1, source_target_pairs={{0,508},{4,8},{8,4},{12,16},{16,12},{20,24},{24,20},{28,32},{32,28... | collective-permute-start | bytes 1572872 | tf_op jit(solution)/shard_map/ppermute | solution.py:32
  70.4 9.4 %all-to-all-start = ((f32[4,168,128]{2,1,0:T(8,128)}), f32[4,168,128]{2,1,0:T(8,128)S(1)}, u32[]{:S(2)}, u32[]{:S(2)}) async-start(f32[4,168,128]{2,1,0:T(8,128)} %bitcast.23), calls=%async_computation | async-start | bytes 688128 | tf_op jit(solution)/shard_map/all_to_all | solution.py:322
  79.9 10.8 %copy-start.2 = (f32[4,168,128]{2,1,0:T(8,128)}, f32[4,168,128]{2,1,0:T(8,128)S(1)}, u32[]{:S(2)}) copy-start(f32[4,168,128]{2,1,0:T(8,128)S(1)} %all-to-all-done) | copy-start | bytes 1032196
  79.9 21.9 %all-to-all-start.1 = ((bf16[4,128,512]{1,2,0:T(8,128)(2,1)}), bf16[4,128,512]{1,2,0:T(8,128)(2,1)S(1)}, u32[]{:S(2)}, u32[]{:S(2)}) async-start(bf16[4,128,512]{1,2,0:T(8,128)(2,1)} %copy.17), calls=%async_computation.1 | async-start | bytes 1048576 | tf_op jit(solution)/shard_map/all_to_all | solution.py:324
  86.3 16.3 %collective-permute-start.8 = (f32[672,128]{1,0:T(8,128)S(1)}, f32[672,128]{1,0:T(8,128)S(1)}, u32[]{:S(2)}, u32[]{:S(2)}) collective-permute-start(f32[672,128]{1,0:T(8,128)S(1)} %bitcast.18), channel_id=1, source_target_pairs={{0,496},{4,500},{8,504},{12,508},{16,32},{20,36},{24,40},{28,44},{... | collective-permute-start | bytes 1032200 | tf_op jit(solution)/shard_map/ppermute | solution.py:32
  90.6 12.7 %collective-permute-start.9 = (f32[672,128]{1,0:T(8,128)S(1)}, f32[672,128]{1,0:T(8,128)}, u32[]{:S(2)}, u32[]{:S(2)}) collective-permute-start(f32[672,128]{1,0:T(8,128)S(1)} %bitcast.19), channel_id=1, source_target_pairs={{0,16},{4,20},{8,24},{12,28},{16,0},{20,4},{24,8},{28,12},{32,48},... | collective-permute-start | bytes 1032200 | tf_op jit(solution)/shard_map/ppermute | solution.py:32
  102.6 0.7 copy-start.3
  109.3 14.3 %collective-permute-start.13 = (bf16[128,1024]{1,0:T(8,128)(2,1)}, bf16[128,1024]{1,0:T(8,128)(2,1)}, u32[]{:S(2)}, u32[]{:S(2)}) collective-permute-start(bf16[128,1024]{1,0:T(8,128)(2,1)} %get-tuple-element.26), channel_id=1, source_target_pairs={{0,2},{1,3},{2,0},{3,1},{4,6},{5,7},{6,4},{7,5},{8,10},{9,11},{10,... | collective-permute-start | bytes 786440 | tf_op jit(solution)/shard_map/ppermute | solution.py:37
  117.6 15.6 %collective-permute-start.10 = (bf16[128,2048]{1,0:T(8,128)(2,1)}, bf16[128,2048]{1,0:T(8,128)(2,1)S(1)}, u32[]{:S(2)}, u32[]{:S(2)}) collective-permute-start(bf16[128,2048]{1,0:T(8,128)(2,1)} %get-tuple-element.24.refs_0_), channel_id=1, source_target_pairs={{0,1},{1,0},{2,3},{3,2},{4,5},{5,4},{6,7},{7,6},{8,9},{9,8},{10,11... | collective-permute-start | bytes 1572872 | tf_op jit(solution)/shard_map/ppermute | solution.py:37
  120.4 10.0 %collective-permute-start.11 = (bf16[128,1024]{1,0:T(8,128)(2,1)}, bf16[128,1024]{1,0:T(8,128)(2,1)S(1)}, u32[]{:S(2)}, u32[]{:S(2)}) collective-permute-start(bf16[128,1024]{1,0:T(8,128)(2,1)} %get-tuple-element.25), channel_id=1, source_target_pairs={{0,2},{1,3},{2,0},{3,1},{4,6},{5,7},{6,4},{7,5},{8,10},{9,11},{10,... | collective-permute-start | bytes 786440 | tf_op jit(solution)/shard_map/ppermute | solution.py:37
  123.6 9.6 %collective-permute-start.14 = (bf16[128,1024]{1,0:T(8,128)(2,1)}, bf16[128,1024]{1,0:T(8,128)(2,1)S(1)}, u32[]{:S(2)}, u32[]{:S(2)}) collective-permute-start(bf16[128,1024]{1,0:T(8,128)(2,1)} %collective-permute-done.13.refs_2_), channel_id=1, source_target_pairs={{0,1},{1,0},{2,3},{3,2},{4,5},{5,4},{6,7},{7,6},{8,9},{9,8},{10,11... | collective-permute-start | bytes 786440 | tf_op jit(solution)/shard_map/ppermute | solution.py:37
  130.5 7.5 %collective-permute-start.12 = (bf16[128,1024]{1,0:T(8,128)(2,1)S(1)}, bf16[128,1024]{1,0:T(8,128)(2,1)S(1)}, u32[]{:S(2)}, u32[]{:S(2)}) collective-permute-start(bf16[128,1024]{1,0:T(8,128)(2,1)S(1)} %collective-permute-done.11.refs_2_), channel_id=1, source_target_pairs={{0,1},{1,0},{2,3},{3,2},{4,5},{5,4},{6,7},{7,6},{8,9},{9,8},{10,11... | collective-permute-start | bytes 786440 | tf_op jit(solution)/shard_map/ppermute | solution.py:37
  133.2 1.0 copy-start
  134.2 1.0 copy-start.1

commit v7 on v5

--- a/solution.py
+++ b/solution.py
@@ -16,6 +16,7 @@
 HALVES = 2
 WIDE = 512
 VMEM = pl.BlockSpec(memory_space=pltpu.VMEM)
+ANY = pl.BlockSpec(memory_space=pl.ANY)
 PARAMS = pltpu.CompilerParams(vmem_limit_bytes=24 << 20)
 FAR = 1e30
 
@@ -134,21 +135,30 @@
     return jnp.concatenate(lse_rows, 1), jnp.concatenate(delta_rows, 1)
 
 
-def grads_kernel(first_step, each, place_ref, *refs):
+def grads_kernel(first, replica_ref, *refs):
     count = len(DOCS)
     stat_refs, (keys_ref, values_ref), refs = refs[:3], refs[3:5], refs[5:]
     query_refs, grad_refs = refs[:count], refs[count : 2 * count]
-    key_out, value_out, stat_ref = refs[-3:]
+    key_half, key_out, value_out, stat_ref, value_buffer, sems = refs[-6:]
+    half = key_half.shape[1]
+    each = half // (STEP * HD)
     steps = keys_ref.shape[1] // (STEP * HD)
     size = stat_refs[0].shape[0]
-
-    above = 2 - 2 * place_ref[1]
-    for at, ref in ((above, stat_refs[0]), (1, stat_refs[1]), (2 - above, stat_refs[2])):
-        stat_ref[pl.ds(pl.multiple_of(at * size, TILE), size), :] = ref[...]
+    replica = replica_ref[0]
+
+    above = 2 - 2 * (replica // GROUP % 2)
+    stat_copies = [
+        pltpu.make_async_copy(ref, stat_ref.at[pl.ds(pl.multiple_of(place * size, TILE), size), :], sems.at[at])
+        for at, (place, ref) in enumerate(zip((above, 1, 2 - above), stat_refs))
+    ]
+    for copy in stat_copies:
+        copy.start()
+    for copy in stat_copies:
+        copy.wait()
 
     def group(at, carry):
-        step = at + first_step
-        lse, delta = merged(stat_ref, place_ref[0], step, steps)
+        step = at + first
+        lse, delta = merged(stat_ref, replica % GROUP, step, steps)
         for head in range(STEP):
             cols = pl.ds(pl.multiple_of((step * STEP + head) * HD, HD), HD)
             out_cols = pl.ds(pl.multiple_of((at * STEP + head) * HD, HD), HD)
@@ -160,18 +170,53 @@
             score_grad = probs * (prob_grad - delta[head : head + 1]) * (HD ** (-0.5))
             key_total = dot_nn(score_grad.astype(jnp.bfloat16), query_rows)
             value_total = dot_nn(probs.astype(jnp.bfloat16), grad_rows)
-            key_out[:, out_cols] = key_total.astype(jnp.bfloat16)
-            value_out[:, out_cols] = value_total.astype(jnp.bfloat16)
+            key_half[:, out_cols] = key_total.astype(jnp.bfloat16)
+            value_buffer[:, out_cols] = value_total.astype(jnp.bfloat16)
         return carry
 
     lax.fori_loop(0, each, group, 0)
-
-
-def weight_kernel(inputs_ref, *refs):
-    low = pl.multiple_of(pl.program_id(0) * refs[-1].shape[1], HD)
-    cols = pl.ds(low, refs[-1].shape[1])
-    grads = jnp.concatenate([ref[:, cols] for ref in refs[:4]], 0)
-    refs[-1][...] = dot_nn(inputs_ref[...], grads).astype(jnp.bfloat16)
+    cols = pl.ds(first * STEP * HD, half)
+    out_copies = [
+        pltpu.make_async_copy(key_half, key_out.at[:, cols], sems.at[3]),
+        pltpu.make_async_copy(value_buffer, value_out.at[:, cols], sems.at[4]),
+    ]
+    for copy in out_copies:
+        copy.start()
+    for copy in out_copies:
+        copy.wait()
+
+
+def spread_kernel(input_ref, out_ref, sems):
+    rows, features = input_ref.shape
+    width = out_ref.shape[1]
+    copies = [
+        pltpu.make_async_copy(
+            input_ref.at[:, pl.ds(place * width, width)], out_ref.at[pl.ds(place * rows, rows), :], sems.at[place]
+        )
+        for place in range(features // width)
+    ]
+    for copy in copies:
+        copy.start()
+    for copy in copies:
+        copy.wait()
+
+
+def weight_kernel(low, mine_ref, inputs_ref, *refs):
+    pieces, out_ref, turned_ref, grads_ref = refs[:4], *refs[-3:]
+    wide = out_ref.shape[1]
+    rows = pieces[0].shape[0]
+    step = pl.program_id(0)
+
+    @pl.when(step == 0)
+    def _():
+        turned_ref[...] = inputs_ref[...].T
+
+    here = pl.ds(pl.multiple_of(step * wide, HD), wide)
+    whole = pl.ds(pl.multiple_of((low + step) * wide, HD), wide)
+    for k, (ref, cols) in enumerate(zip(pieces, (here, whole, here, here))):
+        place = pl.multiple_of((mine_ref[0] ^ k) * rows, rows)
+        grads_ref[pl.ds(place, rows), :] = ref[:, cols]
+    out_ref[...] = dot_nn(turned_ref[...], grads_ref[...]).astype(jnp.bfloat16)
 
 
 def call_stats(low, high, partner_offsets, arrays, before):
@@ -193,49 +238,76 @@
     )(partner_offsets, *map(in_vmem, arrays), *map(in_vmem, before))
 
 
-def call_grads(low, each, place, stat_parts, arrays):
+def call_grads(first, each, replica, stat_parts, arrays, held):
     rows, features = arrays[0].shape
     pairs = rows * rows * len(DOCS) * each * STEP
     half = (rows, each * STEP * HD)
+    whole = jax.ShapeDtypeStruct((rows, features), jnp.bfloat16)
+    count = 1 + len(stat_parts) + len(arrays)
     return pl.pallas_call(
-        functools.partial(grads_kernel, low, each),
-        in_specs=[pl.BlockSpec(memory_space=pltpu.SMEM)] + [VMEM] * (3 + len(arrays)),
-        out_specs=[VMEM, VMEM],
-        out_shape=[pltpu.VMEM(half, jnp.bfloat16), pltpu.VMEM(half, jnp.bfloat16)],
-        scratch_shapes=[pltpu.VMEM((3 * stat_parts[0].shape[0], rows), jnp.float32)],
+        functools.partial(grads_kernel, first),
+        in_specs=[pl.BlockSpec(memory_space=pltpu.SMEM)]
+        + [ANY] * len(stat_parts)
+        + [VMEM] * len(arrays)
+        + [ANY] * len(held),
+        out_specs=[VMEM, ANY, ANY],
+        out_shape=[pltpu.VMEM(half, jnp.bfloat16), whole, whole],
+        scratch_shapes=[
+            pltpu.VMEM((3 * stat_parts[0].shape[0], rows), jnp.float32),
+            pltpu.VMEM(half, jnp.bfloat16),
+            pltpu.SemaphoreType.DMA((5,)),
+        ],
+        input_output_aliases={count + at: 1 + at for at in range(len(held))},
         compiler_params=PARAMS,
         cost_estimate=pl.CostEstimate(
             flops=8 * pairs * HD, bytes_accessed=2 * len(arrays) * half[0] * half[1], transcendentals=pairs
         ),
         name="grads",
-    )(place, *map(in_vmem, stat_parts), *map(in_vmem, arrays))
-
-
-def call_weight(low, columns, pieces, features, held):
-    half = pieces[0].shape[1]
-    blocks = half // WIDE
-    width, tokens = columns.shape
+    )(replica, *stat_parts, *map(in_vmem, arrays), *held)
+
+
+def call_spread(layer_input, places):
+    rows, features = layer_input.shape
     return pl.pallas_call(
-        weight_kernel,
+        spread_kernel,
+        in_specs=[ANY],
+        out_specs=ANY,
+        out_shape=jax.ShapeDtypeStruct((places * rows, features // places), jnp.bfloat16),
+        scratch_shapes=[pltpu.SemaphoreType.DMA((places,))],
+        compiler_params=PARAMS,
+        cost_estimate=pl.CostEstimate(flops=0, bytes_accessed=4 * rows * features, transcendentals=0),
+        name="spread",
+    )(layer_input)
+
+
+def call_weight(half, mine, columns, pieces, held):
+    features, part = pieces[1].shape[1], pieces[0].shape[1]
+    blocks = part // WIDE
+    tokens, width = columns.shape
+    return pl.pallas_call(
+        functools.partial(weight_kernel, half * blocks),
         grid=(blocks,),
-        in_specs=[VMEM] * (1 + len(pieces)) + [pl.BlockSpec(memory_space=pl.ANY)] * len(held),
-        out_specs=pl.BlockSpec((width, WIDE), lambda step: (0, step + low * blocks)),
+        in_specs=[pl.BlockSpec(memory_space=pltpu.SMEM)] + [VMEM] * (1 + len(pieces)) + [ANY] * len(held),
+        out_specs=pl.BlockSpec((width, WIDE), lambda step: (0, step + half * blocks)),
         out_shape=jax.ShapeDtypeStruct((width, features), jnp.bfloat16),
-        input_output_aliases={1 + len(pieces): 0} if held else {},
+        scratch_shapes=[pltpu.VMEM((width, tokens), jnp.bfloat16), pltpu.VMEM((tokens, WIDE), jnp.bfloat16)],
+        input_output_aliases={2 + len(pieces): 0} if held else {},
         compiler_params=PARAMS,
         cost_estimate=pl.CostEstimate(
-            flops=2 * width * tokens * half, bytes_accessed=2 * half * (tokens + width), transcendentals=0
+            flops=2 * width * tokens * part, bytes_accessed=2 * part * (tokens + width), transcendentals=0
         ),
         name="weight",
-    )(*map(in_vmem, [columns, *pieces]), *held)
+    )(mine, *map(in_vmem, [columns, *pieces]), *held)
 
 
 def local(layer_input, queries, key_vectors, value_vectors, output_grad, partner_offsets):
     rows, features = queries.shape
     steps = features // (HD * STEP)
     docs = len(DOCS)
-    mine = lax.axis_index("fsdp")
     places = lax.axis_size("fsdp")
+    mine = lax.axis_index("fsdp").astype(jnp.int32).reshape(1)
+    replica = lax.axis_index("dp").astype(jnp.int32).reshape(1)
+    queries, mine, replica = lax.optimization_barrier((queries, mine, replica))
 
     others = [traded(array, "dp", 1, True) for array in (queries, output_grad)]
     firsts = [traded(array, "dp", 1, False) for array in (queries, output_grad)]
@@ -248,37 +320,32 @@
 
     own = [key_vectors, value_vectors]
     stats = call_stats(0, NEAR, partner_offsets, own + query_docs[:NEAR] + grad_docs[:NEAR], [])
-
+    columns = call_spread(layer_input, places)
+    stats, columns = lax.optimization_barrier((stats, columns))
+    columns = lax.all_to_all(columns, "fsdp", 0, 0, tiled=True)
     stats = call_stats(NEAR, docs, partner_offsets, own + query_docs[NEAR:] + grad_docs[NEAR:], [stats])
-
-    width = layer_input.shape[1] // places
-    stats, layer_input = lax.optimization_barrier((stats, layer_input))
-    columns = []
-    for k in range(places):
-        piece = lax.dynamic_slice_in_dim(layer_input, (mine ^ k) * width, width, 1)
-        columns.append(swapped(piece, "fsdp", k) if k else piece)
-    columns = jnp.concatenate(columns, 0).T
 
     replicas = lax.axis_size("dp")
     groups = [list(range(low, low + GROUP)) for low in range(0, replicas, GROUP)]
     here = lax.all_to_all(stats, "dp", 0, 0, axis_index_groups=groups, tiled=True)
+    after_even = traded(here, "dp", GROUP, False)
     here, columns = lax.optimization_barrier((here, columns))
-    after_odd = traded(here, "dp", GROUP, True)
-    stat_parts = [traded(here, "dp", GROUP, False), here, after_odd]
-    replica = lax.axis_index("dp")
-    place = jnp.stack([replica % GROUP, replica // GROUP % 2]).astype(jnp.int32)
+    stat_parts = [after_even, here, traded(here, "dp", GROUP, True)]
 
     each = steps // HALVES
-    arrays = own + query_docs + grad_docs
-    parts = [call_grads(half * each, each, place, stat_parts, arrays) for half in range(HALVES)]
-
-    weight = None
-    for half, (key_part, _) in enumerate(parts):
-        across = swapped(key_part, "fsdp", 2)
-        pieces = [key_part, swapped(key_part, "fsdp", 1), across, swapped(across, "fsdp", 1)]
-        held = [] if weight is None else [weight]
-        weight = call_weight(half, columns, pieces, features, held)
-    return weight[None], jnp.concatenate([value_part for _, value_part in parts], 1)
+    halves, held = [], []
+    for half in range(HALVES):
+        key_half, *held = call_grads(half * each, each, replica, stat_parts, own + query_docs + grad_docs, held)
+        halves.append(key_half)
+    key_grad, value_grad = held
+
+    beside = swapped(key_grad, "fsdp", 1)
+    held = []
+    for half, key_half in enumerate(halves):
+        across = swapped(key_half, "fsdp", 2)
+        pieces = [key_half, beside, across, swapped(across, "fsdp", 1)]
+        held = [call_weight(half, mine, columns, pieces, held)]
+    return held[0][None], value_grad
 
 
 def solution(mesh):

time: 140 us -> 134 us (0.957)
  blocking collectives: 0 us -> 8.93 us
  local copies, waits for them, and re-layouts: 13 us -> 5.87 us
  waiting for transfers between devices: 22.6 us -> 16.1 us
  starting transfers between devices: 82.7 us -> 77.3 us
  Pallas kernels: 18.3 us -> 23.5 us
    ppermute x10, waiting for transfers between devices: 20.4 us -> 10.1 us  [traded(): return lax.ppermute(value, axis, pairs)]
    all_to_all x0 -> x1, blocking collectives: none -> 8.93 us  [local(): lax.all_to_all(stats, 'dp', 0, 0, axis_index_groups=groups, tiled=True)]
    ppermute x9 -> x5, starting transfers between devices: 24.6 us -> 15.9 us  [swapped(): return lax.ppermute(value, axis, pairs)]
    unnamed x38 -> x22, local copies, waits for them, and re-layouts: 11.6 us -> 5.87 us
    pallas_call x4 -> x5, Pallas kernels: 11.8 us -> 16.5 us  [the longest x2 11.8 us: call_grads(): pl.pallas_call(functools.partial(grads_kernel, first), in_specs=[pl.Block...]
    ppermute x9 -> x5, waiting for transfers between devices: 2.14 us -> 4.56 us  [swapped(): return lax.ppermute(value, axis, pairs)]
    all_to_all x1, starting transfers between devices: 3.6 us -> 5.55 us  [local(): columns = lax.all_to_all(columns, 'fsdp', 0, 0, tiled=True)]
    all_to_all x1, waiting for transfers between devices: 0.01 us -> 1.46 us  [local(): columns = lax.all_to_all(columns, 'fsdp', 0, 0, tiled=True)]
  transfers between devices with their start and end apart: 20 -> 16, of which waited for: 5 -> 5; matrix products, arithmetic and copies ran while one was open for 2% -> 0% of each run, Pallas kernels for 6% -> 12%
where the time goes in v7:
time: 134 us; the launch traced here: 133 us
  starting transfers between devices  77.3 us (58%)
  Pallas kernels  23.5 us (18%)
  waiting for transfers between devices  16.1 us (12%)
  blocking collectives  8.93 us (7%)
  local copies, waits for them, and re-layouts  5.87 us (4%)
    ppermute x10, starting transfers between devices, traded(): return lax.ppermute(value, axis, pairs)  55.8 us
    ppermute x5, starting transfers between devices, swapped(): return lax.ppermute(value, axis, pairs)  15.9 us
    pallas_call x2, Pallas kernels, call_grads(): pl.pallas_call(functools.partial(grads_kernel, first), in_specs=[pl.Block...  11.8 us
    ppermute x10, waiting for transfers between devices, traded(): return lax.ppermute(value, axis, pairs)  10.1 us
    all_to_all x1, blocking collectives, local(): lax.all_to_all(stats, 'dp', 0, 0, axis_index_groups=groups, tiled=True)  8.93 us
    pallas_call x2, Pallas kernels, call_stats(): pl.pallas_call(functools.partial(stats_kernel, low), in_specs=[pl.BlockSp...  7 us
    unnamed x22, local copies, waits for them, and re-layouts  5.87 us
    all_to_all x1, starting transfers between devices, local(): columns = lax.all_to_all(columns, 'fsdp', 0, 0, tiled=True)  5.55 us
  transfers between devices with their start and end apart: 16, of which 5 were waited for; matrix products, arithmetic and copies ran while one was open for 0% of the time, Pallas kernels for 12%

profile of v7, /device:TPU:1, one launch (start us, length us, event | category | flops | bytes accessed | tf_op | source)
XLA Modules:
  0.0 132.7 jit_solution(8491701003185987000)
XLA Ops:
  0.6 4.0 %collective-permute-start.2 = (bf16[128,2048]{1,0:T(8,128)(2,1)}, bf16[128,2048]{1,0:T(8,128)(2,1)S(1)}, u32[]{:S(2)}, u32[]{:S(2)}) collective-permute-start(bf16[128,2048]{1,0:T(8,128)(2,1)} %refs_5_.1), channel_id=1, source_target_pairs={{0,4},{4,0},{8,12},{12,8},{16,20},{20,16},{24,28},{28,24},{32,36},... | collective-permute-start | bytes 1572872 | tf_op jit(solution)/shard_map/ppermute | solution.py:32
  4.7 15.2 %collective-permute-start = (bf16[128,2048]{1,0:T(8,128)(2,1)}, bf16[128,2048]{1,0:T(8,128)(2,1)}, u32[]{:S(2)}, u32[]{:S(2)}) collective-permute-start(bf16[128,2048]{1,0:T(8,128)(2,1)} %refs_5_.1), channel_id=1, source_target_pairs={{0,508},{4,8},{8,4},{12,16},{16,12},{20,24},{24,20},{28,32},{32,28... | collective-permute-start | bytes 1572872 | tf_op jit(solution)/shard_map/ppermute | solution.py:32
  19.9 1.9 %collective-permute-start.6 = (bf16[128,2048]{1,0:T(8,128)(2,1)}, bf16[128,2048]{1,0:T(8,128)(2,1)}, u32[]{:S(2)}, u32[]{:S(2)}) collective-permute-start(bf16[128,2048]{1,0:T(8,128)(2,1)} %refs_10_.3), channel_id=1, source_target_pairs={{0,4},{4,0},{8,12},{12,8},{16,20},{20,16},{24,28},{28,24},{32,36},... | collective-permute-start | bytes 1572872 | tf_op jit(solution)/shard_map/ppermute | solution.py:32
  21.8 2.9 %collective-permute-start.4 = (bf16[128,2048]{1,0:T(8,128)(2,1)}, bf16[128,2048]{1,0:T(8,128)(2,1)}, u32[]{:S(2)}, u32[]{:S(2)}) collective-permute-start(bf16[128,2048]{1,0:T(8,128)(2,1)} %refs_10_.3), channel_id=1, source_target_pairs={{0,508},{4,8},{8,4},{12,16},{16,12},{20,24},{24,20},{28,32},{32,28... | collective-permute-start | bytes 1572872 | tf_op jit(solution)/shard_map/ppermute | solution.py:32
  24.7 0.0 collective-permute-done.2.refs_1_.refs_6_
  24.8 8.1 %collective-permute-start.3 = (bf16[128,2048]{1,0:T(8,128)(2,1)S(1)}, bf16[128,2048]{1,0:T(8,128)(2,1)}, u32[]{:S(2)}, u32[]{:S(2)}) collective-permute-start(bf16[128,2048]{1,0:T(8,128)(2,1)S(1)} %collective-permute-done.2.refs_1_.refs_6_), channel_id=1, source_target_pairs={{0,508},{4,8},{8,4},{12,16},{16,12},{20,24},{24,20},{28,32},{32,28... | collective-permute-start | bytes 1572872 | tf_op jit(solution)/shard_map/ppermute | solution.py:32
  32.9 0.0 collective-permute-done.refs_2_.refs_7_
  32.9 1.9 %collective-permute-start.1 = (bf16[128,2048]{1,0:T(8,128)(2,1)}, bf16[128,2048]{1,0:T(8,128)(2,1)}, u32[]{:S(2)}, u32[]{:S(2)}) collective-permute-start(bf16[128,2048]{1,0:T(8,128)(2,1)} %collective-permute-done.refs_2_.refs_7_), channel_id=1, source_target_pairs={{0,4},{4,0},{8,12},{12,8},{16,20},{20,16},{24,28},{28,24},{32,36},... | collective-permute-start | bytes 1572872 | tf_op jit(solution)/shard_map/ppermute | solution.py:32
  34.8 0.0 collective-permute-done.6.refs_4_.refs_11_
  34.8 8.9 %collective-permute-start.7 = (bf16[128,2048]{1,0:T(8,128)(2,1)}, bf16[128,2048]{1,0:T(8,128)(2,1)}, u32[]{:S(2)}, u32[]{:S(2)}) collective-permute-start(bf16[128,2048]{1,0:T(8,128)(2,1)} %collective-permute-done.6.refs_4_.refs_11_), channel_id=1, source_target_pairs={{0,508},{4,8},{8,4},{12,16},{16,12},{20,24},{24,20},{28,32},{32,28... | collective-permute-start | bytes 1572872 | tf_op jit(solution)/shard_map/ppermute | solution.py:32
  43.7 0.0 collective-permute-done.4.refs_5_.refs_12_
  43.7 1.9 %collective-permute-start.5 = (bf16[128,2048]{1,0:T(8,128)(2,1)}, bf16[128,2048]{1,0:T(8,128)(2,1)}, u32[]{:S(2)}, u32[]{:S(2)}) collective-permute-start(bf16[128,2048]{1,0:T(8,128)(2,1)} %collective-permute-done.4.refs_5_.refs_12_), channel_id=1, source_target_pairs={{0,4},{4,0},{8,12},{12,8},{16,20},{20,16},{24,28},{28,24},{32,36},... | collective-permute-start | bytes 1572872 | tf_op jit(solution)/shard_map/ppermute | solution.py:32
  45.7 0.0 copy-start.8
  45.7 1.0 copy-done.8
  46.7 0.8 spread.1
  47.5 0.0 copy-start
  47.6 1.0 copy-done
  48.6 0.0 copy-start.2
  48.6 1.0 copy-done.2
  49.6 0.0 copy-start.4
  49.6 1.0 copy-done.4
  50.7 0.0 copy-start.6
  50.7 1.0 copy-done.6
  51.7 0.0 copy-start.9
  51.7 0.7 copy-done.9
  52.4 0.0 copy-start.1
  52.4 0.0 copy-start.3
  52.4 0.0 copy-start.10
  52.4 3.7 %stats.2.refs_4_ = f32[96,128]{1,0:T(8,128)S(1)} custom-call(s32[1,2]{1,0:T(1,128)S(1)} %copy-done.9, bf16[128,2048]{1,0:T(8,128)(2,1)S(1)} %copy-done, bf16[128,2048]{1,0:T(8,128)(2,1)S(1)} %copy-done.2, bf16[128,2048]{1,0:T(8,128)(2,1)S(1)} %copy-done.4, bf16[128,2048]{1,0:T(8,128)(2,1)S(1)} %collective-permute-done.2.refs_1_.refs_6_, ...), custom_call_target="tpu_custom_call" | custom-call | flops 402653184 | bytes 4194304 | tf_op jit(solution)/shard_map/stats/pallas_call | solution.py:228
  56.1 5.6 %all-to-all-start.1 = ((bf16[4,128,512]{2,1,0:T(8,128)(2,1)}), bf16[4,128,512]{2,1,0:T(8,128)(2,1)S(1)}, u32[]{:S(2)}, u32[]{:S(2)}) async-start(bf16[4,128,512]{2,1,0:T(8,128)(2,1)} %bitcast.4), calls=%async_computation.1 | async-start | bytes 1048576 | tf_op jit(solution)/shard_map/all_to_all | solution.py:325
  61.6 0.0 copy-start.5
  61.7 0.0 copy-start.7
  61.7 0.0 collective-permute-done.3.refs_1_.refs_9_
  61.7 0.0 collective-permute-done.1.refs_0_.refs_8_
  61.7 3.2 %collective-permute-done.7.refs_3_.refs_14_ = bf16[128,2048]{1,0:T(8,128)(2,1)} collective-permute-done((bf16[128,2048]{1,0:T(8,128)(2,1)}, bf16[128,2048]{1,0:T(8,128)(2,1)}, u32[]{:S(2)}, u32[]{:S(2)}) %collective-permute-start.7) | collective-permute-done | bytes 524320 | tf_op jit(solution)/shard_map/ppermute | solution.py:32
  64.9 0.0 collective-permute-done.5.refs_2_.refs_13_
  64.9 0.0 copy-done.1
  64.9 0.0 copy-done.3
  64.9 0.0 copy-done.10
  64.9 3.3 %stats.3 = f32[672,128]{1,0:T(8,128)S(1)} custom-call(s32[1,2]{1,0:T(1,128)S(1)} %copy-done.10, bf16[128,2048]{1,0:T(8,128)(2,1)S(1)} %copy-done.1, bf16[128,2048]{1,0:T(8,128)(2,1)S(1)} %copy-done.3, bf16[128,2048]{1,0:T(8,128)(2,1)} %collective-permute-done.1.refs_0_.refs_8_, bf16[128,2048]{1,0:T(8,128)(2,1)} %collective-permute-done.3.refs_1_.refs_9_, ...), custom_call_target="tpu_custom_call" | custom-call | flops 268435456 | bytes 3145728 | tf_op jit(solution)/shard_map/stats/pallas_call | solution.py:228
  68.2 1.5 %all-to-all-done.1 = bf16[4,128,512]{2,1,0:T(8,128)(2,1)S(1)} async-done(((bf16[4,128,512]{2,1,0:T(8,128)(2,1)}), bf16[4,128,512]{2,1,0:T(8,128)(2,1)S(1)}, u32[]{:S(2)}, u32[]{:S(2)}) %all-to-all-start.1) | async-done | bytes 524320 | tf_op jit(solution)/shard_map/all_to_all | solution.py:325
  69.6 8.9 %all_to_all.24 = f32[4,168,128]{2,1,0:T(8,128)S(1)} all-to-all(f32[4,168,128]{2,1,0:T(8,128)S(1)} %bitcast.13), channel_id=1, replica_groups={{0,4,8,12},{16,20,24,28},{32,36,40,44},{48,52,56,60},{64,68,72,76},{80,..., dimensions={0} | all-to-all | bytes 688128 | tf_op jit(solution)/shard_map/all_to_all | solution.py:330
  78.6 9.0 %collective-permute-start.9 = (f32[672,128]{1,0:T(8,128)S(1)}, f32[672,128]{1,0:T(8,128)S(1)}, u32[]{:S(2)}, u32[]{:S(2)}) collective-permute-start(f32[672,128]{1,0:T(8,128)S(1)} %bitcast.9), channel_id=1, source_target_pairs={{0,496},{4,500},{8,504},{12,508},{16,32},{20,36},{24,40},{28,44},{... | collective-permute-start | bytes 1032200 | tf_op jit(solution)/shard_map/ppermute | solution.py:32
  87.6 1.9 %collective-permute-start.8 = (f32[672,128]{1,0:T(8,128)S(1)}, f32[672,128]{1,0:T(8,128)S(1)}, u32[]{:S(2)}, u32[]{:S(2)}) collective-permute-start(f32[672,128]{1,0:T(8,128)S(1)} %bitcast.10), channel_id=1, source_target_pairs={{0,16},{4,20},{8,24},{12,28},{16,0},{20,4},{24,8},{28,12},{32,48},... | collective-permute-start | bytes 1032200 | tf_op jit(solution)/shard_map/ppermute | solution.py:32
  89.5 4.1 %collective-permute-done.9.refs_2_ = f32[672,128]{1,0:T(8,128)S(1)} collective-permute-done((f32[672,128]{1,0:T(8,128)S(1)}, f32[672,128]{1,0:T(8,128)S(1)}, u32[]{:S(2)}, u32[]{:S(2)}) %collective-permute-start.9) | collective-permute-done | bytes 344096 | tf_op jit(solution)/shard_map/ppermute | solution.py:32
  93.5 2.8 %collective-permute-done.8.refs_0_ = f32[672,128]{1,0:T(8,128)S(1)} collective-permute-done((f32[672,128]{1,0:T(8,128)S(1)}, f32[672,128]{1,0:T(8,128)S(1)}, u32[]{:S(2)}, u32[]{:S(2)}) %collective-permute-start.8) | collective-permute-done | bytes 344096 | tf_op jit(solution)/shard_map/ppermute | solution.py:32
  96.4 0.0 copy-done.5
  96.4 0.0 copy-done.7
  96.4 5.9 %grads.2 = (bf16[128,1024]{1,0:T(8,128)(2,1)S(1)}, bf16[128,2048]{1,0:T(8,128)(2,1)S(1)}, bf16[128,2048]{1,0:T(8,128)(2,1)}) custom-call(s32[1]{0:T(128)} %bitcast.1.replica_ref, f32[672,128]{1,0:T(8,128)S(1)} %collective-permute-done.8.refs_0_, f32[672,128]{1,0:T(8,128)S(1)} %bitcast.11, f32[672,128]{1,0:T(8,128)S(1)} %collective-permute-done.9.refs_2_, ...), custom_call_target="tpu_custom_call" | custom-call | flops 671088640 | bytes 3145728 | tf_op jit(solution)/shard_map/grads/pallas_call | solution.py:247
  102.3 2.8 %collective-permute-start.13 = (bf16[128,1024]{1,0:T(8,128)(2,1)S(1)}, bf16[128,1024]{1,0:T(8,128)(2,1)S(1)}, u32[]{:S(2)}, u32[]{:S(2)}) collective-permute-start(bf16[128,1024]{1,0:T(8,128)(2,1)S(1)} %get-tuple-element.26.refs_0_), channel_id=1, source_target_pairs={{0,2},{1,3},{2,0},{3,1},{4,6},{5,7},{6,4},{7,5},{8,10},{9,11},{10,... | collective-permute-start | bytes 786440 | tf_op jit(solution)/shard_map/ppermute | solution.py:37
  105.1 5.9 %grads.3 = (bf16[128,1024]{1,0:T(8,128)(2,1)S(1)}, bf16[128,2048]{1,0:T(8,128)(2,1)S(1)}, bf16[128,2048]{1,0:T(8,128)(2,1)}) custom-call(s32[1]{0:T(128)} %bitcast.1.replica_ref, f32[672,128]{1,0:T(8,128)S(1)} %collective-permute-done.8.refs_0_, f32[672,128]{1,0:T(8,128)S(1)} %bitcast.12, ...), custom_call_target="tpu_custom_call", output_to_operand_aliasing={{1}: (16, {}), {2}: (17, {})} | custom-call | flops 671088640 | bytes 3145728 | tf_op jit(solution)/shard_map/grads/pallas_call | solution.py:247
  111.0 5.2 %collective-permute-start.10 = (bf16[128,2048]{1,0:T(8,128)(2,1)S(1)}, bf16[128,2048]{1,0:T(8,128)(2,1)S(1)}, u32[]{:S(2)}, u32[]{:S(2)}) collective-permute-start(bf16[128,2048]{1,0:T(8,128)(2,1)S(1)} %get-tuple-element.25), channel_id=1, source_target_pairs={{0,1},{1,0},{2,3},{3,2},{4,5},{5,4},{6,7},{7,6},{8,9},{9,8},{10,11... | collective-permute-start | bytes 1572872 | tf_op jit(solution)/shard_map/ppermute | solution.py:37
  116.2 3.0 %collective-permute-start.11 = (bf16[128,1024]{1,0:T(8,128)(2,1)S(1)}, bf16[128,1024]{1,0:T(8,128)(2,1)S(1)}, u32[]{:S(2)}, u32[]{:S(2)}) collective-permute-start(bf16[128,1024]{1,0:T(8,128)(2,1)S(1)} %get-tuple-element.24.refs_0_), channel_id=1, source_target_pairs={{0,2},{1,3},{2,0},{3,1},{4,6},{5,7},{6,4},{7,5},{8,10},{9,11},{10,... | collective-permute-start | bytes 786440 | tf_op jit(solution)/shard_map/ppermute | solution.py:37
  119.2 0.0 collective-permute-done.13.refs_2_
  119.3 2.2 %collective-permute-start.14 = (bf16[128,1024]{1,0:T(8,128)(2,1)S(1)}, bf16[128,1024]{1,0:T(8,128)(2,1)S(1)}, u32[]{:S(2)}, u32[]{:S(2)}) collective-permute-start(bf16[128,1024]{1,0:T(8,128)(2,1)S(1)} %collective-permute-done.13.refs_2_), channel_id=1, source_target_pairs={{0,1},{1,0},{2,3},{3,2},{4,5},{5,4},{6,7},{7,6},{8,9},{9,8},{10,11... | collective-permute-start | bytes 786440 | tf_op jit(solution)/shard_map/ppermute | solution.py:37
  121.5 4.5 %collective-permute-done.11.refs_2_ = bf16[128,1024]{1,0:T(8,128)(2,1)S(1)} collective-permute-done((bf16[128,1024]{1,0:T(8,128)(2,1)S(1)}, bf16[128,1024]{1,0:T(8,128)(2,1)S(1)}, u32[]{:S(2)}, u32[]{:S(2)}) %collective-permute-start.11) | collective-permute-done | bytes 262176 | tf_op jit(solution)/shard_map/ppermute | solution.py:37
  126.0 2.7 %collective-permute-start.12 = (bf16[128,1024]{1,0:T(8,128)(2,1)S(1)}, bf16[128,1024]{1,0:T(8,128)(2,1)S(1)}, u32[]{:S(2)}, u32[]{:S(2)}) collective-permute-start(bf16[128,1024]{1,0:T(8,128)(2,1)S(1)} %collective-permute-done.11.refs_2_), channel_id=1, source_target_pairs={{0,1},{1,0},{2,3},{3,2},{4,5},{5,4},{6,7},{7,6},{8,9},{9,8},{10,11... | collective-permute-start | bytes 786440 | tf_op jit(solution)/shard_map/ppermute | solution.py:37
  128.7 0.0 collective-permute-done.14.refs_3_
  128.7 0.0 collective-permute-done.10.refs_1_
  128.7 2.0 %weight.2.refs_4_ = bf16[512,2048]{1,0:T(8,128)(2,1)} custom-call(s32[1]{0:T(128)} %bitcast.mine_ref, bf16[512,512]{1,0:T(8,128)(2,1)S(1)} %bitcast.7, bf16[128,1024]{1,0:T(8,128)(2,1)S(1)} %get-tuple-element.26.refs_0_, bf16[128,2048]{1,0:T(8,128)(2,1)S(1)} %collective-permute-done.10.refs_1_, bf16[128,1024]{1,0:T(8,128)(2,1)S(1)} %collective-permute-done.13.refs_2_, ...), custom_call_target="tpu_custom_call" | custom-call | flops 536870912 | bytes 2097152 | tf_op jit(solution)/shard_map/weight/pallas_call | solution.py:287
  130.7 0.0 collective-permute-done.12.refs_3_
  130.7 2.0 %weight.3 = bf16[512,2048]{1,0:T(8,128)(2,1)} custom-call(s32[1]{0:T(128)} %bitcast.mine_ref, bf16[512,512]{1,0:T(8,128)(2,1)S(1)} %bitcast.8, bf16[128,1024]{1,0:T(8,128)(2,1)S(1)} %get-tuple-element.24.refs_0_, bf16[128,2048]{1,0:T(8,128)(2,1)S(1)} %collective-permute-done.10.refs_1_, ...), custom_call_target="tpu_custom_call", output_to_operand_aliasing={{}: (6, {})} | custom-call | flops 536870912 | bytes 2097152 | tf_op jit(solution)/shard_map/weight/pallas_call | solution.py:287
Async XLA Ops:
  0.6 24.1 %collective-permute-start.2 = (bf16[128,2048]{1,0:T(8,128)(2,1)}, bf16[128,2048]{1,0:T(8,128)(2,1)S(1)}, u32[]{:S(2)}, u32[]{:S(2)}) collective-permute-start(bf16[128,2048]{1,0:T(8,128)(2,1)} %refs_5_.1), channel_id=1, source_target_pairs={{0,4},{4,0},{8,12},{12,8},{16,20},{20,16},{24,28},{28,24},{32,36},... | collective-permute-start | bytes 1572872 | tf_op jit(solution)/shard_map/ppermute | solution.py:32
  4.7 28.2 %collective-permute-start = (bf16[128,2048]{1,0:T(8,128)(2,1)}, bf16[128,2048]{1,0:T(8,128)(2,1)}, u32[]{:S(2)}, u32[]{:S(2)}) collective-permute-start(bf16[128,2048]{1,0:T(8,128)(2,1)} %refs_5_.1), channel_id=1, source_target_pairs={{0,508},{4,8},{8,4},{12,16},{16,12},{20,24},{24,20},{28,32},{32,28... | collective-permute-start | bytes 1572872 | tf_op jit(solution)/shard_map/ppermute | solution.py:32
  19.9 14.9 %collective-permute-start.6 = (bf16[128,2048]{1,0:T(8,128)(2,1)}, bf16[128,2048]{1,0:T(8,128)(2,1)}, u32[]{:S(2)}, u32[]{:S(2)}) collective-permute-start(bf16[128,2048]{1,0:T(8,128)(2,1)} %refs_10_.3), channel_id=1, source_target_pairs={{0,4},{4,0},{8,12},{12,8},{16,20},{20,16},{24,28},{28,24},{32,36},... | collective-permute-start | bytes 1572872 | tf_op jit(solution)/shard_map/ppermute | solution.py:32
  21.8 21.9 %collective-permute-start.4 = (bf16[128,2048]{1,0:T(8,128)(2,1)}, bf16[128,2048]{1,0:T(8,128)(2,1)}, u32[]{:S(2)}, u32[]{:S(2)}) collective-permute-start(bf16[128,2048]{1,0:T(8,128)(2,1)} %refs_10_.3), channel_id=1, source_target_pairs={{0,508},{4,8},{8,4},{12,16},{16,12},{20,24},{24,20},{28,32},{32,28... | collective-permute-start | bytes 1572872 | tf_op jit(solution)/shard_map/ppermute | solution.py:32
  24.8 36.9 %collective-permute-start.3 = (bf16[128,2048]{1,0:T(8,128)(2,1)S(1)}, bf16[128,2048]{1,0:T(8,128)(2,1)}, u32[]{:S(2)}, u32[]{:S(2)}) collective-permute-start(bf16[128,2048]{1,0:T(8,128)(2,1)S(1)} %collective-permute-done.2.refs_1_.refs_6_), channel_id=1, source_target_pairs={{0,508},{4,8},{8,4},{12,16},{16,12},{20,24},{24,20},{28,32},{32,28... | collective-permute-start | bytes 1572872 | tf_op jit(solution)/shard_map/ppermute | solution.py:32
  32.9 28.8 %collective-permute-start.1 = (bf16[128,2048]{1,0:T(8,128)(2,1)}, bf16[128,2048]{1,0:T(8,128)(2,1)}, u32[]{:S(2)}, u32[]{:S(2)}) collective-permute-start(bf16[128,2048]{1,0:T(8,128)(2,1)} %collective-permute-done.refs_2_.refs_7_), channel_id=1, source_target_pairs={{0,4},{4,0},{8,12},{12,8},{16,20},{20,16},{24,28},{28,24},{32,36},... | collective-permute-start | bytes 1572872 | tf_op jit(solution)/shard_map/ppermute | solution.py:32
  34.8 30.1 %collective-permute-start.7 = (bf16[128,2048]{1,0:T(8,128)(2,1)}, bf16[128,2048]{1,0:T(8,128)(2,1)}, u32[]{:S(2)}, u32[]{:S(2)}) collective-permute-start(bf16[128,2048]{1,0:T(8,128)(2,1)} %collective-permute-done.6.refs_4_.refs_11_), channel_id=1, source_target_pairs={{0,508},{4,8},{8,4},{12,16},{16,12},{20,24},{24,20},{28,32},{32,28... | collective-permute-start | bytes 1572872 | tf_op jit(solution)/shard_map/ppermute | solution.py:32
  43.7 21.1 %collective-permute-start.5 = (bf16[128,2048]{1,0:T(8,128)(2,1)}, bf16[128,2048]{1,0:T(8,128)(2,1)}, u32[]{:S(2)}, u32[]{:S(2)}) collective-permute-start(bf16[128,2048]{1,0:T(8,128)(2,1)} %collective-permute-done.4.refs_5_.refs_12_), channel_id=1, source_target_pairs={{0,4},{4,0},{8,12},{12,8},{16,20},{20,16},{24,28},{28,24},{32,36},... | collective-permute-start | bytes 1572872 | tf_op jit(solution)/shard_map/ppermute | solution.py:32
  45.7 1.0 copy-start.8
  47.5 1.0 copy-start
  48.6 1.0 copy-start.2
  49.6 1.0 copy-start.4
  50.7 1.0 copy-start.6
  51.7 0.7 copy-start.9
  52.4 12.5 %copy-start.1 = (bf16[128,2048]{1,0:T(8,128)(2,1)S(1)}, bf16[128,2048]{1,0:T(8,128)(2,1)}, u32[]{:S(2)}) copy-start(bf16[128,2048]{1,0:T(8,128)(2,1)} %refs_3_.5) | copy-start | bytes 1572868
  52.4 12.5 %copy-start.3 = (bf16[128,2048]{1,0:T(8,128)(2,1)S(1)}, bf16[128,2048]{1,0:T(8,128)(2,1)}, u32[]{:S(2)}) copy-start(bf16[128,2048]{1,0:T(8,128)(2,1)} %refs_4_.3) | copy-start | bytes 1572868
  52.4 12.5 %copy-start.10 = (s32[1,2]{1,0:T(1,128)S(1)}, s32[1,2]{1,0:T(1,128)}, u32[]{:S(2)}) copy-start(s32[1,2]{1,0:T(1,128)} %offsets_ref.3) | copy-start | bytes 28
  56.1 13.5 %all-to-all-start.1 = ((bf16[4,128,512]{2,1,0:T(8,128)(2,1)}), bf16[4,128,512]{2,1,0:T(8,128)(2,1)S(1)}, u32[]{:S(2)}, u32[]{:S(2)}) async-start(bf16[4,128,512]{2,1,0:T(8,128)(2,1)} %bitcast.4), calls=%async_computation.1 | async-start | bytes 1048576 | tf_op jit(solution)/shard_map/all_to_all | solution.py:325
  61.6 34.7 %copy-start.5 = (bf16[128,2048]{1,0:T(8,128)(2,1)S(1)}, bf16[128,2048]{1,0:T(8,128)(2,1)}, u32[]{:S(2)}) copy-start(bf16[128,2048]{1,0:T(8,128)(2,1)} %refs_5_.1) | copy-start | bytes 1572868
  61.7 34.7 %copy-start.7 = (bf16[128,2048]{1,0:T(8,128)(2,1)S(1)}, bf16[128,2048]{1,0:T(8,128)(2,1)}, u32[]{:S(2)}) copy-start(bf16[128,2048]{1,0:T(8,128)(2,1)} %refs_10_.3) | copy-start | bytes 1572868
  78.6 15.0 %collective-permute-start.9 = (f32[672,128]{1,0:T(8,128)S(1)}, f32[672,128]{1,0:T(8,128)S(1)}, u32[]{:S(2)}, u32[]{:S(2)}) collective-permute-start(f32[672,128]{1,0:T(8,128)S(1)} %bitcast.9), channel_id=1, source_target_pairs={{0,496},{4,500},{8,504},{12,508},{16,32},{20,36},{24,40},{28,44},{... | collective-permute-start | bytes 1032200 | tf_op jit(solution)/shard_map/ppermute | solution.py:32
  87.6 8.8 %collective-permute-start.8 = (f32[672,128]{1,0:T(8,128)S(1)}, f32[672,128]{1,0:T(8,128)S(1)}, u32[]{:S(2)}, u32[]{:S(2)}) collective-permute-start(f32[672,128]{1,0:T(8,128)S(1)} %bitcast.10), channel_id=1, source_target_pairs={{0,16},{4,20},{8,24},{12,28},{16,0},{20,4},{24,8},{28,12},{32,48},... | collective-permute-start | bytes 1032200 | tf_op jit(solution)/shard_map/ppermute | solution.py:32
  102.3 17.0 %collective-permute-start.13 = (bf16[128,1024]{1,0:T(8,128)(2,1)S(1)}, bf16[128,1024]{1,0:T(8,128)(2,1)S(1)}, u32[]{:S(2)}, u32[]{:S(2)}) collective-permute-start(bf16[128,1024]{1,0:T(8,128)(2,1)S(1)} %get-tuple-element.26.refs_0_), channel_id=1, source_target_pairs={{0,2},{1,3},{2,0},{3,1},{4,6},{5,7},{6,4},{7,5},{8,10},{9,11},{10,... | collective-permute-start | bytes 786440 | tf_op jit(solution)/shard_map/ppermute | solution.py:37
  111.0 17.7 %collective-permute-start.10 = (bf16[128,2048]{1,0:T(8,128)(2,1)S(1)}, bf16[128,2048]{1,0:T(8,128)(2,1)S(1)}, u32[]{:S(2)}, u32[]{:S(2)}) collective-permute-start(bf16[128,2048]{1,0:T(8,128)(2,1)S(1)} %get-tuple-element.25), channel_id=1, source_target_pairs={{0,1},{1,0},{2,3},{3,2},{4,5},{5,4},{6,7},{7,6},{8,9},{9,8},{10,11... | collective-permute-start | bytes 1572872 | tf_op jit(solution)/shard_map/ppermute | solution.py:37
  116.2 9.8 %collective-permute-start.11 = (bf16[128,1024]{1,0:T(8,128)(2,1)S(1)}, bf16[128,1024]{1,0:T(8,128)(2,1)S(1)}, u32[]{:S(2)}, u32[]{:S(2)}) collective-permute-start(bf16[128,1024]{1,0:T(8,128)(2,1)S(1)} %get-tuple-element.24.refs_0_), channel_id=1, source_target_pairs={{0,2},{1,3},{2,0},{3,1},{4,6},{5,7},{6,4},{7,5},{8,10},{9,11},{10,... | collective-permute-start | bytes 786440 | tf_op jit(solution)/shard_map/ppermute | solution.py:37
  119.3 9.5 %collective-permute-start.14 = (bf16[128,1024]{1,0:T(8,128)(2,1)S(1)}, bf16[128,1024]{1,0:T(8,128)(2,1)S(1)}, u32[]{:S(2)}, u32[]{:S(2)}) collective-permute-start(bf16[128,1024]{1,0:T(8,128)(2,1)S(1)} %collective-permute-done.13.refs_2_), channel_id=1, source_target_pairs={{0,1},{1,0},{2,3},{3,2},{4,5},{5,4},{6,7},{7,6},{8,9},{9,8},{10,11... | collective-permute-start | bytes 786440 | tf_op jit(solution)/shard_map/ppermute | solution.py:37
  126.0 4.7 %collective-permute-start.12 = (bf16[128,1024]{1,0:T(8,128)(2,1)S(1)}, bf16[128,1024]{1,0:T(8,128)(2,1)S(1)}, u32[]{:S(2)}, u32[]{:S(2)}) collective-permute-start(bf16[128,1024]{1,0:T(8,128)(2,1)S(1)} %collective-permute-done.11.refs_2_), channel_id=1, source_target_pairs={{0,1},{1,0},{2,3},{3,2},{4,5},{5,4},{6,7},{7,6},{8,9},{9,8},{10,11... | collective-permute-start | bytes 786440 | tf_op jit(solution)/shard_map/ppermute | solution.py:37

commit v8 on v7

--- a/solution.py
+++ b/solution.py
@@ -147,14 +147,16 @@
     replica = replica_ref[0]
 
     above = 2 - 2 * (replica // GROUP % 2)
-    stat_copies = [
-        pltpu.make_async_copy(ref, stat_ref.at[pl.ds(pl.multiple_of(place * size, TILE), size), :], sems.at[at])
-        for at, (place, ref) in enumerate(zip((above, 1, 2 - above), stat_refs))
-    ]
-    for copy in stat_copies:
-        copy.start()
-    for copy in stat_copies:
-        copy.wait()
+    for place, ref in zip((2 - above, 1, above), stat_refs):
+        stat_ref[pl.ds(pl.multiple_of(place * size, TILE), size), :] = ref[...]
+
+    def writes(at):
+        cols = pl.ds(pl.multiple_of((at + first) * STEP * HD, HD), STEP * HD)
+        part = pl.ds(pl.multiple_of(at * STEP * HD, HD), STEP * HD)
+        return [
+            pltpu.make_async_copy(source.at[:, part], target.at[:, cols], sems.at[kind, at])
+            for kind, (source, target) in enumerate(((key_half, key_out), (value_buffer, value_out)))
+        ]
 
     def group(at, carry):
         step = at + first
@@ -172,18 +174,14 @@
             value_total = dot_nn(probs.astype(jnp.bfloat16), grad_rows)
             key_half[:, out_cols] = key_total.astype(jnp.bfloat16)
             value_buffer[:, out_cols] = value_total.astype(jnp.bfloat16)
+        for copy in writes(at):
+            copy.start()
         return carry
 
     lax.fori_loop(0, each, group, 0)
-    cols = pl.ds(first * STEP * HD, half)
-    out_copies = [
-        pltpu.make_async_copy(key_half, key_out.at[:, cols], sems.at[3]),
-        pltpu.make_async_copy(value_buffer, value_out.at[:, cols], sems.at[4]),
-    ]
-    for copy in out_copies:
-        copy.start()
-    for copy in out_copies:
-        copy.wait()
+    for at in range(each):
+        for copy in writes(at):
+            copy.wait()
 
 
 def spread_kernel(input_ref, out_ref, sems):
@@ -247,15 +245,14 @@
     return pl.pallas_call(
         functools.partial(grads_kernel, first),
         in_specs=[pl.BlockSpec(memory_space=pltpu.SMEM)]
-        + [ANY] * len(stat_parts)
-        + [VMEM] * len(arrays)
+        + [VMEM] * (len(stat_parts) + len(arrays))
         + [ANY] * len(held),
         out_specs=[VMEM, ANY, ANY],
         out_shape=[pltpu.VMEM(half, jnp.bfloat16), whole, whole],
         scratch_shapes=[
             pltpu.VMEM((3 * stat_parts[0].shape[0], rows), jnp.float32),
             pltpu.VMEM(half, jnp.bfloat16),
-            pltpu.SemaphoreType.DMA((5,)),
+            pltpu.SemaphoreType.DMA((2, each)),
         ],
         input_output_aliases={count + at: 1 + at for at in range(len(held))},
         compiler_params=PARAMS,
@@ -263,7 +260,7 @@
             flops=8 * pairs * HD, bytes_accessed=2 * len(arrays) * half[0] * half[1], transcendentals=pairs
         ),
         name="grads",
-    )(replica, *stat_parts, *map(in_vmem, arrays), *held)
+    )(replica, *map(in_vmem, [*stat_parts, *arrays]), *held)
 
 
 def call_spread(layer_input, places):
@@ -328,9 +325,9 @@
     replicas = lax.axis_size("dp")
     groups = [list(range(low, low + GROUP)) for low in range(0, replicas, GROUP)]
     here = lax.all_to_all(stats, "dp", 0, 0, axis_index_groups=groups, tiled=True)
-    after_even = traded(here, "dp", GROUP, False)
+    after_odd = traded(here, "dp", GROUP, True)
     here, columns = lax.optimization_barrier((here, columns))
-    stat_parts = [after_even, here, traded(here, "dp", GROUP, True)]
+    stat_parts = [after_odd, here, traded(here, "dp", GROUP, False)]
 
     each = steps // HALVES
     halves, held = [], []

time: 134 us -> 131 us (0.978)
  transfers between devices with their start and end apart: 16 -> 16, of which waited for: 5 -> 4; matrix products, arithmetic and copies ran while one was open for 0% -> 0% of each run, Pallas kernels for 12% -> 12%
where the time goes in v8:
time: 131 us; the launch traced here: 130 us
  starting transfers between devices  76.8 us (59%)
  Pallas kernels  22.8 us (17%)
  waiting for transfers between devices  15.2 us (12%)
  blocking collectives  8.93 us (7%)
  local copies, waits for them, and re-layouts  5.87 us (4%)
    ppermute x10, starting transfers between devices, traded(): return lax.ppermute(value, axis, pairs)  55.8 us
    ppermute x5, starting transfers between devices, swapped(): return lax.ppermute(value, axis, pairs)  15.4 us
    pallas_call x2, Pallas kernels, call_grads(): pl.pallas_call(functools.partial(grads_kernel, first), in_specs=[pl.Block...  11 us
    ppermute x10, waiting for transfers between devices, traded(): return lax.ppermute(value, axis, pairs)  9.19 us
    all_to_all x1, blocking collectives, local(): lax.all_to_all(stats, 'dp', 0, 0, axis_index_groups=groups, tiled=True)  8.93 us
    pallas_call x2, Pallas kernels, call_stats(): pl.pallas_call(functools.partial(stats_kernel, low), in_specs=[pl.BlockSp...  7 us
    unnamed x22, local copies, waits for them, and re-layouts  5.87 us
    all_to_all x1, starting transfers between devices, local(): columns = lax.all_to_all(columns, 'fsdp', 0, 0, tiled=True)  5.55 us
  transfers between devices with their start and end apart: 16, of which 4 were waited for; matrix products, arithmetic and copies ran while one was open for 0% of the time, Pallas kernels for 12%

profile of v8, /device:TPU:1, one launch (start us, length us, event | category | flops | bytes accessed | tf_op | source)
XLA Modules:
  0.0 130.4 jit_solution(3114843001343279176)
XLA Ops:
  0.6 4.0 %collective-permute-start.2 = (bf16[128,2048]{1,0:T(8,128)(2,1)}, bf16[128,2048]{1,0:T(8,128)(2,1)S(1)}, u32[]{:S(2)}, u32[]{:S(2)}) collective-permute-start(bf16[128,2048]{1,0:T(8,128)(2,1)} %refs_5_.1), channel_id=1, source_target_pairs={{0,4},{4,0},{8,12},{12,8},{16,20},{20,16},{24,28},{28,24},{32,36},... | collective-permute-start | bytes 1572872 | tf_op jit(solution)/shard_map/ppermute | solution.py:32
  4.7 15.2 %collective-permute-start = (bf16[128,2048]{1,0:T(8,128)(2,1)}, bf16[128,2048]{1,0:T(8,128)(2,1)}, u32[]{:S(2)}, u32[]{:S(2)}) collective-permute-start(bf16[128,2048]{1,0:T(8,128)(2,1)} %refs_5_.1), channel_id=1, source_target_pairs={{0,508},{4,8},{8,4},{12,16},{16,12},{20,24},{24,20},{28,32},{32,28... | collective-permute-start | bytes 1572872 | tf_op jit(solution)/shard_map/ppermute | solution.py:32
  19.9 1.9 %collective-permute-start.6 = (bf16[128,2048]{1,0:T(8,128)(2,1)}, bf16[128,2048]{1,0:T(8,128)(2,1)}, u32[]{:S(2)}, u32[]{:S(2)}) collective-permute-start(bf16[128,2048]{1,0:T(8,128)(2,1)} %refs_10_.3), channel_id=1, source_target_pairs={{0,4},{4,0},{8,12},{12,8},{16,20},{20,16},{24,28},{28,24},{32,36},... | collective-permute-start | bytes 1572872 | tf_op jit(solution)/shard_map/ppermute | solution.py:32
  21.8 2.9 %collective-permute-start.4 = (bf16[128,2048]{1,0:T(8,128)(2,1)}, bf16[128,2048]{1,0:T(8,128)(2,1)}, u32[]{:S(2)}, u32[]{:S(2)}) collective-permute-start(bf16[128,2048]{1,0:T(8,128)(2,1)} %refs_10_.3), channel_id=1, source_target_pairs={{0,508},{4,8},{8,4},{12,16},{16,12},{20,24},{24,20},{28,32},{32,28... | collective-permute-start | bytes 1572872 | tf_op jit(solution)/shard_map/ppermute | solution.py:32
  24.7 0.0 collective-permute-done.2.refs_1_.refs_6_
  24.8 8.1 %collective-permute-start.3 = (bf16[128,2048]{1,0:T(8,128)(2,1)S(1)}, bf16[128,2048]{1,0:T(8,128)(2,1)}, u32[]{:S(2)}, u32[]{:S(2)}) collective-permute-start(bf16[128,2048]{1,0:T(8,128)(2,1)S(1)} %collective-permute-done.2.refs_1_.refs_6_), channel_id=1, source_target_pairs={{0,508},{4,8},{8,4},{12,16},{16,12},{20,24},{24,20},{28,32},{32,28... | collective-permute-start | bytes 1572872 | tf_op jit(solution)/shard_map/ppermute | solution.py:32
  32.9 0.0 collective-permute-done.refs_2_.refs_7_
  32.9 1.9 %collective-permute-start.1 = (bf16[128,2048]{1,0:T(8,128)(2,1)}, bf16[128,2048]{1,0:T(8,128)(2,1)}, u32[]{:S(2)}, u32[]{:S(2)}) collective-permute-start(bf16[128,2048]{1,0:T(8,128)(2,1)} %collective-permute-done.refs_2_.refs_7_), channel_id=1, source_target_pairs={{0,4},{4,0},{8,12},{12,8},{16,20},{20,16},{24,28},{28,24},{32,36},... | collective-permute-start | bytes 1572872 | tf_op jit(solution)/shard_map/ppermute | solution.py:32
  34.8 0.0 collective-permute-done.6.refs_4_.refs_11_
  34.8 8.9 %collective-permute-start.7 = (bf16[128,2048]{1,0:T(8,128)(2,1)}, bf16[128,2048]{1,0:T(8,128)(2,1)}, u32[]{:S(2)}, u32[]{:S(2)}) collective-permute-start(bf16[128,2048]{1,0:T(8,128)(2,1)} %collective-permute-done.6.refs_4_.refs_11_), channel_id=1, source_target_pairs={{0,508},{4,8},{8,4},{12,16},{16,12},{20,24},{24,20},{28,32},{32,28... | collective-permute-start | bytes 1572872 | tf_op jit(solution)/shard_map/ppermute | solution.py:32
  43.7 0.0 collective-permute-done.4.refs_5_.refs_12_
  43.7 1.9 %collective-permute-start.5 = (bf16[128,2048]{1,0:T(8,128)(2,1)}, bf16[128,2048]{1,0:T(8,128)(2,1)}, u32[]{:S(2)}, u32[]{:S(2)}) collective-permute-start(bf16[128,2048]{1,0:T(8,128)(2,1)} %collective-permute-done.4.refs_5_.refs_12_), channel_id=1, source_target_pairs={{0,4},{4,0},{8,12},{12,8},{16,20},{20,16},{24,28},{28,24},{32,36},... | collective-permute-start | bytes 1572872 | tf_op jit(solution)/shard_map/ppermute | solution.py:32
  45.7 0.0 copy-start.8
  45.7 1.0 copy-done.8
  46.7 0.8 spread.1
  47.5 0.0 copy-start
  47.6 1.0 copy-done
  48.6 0.0 copy-start.2
  48.6 1.0 copy-done.2
  49.6 0.0 copy-start.4
  49.6 1.0 copy-done.4
  50.7 0.0 copy-start.6
  50.7 1.0 copy-done.6
  51.7 0.0 copy-start.9
  51.7 0.7 copy-done.9
  52.4 0.0 copy-start.1
  52.4 0.0 copy-start.3
  52.4 0.0 copy-start.10
  52.4 3.7 %stats.2.refs_4_ = f32[96,128]{1,0:T(8,128)S(1)} custom-call(s32[1,2]{1,0:T(1,128)S(1)} %copy-done.9, bf16[128,2048]{1,0:T(8,128)(2,1)S(1)} %copy-done, bf16[128,2048]{1,0:T(8,128)(2,1)S(1)} %copy-done.2, bf16[128,2048]{1,0:T(8,128)(2,1)S(1)} %copy-done.4, bf16[128,2048]{1,0:T(8,128)(2,1)S(1)} %collective-permute-done.2.refs_1_.refs_6_, ...), custom_call_target="tpu_custom_call" | custom-call | flops 402653184 | bytes 4194304 | tf_op jit(solution)/shard_map/stats/pallas_call | solution.py:226
  56.1 5.6 %all-to-all-start.1 = ((bf16[4,128,512]{2,1,0:T(8,128)(2,1)}), bf16[4,128,512]{2,1,0:T(8,128)(2,1)S(1)}, u32[]{:S(2)}, u32[]{:S(2)}) async-start(bf16[4,128,512]{2,1,0:T(8,128)(2,1)} %bitcast.4), calls=%async_computation.1 | async-start | bytes 1048576 | tf_op jit(solution)/shard_map/all_to_all | solution.py:322
  61.6 0.0 copy-start.5
  61.7 0.0 copy-start.7
  61.7 0.0 collective-permute-done.3.refs_1_.refs_9_
  61.7 0.0 collective-permute-done.1.refs_0_.refs_8_
  61.7 3.2 %collective-permute-done.7.refs_3_.refs_14_ = bf16[128,2048]{1,0:T(8,128)(2,1)} collective-permute-done((bf16[128,2048]{1,0:T(8,128)(2,1)}, bf16[128,2048]{1,0:T(8,128)(2,1)}, u32[]{:S(2)}, u32[]{:S(2)}) %collective-permute-start.7) | collective-permute-done | bytes 524320 | tf_op jit(solution)/shard_map/ppermute | solution.py:32
  64.9 0.0 collective-permute-done.5.refs_2_.refs_13_
  64.9 0.0 copy-done.1
  64.9 0.0 copy-done.3
  64.9 0.0 copy-done.10
  64.9 3.3 %stats.3 = f32[672,128]{1,0:T(8,128)S(1)} custom-call(s32[1,2]{1,0:T(1,128)S(1)} %copy-done.10, bf16[128,2048]{1,0:T(8,128)(2,1)S(1)} %copy-done.1, bf16[128,2048]{1,0:T(8,128)(2,1)S(1)} %copy-done.3, bf16[128,2048]{1,0:T(8,128)(2,1)} %collective-permute-done.1.refs_0_.refs_8_, bf16[128,2048]{1,0:T(8,128)(2,1)} %collective-permute-done.3.refs_1_.refs_9_, ...), custom_call_target="tpu_custom_call" | custom-call | flops 268435456 | bytes 3145728 | tf_op jit(solution)/shard_map/stats/pallas_call | solution.py:226
  68.2 1.5 %all-to-all-done.1 = bf16[4,128,512]{2,1,0:T(8,128)(2,1)S(1)} async-done(((bf16[4,128,512]{2,1,0:T(8,128)(2,1)}), bf16[4,128,512]{2,1,0:T(8,128)(2,1)S(1)}, u32[]{:S(2)}, u32[]{:S(2)}) %all-to-all-start.1) | async-done | bytes 524320 | tf_op jit(solution)/shard_map/all_to_all | solution.py:322
  69.6 8.9 %all_to_all.24 = f32[4,168,128]{2,1,0:T(8,128)S(1)} all-to-all(f32[4,168,128]{2,1,0:T(8,128)S(1)} %bitcast.13), channel_id=1, replica_groups={{0,4,8,12},{16,20,24,28},{32,36,40,44},{48,52,56,60},{64,68,72,76},{80,..., dimensions={0} | all-to-all | bytes 688128 | tf_op jit(solution)/shard_map/all_to_all | solution.py:327
  78.6 1.9 %collective-permute-start.9 = (f32[672,128]{1,0:T(8,128)S(1)}, f32[672,128]{1,0:T(8,128)S(1)}, u32[]{:S(2)}, u32[]{:S(2)}) collective-permute-start(f32[672,128]{1,0:T(8,128)S(1)} %bitcast.9), channel_id=1, source_target_pairs={{0,16},{4,20},{8,24},{12,28},{16,0},{20,4},{24,8},{28,12},{32,48},... | collective-permute-start | bytes 1032200 | tf_op jit(solution)/shard_map/ppermute | solution.py:32
  80.5 9.0 %collective-permute-start.8 = (f32[672,128]{1,0:T(8,128)S(1)}, f32[672,128]{1,0:T(8,128)S(1)}, u32[]{:S(2)}, u32[]{:S(2)}) collective-permute-start(f32[672,128]{1,0:T(8,128)S(1)} %bitcast.10), channel_id=1, source_target_pairs={{0,496},{4,500},{8,504},{12,508},{16,32},{20,36},{24,40},{28,44},{... | collective-permute-start | bytes 1032200 | tf_op jit(solution)/shard_map/ppermute | solution.py:32
  89.5 0.0 collective-permute-done.9.refs_2_
  89.5 6.0 %collective-permute-done.8.refs_0_ = f32[672,128]{1,0:T(8,128)S(1)} collective-permute-done((f32[672,128]{1,0:T(8,128)S(1)}, f32[672,128]{1,0:T(8,128)S(1)}, u32[]{:S(2)}, u32[]{:S(2)}) %collective-permute-start.8) | collective-permute-done | bytes 344096 | tf_op jit(solution)/shard_map/ppermute | solution.py:32
  95.5 0.0 copy-done.5
  95.5 0.0 copy-done.7
  95.5 5.5 %grads.2 = (bf16[128,1024]{1,0:T(8,128)(2,1)S(1)}, bf16[128,2048]{1,0:T(8,128)(2,1)S(1)}, bf16[128,2048]{1,0:T(8,128)(2,1)}) custom-call(s32[1]{0:T(128)} %bitcast.1.replica_ref, f32[672,128]{1,0:T(8,128)S(1)} %collective-permute-done.8.refs_0_, f32[672,128]{1,0:T(8,128)S(1)} %bitcast.11, f32[672,128]{1,0:T(8,128)S(1)} %collective-permute-done.9.refs_2_, ...), custom_call_target="tpu_custom_call" | custom-call | flops 671088640 | bytes 3145728 | tf_op jit(solution)/shard_map/grads/pallas_call | solution.py:245
  101.0 2.8 %collective-permute-start.13 = (bf16[128,1024]{1,0:T(8,128)(2,1)S(1)}, bf16[128,1024]{1,0:T(8,128)(2,1)S(1)}, u32[]{:S(2)}, u32[]{:S(2)}) collective-permute-start(bf16[128,1024]{1,0:T(8,128)(2,1)S(1)} %get-tuple-element.26.refs_0_), channel_id=1, source_target_pairs={{0,2},{1,3},{2,0},{3,1},{4,6},{5,7},{6,4},{7,5},{8,10},{9,11},{10,... | collective-permute-start | bytes 786440 | tf_op jit(solution)/shard_map/ppermute | solution.py:37
  103.8 5.5 %grads.3 = (bf16[128,1024]{1,0:T(8,128)(2,1)S(1)}, bf16[128,2048]{1,0:T(8,128)(2,1)S(1)}, bf16[128,2048]{1,0:T(8,128)(2,1)}) custom-call(s32[1]{0:T(128)} %bitcast.1.replica_ref, f32[672,128]{1,0:T(8,128)S(1)} %collective-permute-done.8.refs_0_, f32[672,128]{1,0:T(8,128)S(1)} %bitcast.12, ...), custom_call_target="tpu_custom_call", output_to_operand_aliasing={{1}: (16, {}), {2}: (17, {})} | custom-call | flops 671088640 | bytes 3145728 | tf_op jit(solution)/shard_map/grads/pallas_call | solution.py:245
  109.3 4.6 %collective-permute-start.10 = (bf16[128,2048]{1,0:T(8,128)(2,1)S(1)}, bf16[128,2048]{1,0:T(8,128)(2,1)S(1)}, u32[]{:S(2)}, u32[]{:S(2)}) collective-permute-start(bf16[128,2048]{1,0:T(8,128)(2,1)S(1)} %get-tuple-element.25), channel_id=1, source_target_pairs={{0,1},{1,0},{2,3},{3,2},{4,5},{5,4},{6,7},{7,6},{8,9},{9,8},{10,11... | collective-permute-start | bytes 1572872 | tf_op jit(solution)/shard_map/ppermute | solution.py:37
  114.0 3.0 %collective-permute-start.11 = (bf16[128,1024]{1,0:T(8,128)(2,1)S(1)}, bf16[128,1024]{1,0:T(8,128)(2,1)S(1)}, u32[]{:S(2)}, u32[]{:S(2)}) collective-permute-start(bf16[128,1024]{1,0:T(8,128)(2,1)S(1)} %get-tuple-element.24.refs_0_), channel_id=1, source_target_pairs={{0,2},{1,3},{2,0},{3,1},{4,6},{5,7},{6,4},{7,5},{8,10},{9,11},{10,... | collective-permute-start | bytes 786440 | tf_op jit(solution)/shard_map/ppermute | solution.py:37
  117.0 0.0 collective-permute-done.13.refs_2_
  117.0 2.2 %collective-permute-start.14 = (bf16[128,1024]{1,0:T(8,128)(2,1)S(1)}, bf16[128,1024]{1,0:T(8,128)(2,1)S(1)}, u32[]{:S(2)}, u32[]{:S(2)}) collective-permute-start(bf16[128,1024]{1,0:T(8,128)(2,1)S(1)} %collective-permute-done.13.refs_2_), channel_id=1, source_target_pairs={{0,1},{1,0},{2,3},{3,2},{4,5},{5,4},{6,7},{7,6},{8,9},{9,8},{10,11... | collective-permute-start | bytes 786440 | tf_op jit(solution)/shard_map/ppermute | solution.py:37
  119.2 4.6 %collective-permute-done.11.refs_2_ = bf16[128,1024]{1,0:T(8,128)(2,1)S(1)} collective-permute-done((bf16[128,1024]{1,0:T(8,128)(2,1)S(1)}, bf16[128,1024]{1,0:T(8,128)(2,1)S(1)}, u32[]{:S(2)}, u32[]{:S(2)}) %collective-permute-start.11) | collective-permute-done | bytes 262176 | tf_op jit(solution)/shard_map/ppermute | solution.py:37
  123.8 2.7 %collective-permute-start.12 = (bf16[128,1024]{1,0:T(8,128)(2,1)S(1)}, bf16[128,1024]{1,0:T(8,128)(2,1)S(1)}, u32[]{:S(2)}, u32[]{:S(2)}) collective-permute-start(bf16[128,1024]{1,0:T(8,128)(2,1)S(1)} %collective-permute-done.11.refs_2_), channel_id=1, source_target_pairs={{0,1},{1,0},{2,3},{3,2},{4,5},{5,4},{6,7},{7,6},{8,9},{9,8},{10,11... | collective-permute-start | bytes 786440 | tf_op jit(solution)/shard_map/ppermute | solution.py:37
  126.5 0.0 collective-permute-done.14.refs_3_
  126.5 0.0 collective-permute-done.10.refs_1_
  126.5 2.0 %weight.2.refs_4_ = bf16[512,2048]{1,0:T(8,128)(2,1)} custom-call(s32[1]{0:T(128)} %bitcast.mine_ref, bf16[512,512]{1,0:T(8,128)(2,1)S(1)} %bitcast.7, bf16[128,1024]{1,0:T(8,128)(2,1)S(1)} %get-tuple-element.26.refs_0_, bf16[128,2048]{1,0:T(8,128)(2,1)S(1)} %collective-permute-done.10.refs_1_, bf16[128,1024]{1,0:T(8,128)(2,1)S(1)} %collective-permute-done.13.refs_2_, ...), custom_call_target="tpu_custom_call" | custom-call | flops 536870912 | bytes 2097152 | tf_op jit(solution)/shard_map/weight/pallas_call | solution.py:284
  128.5 0.0 collective-permute-done.12.refs_3_
  128.5 2.0 %weight.3 = bf16[512,2048]{1,0:T(8,128)(2,1)} custom-call(s32[1]{0:T(128)} %bitcast.mine_ref, bf16[512,512]{1,0:T(8,128)(2,1)S(1)} %bitcast.8, bf16[128,1024]{1,0:T(8,128)(2,1)S(1)} %get-tuple-element.24.refs_0_, bf16[128,2048]{1,0:T(8,128)(2,1)S(1)} %collective-permute-done.10.refs_1_, ...), custom_call_target="tpu_custom_call", output_to_operand_aliasing={{}: (6, {})} | custom-call | flops 536870912 | bytes 2097152 | tf_op jit(solution)/shard_map/weight/pallas_call | solution.py:284
Async XLA Ops:
  0.6 24.1 %collective-permute-start.2 = (bf16[128,2048]{1,0:T(8,128)(2,1)}, bf16[128,2048]{1,0:T(8,128)(2,1)S(1)}, u32[]{:S(2)}, u32[]{:S(2)}) collective-permute-start(bf16[128,2048]{1,0:T(8,128)(2,1)} %refs_5_.1), channel_id=1, source_target_pairs={{0,4},{4,0},{8,12},{12,8},{16,20},{20,16},{24,28},{28,24},{32,36},... | collective-permute-start | bytes 1572872 | tf_op jit(solution)/shard_map/ppermute | solution.py:32
  4.7 28.2 %collective-permute-start = (bf16[128,2048]{1,0:T(8,128)(2,1)}, bf16[128,2048]{1,0:T(8,128)(2,1)}, u32[]{:S(2)}, u32[]{:S(2)}) collective-permute-start(bf16[128,2048]{1,0:T(8,128)(2,1)} %refs_5_.1), channel_id=1, source_target_pairs={{0,508},{4,8},{8,4},{12,16},{16,12},{20,24},{24,20},{28,32},{32,28... | collective-permute-start | bytes 1572872 | tf_op jit(solution)/shard_map/ppermute | solution.py:32
  19.9 14.9 %collective-permute-start.6 = (bf16[128,2048]{1,0:T(8,128)(2,1)}, bf16[128,2048]{1,0:T(8,128)(2,1)}, u32[]{:S(2)}, u32[]{:S(2)}) collective-permute-start(bf16[128,2048]{1,0:T(8,128)(2,1)} %refs_10_.3), channel_id=1, source_target_pairs={{0,4},{4,0},{8,12},{12,8},{16,20},{20,16},{24,28},{28,24},{32,36},... | collective-permute-start | bytes 1572872 | tf_op jit(solution)/shard_map/ppermute | solution.py:32
  21.8 21.9 %collective-permute-start.4 = (bf16[128,2048]{1,0:T(8,128)(2,1)}, bf16[128,2048]{1,0:T(8,128)(2,1)}, u32[]{:S(2)}, u32[]{:S(2)}) collective-permute-start(bf16[128,2048]{1,0:T(8,128)(2,1)} %refs_10_.3), channel_id=1, source_target_pairs={{0,508},{4,8},{8,4},{12,16},{16,12},{20,24},{24,20},{28,32},{32,28... | collective-permute-start | bytes 1572872 | tf_op jit(solution)/shard_map/ppermute | solution.py:32
  24.8 36.9 %collective-permute-start.3 = (bf16[128,2048]{1,0:T(8,128)(2,1)S(1)}, bf16[128,2048]{1,0:T(8,128)(2,1)}, u32[]{:S(2)}, u32[]{:S(2)}) collective-permute-start(bf16[128,2048]{1,0:T(8,128)(2,1)S(1)} %collective-permute-done.2.refs_1_.refs_6_), channel_id=1, source_target_pairs={{0,508},{4,8},{8,4},{12,16},{16,12},{20,24},{24,20},{28,32},{32,28... | collective-permute-start | bytes 1572872 | tf_op jit(solution)/shard_map/ppermute | solution.py:32
  32.9 28.8 %collective-permute-start.1 = (bf16[128,2048]{1,0:T(8,128)(2,1)}, bf16[128,2048]{1,0:T(8,128)(2,1)}, u32[]{:S(2)}, u32[]{:S(2)}) collective-permute-start(bf16[128,2048]{1,0:T(8,128)(2,1)} %collective-permute-done.refs_2_.refs_7_), channel_id=1, source_target_pairs={{0,4},{4,0},{8,12},{12,8},{16,20},{20,16},{24,28},{28,24},{32,36},... | collective-permute-start | bytes 1572872 | tf_op jit(solution)/shard_map/ppermute | solution.py:32
  34.8 30.1 %collective-permute-start.7 = (bf16[128,2048]{1,0:T(8,128)(2,1)}, bf16[128,2048]{1,0:T(8,128)(2,1)}, u32[]{:S(2)}, u32[]{:S(2)}) collective-permute-start(bf16[128,2048]{1,0:T(8,128)(2,1)} %collective-permute-done.6.refs_4_.refs_11_), channel_id=1, source_target_pairs={{0,508},{4,8},{8,4},{12,16},{16,12},{20,24},{24,20},{28,32},{32,28... | collective-permute-start | bytes 1572872 | tf_op jit(solution)/shard_map/ppermute | solution.py:32
  43.7 21.1 %collective-permute-start.5 = (bf16[128,2048]{1,0:T(8,128)(2,1)}, bf16[128,2048]{1,0:T(8,128)(2,1)}, u32[]{:S(2)}, u32[]{:S(2)}) collective-permute-start(bf16[128,2048]{1,0:T(8,128)(2,1)} %collective-permute-done.4.refs_5_.refs_12_), channel_id=1, source_target_pairs={{0,4},{4,0},{8,12},{12,8},{16,20},{20,16},{24,28},{28,24},{32,36},... | collective-permute-start | bytes 1572872 | tf_op jit(solution)/shard_map/ppermute | solution.py:32
  45.7 1.0 copy-start.8
  47.5 1.0 copy-start
  48.6 1.0 copy-start.2
  49.6 1.0 copy-start.4
  50.7 1.0 copy-start.6
  51.7 0.7 copy-start.9
  52.4 12.5 %copy-start.1 = (bf16[128,2048]{1,0:T(8,128)(2,1)S(1)}, bf16[128,2048]{1,0:T(8,128)(2,1)}, u32[]{:S(2)}) copy-start(bf16[128,2048]{1,0:T(8,128)(2,1)} %refs_3_.5) | copy-start | bytes 1572868
  52.4 12.5 %copy-start.3 = (bf16[128,2048]{1,0:T(8,128)(2,1)S(1)}, bf16[128,2048]{1,0:T(8,128)(2,1)}, u32[]{:S(2)}) copy-start(bf16[128,2048]{1,0:T(8,128)(2,1)} %refs_4_.3) | copy-start | bytes 1572868
  52.4 12.5 %copy-start.10 = (s32[1,2]{1,0:T(1,128)S(1)}, s32[1,2]{1,0:T(1,128)}, u32[]{:S(2)}) copy-start(s32[1,2]{1,0:T(1,128)} %offsets_ref.3) | copy-start | bytes 28
  56.1 13.5 %all-to-all-start.1 = ((bf16[4,128,512]{2,1,0:T(8,128)(2,1)}), bf16[4,128,512]{2,1,0:T(8,128)(2,1)S(1)}, u32[]{:S(2)}, u32[]{:S(2)}) async-start(bf16[4,128,512]{2,1,0:T(8,128)(2,1)} %bitcast.4), calls=%async_computation.1 | async-start | bytes 1048576 | tf_op jit(solution)/shard_map/all_to_all | solution.py:322
  61.6 33.8 %copy-start.5 = (bf16[128,2048]{1,0:T(8,128)(2,1)S(1)}, bf16[128,2048]{1,0:T(8,128)(2,1)}, u32[]{:S(2)}) copy-start(bf16[128,2048]{1,0:T(8,128)(2,1)} %refs_5_.1) | copy-start | bytes 1572868
  61.7 33.8 %copy-start.7 = (bf16[128,2048]{1,0:T(8,128)(2,1)S(1)}, bf16[128,2048]{1,0:T(8,128)(2,1)}, u32[]{:S(2)}) copy-start(bf16[128,2048]{1,0:T(8,128)(2,1)} %refs_10_.3) | copy-start | bytes 1572868
  78.6 10.9 %collective-permute-start.9 = (f32[672,128]{1,0:T(8,128)S(1)}, f32[672,128]{1,0:T(8,128)S(1)}, u32[]{:S(2)}, u32[]{:S(2)}) collective-permute-start(f32[672,128]{1,0:T(8,128)S(1)} %bitcast.9), channel_id=1, source_target_pairs={{0,16},{4,20},{8,24},{12,28},{16,0},{20,4},{24,8},{28,12},{32,48},... | collective-permute-start | bytes 1032200 | tf_op jit(solution)/shard_map/ppermute | solution.py:32
  80.5 15.0 %collective-permute-start.8 = (f32[672,128]{1,0:T(8,128)S(1)}, f32[672,128]{1,0:T(8,128)S(1)}, u32[]{:S(2)}, u32[]{:S(2)}) collective-permute-start(f32[672,128]{1,0:T(8,128)S(1)} %bitcast.10), channel_id=1, source_target_pairs={{0,496},{4,500},{8,504},{12,508},{16,32},{20,36},{24,40},{28,44},{... | collective-permute-start | bytes 1032200 | tf_op jit(solution)/shard_map/ppermute | solution.py:32
  101.0 16.0 %collective-permute-start.13 = (bf16[128,1024]{1,0:T(8,128)(2,1)S(1)}, bf16[128,1024]{1,0:T(8,128)(2,1)S(1)}, u32[]{:S(2)}, u32[]{:S(2)}) collective-permute-start(bf16[128,1024]{1,0:T(8,128)(2,1)S(1)} %get-tuple-element.26.refs_0_), channel_id=1, source_target_pairs={{0,2},{1,3},{2,0},{3,1},{4,6},{5,7},{6,4},{7,5},{8,10},{9,11},{10,... | collective-permute-start | bytes 786440 | tf_op jit(solution)/shard_map/ppermute | solution.py:37
  109.3 17.2 %collective-permute-start.10 = (bf16[128,2048]{1,0:T(8,128)(2,1)S(1)}, bf16[128,2048]{1,0:T(8,128)(2,1)S(1)}, u32[]{:S(2)}, u32[]{:S(2)}) collective-permute-start(bf16[128,2048]{1,0:T(8,128)(2,1)S(1)} %get-tuple-element.25), channel_id=1, source_target_pairs={{0,1},{1,0},{2,3},{3,2},{4,5},{5,4},{6,7},{7,6},{8,9},{9,8},{10,11... | collective-permute-start | bytes 1572872 | tf_op jit(solution)/shard_map/ppermute | solution.py:37
  114.0 9.8 %collective-permute-start.11 = (bf16[128,1024]{1,0:T(8,128)(2,1)S(1)}, bf16[128,1024]{1,0:T(8,128)(2,1)S(1)}, u32[]{:S(2)}, u32[]{:S(2)}) collective-permute-start(bf16[128,1024]{1,0:T(8,128)(2,1)S(1)} %get-tuple-element.24.refs_0_), channel_id=1, source_target_pairs={{0,2},{1,3},{2,0},{3,1},{4,6},{5,7},{6,4},{7,5},{8,10},{9,11},{10,... | collective-permute-start | bytes 786440 | tf_op jit(solution)/shard_map/ppermute | solution.py:37
  117.0 9.5 %collective-permute-start.14 = (bf16[128,1024]{1,0:T(8,128)(2,1)S(1)}, bf16[128,1024]{1,0:T(8,128)(2,1)S(1)}, u32[]{:S(2)}, u32[]{:S(2)}) collective-permute-start(bf16[128,1024]{1,0:T(8,128)(2,1)S(1)} %collective-permute-done.13.refs_2_), channel_id=1, source_target_pairs={{0,1},{1,0},{2,3},{3,2},{4,5},{5,4},{6,7},{7,6},{8,9},{9,8},{10,11... | collective-permute-start | bytes 786440 | tf_op jit(solution)/shard_map/ppermute | solution.py:37
  123.8 4.7 %collective-permute-start.12 = (bf16[128,1024]{1,0:T(8,128)(2,1)S(1)}, bf16[128,1024]{1,0:T(8,128)(2,1)S(1)}, u32[]{:S(2)}, u32[]{:S(2)}) collective-permute-start(bf16[128,1024]{1,0:T(8,128)(2,1)S(1)} %collective-permute-done.11.refs_2_), channel_id=1, source_target_pairs={{0,1},{1,0},{2,3},{3,2},{4,5},{5,4},{6,7},{7,6},{8,9},{9,8},{10,11... | collective-permute-start | bytes 786440 | tf_op jit(solution)/shard_map/ppermute | solution.py:37

commit v9 on v8

--- a/solution.py
+++ b/solution.py
@@ -139,7 +139,10 @@
     count = len(DOCS)
     stat_refs, (keys_ref, values_ref), refs = refs[:3], refs[3:5], refs[5:]
     query_refs, grad_refs = refs[:count], refs[count : 2 * count]
-    key_half, key_out, value_out, stat_ref, value_buffer, sems = refs[-6:]
+    key_half, value_out, stat_ref = refs[-3:]
+    skip = value_out.shape[1] - key_half.shape[1]
+    if skip:
+        value_out[:, :skip] = refs[-4][...]
     half = key_half.shape[1]
     each = half // (STEP * HD)
     steps = keys_ref.shape[1] // (STEP * HD)
@@ -149,14 +152,6 @@
     above = 2 - 2 * (replica // GROUP % 2)
     for place, ref in zip((2 - above, 1, above), stat_refs):
         stat_ref[pl.ds(pl.multiple_of(place * size, TILE), size), :] = ref[...]
-
-    def writes(at):
-        cols = pl.ds(pl.multiple_of((at + first) * STEP * HD, HD), STEP * HD)
-        part = pl.ds(pl.multiple_of(at * STEP * HD, HD), STEP * HD)
-        return [
-            pltpu.make_async_copy(source.at[:, part], target.at[:, cols], sems.at[kind, at])
-            for kind, (source, target) in enumerate(((key_half, key_out), (value_buffer, value_out)))
-        ]
 
     def group(at, carry):
         step = at + first
@@ -173,15 +168,11 @@
             key_total = dot_nn(score_grad.astype(jnp.bfloat16), query_rows)
             value_total = dot_nn(probs.astype(jnp.bfloat16), grad_rows)
             key_half[:, out_cols] = key_total.astype(jnp.bfloat16)
-            value_buffer[:, out_cols] = value_total.astype(jnp.bfloat16)
-        for copy in writes(at):
-            copy.start()
+            value_cols = pl.ds(pl.multiple_of(skip + (at * STEP + head) * HD, HD), HD)
+            value_out[:, value_cols] = value_total.astype(jnp.bfloat16)
         return carry
 
     lax.fori_loop(0, each, group, 0)
-    for at in range(each):
-        for copy in writes(at):
-            copy.wait()
 
 
 def spread_kernel(input_ref, out_ref, sems):
@@ -199,22 +190,31 @@
         copy.wait()
 
 
-def weight_kernel(low, mine_ref, inputs_ref, *refs):
-    pieces, out_ref, turned_ref, grads_ref = refs[:4], *refs[-3:]
+def weight_kernel(saves, mine_ref, inputs_ref, *refs):
+    pieces, (turned_ref, grads_ref, sem) = refs[:4], refs[-3:]
+    out_ref = refs[-5] if saves else refs[-4]
     wide = out_ref.shape[1]
     rows = pieces[0].shape[0]
     step = pl.program_id(0)
+    copy = pltpu.make_async_copy(refs[4], refs[-4], sem) if saves else None
 
     @pl.when(step == 0)
     def _():
+        if saves:
+            copy.start()
         turned_ref[...] = inputs_ref[...].T
 
-    here = pl.ds(pl.multiple_of(step * wide, HD), wide)
-    whole = pl.ds(pl.multiple_of((low + step) * wide, HD), wide)
-    for k, (ref, cols) in enumerate(zip(pieces, (here, whole, here, here))):
+    cols = pl.ds(pl.multiple_of(step * wide, HD), wide)
+    for k, ref in enumerate(pieces):
         place = pl.multiple_of((mine_ref[0] ^ k) * rows, rows)
         grads_ref[pl.ds(place, rows), :] = ref[:, cols]
     out_ref[...] = dot_nn(turned_ref[...], grads_ref[...]).astype(jnp.bfloat16)
+
+    if saves:
+
+        @pl.when(step == pl.num_programs(0) - 1)
+        def _():
+            copy.wait()
 
 
 def call_stats(low, high, partner_offsets, arrays, before):
@@ -236,31 +236,24 @@
     )(partner_offsets, *map(in_vmem, arrays), *map(in_vmem, before))
 
 
-def call_grads(first, each, replica, stat_parts, arrays, held):
+def call_grads(first, each, replica, stat_parts, arrays, before):
     rows, features = arrays[0].shape
     pairs = rows * rows * len(DOCS) * each * STEP
     half = (rows, each * STEP * HD)
-    whole = jax.ShapeDtypeStruct((rows, features), jnp.bfloat16)
-    count = 1 + len(stat_parts) + len(arrays)
+    whole = (rows, (len(before) + 1) * half[1])
+    inputs = [*stat_parts, *arrays, *before]
     return pl.pallas_call(
         functools.partial(grads_kernel, first),
-        in_specs=[pl.BlockSpec(memory_space=pltpu.SMEM)]
-        + [VMEM] * (len(stat_parts) + len(arrays))
-        + [ANY] * len(held),
-        out_specs=[VMEM, ANY, ANY],
-        out_shape=[pltpu.VMEM(half, jnp.bfloat16), whole, whole],
-        scratch_shapes=[
-            pltpu.VMEM((3 * stat_parts[0].shape[0], rows), jnp.float32),
-            pltpu.VMEM(half, jnp.bfloat16),
-            pltpu.SemaphoreType.DMA((2, each)),
-        ],
-        input_output_aliases={count + at: 1 + at for at in range(len(held))},
+        in_specs=[pl.BlockSpec(memory_space=pltpu.SMEM)] + [VMEM] * len(inputs),
+        out_specs=[VMEM] * 2,
+        out_shape=[pltpu.VMEM(half, jnp.bfloat16), pltpu.VMEM(whole, jnp.bfloat16)],
+        scratch_shapes=[pltpu.VMEM((3 * stat_parts[0].shape[0], rows), jnp.float32)],
         compiler_params=PARAMS,
         cost_estimate=pl.CostEstimate(
             flops=8 * pairs * HD, bytes_accessed=2 * len(arrays) * half[0] * half[1], transcendentals=pairs
         ),
         name="grads",
-    )(replica, *map(in_vmem, [*stat_parts, *arrays]), *held)
+    )(replica, *map(in_vmem, inputs))
 
 
 def call_spread(layer_input, places):
@@ -277,24 +270,30 @@
     )(layer_input)
 
 
-def call_weight(half, mine, columns, pieces, held):
-    features, part = pieces[1].shape[1], pieces[0].shape[1]
+def call_weight(half, features, mine, columns, pieces, held, saved):
+    part = pieces[0].shape[1]
     blocks = part // WIDE
     tokens, width = columns.shape
+    inputs = [columns, *pieces, *saved]
     return pl.pallas_call(
-        functools.partial(weight_kernel, half * blocks),
+        functools.partial(weight_kernel, bool(saved)),
         grid=(blocks,),
-        in_specs=[pl.BlockSpec(memory_space=pltpu.SMEM)] + [VMEM] * (1 + len(pieces)) + [ANY] * len(held),
-        out_specs=pl.BlockSpec((width, WIDE), lambda step: (0, step + half * blocks)),
-        out_shape=jax.ShapeDtypeStruct((width, features), jnp.bfloat16),
-        scratch_shapes=[pltpu.VMEM((width, tokens), jnp.bfloat16), pltpu.VMEM((tokens, WIDE), jnp.bfloat16)],
-        input_output_aliases={2 + len(pieces): 0} if held else {},
+        in_specs=[pl.BlockSpec(memory_space=pltpu.SMEM)] + [VMEM] * len(inputs) + [ANY] * len(held),
+        out_specs=[pl.BlockSpec((width, WIDE), lambda step: (0, step + half * blocks))] + [ANY] * len(saved),
+        out_shape=[jax.ShapeDtypeStruct((width, features), jnp.bfloat16)]
+        + [jax.ShapeDtypeStruct(array.shape, array.dtype) for array in saved],
+        scratch_shapes=[
+            pltpu.VMEM((width, tokens), jnp.bfloat16),
+            pltpu.VMEM((tokens, WIDE), jnp.bfloat16),
+            pltpu.SemaphoreType.DMA,
+        ],
+        input_output_aliases={1 + len(inputs): 0} if held else {},
         compiler_params=PARAMS,
         cost_estimate=pl.CostEstimate(
             flops=2 * width * tokens * part, bytes_accessed=2 * part * (tokens + width), transcendentals=0
         ),
         name="weight",
-    )(mine, *map(in_vmem, [columns, *pieces]), *held)
+    )(mine, *map(in_vmem, inputs), *held)
 
 
 def local(layer_input, queries, key_vectors, value_vectors, output_grad, partner_offsets):
@@ -330,19 +329,21 @@
     stat_parts = [after_odd, here, traded(here, "dp", GROUP, False)]
 
     each = steps // HALVES
-    halves, held = [], []
+    arrays = own + query_docs + grad_docs
+    halves, values = [], []
     for half in range(HALVES):
-        key_half, *held = call_grads(half * each, each, replica, stat_parts, own + query_docs + grad_docs, held)
+        key_half, value_part = call_grads(half * each, each, replica, stat_parts, arrays, values)
         halves.append(key_half)
-    key_grad, value_grad = held
-
-    beside = swapped(key_grad, "fsdp", 1)
-    held = []
+        values = [value_part]
+
     for half, key_half in enumerate(halves):
         across = swapped(key_half, "fsdp", 2)
-        pieces = [key_half, beside, across, swapped(across, "fsdp", 1)]
-        held = [call_weight(half, mine, columns, pieces, held)]
-    return held[0][None], value_grad
+        pieces = [key_half, swapped(key_half, "fsdp", 1), across, swapped(across, "fsdp", 1)]
+        if half == 0:
+            weight, value_grad = call_weight(half, features, mine, columns, pieces, [], values)
+        else:
+            (weight,) = call_weight(half, features, mine, columns, pieces, [weight], [])
+    return weight[None], value_grad
 
 
 def solution(mesh):

time: 131 us -> 127 us (0.969)
  waiting for transfers between devices: 15.2 us -> 10.7 us
  starting transfers between devices: 76.8 us -> 78.4 us
  Pallas kernels: 22.8 us -> 21.4 us
    ppermute x5 -> x6, waiting for transfers between devices: 4.56 us -> 0.02 us  [swapped(): return lax.ppermute(value, axis, pairs)]
    ppermute x5 -> x6, starting transfers between devices: 15.4 us -> 17 us  [swapped(): return lax.ppermute(value, axis, pairs)]
    pallas_call x2, Pallas kernels: 11 us -> 9.58 us  [call_grads(): pl.pallas_call(functools.partial(grads_kernel, first), in_specs=[pl.Block...]
  transfers between devices with their start and end apart: 16 -> 17, of which waited for: 4 -> 3; matrix products, arithmetic and copies ran while one was open for 0% -> 0% of each run, Pallas kernels for 12% -> 12%
where the time goes in v9:
time: 127 us; the launch traced here: 126 us
  starting transfers between devices  78.4 us (62%)
  Pallas kernels  21.4 us (17%)
  waiting for transfers between devices  10.7 us (8%)
  blocking collectives  8.93 us (7%)
  local copies, waits for them, and re-layouts  5.87 us (5%)
    ppermute x10, starting transfers between devices, traded(): return lax.ppermute(value, axis, pairs)  55.8 us
    ppermute x6, starting transfers between devices, swapped(): return lax.ppermute(value, axis, pairs)  17 us
    pallas_call x2, Pallas kernels, call_grads(): pl.pallas_call(functools.partial(grads_kernel, first), in_specs=[pl.Block...  9.58 us
    ppermute x10, waiting for transfers between devices, traded(): return lax.ppermute(value, axis, pairs)  9.19 us
    all_to_all x1, blocking collectives, local(): lax.all_to_all(stats, 'dp', 0, 0, axis_index_groups=groups, tiled=True)  8.93 us
    pallas_call x2, Pallas kernels, call_stats(): pl.pallas_call(functools.partial(stats_kernel, low), in_specs=[pl.BlockSp...  7 us
    unnamed x22, local copies, waits for them, and re-layouts  5.87 us
    all_to_all x1, starting transfers between devices, local(): columns = lax.all_to_all(columns, 'fsdp', 0, 0, tiled=True)  5.55 us
  transfers between devices with their start and end apart: 17, of which 3 were waited for; matrix products, arithmetic and copies ran while one was open for 0% of the time, Pallas kernels for 12%

profile of v9, /device:TPU:1, one launch (start us, length us, event | category | flops | bytes accessed | tf_op | source)
XLA Modules:
  0.0 126.2 jit_solution(2054888394335922352)
XLA Ops:
  0.6 4.0 %collective-permute-start.2 = (bf16[128,2048]{1,0:T(8,128)(2,1)}, bf16[128,2048]{1,0:T(8,128)(2,1)S(1)}, u32[]{:S(2)}, u32[]{:S(2)}) collective-permute-start(bf16[128,2048]{1,0:T(8,128)(2,1)} %refs_5_.1), channel_id=1, source_target_pairs={{0,4},{4,0},{8,12},{12,8},{16,20},{20,16},{24,28},{28,24},{32,36},... | collective-permute-start | bytes 1572872 | tf_op jit(solution)/shard_map/ppermute | solution.py:32
  4.7 15.2 %collective-permute-start = (bf16[128,2048]{1,0:T(8,128)(2,1)}, bf16[128,2048]{1,0:T(8,128)(2,1)}, u32[]{:S(2)}, u32[]{:S(2)}) collective-permute-start(bf16[128,2048]{1,0:T(8,128)(2,1)} %refs_5_.1), channel_id=1, source_target_pairs={{0,508},{4,8},{8,4},{12,16},{16,12},{20,24},{24,20},{28,32},{32,28... | collective-permute-start | bytes 1572872 | tf_op jit(solution)/shard_map/ppermute | solution.py:32
  19.9 1.9 %collective-permute-start.6 = (bf16[128,2048]{1,0:T(8,128)(2,1)}, bf16[128,2048]{1,0:T(8,128)(2,1)}, u32[]{:S(2)}, u32[]{:S(2)}) collective-permute-start(bf16[128,2048]{1,0:T(8,128)(2,1)} %refs_10_.3), channel_id=1, source_target_pairs={{0,4},{4,0},{8,12},{12,8},{16,20},{20,16},{24,28},{28,24},{32,36},... | collective-permute-start | bytes 1572872 | tf_op jit(solution)/shard_map/ppermute | solution.py:32
  21.8 2.9 %collective-permute-start.4 = (bf16[128,2048]{1,0:T(8,128)(2,1)}, bf16[128,2048]{1,0:T(8,128)(2,1)}, u32[]{:S(2)}, u32[]{:S(2)}) collective-permute-start(bf16[128,2048]{1,0:T(8,128)(2,1)} %refs_10_.3), channel_id=1, source_target_pairs={{0,508},{4,8},{8,4},{12,16},{16,12},{20,24},{24,20},{28,32},{32,28... | collective-permute-start | bytes 1572872 | tf_op jit(solution)/shard_map/ppermute | solution.py:32
  24.7 0.0 collective-permute-done.2.refs_1_.refs_6_
  24.8 8.1 %collective-permute-start.3 = (bf16[128,2048]{1,0:T(8,128)(2,1)S(1)}, bf16[128,2048]{1,0:T(8,128)(2,1)}, u32[]{:S(2)}, u32[]{:S(2)}) collective-permute-start(bf16[128,2048]{1,0:T(8,128)(2,1)S(1)} %collective-permute-done.2.refs_1_.refs_6_), channel_id=1, source_target_pairs={{0,508},{4,8},{8,4},{12,16},{16,12},{20,24},{24,20},{28,32},{32,28... | collective-permute-start | bytes 1572872 | tf_op jit(solution)/shard_map/ppermute | solution.py:32
  32.9 0.0 collective-permute-done.refs_2_.refs_7_
  32.9 1.9 %collective-permute-start.1 = (bf16[128,2048]{1,0:T(8,128)(2,1)}, bf16[128,2048]{1,0:T(8,128)(2,1)}, u32[]{:S(2)}, u32[]{:S(2)}) collective-permute-start(bf16[128,2048]{1,0:T(8,128)(2,1)} %collective-permute-done.refs_2_.refs_7_), channel_id=1, source_target_pairs={{0,4},{4,0},{8,12},{12,8},{16,20},{20,16},{24,28},{28,24},{32,36},... | collective-permute-start | bytes 1572872 | tf_op jit(solution)/shard_map/ppermute | solution.py:32
  34.8 0.0 collective-permute-done.6.refs_4_.refs_11_
  34.8 8.9 %collective-permute-start.7 = (bf16[128,2048]{1,0:T(8,128)(2,1)}, bf16[128,2048]{1,0:T(8,128)(2,1)}, u32[]{:S(2)}, u32[]{:S(2)}) collective-permute-start(bf16[128,2048]{1,0:T(8,128)(2,1)} %collective-permute-done.6.refs_4_.refs_11_), channel_id=1, source_target_pairs={{0,508},{4,8},{8,4},{12,16},{16,12},{20,24},{24,20},{28,32},{32,28... | collective-permute-start | bytes 1572872 | tf_op jit(solution)/shard_map/ppermute | solution.py:32
  43.7 0.0 collective-permute-done.4.refs_5_.refs_12_
  43.7 1.9 %collective-permute-start.5 = (bf16[128,2048]{1,0:T(8,128)(2,1)}, bf16[128,2048]{1,0:T(8,128)(2,1)}, u32[]{:S(2)}, u32[]{:S(2)}) collective-permute-start(bf16[128,2048]{1,0:T(8,128)(2,1)} %collective-permute-done.4.refs_5_.refs_12_), channel_id=1, source_target_pairs={{0,4},{4,0},{8,12},{12,8},{16,20},{20,16},{24,28},{28,24},{32,36},... | collective-permute-start | bytes 1572872 | tf_op jit(solution)/shard_map/ppermute | solution.py:32
  45.7 0.0 copy-start.8
  45.7 1.0 copy-done.8
  46.7 0.8 spread.1
  47.5 0.0 copy-start
  47.6 1.0 copy-done
  48.6 0.0 copy-start.2
  48.6 1.0 copy-done.2
  49.6 0.0 copy-start.4
  49.6 1.0 copy-done.4
  50.7 0.0 copy-start.6
  50.7 1.0 copy-done.6
  51.7 0.0 copy-start.9
  51.7 0.7 copy-done.9
  52.4 0.0 copy-start.1
  52.4 0.0 copy-start.3
  52.4 0.0 copy-start.10
  52.4 3.7 %stats.2.refs_4_ = f32[96,128]{1,0:T(8,128)S(1)} custom-call(s32[1,2]{1,0:T(1,128)S(1)} %copy-done.9, bf16[128,2048]{1,0:T(8,128)(2,1)S(1)} %copy-done, bf16[128,2048]{1,0:T(8,128)(2,1)S(1)} %copy-done.2, bf16[128,2048]{1,0:T(8,128)(2,1)S(1)} %copy-done.4, bf16[128,2048]{1,0:T(8,128)(2,1)S(1)} %collective-permute-done.2.refs_1_.refs_6_, ...), custom_call_target="tpu_custom_call" | custom-call | flops 402653184 | bytes 4194304 | tf_op jit(solution)/shard_map/stats/pallas_call | solution.py:226
  56.1 5.6 %all-to-all-start.1 = ((bf16[4,128,512]{2,1,0:T(8,128)(2,1)}), bf16[4,128,512]{2,1,0:T(8,128)(2,1)S(1)}, u32[]{:S(2)}, u32[]{:S(2)}) async-start(bf16[4,128,512]{2,1,0:T(8,128)(2,1)} %bitcast.4), calls=%async_computation.1 | async-start | bytes 1048576 | tf_op jit(solution)/shard_map/all_to_all | solution.py:321
  61.6 0.0 copy-start.5
  61.7 0.0 copy-start.7
  61.7 0.0 collective-permute-done.3.refs_1_.refs_9_
  61.7 0.0 collective-permute-done.1.refs_0_.refs_8_
  61.7 3.2 %collective-permute-done.7.refs_3_.refs_14_ = bf16[128,2048]{1,0:T(8,128)(2,1)} collective-permute-done((bf16[128,2048]{1,0:T(8,128)(2,1)}, bf16[128,2048]{1,0:T(8,128)(2,1)}, u32[]{:S(2)}, u32[]{:S(2)}) %collective-permute-start.7) | collective-permute-done | bytes 524320 | tf_op jit(solution)/shard_map/ppermute | solution.py:32
  64.9 0.0 collective-permute-done.5.refs_2_.refs_13_
  64.9 0.0 copy-done.1
  64.9 0.0 copy-done.3
  64.9 0.0 copy-done.10
  64.9 3.3 %stats.3 = f32[672,128]{1,0:T(8,128)S(1)} custom-call(s32[1,2]{1,0:T(1,128)S(1)} %copy-done.10, bf16[128,2048]{1,0:T(8,128)(2,1)S(1)} %copy-done.1, bf16[128,2048]{1,0:T(8,128)(2,1)S(1)} %copy-done.3, bf16[128,2048]{1,0:T(8,128)(2,1)} %collective-permute-done.1.refs_0_.refs_8_, bf16[128,2048]{1,0:T(8,128)(2,1)} %collective-permute-done.3.refs_1_.refs_9_, ...), custom_call_target="tpu_custom_call" | custom-call | flops 268435456 | bytes 3145728 | tf_op jit(solution)/shard_map/stats/pallas_call | solution.py:226
  68.2 1.5 %all-to-all-done.1 = bf16[4,128,512]{2,1,0:T(8,128)(2,1)S(1)} async-done(((bf16[4,128,512]{2,1,0:T(8,128)(2,1)}), bf16[4,128,512]{2,1,0:T(8,128)(2,1)S(1)}, u32[]{:S(2)}, u32[]{:S(2)}) %all-to-all-start.1) | async-done | bytes 524320 | tf_op jit(solution)/shard_map/all_to_all | solution.py:321
  69.6 8.9 %all_to_all.24 = f32[4,168,128]{2,1,0:T(8,128)S(1)} all-to-all(f32[4,168,128]{2,1,0:T(8,128)S(1)} %bitcast.13), channel_id=1, replica_groups={{0,4,8,12},{16,20,24,28},{32,36,40,44},{48,52,56,60},{64,68,72,76},{80,..., dimensions={0} | all-to-all | bytes 688128 | tf_op jit(solution)/shard_map/all_to_all | solution.py:326
  78.6 1.9 %collective-permute-start.9 = (f32[672,128]{1,0:T(8,128)S(1)}, f32[672,128]{1,0:T(8,128)S(1)}, u32[]{:S(2)}, u32[]{:S(2)}) collective-permute-start(f32[672,128]{1,0:T(8,128)S(1)} %bitcast.9), channel_id=1, source_target_pairs={{0,16},{4,20},{8,24},{12,28},{16,0},{20,4},{24,8},{28,12},{32,48},... | collective-permute-start | bytes 1032200 | tf_op jit(solution)/shard_map/ppermute | solution.py:32
  80.5 9.0 %collective-permute-start.8 = (f32[672,128]{1,0:T(8,128)S(1)}, f32[672,128]{1,0:T(8,128)S(1)}, u32[]{:S(2)}, u32[]{:S(2)}) collective-permute-start(f32[672,128]{1,0:T(8,128)S(1)} %bitcast.10), channel_id=1, source_target_pairs={{0,496},{4,500},{8,504},{12,508},{16,32},{20,36},{24,40},{28,44},{... | collective-permute-start | bytes 1032200 | tf_op jit(solution)/shard_map/ppermute | solution.py:32
  89.5 0.0 collective-permute-done.9.refs_2_
  89.5 6.0 %collective-permute-done.8.refs_0_ = f32[672,128]{1,0:T(8,128)S(1)} collective-permute-done((f32[672,128]{1,0:T(8,128)S(1)}, f32[672,128]{1,0:T(8,128)S(1)}, u32[]{:S(2)}, u32[]{:S(2)}) %collective-permute-start.8) | collective-permute-done | bytes 344096 | tf_op jit(solution)/shard_map/ppermute | solution.py:32
  95.5 0.0 copy-done.5
  95.5 0.0 copy-done.7
  95.5 4.8 %grads.2 = (bf16[128,1024]{1,0:T(8,128)(2,1)S(1)}, bf16[128,1024]{1,0:T(8,128)(2,1)S(1)}) custom-call(s32[1]{0:T(128)} %bitcast.1.replica_ref, f32[672,128]{1,0:T(8,128)S(1)} %collective-permute-done.8.refs_0_, f32[672,128]{1,0:T(8,128)S(1)} %bitcast.11, f32[672,128]{1,0:T(8,128)S(1)} %collective-permute-done.9.refs_2_, bf16[128,2048]{1,0:T(8,128)(2,1)S(1)} %copy-done.1, ...), custom_call_target="tpu_custom_call" | custom-call | flops 671088640 | bytes 3145728 | tf_op jit(solution)/shard_map/grads/pallas_call | solution.py:245
  100.3 2.8 %collective-permute-start.14 = (bf16[128,1024]{1,0:T(8,128)(2,1)S(1)}, bf16[128,1024]{1,0:T(8,128)(2,1)S(1)}, u32[]{:S(2)}, u32[]{:S(2)}) collective-permute-start(bf16[128,1024]{1,0:T(8,128)(2,1)S(1)} %get-tuple-element.24.refs_0_), channel_id=1, source_target_pairs={{0,2},{1,3},{2,0},{3,1},{4,6},{5,7},{6,4},{7,5},{8,10},{9,11},{10,... | collective-permute-start | bytes 786440 | tf_op jit(solution)/shard_map/ppermute | solution.py:37
  103.1 4.8 %grads.3 = (bf16[128,1024]{1,0:T(8,128)(2,1)S(1)}, bf16[128,2048]{1,0:T(8,128)(2,1)S(1)}) custom-call(s32[1]{0:T(128)} %bitcast.1.replica_ref, f32[672,128]{1,0:T(8,128)S(1)} %collective-permute-done.8.refs_0_, f32[672,128]{1,0:T(8,128)S(1)} %bitcast.12, f32[672,128]{1,0:T(8,128)S(1)} %collective-permute-done.9.refs_2_, bf16[128,2048]{1,0:T(8,128)(2,1)S(1)} %copy-done.1, ...), custom_call_target="tpu_custom_call" | custom-call | flops 671088640 | bytes 3145728 | tf_op jit(solution)/shard_map/grads/pallas_call | solution.py:245
  107.9 2.5 %collective-permute-start.11 = (bf16[128,1024]{1,0:T(8,128)(2,1)S(1)}, bf16[128,1024]{1,0:T(8,128)(2,1)S(1)}, u32[]{:S(2)}, u32[]{:S(2)}) collective-permute-start(bf16[128,1024]{1,0:T(8,128)(2,1)S(1)} %get-tuple-element.23.refs_0_), channel_id=1, source_target_pairs={{0,2},{1,3},{2,0},{3,1},{4,6},{5,7},{6,4},{7,5},{8,10},{9,11},{10,... | collective-permute-start | bytes 786440 | tf_op jit(solution)/shard_map/ppermute | solution.py:37
  110.4 5.5 %collective-permute-start.13 = (bf16[128,1024]{1,0:T(8,128)(2,1)S(1)}, bf16[128,1024]{1,0:T(8,128)(2,1)S(1)}, u32[]{:S(2)}, u32[]{:S(2)}) collective-permute-start(bf16[128,1024]{1,0:T(8,128)(2,1)S(1)} %get-tuple-element.24.refs_0_), channel_id=1, source_target_pairs={{0,1},{1,0},{2,3},{3,2},{4,5},{5,4},{6,7},{7,6},{8,9},{9,8},{10,11... | collective-permute-start | bytes 786440 | tf_op jit(solution)/shard_map/ppermute | solution.py:37
  115.9 0.0 collective-permute-done.14.refs_2_
  115.9 1.9 %collective-permute-start.15 = (bf16[128,1024]{1,0:T(8,128)(2,1)S(1)}, bf16[128,1024]{1,0:T(8,128)(2,1)S(1)}, u32[]{:S(2)}, u32[]{:S(2)}) collective-permute-start(bf16[128,1024]{1,0:T(8,128)(2,1)S(1)} %collective-permute-done.14.refs_2_), channel_id=1, source_target_pairs={{0,1},{1,0},{2,3},{3,2},{4,5},{5,4},{6,7},{7,6},{8,9},{9,8},{10,11... | collective-permute-start | bytes 786440 | tf_op jit(solution)/shard_map/ppermute | solution.py:37
  117.8 2.4 %collective-permute-start.10 = (bf16[128,1024]{1,0:T(8,128)(2,1)S(1)}, bf16[128,1024]{1,0:T(8,128)(2,1)S(1)}, u32[]{:S(2)}, u32[]{:S(2)}) collective-permute-start(bf16[128,1024]{1,0:T(8,128)(2,1)S(1)} %get-tuple-element.23.refs_0_), channel_id=1, source_target_pairs={{0,1},{1,0},{2,3},{3,2},{4,5},{5,4},{6,7},{7,6},{8,9},{9,8},{10,11... | collective-permute-start | bytes 786440 | tf_op jit(solution)/shard_map/ppermute | solution.py:37
  120.2 0.0 collective-permute-done.11.refs_2_
  120.2 1.9 %collective-permute-start.12 = (bf16[128,1024]{1,0:T(8,128)(2,1)S(1)}, bf16[128,1024]{1,0:T(8,128)(2,1)S(1)}, u32[]{:S(2)}, u32[]{:S(2)}) collective-permute-start(bf16[128,1024]{1,0:T(8,128)(2,1)S(1)} %collective-permute-done.11.refs_2_), channel_id=1, source_target_pairs={{0,1},{1,0},{2,3},{3,2},{4,5},{5,4},{6,7},{7,6},{8,9},{9,8},{10,11... | collective-permute-start | bytes 786440 | tf_op jit(solution)/shard_map/ppermute | solution.py:37
  122.2 0.0 collective-permute-done.13.refs_1_
  122.2 0.0 collective-permute-done.15.refs_3_
  122.2 2.0 %weight.2 = (bf16[512,2048]{1,0:T(8,128)(2,1)}, bf16[128,2048]{1,0:T(8,128)(2,1)}) custom-call(s32[1]{0:T(128)} %bitcast.mine_ref, bf16[512,512]{1,0:T(8,128)(2,1)S(1)} %bitcast.7, bf16[128,1024]{1,0:T(8,128)(2,1)S(1)} %get-tuple-element.24.refs_0_, bf16[128,1024]{1,0:T(8,128)(2,1)S(1)} %collective-permute-done.13.refs_1_, ...), custom_call_target="tpu_custom_call" | custom-call | flops 536870912 | bytes 2097152 | tf_op jit(solution)/shard_map/weight/pallas_call | solution.py:278
  124.2 0.0 collective-permute-done.10.refs_1_
  124.2 0.0 collective-permute-done.12.refs_3_
  124.2 2.0 %weight.3 = bf16[512,2048]{1,0:T(8,128)(2,1)} custom-call(s32[1]{0:T(128)} %bitcast.mine_ref, bf16[512,512]{1,0:T(8,128)(2,1)S(1)} %bitcast.8, bf16[128,1024]{1,0:T(8,128)(2,1)S(1)} %get-tuple-element.23.refs_0_, bf16[128,1024]{1,0:T(8,128)(2,1)S(1)} %collective-permute-done.10.refs_1_, ...), custom_call_target="tpu_custom_call", output_to_operand_aliasing={{}: (6, {})} | custom-call | flops 536870912 | bytes 2097152 | tf_op jit(solution)/shard_map/weight/pallas_call | solution.py:278
Async XLA Ops:
  0.6 24.1 %collective-permute-start.2 = (bf16[128,2048]{1,0:T(8,128)(2,1)}, bf16[128,2048]{1,0:T(8,128)(2,1)S(1)}, u32[]{:S(2)}, u32[]{:S(2)}) collective-permute-start(bf16[128,2048]{1,0:T(8,128)(2,1)} %refs_5_.1), channel_id=1, source_target_pairs={{0,4},{4,0},{8,12},{12,8},{16,20},{20,16},{24,28},{28,24},{32,36},... | collective-permute-start | bytes 1572872 | tf_op jit(solution)/shard_map/ppermute | solution.py:32
  4.7 28.2 %collective-permute-start = (bf16[128,2048]{1,0:T(8,128)(2,1)}, bf16[128,2048]{1,0:T(8,128)(2,1)}, u32[]{:S(2)}, u32[]{:S(2)}) collective-permute-start(bf16[128,2048]{1,0:T(8,128)(2,1)} %refs_5_.1), channel_id=1, source_target_pairs={{0,508},{4,8},{8,4},{12,16},{16,12},{20,24},{24,20},{28,32},{32,28... | collective-permute-start | bytes 1572872 | tf_op jit(solution)/shard_map/ppermute | solution.py:32
  19.9 14.9 %collective-permute-start.6 = (bf16[128,2048]{1,0:T(8,128)(2,1)}, bf16[128,2048]{1,0:T(8,128)(2,1)}, u32[]{:S(2)}, u32[]{:S(2)}) collective-permute-start(bf16[128,2048]{1,0:T(8,128)(2,1)} %refs_10_.3), channel_id=1, source_target_pairs={{0,4},{4,0},{8,12},{12,8},{16,20},{20,16},{24,28},{28,24},{32,36},... | collective-permute-start | bytes 1572872 | tf_op jit(solution)/shard_map/ppermute | solution.py:32
  21.8 21.9 %collective-permute-start.4 = (bf16[128,2048]{1,0:T(8,128)(2,1)}, bf16[128,2048]{1,0:T(8,128)(2,1)}, u32[]{:S(2)}, u32[]{:S(2)}) collective-permute-start(bf16[128,2048]{1,0:T(8,128)(2,1)} %refs_10_.3), channel_id=1, source_target_pairs={{0,508},{4,8},{8,4},{12,16},{16,12},{20,24},{24,20},{28,32},{32,28... | collective-permute-start | bytes 1572872 | tf_op jit(solution)/shard_map/ppermute | solution.py:32
  24.8 36.9 %collective-permute-start.3 = (bf16[128,2048]{1,0:T(8,128)(2,1)S(1)}, bf16[128,2048]{1,0:T(8,128)(2,1)}, u32[]{:S(2)}, u32[]{:S(2)}) collective-permute-start(bf16[128,2048]{1,0:T(8,128)(2,1)S(1)} %collective-permute-done.2.refs_1_.refs_6_), channel_id=1, source_target_pairs={{0,508},{4,8},{8,4},{12,16},{16,12},{20,24},{24,20},{28,32},{32,28... | collective-permute-start | bytes 1572872 | tf_op jit(solution)/shard_map/ppermute | solution.py:32
  32.9 28.8 %collective-permute-start.1 = (bf16[128,2048]{1,0:T(8,128)(2,1)}, bf16[128,2048]{1,0:T(8,128)(2,1)}, u32[]{:S(2)}, u32[]{:S(2)}) collective-permute-start(bf16[128,2048]{1,0:T(8,128)(2,1)} %collective-permute-done.refs_2_.refs_7_), channel_id=1, source_target_pairs={{0,4},{4,0},{8,12},{12,8},{16,20},{20,16},{24,28},{28,24},{32,36},... | collective-permute-start | bytes 1572872 | tf_op jit(solution)/shard_map/ppermute | solution.py:32
  34.8 30.1 %collective-permute-start.7 = (bf16[128,2048]{1,0:T(8,128)(2,1)}, bf16[128,2048]{1,0:T(8,128)(2,1)}, u32[]{:S(2)}, u32[]{:S(2)}) collective-permute-start(bf16[128,2048]{1,0:T(8,128)(2,1)} %collective-permute-done.6.refs_4_.refs_11_), channel_id=1, source_target_pairs={{0,508},{4,8},{8,4},{12,16},{16,12},{20,24},{24,20},{28,32},{32,28... | collective-permute-start | bytes 1572872 | tf_op jit(solution)/shard_map/ppermute | solution.py:32
  43.7 21.1 %collective-permute-start.5 = (bf16[128,2048]{1,0:T(8,128)(2,1)}, bf16[128,2048]{1,0:T(8,128)(2,1)}, u32[]{:S(2)}, u32[]{:S(2)}) collective-permute-start(bf16[128,2048]{1,0:T(8,128)(2,1)} %collective-permute-done.4.refs_5_.refs_12_), channel_id=1, source_target_pairs={{0,4},{4,0},{8,12},{12,8},{16,20},{20,16},{24,28},{28,24},{32,36},... | collective-permute-start | bytes 1572872 | tf_op jit(solution)/shard_map/ppermute | solution.py:32
  45.7 1.0 copy-start.8
  47.5 1.0 copy-start
  48.6 1.0 copy-start.2
  49.6 1.0 copy-start.4
  50.7 1.0 copy-start.6
  51.7 0.7 copy-start.9
  52.4 12.5 %copy-start.1 = (bf16[128,2048]{1,0:T(8,128)(2,1)S(1)}, bf16[128,2048]{1,0:T(8,128)(2,1)}, u32[]{:S(2)}) copy-start(bf16[128,2048]{1,0:T(8,128)(2,1)} %refs_3_.5) | copy-start | bytes 1572868
  52.4 12.5 %copy-start.3 = (bf16[128,2048]{1,0:T(8,128)(2,1)S(1)}, bf16[128,2048]{1,0:T(8,128)(2,1)}, u32[]{:S(2)}) copy-start(bf16[128,2048]{1,0:T(8,128)(2,1)} %refs_4_.3) | copy-start | bytes 1572868
  52.4 12.5 %copy-start.10 = (s32[1,2]{1,0:T(1,128)S(1)}, s32[1,2]{1,0:T(1,128)}, u32[]{:S(2)}) copy-start(s32[1,2]{1,0:T(1,128)} %offsets_ref.3) | copy-start | bytes 28
  56.1 13.5 %all-to-all-start.1 = ((bf16[4,128,512]{2,1,0:T(8,128)(2,1)}), bf16[4,128,512]{2,1,0:T(8,128)(2,1)S(1)}, u32[]{:S(2)}, u32[]{:S(2)}) async-start(bf16[4,128,512]{2,1,0:T(8,128)(2,1)} %bitcast.4), calls=%async_computation.1 | async-start | bytes 1048576 | tf_op jit(solution)/shard_map/all_to_all | solution.py:321
  61.6 33.8 %copy-start.5 = (bf16[128,2048]{1,0:T(8,128)(2,1)S(1)}, bf16[128,2048]{1,0:T(8,128)(2,1)}, u32[]{:S(2)}) copy-start(bf16[128,2048]{1,0:T(8,128)(2,1)} %refs_5_.1) | copy-start | bytes 1572868
  61.7 33.8 %copy-start.7 = (bf16[128,2048]{1,0:T(8,128)(2,1)S(1)}, bf16[128,2048]{1,0:T(8,128)(2,1)}, u32[]{:S(2)}) copy-start(bf16[128,2048]{1,0:T(8,128)(2,1)} %refs_10_.3) | copy-start | bytes 1572868
  78.6 10.9 %collective-permute-start.9 = (f32[672,128]{1,0:T(8,128)S(1)}, f32[672,128]{1,0:T(8,128)S(1)}, u32[]{:S(2)}, u32[]{:S(2)}) collective-permute-start(f32[672,128]{1,0:T(8,128)S(1)} %bitcast.9), channel_id=1, source_target_pairs={{0,16},{4,20},{8,24},{12,28},{16,0},{20,4},{24,8},{28,12},{32,48},... | collective-permute-start | bytes 1032200 | tf_op jit(solution)/shard_map/ppermute | solution.py:32
  80.5 15.0 %collective-permute-start.8 = (f32[672,128]{1,0:T(8,128)S(1)}, f32[672,128]{1,0:T(8,128)S(1)}, u32[]{:S(2)}, u32[]{:S(2)}) collective-permute-start(f32[672,128]{1,0:T(8,128)S(1)} %bitcast.10), channel_id=1, source_target_pairs={{0,496},{4,500},{8,504},{12,508},{16,32},{20,36},{24,40},{28,44},{... | collective-permute-start | bytes 1032200 | tf_op jit(solution)/shard_map/ppermute | solution.py:32
  100.3 15.6 %collective-permute-start.14 = (bf16[128,1024]{1,0:T(8,128)(2,1)S(1)}, bf16[128,1024]{1,0:T(8,128)(2,1)S(1)}, u32[]{:S(2)}, u32[]{:S(2)}) collective-permute-start(bf16[128,1024]{1,0:T(8,128)(2,1)S(1)} %get-tuple-element.24.refs_0_), channel_id=1, source_target_pairs={{0,2},{1,3},{2,0},{3,1},{4,6},{5,7},{6,4},{7,5},{8,10},{9,11},{10,... | collective-permute-start | bytes 786440 | tf_op jit(solution)/shard_map/ppermute | solution.py:37
  107.9 12.3 %collective-permute-start.11 = (bf16[128,1024]{1,0:T(8,128)(2,1)S(1)}, bf16[128,1024]{1,0:T(8,128)(2,1)S(1)}, u32[]{:S(2)}, u32[]{:S(2)}) collective-permute-start(bf16[128,1024]{1,0:T(8,128)(2,1)S(1)} %get-tuple-element.23.refs_0_), channel_id=1, source_target_pairs={{0,2},{1,3},{2,0},{3,1},{4,6},{5,7},{6,4},{7,5},{8,10},{9,11},{10,... | collective-permute-start | bytes 786440 | tf_op jit(solution)/shard_map/ppermute | solution.py:37
  110.4 11.8 %collective-permute-start.13 = (bf16[128,1024]{1,0:T(8,128)(2,1)S(1)}, bf16[128,1024]{1,0:T(8,128)(2,1)S(1)}, u32[]{:S(2)}, u32[]{:S(2)}) collective-permute-start(bf16[128,1024]{1,0:T(8,128)(2,1)S(1)} %get-tuple-element.24.refs_0_), channel_id=1, source_target_pairs={{0,1},{1,0},{2,3},{3,2},{4,5},{5,4},{6,7},{7,6},{8,9},{9,8},{10,11... | collective-permute-start | bytes 786440 | tf_op jit(solution)/shard_map/ppermute | solution.py:37
  115.9 6.3 %collective-permute-start.15 = (bf16[128,1024]{1,0:T(8,128)(2,1)S(1)}, bf16[128,1024]{1,0:T(8,128)(2,1)S(1)}, u32[]{:S(2)}, u32[]{:S(2)}) collective-permute-start(bf16[128,1024]{1,0:T(8,128)(2,1)S(1)} %collective-permute-done.14.refs_2_), channel_id=1, source_target_pairs={{0,1},{1,0},{2,3},{3,2},{4,5},{5,4},{6,7},{7,6},{8,9},{9,8},{10,11... | collective-permute-start | bytes 786440 | tf_op jit(solution)/shard_map/ppermute | solution.py:37
  117.8 6.4 %collective-permute-start.10 = (bf16[128,1024]{1,0:T(8,128)(2,1)S(1)}, bf16[128,1024]{1,0:T(8,128)(2,1)S(1)}, u32[]{:S(2)}, u32[]{:S(2)}) collective-permute-start(bf16[128,1024]{1,0:T(8,128)(2,1)S(1)} %get-tuple-element.23.refs_0_), channel_id=1, source_target_pairs={{0,1},{1,0},{2,3},{3,2},{4,5},{5,4},{6,7},{7,6},{8,9},{9,8},{10,11... | collective-permute-start | bytes 786440 | tf_op jit(solution)/shard_map/ppermute | solution.py:37
  120.2 4.0 %collective-permute-start.12 = (bf16[128,1024]{1,0:T(8,128)(2,1)S(1)}, bf16[128,1024]{1,0:T(8,128)(2,1)S(1)}, u32[]{:S(2)}, u32[]{:S(2)}) collective-permute-start(bf16[128,1024]{1,0:T(8,128)(2,1)S(1)} %collective-permute-done.11.refs_2_), channel_id=1, source_target_pairs={{0,1},{1,0},{2,3},{3,2},{4,5},{5,4},{6,7},{7,6},{8,9},{9,8},{10,11... | collective-permute-start | bytes 786440 | tf_op jit(solution)/shard_map/ppermute | solution.py:37

commit v10 on v9

--- a/solution.py
+++ b/solution.py
@@ -159,8 +159,8 @@
         for head in range(STEP):
             cols = pl.ds(pl.multiple_of((step * STEP + head) * HD, HD), HD)
             out_cols = pl.ds(pl.multiple_of((at * STEP + head) * HD, HD), HD)
-            query_rows = head_rows(query_refs, cols)
-            grad_rows = head_rows(grad_refs, cols)
+            query_rows = jnp.concatenate([query_refs[0][:, cols], head_rows(query_refs[1:], out_cols)], 0)
+            grad_rows = jnp.concatenate([grad_refs[0][:, cols], head_rows(grad_refs[1:], out_cols)], 0)
             scores = scores_of(keys_ref[:, cols], query_rows, True)
             prob_grad = dot_nt(values_ref[:, cols], grad_rows)
             probs = jnp.exp(scores - lse[head : head + 1])
@@ -236,24 +236,40 @@
     )(partner_offsets, *map(in_vmem, arrays), *map(in_vmem, before))
 
 
-def call_grads(first, each, replica, stat_parts, arrays, before):
-    rows, features = arrays[0].shape
-    pairs = rows * rows * len(DOCS) * each * STEP
+def call_grads(first, each, replica, stat_parts, own, query_docs, grad_docs, before):
+    rows, features = own[0].shape
+    count = len(query_docs)
+    pairs = rows * rows * count * each * STEP
     half = (rows, each * STEP * HD)
     whole = (rows, (len(before) + 1) * half[1])
-    inputs = [*stat_parts, *arrays, *before]
+    block = pl.BlockSpec(half, lambda step: (0, first // each))
+    docs = [VMEM] + [block] * (count - 1)
     return pl.pallas_call(
         functools.partial(grads_kernel, first),
-        in_specs=[pl.BlockSpec(memory_space=pltpu.SMEM)] + [VMEM] * len(inputs),
+        grid=(1,),
+        in_specs=[pl.BlockSpec(memory_space=pltpu.SMEM)]
+        + [VMEM] * (len(stat_parts) + len(own))
+        + docs * 2
+        + [VMEM] * len(before),
         out_specs=[VMEM] * 2,
         out_shape=[pltpu.VMEM(half, jnp.bfloat16), pltpu.VMEM(whole, jnp.bfloat16)],
         scratch_shapes=[pltpu.VMEM((3 * stat_parts[0].shape[0], rows), jnp.float32)],
         compiler_params=PARAMS,
         cost_estimate=pl.CostEstimate(
-            flops=8 * pairs * HD, bytes_accessed=2 * len(arrays) * half[0] * half[1], transcendentals=pairs
+            flops=8 * pairs * HD,
+            bytes_accessed=2 * (2 + 2 * count) * half[0] * half[1],
+            transcendentals=pairs,
         ),
         name="grads",
-    )(replica, *map(in_vmem, inputs))
+    )(
+        replica,
+        *map(in_vmem, [*stat_parts, *own]),
+        in_vmem(query_docs[0]),
+        *query_docs[1:],
+        in_vmem(grad_docs[0]),
+        *grad_docs[1:],
+        *map(in_vmem, before),
+    )
 
 
 def call_spread(layer_input, places):
@@ -329,10 +345,9 @@
     stat_parts = [after_odd, here, traded(here, "dp", GROUP, False)]
 
     each = steps // HALVES
-    arrays = own + query_docs + grad_docs
     halves, values = [], []
     for half in range(HALVES):
-        key_half, value_part = call_grads(half * each, each, replica, stat_parts, arrays, values)
+        key_half, value_part = call_grads(half * each, each, replica, stat_parts, own, query_docs, grad_docs, values)
         halves.append(key_half)
         values = [value_part]
 

time: 127 us -> 126 us (level)
  transfers between devices with their start and end apart: 17 -> 17, of which waited for: 3 -> 3; matrix products, arithmetic and copies ran while one was open for 0% -> 0% of each run, Pallas kernels for 12% -> 11%
where the time goes in v10:
time: 126 us; the launch traced here: 125 us
  starting transfers between devices  78.4 us (62%)
  Pallas kernels  20.3 us (16%)
  waiting for transfers between devices  10.7 us (8%)
  blocking collectives  8.93 us (7%)
  local copies, waits for them, and re-layouts  5.87 us (5%)
    ppermute x10, starting transfers between devices, traded(): return lax.ppermute(value, axis, pairs)  55.8 us
    ppermute x6, starting transfers between devices, swapped(): return lax.ppermute(value, axis, pairs)  17 us
    ppermute x10, waiting for transfers between devices, traded(): return lax.ppermute(value, axis, pairs)  9.19 us
    all_to_all x1, blocking collectives, local(): lax.all_to_all(stats, 'dp', 0, 0, axis_index_groups=groups, tiled=True)  8.93 us
    pallas_call x2, Pallas kernels, call_grads(): pl.pallas_call(functools.partial(grads_kernel, first), grid=(1,), in_spec...  8.46 us
    pallas_call x2, Pallas kernels, call_stats(): pl.pallas_call(functools.partial(stats_kernel, low), in_specs=[pl.BlockSp...  7 us
    unnamed x22, local copies, waits for them, and re-layouts  5.87 us
    all_to_all x1, starting transfers between devices, local(): columns = lax.all_to_all(columns, 'fsdp', 0, 0, tiled=True)  5.55 us
  transfers between devices with their start and end apart: 17, of which 3 were waited for; matrix products, arithmetic and copies ran while one was open for 0% of the time, Pallas kernels for 11%

profile of v10, /device:TPU:1, one launch (start us, length us, event | category | flops | bytes accessed | tf_op | source)
XLA Modules:
  0.0 125.1 jit_solution(14503177435770334457)
XLA Ops:
  0.6 4.0 %collective-permute-start.2 = (bf16[128,2048]{1,0:T(8,128)(2,1)}, bf16[128,2048]{1,0:T(8,128)(2,1)S(1)}, u32[]{:S(2)}, u32[]{:S(2)}) collective-permute-start(bf16[128,2048]{1,0:T(8,128)(2,1)} %refs_5_.1), channel_id=1, source_target_pairs={{0,4},{4,0},{8,12},{12,8},{16,20},{20,16},{24,28},{28,24},{32,36},... | collective-permute-start | bytes 1572872 | tf_op jit(solution)/shard_map/ppermute | solution.py:32
  4.7 15.2 %collective-permute-start = (bf16[128,2048]{1,0:T(8,128)(2,1)}, bf16[128,2048]{1,0:T(8,128)(2,1)}, u32[]{:S(2)}, u32[]{:S(2)}) collective-permute-start(bf16[128,2048]{1,0:T(8,128)(2,1)} %refs_5_.1), channel_id=1, source_target_pairs={{0,508},{4,8},{8,4},{12,16},{16,12},{20,24},{24,20},{28,32},{32,28... | collective-permute-start | bytes 1572872 | tf_op jit(solution)/shard_map/ppermute | solution.py:32
  19.9 1.9 %collective-permute-start.6 = (bf16[128,2048]{1,0:T(8,128)(2,1)}, bf16[128,2048]{1,0:T(8,128)(2,1)}, u32[]{:S(2)}, u32[]{:S(2)}) collective-permute-start(bf16[128,2048]{1,0:T(8,128)(2,1)} %refs_10_.3), channel_id=1, source_target_pairs={{0,4},{4,0},{8,12},{12,8},{16,20},{20,16},{24,28},{28,24},{32,36},... | collective-permute-start | bytes 1572872 | tf_op jit(solution)/shard_map/ppermute | solution.py:32
  21.8 2.9 %collective-permute-start.4 = (bf16[128,2048]{1,0:T(8,128)(2,1)}, bf16[128,2048]{1,0:T(8,128)(2,1)}, u32[]{:S(2)}, u32[]{:S(2)}) collective-permute-start(bf16[128,2048]{1,0:T(8,128)(2,1)} %refs_10_.3), channel_id=1, source_target_pairs={{0,508},{4,8},{8,4},{12,16},{16,12},{20,24},{24,20},{28,32},{32,28... | collective-permute-start | bytes 1572872 | tf_op jit(solution)/shard_map/ppermute | solution.py:32
  24.7 0.0 collective-permute-done.2.refs_1_.refs_6_
  24.8 8.1 %collective-permute-start.3 = (bf16[128,2048]{1,0:T(8,128)(2,1)S(1)}, bf16[128,2048]{1,0:T(8,128)(2,1)}, u32[]{:S(2)}, u32[]{:S(2)}) collective-permute-start(bf16[128,2048]{1,0:T(8,128)(2,1)S(1)} %collective-permute-done.2.refs_1_.refs_6_), channel_id=1, source_target_pairs={{0,508},{4,8},{8,4},{12,16},{16,12},{20,24},{24,20},{28,32},{32,28... | collective-permute-start | bytes 1572872 | tf_op jit(solution)/shard_map/ppermute | solution.py:32
  32.9 0.0 collective-permute-done.refs_2_.refs_7_
  32.9 1.9 %collective-permute-start.1 = (bf16[128,2048]{1,0:T(8,128)(2,1)}, bf16[128,2048]{1,0:T(8,128)(2,1)}, u32[]{:S(2)}, u32[]{:S(2)}) collective-permute-start(bf16[128,2048]{1,0:T(8,128)(2,1)} %collective-permute-done.refs_2_.refs_7_), channel_id=1, source_target_pairs={{0,4},{4,0},{8,12},{12,8},{16,20},{20,16},{24,28},{28,24},{32,36},... | collective-permute-start | bytes 1572872 | tf_op jit(solution)/shard_map/ppermute | solution.py:32
  34.8 0.0 collective-permute-done.6.refs_4_.refs_11_
  34.8 8.9 %collective-permute-start.7 = (bf16[128,2048]{1,0:T(8,128)(2,1)}, bf16[128,2048]{1,0:T(8,128)(2,1)}, u32[]{:S(2)}, u32[]{:S(2)}) collective-permute-start(bf16[128,2048]{1,0:T(8,128)(2,1)} %collective-permute-done.6.refs_4_.refs_11_), channel_id=1, source_target_pairs={{0,508},{4,8},{8,4},{12,16},{16,12},{20,24},{24,20},{28,32},{32,28... | collective-permute-start | bytes 1572872 | tf_op jit(solution)/shard_map/ppermute | solution.py:32
  43.7 0.0 collective-permute-done.4.refs_5_.refs_12_
  43.7 1.9 %collective-permute-start.5 = (bf16[128,2048]{1,0:T(8,128)(2,1)}, bf16[128,2048]{1,0:T(8,128)(2,1)}, u32[]{:S(2)}, u32[]{:S(2)}) collective-permute-start(bf16[128,2048]{1,0:T(8,128)(2,1)} %collective-permute-done.4.refs_5_.refs_12_), channel_id=1, source_target_pairs={{0,4},{4,0},{8,12},{12,8},{16,20},{20,16},{24,28},{28,24},{32,36},... | collective-permute-start | bytes 1572872 | tf_op jit(solution)/shard_map/ppermute | solution.py:32
  45.7 0.0 copy-start.8
  45.7 1.0 copy-done.8
  46.7 0.8 spread.1
  47.5 0.0 copy-start
  47.6 1.0 copy-done
  48.6 0.0 copy-start.2
  48.6 1.0 copy-done.2
  49.6 0.0 copy-start.4
  49.6 1.0 copy-done.4
  50.7 0.0 copy-start.6
  50.7 1.0 copy-done.6
  51.7 0.0 copy-start.9
  51.7 0.7 copy-done.9
  52.4 0.0 copy-start.1
  52.4 0.0 copy-start.3
  52.4 0.0 copy-start.10
  52.4 3.7 %stats.2.refs_4_ = f32[96,128]{1,0:T(8,128)S(1)} custom-call(s32[1,2]{1,0:T(1,128)S(1)} %copy-done.9, bf16[128,2048]{1,0:T(8,128)(2,1)S(1)} %copy-done, bf16[128,2048]{1,0:T(8,128)(2,1)S(1)} %copy-done.2, bf16[128,2048]{1,0:T(8,128)(2,1)S(1)} %copy-done.4, bf16[128,2048]{1,0:T(8,128)(2,1)S(1)} %collective-permute-done.2.refs_1_.refs_6_, ...), custom_call_target="tpu_custom_call" | custom-call | flops 402653184 | bytes 4194304 | tf_op jit(solution)/shard_map/stats/pallas_call | solution.py:226
  56.1 5.6 %all-to-all-start.1 = ((bf16[4,128,512]{2,1,0:T(8,128)(2,1)}), bf16[4,128,512]{2,1,0:T(8,128)(2,1)S(1)}, u32[]{:S(2)}, u32[]{:S(2)}) async-start(bf16[4,128,512]{2,1,0:T(8,128)(2,1)} %bitcast.4), calls=%async_computation.1 | async-start | bytes 1048576 | tf_op jit(solution)/shard_map/all_to_all | solution.py:337
  61.6 0.0 copy-start.5
  61.7 0.0 copy-start.7
  61.7 0.0 collective-permute-done.3.refs_1_.refs_9_
  61.7 0.0 collective-permute-done.1.refs_0_.refs_8_
  61.7 3.2 %collective-permute-done.7.refs_3_.refs_14_ = bf16[128,2048]{1,0:T(8,128)(2,1)} collective-permute-done((bf16[128,2048]{1,0:T(8,128)(2,1)}, bf16[128,2048]{1,0:T(8,128)(2,1)}, u32[]{:S(2)}, u32[]{:S(2)}) %collective-permute-start.7) | collective-permute-done | bytes 524320 | tf_op jit(solution)/shard_map/ppermute | solution.py:32
  64.9 0.0 collective-permute-done.5.refs_2_.refs_13_
  64.9 0.0 copy-done.1
  64.9 0.0 copy-done.3
  64.9 0.0 copy-done.10
  64.9 3.3 %stats.3 = f32[672,128]{1,0:T(8,128)S(1)} custom-call(s32[1,2]{1,0:T(1,128)S(1)} %copy-done.10, bf16[128,2048]{1,0:T(8,128)(2,1)S(1)} %copy-done.1, bf16[128,2048]{1,0:T(8,128)(2,1)S(1)} %copy-done.3, bf16[128,2048]{1,0:T(8,128)(2,1)} %collective-permute-done.1.refs_0_.refs_8_, bf16[128,2048]{1,0:T(8,128)(2,1)} %collective-permute-done.3.refs_1_.refs_9_, ...), custom_call_target="tpu_custom_call" | custom-call | flops 268435456 | bytes 3145728 | tf_op jit(solution)/shard_map/stats/pallas_call | solution.py:226
  68.2 1.5 %all-to-all-done.1 = bf16[4,128,512]{2,1,0:T(8,128)(2,1)S(1)} async-done(((bf16[4,128,512]{2,1,0:T(8,128)(2,1)}), bf16[4,128,512]{2,1,0:T(8,128)(2,1)S(1)}, u32[]{:S(2)}, u32[]{:S(2)}) %all-to-all-start.1) | async-done | bytes 524320 | tf_op jit(solution)/shard_map/all_to_all | solution.py:337
  69.6 8.9 %all_to_all.24 = f32[4,168,128]{2,1,0:T(8,128)S(1)} all-to-all(f32[4,168,128]{2,1,0:T(8,128)S(1)} %bitcast.13), channel_id=1, replica_groups={{0,4,8,12},{16,20,24,28},{32,36,40,44},{48,52,56,60},{64,68,72,76},{80,..., dimensions={0} | all-to-all | bytes 688128 | tf_op jit(solution)/shard_map/all_to_all | solution.py:342
  78.6 1.9 %collective-permute-start.9 = (f32[672,128]{1,0:T(8,128)S(1)}, f32[672,128]{1,0:T(8,128)S(1)}, u32[]{:S(2)}, u32[]{:S(2)}) collective-permute-start(f32[672,128]{1,0:T(8,128)S(1)} %bitcast.9), channel_id=1, source_target_pairs={{0,16},{4,20},{8,24},{12,28},{16,0},{20,4},{24,8},{28,12},{32,48},... | collective-permute-start | bytes 1032200 | tf_op jit(solution)/shard_map/ppermute | solution.py:32
  80.5 9.0 %collective-permute-start.8 = (f32[672,128]{1,0:T(8,128)S(1)}, f32[672,128]{1,0:T(8,128)S(1)}, u32[]{:S(2)}, u32[]{:S(2)}) collective-permute-start(f32[672,128]{1,0:T(8,128)S(1)} %bitcast.10), channel_id=1, source_target_pairs={{0,496},{4,500},{8,504},{12,508},{16,32},{20,36},{24,40},{28,44},{... | collective-permute-start | bytes 1032200 | tf_op jit(solution)/shard_map/ppermute | solution.py:32
  89.5 0.0 collective-permute-done.9.refs_2_
  89.5 6.0 %collective-permute-done.8.refs_0_ = f32[672,128]{1,0:T(8,128)S(1)} collective-permute-done((f32[672,128]{1,0:T(8,128)S(1)}, f32[672,128]{1,0:T(8,128)S(1)}, u32[]{:S(2)}, u32[]{:S(2)}) %collective-permute-start.8) | collective-permute-done | bytes 344096 | tf_op jit(solution)/shard_map/ppermute | solution.py:32
  95.5 0.0 copy-done.5
  95.5 0.0 copy-done.7
  95.5 4.2 %grads.2 = (bf16[128,1024]{1,0:T(8,128)(2,1)S(1)}, bf16[128,1024]{1,0:T(8,128)(2,1)S(1)}) custom-call(s32[1]{0:T(128)} %bitcast.1.replica_ref, f32[672,128]{1,0:T(8,128)S(1)} %collective-permute-done.8.refs_0_, f32[672,128]{1,0:T(8,128)S(1)} %bitcast.11, f32[672,128]{1,0:T(8,128)S(1)} %collective-permute-done.9.refs_2_, bf16[128,2048]{1,0:T(8,128)(2,1)S(1)} %copy-done.1, ...), custom_call_target="tpu_custom_call" | custom-call | flops 671088640 | bytes 3145728 | tf_op jit(solution)/shard_map/grads/pallas_call | solution.py:247
  99.7 2.8 %collective-permute-start.14 = (bf16[128,1024]{1,0:T(8,128)(2,1)S(1)}, bf16[128,1024]{1,0:T(8,128)(2,1)S(1)}, u32[]{:S(2)}, u32[]{:S(2)}) collective-permute-start(bf16[128,1024]{1,0:T(8,128)(2,1)S(1)} %get-tuple-element.24.refs_0_), channel_id=1, source_target_pairs={{0,2},{1,3},{2,0},{3,1},{4,6},{5,7},{6,4},{7,5},{8,10},{9,11},{10,... | collective-permute-start | bytes 786440 | tf_op jit(solution)/shard_map/ppermute | solution.py:37
  102.5 4.2 %grads.3 = (bf16[128,1024]{1,0:T(8,128)(2,1)S(1)}, bf16[128,2048]{1,0:T(8,128)(2,1)S(1)}) custom-call(s32[1]{0:T(128)} %bitcast.1.replica_ref, f32[672,128]{1,0:T(8,128)S(1)} %collective-permute-done.8.refs_0_, f32[672,128]{1,0:T(8,128)S(1)} %bitcast.12, f32[672,128]{1,0:T(8,128)S(1)} %collective-permute-done.9.refs_2_, bf16[128,2048]{1,0:T(8,128)(2,1)S(1)} %copy-done.1, ...), custom_call_target="tpu_custom_call" | custom-call | flops 671088640 | bytes 3145728 | tf_op jit(solution)/shard_map/grads/pallas_call | solution.py:247
  106.8 2.5 %collective-permute-start.11 = (bf16[128,1024]{1,0:T(8,128)(2,1)S(1)}, bf16[128,1024]{1,0:T(8,128)(2,1)S(1)}, u32[]{:S(2)}, u32[]{:S(2)}) collective-permute-start(bf16[128,1024]{1,0:T(8,128)(2,1)S(1)} %get-tuple-element.23.refs_0_), channel_id=1, source_target_pairs={{0,2},{1,3},{2,0},{3,1},{4,6},{5,7},{6,4},{7,5},{8,10},{9,11},{10,... | collective-permute-start | bytes 786440 | tf_op jit(solution)/shard_map/ppermute | solution.py:37
  109.3 5.5 %collective-permute-start.13 = (bf16[128,1024]{1,0:T(8,128)(2,1)S(1)}, bf16[128,1024]{1,0:T(8,128)(2,1)S(1)}, u32[]{:S(2)}, u32[]{:S(2)}) collective-permute-start(bf16[128,1024]{1,0:T(8,128)(2,1)S(1)} %get-tuple-element.24.refs_0_), channel_id=1, source_target_pairs={{0,1},{1,0},{2,3},{3,2},{4,5},{5,4},{6,7},{7,6},{8,9},{9,8},{10,11... | collective-permute-start | bytes 786440 | tf_op jit(solution)/shard_map/ppermute | solution.py:37
  114.7 0.0 collective-permute-done.14.refs_2_
  114.7 1.9 %collective-permute-start.15 = (bf16[128,1024]{1,0:T(8,128)(2,1)S(1)}, bf16[128,1024]{1,0:T(8,128)(2,1)S(1)}, u32[]{:S(2)}, u32[]{:S(2)}) collective-permute-start(bf16[128,1024]{1,0:T(8,128)(2,1)S(1)} %collective-permute-done.14.refs_2_), channel_id=1, source_target_pairs={{0,1},{1,0},{2,3},{3,2},{4,5},{5,4},{6,7},{7,6},{8,9},{9,8},{10,11... | collective-permute-start | bytes 786440 | tf_op jit(solution)/shard_map/ppermute | solution.py:37
  116.7 2.4 %collective-permute-start.10 = (bf16[128,1024]{1,0:T(8,128)(2,1)S(1)}, bf16[128,1024]{1,0:T(8,128)(2,1)S(1)}, u32[]{:S(2)}, u32[]{:S(2)}) collective-permute-start(bf16[128,1024]{1,0:T(8,128)(2,1)S(1)} %get-tuple-element.23.refs_0_), channel_id=1, source_target_pairs={{0,1},{1,0},{2,3},{3,2},{4,5},{5,4},{6,7},{7,6},{8,9},{9,8},{10,11... | collective-permute-start | bytes 786440 | tf_op jit(solution)/shard_map/ppermute | solution.py:37
  119.1 0.0 collective-permute-done.11.refs_2_
  119.1 1.9 %collective-permute-start.12 = (bf16[128,1024]{1,0:T(8,128)(2,1)S(1)}, bf16[128,1024]{1,0:T(8,128)(2,1)S(1)}, u32[]{:S(2)}, u32[]{:S(2)}) collective-permute-start(bf16[128,1024]{1,0:T(8,128)(2,1)S(1)} %collective-permute-done.11.refs_2_), channel_id=1, source_target_pairs={{0,1},{1,0},{2,3},{3,2},{4,5},{5,4},{6,7},{7,6},{8,9},{9,8},{10,11... | collective-permute-start | bytes 786440 | tf_op jit(solution)/shard_map/ppermute | solution.py:37
  121.0 0.0 collective-permute-done.13.refs_1_
  121.0 0.0 collective-permute-done.15.refs_3_
  121.1 2.0 %weight.2 = (bf16[512,2048]{1,0:T(8,128)(2,1)}, bf16[128,2048]{1,0:T(8,128)(2,1)}) custom-call(s32[1]{0:T(128)} %bitcast.mine_ref, bf16[512,512]{1,0:T(8,128)(2,1)S(1)} %bitcast.7, bf16[128,1024]{1,0:T(8,128)(2,1)S(1)} %get-tuple-element.24.refs_0_, bf16[128,1024]{1,0:T(8,128)(2,1)S(1)} %collective-permute-done.13.refs_1_, ...), custom_call_target="tpu_custom_call" | custom-call | flops 536870912 | bytes 2097152 | tf_op jit(solution)/shard_map/weight/pallas_call | solution.py:294
  123.1 0.0 collective-permute-done.10.refs_1_
  123.1 0.0 collective-permute-done.12.refs_3_
  123.1 2.0 %weight.3 = bf16[512,2048]{1,0:T(8,128)(2,1)} custom-call(s32[1]{0:T(128)} %bitcast.mine_ref, bf16[512,512]{1,0:T(8,128)(2,1)S(1)} %bitcast.8, bf16[128,1024]{1,0:T(8,128)(2,1)S(1)} %get-tuple-element.23.refs_0_, bf16[128,1024]{1,0:T(8,128)(2,1)S(1)} %collective-permute-done.10.refs_1_, ...), custom_call_target="tpu_custom_call", output_to_operand_aliasing={{}: (6, {})} | custom-call | flops 536870912 | bytes 2097152 | tf_op jit(solution)/shard_map/weight/pallas_call | solution.py:294
Async XLA Ops:
  0.6 24.1 %collective-permute-start.2 = (bf16[128,2048]{1,0:T(8,128)(2,1)}, bf16[128,2048]{1,0:T(8,128)(2,1)S(1)}, u32[]{:S(2)}, u32[]{:S(2)}) collective-permute-start(bf16[128,2048]{1,0:T(8,128)(2,1)} %refs_5_.1), channel_id=1, source_target_pairs={{0,4},{4,0},{8,12},{12,8},{16,20},{20,16},{24,28},{28,24},{32,36},... | collective-permute-start | bytes 1572872 | tf_op jit(solution)/shard_map/ppermute | solution.py:32
  4.7 28.2 %collective-permute-start = (bf16[128,2048]{1,0:T(8,128)(2,1)}, bf16[128,2048]{1,0:T(8,128)(2,1)}, u32[]{:S(2)}, u32[]{:S(2)}) collective-permute-start(bf16[128,2048]{1,0:T(8,128)(2,1)} %refs_5_.1), channel_id=1, source_target_pairs={{0,508},{4,8},{8,4},{12,16},{16,12},{20,24},{24,20},{28,32},{32,28... | collective-permute-start | bytes 1572872 | tf_op jit(solution)/shard_map/ppermute | solution.py:32
  19.9 14.9 %collective-permute-start.6 = (bf16[128,2048]{1,0:T(8,128)(2,1)}, bf16[128,2048]{1,0:T(8,128)(2,1)}, u32[]{:S(2)}, u32[]{:S(2)}) collective-permute-start(bf16[128,2048]{1,0:T(8,128)(2,1)} %refs_10_.3), channel_id=1, source_target_pairs={{0,4},{4,0},{8,12},{12,8},{16,20},{20,16},{24,28},{28,24},{32,36},... | collective-permute-start | bytes 1572872 | tf_op jit(solution)/shard_map/ppermute | solution.py:32
  21.8 21.9 %collective-permute-start.4 = (bf16[128,2048]{1,0:T(8,128)(2,1)}, bf16[128,2048]{1,0:T(8,128)(2,1)}, u32[]{:S(2)}, u32[]{:S(2)}) collective-permute-start(bf16[128,2048]{1,0:T(8,128)(2,1)} %refs_10_.3), channel_id=1, source_target_pairs={{0,508},{4,8},{8,4},{12,16},{16,12},{20,24},{24,20},{28,32},{32,28... | collective-permute-start | bytes 1572872 | tf_op jit(solution)/shard_map/ppermute | solution.py:32
  24.8 36.9 %collective-permute-start.3 = (bf16[128,2048]{1,0:T(8,128)(2,1)S(1)}, bf16[128,2048]{1,0:T(8,128)(2,1)}, u32[]{:S(2)}, u32[]{:S(2)}) collective-permute-start(bf16[128,2048]{1,0:T(8,128)(2,1)S(1)} %collective-permute-done.2.refs_1_.refs_6_), channel_id=1, source_target_pairs={{0,508},{4,8},{8,4},{12,16},{16,12},{20,24},{24,20},{28,32},{32,28... | collective-permute-start | bytes 1572872 | tf_op jit(solution)/shard_map/ppermute | solution.py:32
  32.9 28.8 %collective-permute-start.1 = (bf16[128,2048]{1,0:T(8,128)(2,1)}, bf16[128,2048]{1,0:T(8,128)(2,1)}, u32[]{:S(2)}, u32[]{:S(2)}) collective-permute-start(bf16[128,2048]{1,0:T(8,128)(2,1)} %collective-permute-done.refs_2_.refs_7_), channel_id=1, source_target_pairs={{0,4},{4,0},{8,12},{12,8},{16,20},{20,16},{24,28},{28,24},{32,36},... | collective-permute-start | bytes 1572872 | tf_op jit(solution)/shard_map/ppermute | solution.py:32
  34.8 30.1 %collective-permute-start.7 = (bf16[128,2048]{1,0:T(8,128)(2,1)}, bf16[128,2048]{1,0:T(8,128)(2,1)}, u32[]{:S(2)}, u32[]{:S(2)}) collective-permute-start(bf16[128,2048]{1,0:T(8,128)(2,1)} %collective-permute-done.6.refs_4_.refs_11_), channel_id=1, source_target_pairs={{0,508},{4,8},{8,4},{12,16},{16,12},{20,24},{24,20},{28,32},{32,28... | collective-permute-start | bytes 1572872 | tf_op jit(solution)/shard_map/ppermute | solution.py:32
  43.7 21.1 %collective-permute-start.5 = (bf16[128,2048]{1,0:T(8,128)(2,1)}, bf16[128,2048]{1,0:T(8,128)(2,1)}, u32[]{:S(2)}, u32[]{:S(2)}) collective-permute-start(bf16[128,2048]{1,0:T(8,128)(2,1)} %collective-permute-done.4.refs_5_.refs_12_), channel_id=1, source_target_pairs={{0,4},{4,0},{8,12},{12,8},{16,20},{20,16},{24,28},{28,24},{32,36},... | collective-permute-start | bytes 1572872 | tf_op jit(solution)/shard_map/ppermute | solution.py:32
  45.7 1.0 copy-start.8
  47.5 1.0 copy-start
  48.6 1.0 copy-start.2
  49.6 1.0 copy-start.4
  50.7 1.0 copy-start.6
  51.7 0.7 copy-start.9
  52.4 12.5 %copy-start.1 = (bf16[128,2048]{1,0:T(8,128)(2,1)S(1)}, bf16[128,2048]{1,0:T(8,128)(2,1)}, u32[]{:S(2)}) copy-start(bf16[128,2048]{1,0:T(8,128)(2,1)} %refs_3_.5) | copy-start | bytes 1572868
  52.4 12.5 %copy-start.3 = (bf16[128,2048]{1,0:T(8,128)(2,1)S(1)}, bf16[128,2048]{1,0:T(8,128)(2,1)}, u32[]{:S(2)}) copy-start(bf16[128,2048]{1,0:T(8,128)(2,1)} %refs_4_.3) | copy-start | bytes 1572868
  52.4 12.5 %copy-start.10 = (s32[1,2]{1,0:T(1,128)S(1)}, s32[1,2]{1,0:T(1,128)}, u32[]{:S(2)}) copy-start(s32[1,2]{1,0:T(1,128)} %offsets_ref.3) | copy-start | bytes 28
  56.1 13.5 %all-to-all-start.1 = ((bf16[4,128,512]{2,1,0:T(8,128)(2,1)}), bf16[4,128,512]{2,1,0:T(8,128)(2,1)S(1)}, u32[]{:S(2)}, u32[]{:S(2)}) async-start(bf16[4,128,512]{2,1,0:T(8,128)(2,1)} %bitcast.4), calls=%async_computation.1 | async-start | bytes 1048576 | tf_op jit(solution)/shard_map/all_to_all | solution.py:337
  61.6 33.8 %copy-start.5 = (bf16[128,2048]{1,0:T(8,128)(2,1)S(1)}, bf16[128,2048]{1,0:T(8,128)(2,1)}, u32[]{:S(2)}) copy-start(bf16[128,2048]{1,0:T(8,128)(2,1)} %refs_5_.1) | copy-start | bytes 1572868
  61.7 33.8 %copy-start.7 = (bf16[128,2048]{1,0:T(8,128)(2,1)S(1)}, bf16[128,2048]{1,0:T(8,128)(2,1)}, u32[]{:S(2)}) copy-start(bf16[128,2048]{1,0:T(8,128)(2,1)} %refs_10_.3) | copy-start | bytes 1572868
  78.6 10.9 %collective-permute-start.9 = (f32[672,128]{1,0:T(8,128)S(1)}, f32[672,128]{1,0:T(8,128)S(1)}, u32[]{:S(2)}, u32[]{:S(2)}) collective-permute-start(f32[672,128]{1,0:T(8,128)S(1)} %bitcast.9), channel_id=1, source_target_pairs={{0,16},{4,20},{8,24},{12,28},{16,0},{20,4},{24,8},{28,12},{32,48},... | collective-permute-start | bytes 1032200 | tf_op jit(solution)/shard_map/ppermute | solution.py:32
  80.5 15.0 %collective-permute-start.8 = (f32[672,128]{1,0:T(8,128)S(1)}, f32[672,128]{1,0:T(8,128)S(1)}, u32[]{:S(2)}, u32[]{:S(2)}) collective-permute-start(f32[672,128]{1,0:T(8,128)S(1)} %bitcast.10), channel_id=1, source_target_pairs={{0,496},{4,500},{8,504},{12,508},{16,32},{20,36},{24,40},{28,44},{... | collective-permute-start | bytes 1032200 | tf_op jit(solution)/shard_map/ppermute | solution.py:32
  99.7 15.0 %collective-permute-start.14 = (bf16[128,1024]{1,0:T(8,128)(2,1)S(1)}, bf16[128,1024]{1,0:T(8,128)(2,1)S(1)}, u32[]{:S(2)}, u32[]{:S(2)}) collective-permute-start(bf16[128,1024]{1,0:T(8,128)(2,1)S(1)} %get-tuple-element.24.refs_0_), channel_id=1, source_target_pairs={{0,2},{1,3},{2,0},{3,1},{4,6},{5,7},{6,4},{7,5},{8,10},{9,11},{10,... | collective-permute-start | bytes 786440 | tf_op jit(solution)/shard_map/ppermute | solution.py:37
  106.8 12.3 %collective-permute-start.11 = (bf16[128,1024]{1,0:T(8,128)(2,1)S(1)}, bf16[128,1024]{1,0:T(8,128)(2,1)S(1)}, u32[]{:S(2)}, u32[]{:S(2)}) collective-permute-start(bf16[128,1024]{1,0:T(8,128)(2,1)S(1)} %get-tuple-element.23.refs_0_), channel_id=1, source_target_pairs={{0,2},{1,3},{2,0},{3,1},{4,6},{5,7},{6,4},{7,5},{8,10},{9,11},{10,... | collective-permute-start | bytes 786440 | tf_op jit(solution)/shard_map/ppermute | solution.py:37
  109.3 11.8 %collective-permute-start.13 = (bf16[128,1024]{1,0:T(8,128)(2,1)S(1)}, bf16[128,1024]{1,0:T(8,128)(2,1)S(1)}, u32[]{:S(2)}, u32[]{:S(2)}) collective-permute-start(bf16[128,1024]{1,0:T(8,128)(2,1)S(1)} %get-tuple-element.24.refs_0_), channel_id=1, source_target_pairs={{0,1},{1,0},{2,3},{3,2},{4,5},{5,4},{6,7},{7,6},{8,9},{9,8},{10,11... | collective-permute-start | bytes 786440 | tf_op jit(solution)/shard_map/ppermute | solution.py:37
  114.7 6.3 %collective-permute-start.15 = (bf16[128,1024]{1,0:T(8,128)(2,1)S(1)}, bf16[128,1024]{1,0:T(8,128)(2,1)S(1)}, u32[]{:S(2)}, u32[]{:S(2)}) collective-permute-start(bf16[128,1024]{1,0:T(8,128)(2,1)S(1)} %collective-permute-done.14.refs_2_), channel_id=1, source_target_pairs={{0,1},{1,0},{2,3},{3,2},{4,5},{5,4},{6,7},{7,6},{8,9},{9,8},{10,11... | collective-permute-start | bytes 786440 | tf_op jit(solution)/shard_map/ppermute | solution.py:37
  116.7 6.4 %collective-permute-start.10 = (bf16[128,1024]{1,0:T(8,128)(2,1)S(1)}, bf16[128,1024]{1,0:T(8,128)(2,1)S(1)}, u32[]{:S(2)}, u32[]{:S(2)}) collective-permute-start(bf16[128,1024]{1,0:T(8,128)(2,1)S(1)} %get-tuple-element.23.refs_0_), channel_id=1, source_target_pairs={{0,1},{1,0},{2,3},{3,2},{4,5},{5,4},{6,7},{7,6},{8,9},{9,8},{10,11... | collective-permute-start | bytes 786440 | tf_op jit(solution)/shard_map/ppermute | solution.py:37
  119.1 4.0 %collective-permute-start.12 = (bf16[128,1024]{1,0:T(8,128)(2,1)S(1)}, bf16[128,1024]{1,0:T(8,128)(2,1)S(1)}, u32[]{:S(2)}, u32[]{:S(2)}) collective-permute-start(bf16[128,1024]{1,0:T(8,128)(2,1)S(1)} %collective-permute-done.11.refs_2_), channel_id=1, source_target_pairs={{0,1},{1,0},{2,3},{3,2},{4,5},{5,4},{6,7},{7,6},{8,9},{9,8},{10,11... | collective-permute-start | bytes 786440 | tf_op jit(solution)/shard_map/ppermute | solution.py:37
